TPU v7x, 32 devices: a whole 2x2x4 slice. The times are simulated.
32 devices in a mesh: depth: 4 (over y, x), dp: 8 (over z, core).
Axes of the slice: x: 2, y: 2, z: 4, core: 2. Of those that a mesh axis runs over, the one named last changes fastest.
Arguments:
- object_slices: float32 [4, 2, 768, 768], P('depth'), may hold values from -1.02 to 1.02, as said below
- positions: int32 [16, 2], P('dp'), may hold values from 0 to 640, as said below
- probe_field: float32 [2, 128, 128], replicated, may hold values from -6 to 6
- propagator_phase: float32 [128, 128], replicated, may hold values from -3.140625 to 3.140625
- measured: float32 [16, 128, 128], P('dp'), may hold values from 0.5 to 4
Outputs:
- slice_gradient: float32 [4, 2, 768, 768], P('depth', None, 'dp')
Inputs may be any that keep to these rules, and one draw needn't show every extreme that they name: `object_slices`: every complex entry has magnitude between exp(-0.03) and exp(0.01). `positions`: each window lies inside the object; some window touches the last row and some the last column.
All inputs are finite; a program needn't handle non-finite values.
Results may differ from a plain program's by a relative error of at most 0.034.
Values may be sent and summed in bfloat16 or wider, within the bound.
No kernel may reach another device: no remote copies, remote signals or barrier semaphores. Data moves between devices by JAX's collectives and lax.ppermute only.
A program may use at most 64 MiB of HBM per device.

v0:
```python
import math

import jax
import jax.numpy as jnp
from jax import lax
from jax.sharding import PartitionSpec as P

grad_scale = 0.03125


def passed_along(block, axis, distance):
    devices = range(lax.axis_size(axis))
    route = [(i - distance, i) for i in devices if i - distance in devices]
    return lax.ppermute(block, axis, route)


def dft_tables(size):
    indices = jnp.arange(size, dtype=jnp.int32)
    folded = indices[:, None] * indices[None, :] % size
    angles = folded.astype(jnp.float32) * (2.0 * math.pi / size)
    norm_factor = 1.0 / math.sqrt(size)
    return jnp.stack([jnp.cos(angles) * norm_factor, jnp.sin(angles) * norm_factor])


def combine(result, sign_value):
    return jnp.stack(
        [
            result[:, 0, 0] - sign_value * result[:, 1, 1],
            result[:, 0, 1] + sign_value * result[:, 1, 0],
        ],
        axis=1,
    )


def along_rows(field_in, tables, sign_value):
    result = jnp.einsum("tjk,mckl->mtcjl", tables, field_in, precision=lax.Precision.HIGHEST)
    return combine(result, sign_value)


def along_cols(field_in, tables, sign_value):
    result = jnp.einsum("mckl,tlj->mtckj", field_in, tables, precision=lax.Precision.HIGHEST)
    return combine(result, sign_value)


def transform(field_in, tables, sign_value):
    return along_cols(along_rows(field_in, tables, sign_value), tables, sign_value)


def complex_mul(left, right, conj_left):
    if conj_left:
        return jnp.stack(
            [
                left[:, 0] * right[:, 0] + left[:, 1] * right[:, 1],
                left[:, 0] * right[:, 1] - left[:, 1] * right[:, 0],
            ],
            axis=1,
        )
    return jnp.stack(
        [
            left[:, 0] * right[:, 0] - left[:, 1] * right[:, 1],
            left[:, 0] * right[:, 1] + left[:, 1] * right[:, 0],
        ],
        axis=1,
    )


def propagate(field_in, kernel, tables):
    spectrum = transform(field_in, tables, -1.0)
    spectrum = complex_mul(spectrum, kernel[None], False)
    return transform(spectrum, tables, 1.0)


def far_field(exit_wave, measured, tables):
    spectrum = transform(exit_wave, tables, -1.0)
    intensity = spectrum[:, 0] * spectrum[:, 0] + spectrum[:, 1] * spectrum[:, 1]
    residue = intensity - measured
    return transform(2.0 * residue[:, None] * spectrum, tables, 1.0)


def windows(layer_field, offsets, window):

    def pick(row_off, col_off):
        return lax.dynamic_slice(layer_field, (0, row_off, col_off), (2, window, window))

    return jax.vmap(pick)(offsets[:, 0], offsets[:, 1])


def add_windows(layer_grad, contrib, offsets, window):
    for member in range(contrib.shape[0]):
        row_off = offsets[member, 0]
        col_off = offsets[member, 1]
        current = lax.dynamic_slice(layer_grad, (0, row_off, col_off), (2, window, window))
        layer_grad = lax.dynamic_update_slice(
            layer_grad, current + contrib[member], (0, row_off, col_off)
        )
    return layer_grad


def on_device(object_slices, positions, probe_field, propagator_phase, measured):
    depth_count = lax.axis_size("depth")
    depth_index = lax.axis_index("depth")
    layers = object_slices.shape[0]
    pos_count = positions.shape[0]
    window = probe_field.shape[-1]
    groups = pos_count // 2
    batch_size = pos_count // groups
    tables = dft_tables(window)
    kernel = jnp.stack([jnp.cos(propagator_phase), jnp.sin(propagator_phase)])
    conj_kernel = jnp.stack([jnp.cos(propagator_phase), -jnp.sin(propagator_phase)])
    grouped_offsets = positions.reshape(groups, batch_size, 2)
    grouped_measured = measured.reshape(groups, batch_size, window, window)
    start_wave = jnp.broadcast_to(probe_field, (batch_size, 2, window, window))
    sections = depth_count + groups - 1

    def forward_section(step_index, carry):
        group_no = step_index - depth_index
        active = (group_no >= 0) & (group_no < groups)
        slot_no = jnp.clip(group_no, 0, groups - 1)

        def forward_advance(state):
            incoming, stored_waves, exit_waves = state
            current = jnp.where(depth_index == 0, start_wave, incoming.astype(jnp.float32))
            offsets = lax.dynamic_index_in_dim(grouped_offsets, slot_no, 0, keepdims=False)
            kept = [current]
            transmit = windows(object_slices[0], offsets, window)
            current = propagate(complex_mul(transmit, current, False), kernel, tables)
            stored_waves = lax.dynamic_update_index_in_dim(
                stored_waves, jnp.stack(kept), slot_no, 0
            )
            exit_waves = lax.dynamic_update_index_in_dim(exit_waves, current, slot_no, 0)
            return (current.astype(jnp.bfloat16), stored_waves, exit_waves)

        def forward_passive(state):
            return (jnp.zeros_like(state[0]), state[1], state[2])

        outgoing, stored_waves, exit_waves = lax.cond(
            active, forward_advance, forward_passive, carry
        )
        incoming = passed_along(outgoing, "depth", 1)
        return (incoming, stored_waves, exit_waves)

    empty_wave = jnp.zeros((batch_size, 2, window, window), jnp.bfloat16)
    initial = (
        empty_wave,
        jnp.zeros((groups, layers, batch_size, 2, window, window), jnp.float32),
        jnp.zeros((groups, batch_size, 2, window, window), jnp.float32),
    )
    unused, stored_waves, exit_waves = lax.fori_loop(0, sections, forward_section, initial)

    def backward_section(step_index, carry):
        group_no = step_index - (depth_count - 1 - depth_index)
        active = (group_no >= 0) & (group_no < groups)
        slot_no = jnp.clip(group_no, 0, groups - 1)

        def backward_advance(state):
            incoming, layer_grads = state
            offsets = lax.dynamic_index_in_dim(grouped_offsets, slot_no, 0, keepdims=False)
            exit_now = lax.dynamic_index_in_dim(exit_waves, slot_no, 0, keepdims=False)
            measured_now = lax.dynamic_index_in_dim(grouped_measured, slot_no, 0, keepdims=False)
            adjoint = lax.cond(
                depth_index == depth_count - 1,
                lambda: far_field(exit_now, measured_now, tables),
                lambda: incoming.astype(jnp.float32),
            )
            kept = lax.dynamic_index_in_dim(stored_waves, slot_no, 0, keepdims=False)
            for layer_no in reversed(range(layers)):
                returned = propagate(adjoint, conj_kernel, tables)
                transmit = windows(object_slices[layer_no], offsets, window)
                contrib = complex_mul(kept[layer_no], returned, True)
                layer_grads = layer_grads.at[layer_no].set(
                    add_windows(layer_grads[layer_no], contrib, offsets, window)
                )
                adjoint = complex_mul(transmit, returned, True)
            return (adjoint.astype(jnp.bfloat16), layer_grads)

        def backward_passive(state):
            return (jnp.zeros_like(state[0]), state[1])

        outgoing, layer_grads = lax.cond(active, backward_advance, backward_passive, carry)
        incoming = passed_along(outgoing, "depth", -1)
        return (incoming, layer_grads)

    grad_init = jnp.zeros(object_slices.shape, jnp.float32)
    unused_wave, layer_grads = lax.fori_loop(0, sections, backward_section, (empty_wave, grad_init))
    return lax.psum_scatter(layer_grads * grad_scale, "dp", scatter_dimension=2, tiled=True)


def solution(mesh):
    placed = (P("depth", None, None, None), P("dp", None), P(), P(), P("dp", None, None))
    return jax.shard_map(
        on_device,
        mesh=mesh,
        in_specs=placed,
        out_specs=P("depth", None, "dp", None),
        check_vma=False,
    )
```

profile of v0, /device:TPU:0, one launch (start us, length us, event | category | flops | bytes accessed | tf_op | source)
XLA Modules:
  0.0 278.7 jit_solution(14333823702528235216)
XLA Ops:
  10.2 55.1 %while.46 = (s32[]{:T(128)}, bf16[2,2,128,128]{3,2,0,1:T(8,128)(2,1)S(1)}, f32[1,1,2,2,128,128]{4,5,3,2,1,0:T(8,128)S(1)}, f32[1,2,2,128,128]{4,3,1,2,0:T(8,128)...) while((s32[]{:T(128)}, ...), condition=%wide.region_3.4_spmd.clone, body=%wide.region_0.3_spmd.clone.sunk | while | flops 806748160 | bytes 11534903 | solution.py:148
  10.2 10.1 %conditional.7 = (bf16[2,2,128,128]{3,2,0,1:T(8,128)(2,1)S(1)}, f32[1,1,2,2,128,128]{4,5,3,2,1,0:T(8,128)S(1)}, f32[1,2,2,128,128]{4,3,1,2,0:T(8,128)S(1)}) conditional(s32[]{:T(128)} %convert_element_type.64, (f32[1,1,2,2,128,128]{4,5,3,2,1,0:T(8,128)S(1)}, f32[1,2,2,128,128]{4,3,1,2,0:T(8,128)S(1)}) %tuple.147, (f32[1,2,768,768]{3,2,1,0:T(8,128)}, ...), branch_computations={%region_1.1_spmd, %region_2.2_spmd} | conditional | flops 806748160 | bytes 11010348 | solution.py:136
  11.3 6.3 %while.44 = (s32[]{:T(128)}, f32[2,768,768]{2,1,0:T(8,128)}, s32[2,3]{1,0:T(2,128)S(1)}, f32[2,2,128,128]{2,3,1,0:T(8,128)S(1)}, s32[]{:T(128)}) while((s32[]{:T(128)}, f32[2,768,768]{2,1,0:T(8,128)}, s32[2,3]{1,0:T(2,128)S(1)}, f32[2,2,128,128]{2,3,1,0:T(8,128)S(1)}, s32[]{:T(128)}) %tuple.174), condition=%wide.while_cond.1, body=%wide.while_body.1.sunk | while | flops 2 | bytes 786557 | solution.py:83
  12.0 2.3 dynamic-slice_bitcast_fusion.2
  15.2 2.3 dynamic-slice_bitcast_fusion.2
  21.6 3.6 %collective-permute-done = bf16[2,2,128,128]{3,2,0,1:T(8,128)(2,1)S(1)} collective-permute-done((bf16[2,2,128,128]{3,2,0,1:T(8,128)(2,1)S(1)}, bf16[2,2,128,128]{3,2,0,1:T(8,128)(2,1)S(1)}, u32[]{:S(2)}, u32[]{:S(2)}) %collective-permute-start) | collective-permute-done | bytes 131104 | tf_op jit(solution)/shard_map/while/body/eval_jaxpr/ppermute | solution.py:14
  25.3 14.5 %collective-permute-start = (bf16[2,2,128,128]{3,2,0,1:T(8,128)(2,1)S(1)}, bf16[2,2,128,128]{3,2,0,1:T(8,128)(2,1)S(1)}, u32[]{:S(2)}, u32[]{:S(2)}) collective-permute-start(bf16[2,2,128,128]{3,2,0,1:T(8,128)(2,1)S(1)} %get-tuple-element.913), channel_id=1, source_target_pairs={{0,8},{8,16},{16,24},{1,9},{9,17},{17,25},{2,10},{10,18},{18,26},{... | collective-permute-start | bytes 393224 | tf_op jit(solution)/shard_map/while/body/eval_jaxpr/ppermute | solution.py:14
  39.8 2.8 collective-permute-done
  42.6 4.4 %collective-permute-start = (bf16[2,2,128,128]{3,2,0,1:T(8,128)(2,1)S(1)}, bf16[2,2,128,128]{3,2,0,1:T(8,128)(2,1)S(1)}, u32[]{:S(2)}, u32[]{:S(2)}) collective-permute-start(bf16[2,2,128,128]{3,2,0,1:T(8,128)(2,1)S(1)} %get-tuple-element.913), channel_id=1, source_target_pairs={{0,8},{8,16},{16,24},{1,9},{9,17},{17,25},{2,10},{10,18},{18,26},{... | collective-permute-start | bytes 393224 | tf_op jit(solution)/shard_map/while/body/eval_jaxpr/ppermute | solution.py:14
  47.0 2.5 collective-permute-done
  49.6 13.2 %collective-permute-start = (bf16[2,2,128,128]{3,2,0,1:T(8,128)(2,1)S(1)}, bf16[2,2,128,128]{3,2,0,1:T(8,128)(2,1)S(1)}, u32[]{:S(2)}, u32[]{:S(2)}) collective-permute-start(bf16[2,2,128,128]{3,2,0,1:T(8,128)(2,1)S(1)} %get-tuple-element.913), channel_id=1, source_target_pairs={{0,8},{8,16},{16,24},{1,9},{9,17},{17,25},{2,10},{10,18},{18,26},{... | collective-permute-start | bytes 393224 | tf_op jit(solution)/shard_map/while/body/eval_jaxpr/ppermute | solution.py:14
  62.8 2.5 collective-permute-done
  65.5 2.5 broadcast_in_dim.37
  68.0 144.5 %while.45 = (s32[]{:T(128)}, bf16[2,2,128,128]{3,2,0,1:T(8,128)(2,1)S(1)}, f32[1,2,768,768]{3,2,1,0:T(8,128)}, s32[]{:T(128)}, f32[1,2,768,768]{3,2,1,0:T(8,128)...) while((s32[]{:T(128)}, ...), condition=%wide.region_9.10_spmd, body=%wide.region_4.9_spmd.sunk | while | flops 1613070336 | bytes 19530540 | solution.py:184
  69.3 6.9 %collective-permute-done.1 = bf16[2,2,128,128]{3,2,0,1:T(8,128)(2,1)S(1)} collective-permute-done((bf16[2,2,128,128]{3,2,0,1:T(8,128)(2,1)S(1)}, bf16[2,2,128,128]{3,2,0,1:T(8,128)(2,1)S(1)}, u32[]{:S(2)}, u32[]{:S(2)}) %collective-permute-start.1) | collective-permute-done | bytes 131104 | tf_op jit(solution)/shard_map/while/body/eval_jaxpr/ppermute | solution.py:14
  77.6 12.8 %collective-permute-done.1 = bf16[2,2,128,128]{3,2,0,1:T(8,128)(2,1)S(1)} collective-permute-done((bf16[2,2,128,128]{3,2,0,1:T(8,128)(2,1)S(1)}, bf16[2,2,128,128]{3,2,0,1:T(8,128)(2,1)S(1)}, u32[]{:S(2)}, u32[]{:S(2)}) %collective-permute-start.1) | collective-permute-done | bytes 131104 | tf_op jit(solution)/shard_map/while/body/eval_jaxpr/ppermute | solution.py:14
  91.7 87.4 %collective-permute-done.1 = bf16[2,2,128,128]{3,2,0,1:T(8,128)(2,1)S(1)} collective-permute-done((bf16[2,2,128,128]{3,2,0,1:T(8,128)(2,1)S(1)}, bf16[2,2,128,128]{3,2,0,1:T(8,128)(2,1)S(1)}, u32[]{:S(2)}, u32[]{:S(2)}) %collective-permute-start.1) | collective-permute-done | bytes 131104 | tf_op jit(solution)/shard_map/while/body/eval_jaxpr/ppermute | solution.py:14
  179.1 26.5 %conditional.6 = (bf16[2,2,128,128]{3,2,0,1:T(8,128)(2,1)S(1)}, f32[1,2,768,768]{3,2,1,0:T(8,128)}) conditional(s32[]{:T(128)} %convert_element_type.63, f32[1,2,768,768]{3,2,1,0:T(8,128)} %get-tuple-element.1020, (f32[1,2,768,768]{3,2,1,0:T(8,128)}, s32[1,2,2]{2,1,0:T(2,128)S(1)}, s32[]{:T(128)}, bf16[2,2,128,128]{3,2,0,1:T(8,128)(2,1)S(1)}, ...), branch_computations={%region_5.5_spmd, %region_6.8_spmd} | conditional | flops 1613070336 | bytes 19005960 | solution.py:179
  190.1 5.9 %while.43 = (s32[]{:T(128)}, f32[2,768,768]{2,1,0:T(8,128)}, s32[2,3]{1,0:T(2,128)S(1)}, f32[2,2,128,128]{3,2,0,1:T(8,128)S(1)}, s32[]{:T(128)}) while((s32[]{:T(128)}, f32[2,768,768]{2,1,0:T(8,128)}, s32[2,3]{1,0:T(2,128)S(1)}, f32[2,2,128,128]{3,2,0,1:T(8,128)S(1)}, s32[]{:T(128)}) %tuple.176), condition=%wide.while_cond.2, body=%wide.while_body.2.sunk | while | flops 2 | bytes 262269 | solution.py:83
  197.2 3.7 %dynamic_update_slice.13 = f32[2,768,768]{2,1,0:T(8,128)} dynamic-update-slice(f32[2,768,768]{2,1,0:T(8,128)} %bitcast.359, f32[2,128,128]{2,1,0:T(8,128)S(1)} %fusion.66, s32[]{:T(128)} %constant.151.clone, s32[]{:T(128)S(6)} %select_n.77, s32[]{:T(128)S(6)} %select_n.78) | dynamic-update-slice | bytes 262148 | tf_op jit(solution)/shard_map/while/body/eval_jaxpr/cond/branch_1_fun/dynamic_update_slice | solution.py:93
  201.9 3.7 %dynamic_update_slice.14 = f32[1,2,768,768]{3,2,1,0:T(8,128)} dynamic-update-slice(f32[1,2,768,768]{3,2,1,0:T(8,128)} %bitcast.360, f32[1,2,128,128]{3,2,1,0:T(8,128)S(1)} %fusion.69, s32[]{:T(128)} %constant.151.clone, s32[]{:T(128)} %constant.151.clone, s32[]{:T(128)S(6)} %select_n.79, s32[]{:T(128)S(6)} %select_n.80) | dynamic-update-slice | bytes 262148 | tf_op jit(solution)/shard_map/while/body/eval_jaxpr/cond/branch_1_fun/dynamic_update_slice | solution.py:93
  206.9 5.6 %collective-permute-done.1 = bf16[2,2,128,128]{3,2,0,1:T(8,128)(2,1)S(1)} collective-permute-done((bf16[2,2,128,128]{3,2,0,1:T(8,128)(2,1)S(1)}, bf16[2,2,128,128]{3,2,0,1:T(8,128)(2,1)S(1)}, u32[]{:S(2)}, u32[]{:S(2)}) %collective-permute-start.1) | collective-permute-done | bytes 131104 | tf_op jit(solution)/shard_map/while/body/eval_jaxpr/ppermute | solution.py:14
  212.5 4.8 %broadcast_multiply_fusion = f32[1,2,768,768]{3,2,1,0:T(8,128)} fusion(f32[1,2,768,768]{3,2,1,0:T(8,128)} %get-tuple-element.546), kind=kLoop, calls=%fused_computation.177 | loop fusion | flops 1179648 | bytes 9437184 | tf_op jit(solution)/shard_map/mul | solution.py:185
  217.3 54.5 %reduce-scatter.2.cloned.1.call-done = f32[1,2,96,768]{3,2,1,0:T(8,128)} async-done(((f32[1,2,768,768]{3,2,1,0:T(8,128)}), f32[1,2,96,768]{3,2,1,0:T(8,128)}) %reduce-scatter.2.cloned.1.call-update) | async-done | bytes 589840 | tf_op jit(solution)/shard_map/reduce_scatter | solution.py:185
  (93 shorter events, 27.4 us)
Async XLA Ops:
  6.5 265.3 %reduce-scatter.2.cloned.1.call-start = ((), (), s32[]{:S(2)}) async-start(), calls=%async_computation.1 | async-start | bytes 5308416 | tf_op jit(solution)/shard_map/reduce_scatter | solution.py:185
  20.3 4.9 %collective-permute-start = (bf16[2,2,128,128]{3,2,0,1:T(8,128)(2,1)S(1)}, bf16[2,2,128,128]{3,2,0,1:T(8,128)(2,1)S(1)}, u32[]{:S(2)}, u32[]{:S(2)}) collective-permute-start(bf16[2,2,128,128]{3,2,0,1:T(8,128)(2,1)S(1)} %get-tuple-element.913), channel_id=1, source_target_pairs={{0,8},{8,16},{16,24},{1,9},{9,17},{17,25},{2,10},{10,18},{18,26},{... | collective-permute-start | bytes 393224 | tf_op jit(solution)/shard_map/while/body/eval_jaxpr/ppermute | solution.py:14
  25.3 17.3 %collective-permute-start = (bf16[2,2,128,128]{3,2,0,1:T(8,128)(2,1)S(1)}, bf16[2,2,128,128]{3,2,0,1:T(8,128)(2,1)S(1)}, u32[]{:S(2)}, u32[]{:S(2)}) collective-permute-start(bf16[2,2,128,128]{3,2,0,1:T(8,128)(2,1)S(1)} %get-tuple-element.913), channel_id=1, source_target_pairs={{0,8},{8,16},{16,24},{1,9},{9,17},{17,25},{2,10},{10,18},{18,26},{... | collective-permute-start | bytes 393224 | tf_op jit(solution)/shard_map/while/body/eval_jaxpr/ppermute | solution.py:14
  42.6 6.9 %collective-permute-start = (bf16[2,2,128,128]{3,2,0,1:T(8,128)(2,1)S(1)}, bf16[2,2,128,128]{3,2,0,1:T(8,128)(2,1)S(1)}, u32[]{:S(2)}, u32[]{:S(2)}) collective-permute-start(bf16[2,2,128,128]{3,2,0,1:T(8,128)(2,1)S(1)} %get-tuple-element.913), channel_id=1, source_target_pairs={{0,8},{8,16},{16,24},{1,9},{9,17},{17,25},{2,10},{10,18},{18,26},{... | collective-permute-start | bytes 393224 | tf_op jit(solution)/shard_map/while/body/eval_jaxpr/ppermute | solution.py:14
  49.6 15.7 %collective-permute-start = (bf16[2,2,128,128]{3,2,0,1:T(8,128)(2,1)S(1)}, bf16[2,2,128,128]{3,2,0,1:T(8,128)(2,1)S(1)}, u32[]{:S(2)}, u32[]{:S(2)}) collective-permute-start(bf16[2,2,128,128]{3,2,0,1:T(8,128)(2,1)S(1)} %get-tuple-element.913), channel_id=1, source_target_pairs={{0,8},{8,16},{16,24},{1,9},{9,17},{17,25},{2,10},{10,18},{18,26},{... | collective-permute-start | bytes 393224 | tf_op jit(solution)/shard_map/while/body/eval_jaxpr/ppermute | solution.py:14
  65.2 2.8 copy-start
  68.0 8.2 %collective-permute-start.1 = (bf16[2,2,128,128]{3,2,0,1:T(8,128)(2,1)S(1)}, bf16[2,2,128,128]{3,2,0,1:T(8,128)(2,1)S(1)}, u32[]{:S(2)}, u32[]{:S(2)}) collective-permute-start(bf16[2,2,128,128]{3,2,0,1:T(8,128)(2,1)S(1)} %get-tuple-element.901), channel_id=1, source_target_pairs={{8,0},{16,8},{24,16},{9,1},{17,9},{25,17},{10,2},{18,10},{26,18},{... | collective-permute-start | bytes 393224 | tf_op jit(solution)/shard_map/while/body/eval_jaxpr/ppermute | solution.py:14
  76.3 14.1 %collective-permute-start.1 = (bf16[2,2,128,128]{3,2,0,1:T(8,128)(2,1)S(1)}, bf16[2,2,128,128]{3,2,0,1:T(8,128)(2,1)S(1)}, u32[]{:S(2)}, u32[]{:S(2)}) collective-permute-start(bf16[2,2,128,128]{3,2,0,1:T(8,128)(2,1)S(1)} %get-tuple-element.901), channel_id=1, source_target_pairs={{8,0},{16,8},{24,16},{9,1},{17,9},{25,17},{10,2},{18,10},{26,18},{... | collective-permute-start | bytes 393224 | tf_op jit(solution)/shard_map/while/body/eval_jaxpr/ppermute | solution.py:14
  90.4 88.7 %collective-permute-start.1 = (bf16[2,2,128,128]{3,2,0,1:T(8,128)(2,1)S(1)}, bf16[2,2,128,128]{3,2,0,1:T(8,128)(2,1)S(1)}, u32[]{:S(2)}, u32[]{:S(2)}) collective-permute-start(bf16[2,2,128,128]{3,2,0,1:T(8,128)(2,1)S(1)} %get-tuple-element.901), channel_id=1, source_target_pairs={{8,0},{16,8},{24,16},{9,1},{17,9},{25,17},{10,2},{18,10},{26,18},{... | collective-permute-start | bytes 393224 | tf_op jit(solution)/shard_map/while/body/eval_jaxpr/ppermute | solution.py:14
  205.7 6.8 %collective-permute-start.1 = (bf16[2,2,128,128]{3,2,0,1:T(8,128)(2,1)S(1)}, bf16[2,2,128,128]{3,2,0,1:T(8,128)(2,1)S(1)}, u32[]{:S(2)}, u32[]{:S(2)}) collective-permute-start(bf16[2,2,128,128]{3,2,0,1:T(8,128)(2,1)S(1)} %get-tuple-element.901), channel_id=1, source_target_pairs={{8,0},{16,8},{24,16},{9,1},{17,9},{25,17},{10,2},{18,10},{26,18},{... | collective-permute-start | bytes 393224 | tf_op jit(solution)/shard_map/while/body/eval_jaxpr/ppermute | solution.py:14
Sparse Core Ops, SparseCore 0:
  217.5 54.3 reduce-scatter.1
where the time goes:
time: 279 us
  waiting for transfers between devices  179 us (64%)
  starting transfers between devices  38.5 us (14%)
  local copies, waits for them, and re-layouts  26.3 us (9%)
  between operations  13.5 us (5%)
  other arithmetic  8.88 us (3%)
  loops' own time  8.14 us (3%)
  matrix products  4.84 us (2%)
    ppermute x8, waiting for transfers between devices, passed_along(): return lax.ppermute(block, axis, route)  124 us
    reduce_scatter x1, waiting for transfers between devices, on_device(): lax.psum_scatter(layer_grads * grad_scale, 'dp', scatter_dimension=2, til...  54.5 us
    ppermute x8, starting transfers between devices, passed_along(): return lax.ppermute(block, axis, route)  38.5 us
    gather x16, local copies, waits for them, and re-layouts  12 us
    another operation x4, loops' own time, backward_section(): lax.cond(active, backward_advance, backward_passive, carry)  7.6 us
    dynamic_update_slice x2, local copies, waits for them, and re-layouts, add_windows(): lax.dynamic_update_slice(layer_grad, current + contrib[member], (0, row_o...  7.4 us
  transfers between devices with their start and end apart: 9, of which 9 were waited for; matrix products, arithmetic and copies ran while one was open for 0% of the time, Pallas kernels for 0%

commit v1 on v0

v1 whole, which is shorter than its diff:
```python
import functools
import math

import jax
import jax.numpy as jnp
import numpy as np
from jax import lax
from jax.experimental import pallas as pl
from jax.experimental.pallas import tpu as pltpu
from jax.sharding import PartitionSpec as P

grad_scale = 0.03125
f32 = jnp.float32
bf16 = jnp.bfloat16


def dft_matrices(size):
    k = np.arange(size)
    angles = 2.0 * np.pi * ((k[:, None] * k[None, :]) % size) / size
    c = np.cos(angles) / math.sqrt(size)
    s = np.sin(angles) / math.sqrt(size)
    plus = np.block([[c, s], [-s, c]]).astype(np.float32)
    minus = np.block([[c, -s], [s, c]]).astype(np.float32)
    parts = []
    for full in (plus, minus):
        high = full.astype(bf16)
        low = (full - high.astype(np.float32)).astype(bf16)
        parts.append((high, low))
    (ph, plo), (mh, mlo) = parts
    right = np.stack([np.concatenate([ph, ph, plo], 0), np.concatenate([mh, mh, mlo], 0)])
    left = np.stack([np.concatenate([mh, mh, mlo], 1), np.concatenate([ph, ph, plo], 1)])
    return left, right


def window_kernel(pos_ref, obj_ref, out_ref, buf, sems):
    count, _, window, _ = out_ref.shape
    rows, cols = obj_ref.shape[-2:]
    tall, wide = buf.shape[-2:]

    def corner(p):
        row_base = jnp.minimum(pos_ref[p, 0] // 8, (rows - tall) // 8) * 8
        col_base = jnp.minimum(pos_ref[p, 1] // 128, (cols - wide) // 128) * 128
        return pl.multiple_of(row_base, 8), pl.multiple_of(col_base, 128)

    def copy(p):
        row_base, col_base = corner(p)
        return pltpu.make_async_copy(
            obj_ref.at[:, pl.ds(row_base, tall), pl.ds(col_base, wide)], buf.at[p], sems.at[p]
        )

    for p in range(count):
        copy(p).start()
    for p in range(count):
        copy(p).wait()
        row_base, col_base = corner(p)
        row_off = pos_ref[p, 0] - row_base
        col_off = pos_ref[p, 1] - col_base
        lift = jnp.where(row_off == 0, 0, tall - row_off)
        shift = jnp.where(col_off == 0, 0, wide - col_off)
        for part in range(2):
            block = pltpu.roll(buf[p, part], lift, 0)[:window]
            block = pltpu.roll(block, shift, 1)
            out_ref[p, part] = block[:, :window].astype(out_ref.dtype)


def take_windows(obj, positions, window):
    count = positions.shape[0]
    tall, wide = window + 8, window + 128
    return pl.pallas_call(
        window_kernel,
        out_shape=jax.ShapeDtypeStruct((count, 2, window, window), bf16),
        in_specs=[pl.BlockSpec(memory_space=pltpu.SMEM), pl.BlockSpec(memory_space=pl.ANY)],
        out_specs=pl.BlockSpec(memory_space=pltpu.VMEM),
        scratch_shapes=[
            pltpu.VMEM((count, 2, tall, wide), f32),
            pltpu.SemaphoreType.DMA((count,)),
        ],
        name="take_windows",
    )(positions, obj)


def split(x):
    high = x.astype(bf16)
    return high, (x - high.astype(f32)).astype(bf16)


def cmul(a, b):
    return a[0] * b[0] - a[1] * b[1], a[0] * b[1] + a[1] * b[0]


def cmul_conj(a, b):
    return a[0] * b[0] + a[1] * b[1], a[0] * b[1] - a[1] * b[0]


def wave_kernel(meta_ref, probe_ref, kern_ref, meas_ref, left_ref, right_ref, *rest):
    t_refs, (out_ref, waves) = rest[:-2], rest[-2:]
    slices = len(t_refs)
    count, _, window, _ = out_ref.shape
    own = meta_ref[0]

    def t_of(k, p):
        def pick(m):
            return lambda: (t_refs[m][p, 0], t_refs[m][p, 1])

        return tuple(x.astype(f32) for x in lax.switch(own ^ k, [pick(m) for m in range(slices)]))

    def rows(fields, sign):
        x = jnp.concatenate(
            [jnp.concatenate([f[0], f[1]], axis=0) for f in fields], axis=1
        )
        high, low = split(x)
        y = jnp.dot(
            left_ref[sign], jnp.concatenate([high, low, high], axis=0), preferred_element_type=f32
        )
        return [
            (y[:window, p * window : (p + 1) * window], y[window:, p * window : (p + 1) * window])
            for p in range(len(fields))
        ]

    def cols(fields, sign):
        x = jnp.concatenate(
            [jnp.concatenate([f[0], f[1]], axis=1) for f in fields], axis=0
        )
        high, low = split(x)
        y = jnp.dot(
            jnp.concatenate([high, low, high], axis=1), right_ref[sign], preferred_element_type=f32
        )
        return [
            (y[p * window : (p + 1) * window, :window], y[p * window : (p + 1) * window, window:])
            for p in range(len(fields))
        ]

    plus, minus = 0, 1

    def transform(fields, sign):
        return cols(rows(fields, sign), sign)

    kern = (kern_ref[0], kern_ref[1])
    probe = (probe_ref[0], probe_ref[1])
    psi = [probe] * count
    spectrum = None
    for k in range(slices):

        @pl.when(own == k)
        def _():
            for p in range(count):
                waves[p, 0] = psi[p][0]
                waves[p, 1] = psi[p][1]

        spectrum = transform([cmul(t_of(k, p), psi[p]) for p in range(count)], minus)
        if k < slices - 1:
            psi = transform([cmul(kern, s) for s in spectrum], plus)

    def source(p):
        re, im = spectrum[p]
        scale = 2.0 * (re * re + im * im - meas_ref[p])
        return scale * re, scale * im

    returned = transform([source(p) for p in range(count)], plus)
    for k in reversed(range(slices)):

        @pl.when(own == k)
        def _():
            for p in range(count):
                re, im = cmul_conj((waves[p, 0], waves[p, 1]), returned[p])
                out_ref[p, 0] = (re * grad_scale).astype(out_ref.dtype)
                out_ref[p, 1] = (im * grad_scale).astype(out_ref.dtype)

        if k > 0:
            chi = [cmul_conj(t_of(k, p), returned[p]) for p in range(count)]
            spectrum = transform(chi, minus)
            returned = transform([cmul_conj(kern, s) for s in spectrum], plus)


def run_waves(depth_index, probe, kern, measured, gathered):
    count, _, window, _ = gathered[0].shape
    left, right = dft_matrices(window)
    vmem = pl.BlockSpec(memory_space=pltpu.VMEM)
    return pl.pallas_call(
        wave_kernel,
        out_shape=jax.ShapeDtypeStruct((count, 2, window, window), bf16),
        in_specs=[pl.BlockSpec(memory_space=pltpu.SMEM)] + [vmem] * (5 + len(gathered)),
        out_specs=vmem,
        scratch_shapes=[pltpu.VMEM((count, 2, window, window), f32)],
        compiler_params=pltpu.CompilerParams(vmem_limit_bytes=32 * 1024 * 1024),
        name="run_waves",
    )(depth_index, probe, kern, measured, jnp.asarray(left), jnp.asarray(right), *gathered)


def place_kernel(pos_ref, meta_ref, terms_ref, out_ref, canvas):
    count, _, window, _ = terms_ref.shape
    _, stripe, cols = out_ref.shape
    wide = window + 128
    canvas[:, window : window + stripe, :] = jnp.zeros((2, stripe, canvas.shape[2]), f32)
    first_row = meta_ref[0] * stripe

    def body(p, carry):
        row = pos_ref[p, 0] - first_row + window
        col = pos_ref[p, 1]
        row_base = pl.multiple_of(row // 8 * 8, 8)
        col_base = pl.multiple_of(col // 128 * 128, 128)

        @pl.when((row > 0) & (row < window + stripe))
        def _():
            for part in range(2):
                block = terms_ref[p, part].astype(f32)
                block = jnp.concatenate([block, jnp.zeros((window, 128), f32)], axis=1)
                block = pltpu.roll(block, col - col_base, 1)
                block = jnp.concatenate([block, jnp.zeros((8, wide), f32)], axis=0)
                block = pltpu.roll(block, row - row_base, 0)
                at = (part, pl.ds(row_base, window + 8), pl.ds(col_base, wide))
                canvas[at] = canvas[at] + block

        return carry

    lax.fori_loop(0, count, body, 0)
    out_ref[...] = canvas[:, window : window + stripe, :cols]


def place_windows(positions, dp_index, terms, stripe, cols):
    window = terms.shape[-1]
    vmem = pl.BlockSpec(memory_space=pltpu.VMEM)
    smem = pl.BlockSpec(memory_space=pltpu.SMEM)
    tall = window + (stripe + 7) // 8 * 8 + window + 8
    return pl.pallas_call(
        place_kernel,
        out_shape=jax.ShapeDtypeStruct((2, stripe, cols), f32),
        in_specs=[smem, smem, vmem],
        out_specs=vmem,
        scratch_shapes=[pltpu.VMEM((2, tall, cols + 128), f32)],
        compiler_params=pltpu.CompilerParams(vmem_limit_bytes=40 * 1024 * 1024),
        name="place_windows",
    )(positions, dp_index, terms)


def on_device(object_slices, positions, probe_field, propagator_phase, measured):
    depth_count = lax.axis_size("depth")
    depth_index = lax.axis_index("depth").astype(jnp.int32).reshape(1)
    dp_index = lax.axis_index("dp").astype(jnp.int32).reshape(1)
    window = probe_field.shape[-1]
    rows, cols = object_slices.shape[-2:]
    stripe = rows // lax.axis_size("dp")
    all_positions = lax.all_gather(positions, "dp", axis=0, tiled=True)
    kern = jnp.stack([jnp.cos(propagator_phase), jnp.sin(propagator_phase)])
    own = take_windows(object_slices[0], positions, window)
    gathered = [own] + [
        lax.ppermute(own, "depth", [(i, i ^ m) for i in range(depth_count)])
        for m in range(1, depth_count)
    ]
    terms = run_waves(depth_index, probe_field, kern, measured, gathered)
    all_terms = lax.all_gather(terms, "dp", axis=0, tiled=True)
    return place_windows(all_positions, dp_index, all_terms, stripe, cols)[None]


def solution(mesh):
    placed = (P("depth", None, None, None), P("dp", None), P(), P(), P("dp", None, None))
    return jax.shard_map(
        on_device,
        mesh=mesh,
        in_specs=placed,
        out_specs=P("depth", None, "dp", None),
        check_vma=False,
    )
```

time: 279 us -> 64.9 us (0.23)
  waiting for transfers between devices: 179 us -> 16.6 us
  starting transfers between devices: 38.5 us -> 4.64 us
  local copies, waits for them, and re-layouts: 26.3 us -> 2.38 us
  Pallas kernels: 0 us -> 15.6 us
  blocking collectives: 0 us -> 12 us
  other arithmetic: 8.88 us -> 0.01 us
  loops' own time: 8.14 us -> 0 us
  matrix products: 4.84 us -> 0 us
    ppermute x8 -> x3, waiting for transfers between devices: 124 us -> 5.85 us  [on_device(): lax.ppermute(own, 'depth', [(i, i ^ m) for i in range(depth_count)])]
    reduce_scatter x1 -> x0, waiting for transfers between devices: 54.5 us -> none  [on_device(): lax.psum_scatter(layer_grads * grad_scale, 'dp', scatter_dimension=2, til...]
    ppermute x8 -> x3, starting transfers between devices: 38.5 us -> 4.6 us  [on_device(): lax.ppermute(own, 'depth', [(i, i ^ m) for i in range(depth_count)])]
    pallas_call x0 -> x3, Pallas kernels: none -> 15.6 us  [the longest x1 10.2 us: run_waves(): pl.pallas_call(wave_kernel, out_shape=jax.ShapeDtypeStruct((count, 2, win...]
    all_gather x0 -> x1, blocking collectives: none -> 12 us  [on_device(): all_positions = lax.all_gather(positions, 'dp', axis=0, tiled=True)]
    gather x16 -> x0, local copies, waits for them, and re-layouts: 12 us -> none
    all_gather x0 -> x1, waiting for transfers between devices: none -> 10.7 us  [on_device(): all_terms = lax.all_gather(terms, 'dp', axis=0, tiled=True)]
    another operation x13 -> x0, loops' own time: 8.14 us -> none  [the longest x4 7.6 us: backward_section(): lax.cond(active, backward_advance, backward_passive, carry)]
  transfers between devices with their start and end apart: 9 -> 4, of which waited for: 9 -> 4; matrix products, arithmetic and copies ran while one was open for 0% -> 0% of each run, Pallas kernels for 0% -> 0%
where the time goes in v1:
time: 64.9 us; the launch traced here: 64.7 us
  waiting for transfers between devices  16.6 us (26%)
  Pallas kernels  15.6 us (24%)
  between operations  13.5 us (21%)
  blocking collectives  12 us (18%)
  starting transfers between devices  4.64 us (7%)
  local copies, waits for them, and re-layouts  2.38 us (4%)
    all_gather x1, blocking collectives, on_device(): all_positions = lax.all_gather(positions, 'dp', axis=0, tiled=True)  12 us
    all_gather x1, waiting for transfers between devices, on_device(): all_terms = lax.all_gather(terms, 'dp', axis=0, tiled=True)  10.7 us
    pallas_call x1, Pallas kernels, run_waves(): pl.pallas_call(wave_kernel, out_shape=jax.ShapeDtypeStruct((count, 2, win...  10.2 us
    ppermute x3, waiting for transfers between devices, on_device(): lax.ppermute(own, 'depth', [(i, i ^ m) for i in range(depth_count)])  5.85 us
    ppermute x3, starting transfers between devices, on_device(): lax.ppermute(own, 'depth', [(i, i ^ m) for i in range(depth_count)])  4.6 us
    pallas_call x1, Pallas kernels, take_windows(): pl.pallas_call(window_kernel, out_shape=jax.ShapeDtypeStruct((count, 2, w...  2.78 us
    pallas_call x1, Pallas kernels, place_windows(): pl.pallas_call(place_kernel, out_shape=jax.ShapeDtypeStruct((2, stripe, c...  2.63 us
    unnamed x16, local copies, waits for them, and re-layouts  2.15 us
  transfers between devices with their start and end apart: 4, of which 4 were waited for; matrix products, arithmetic and copies ran while one was open for 0% of the time, Pallas kernels for 0%

profile of v1, /device:TPU:0, one launch (start us, length us, event | category | flops | bytes accessed | tf_op | source)
XLA Modules:
  0.0 64.7 jit_solution(1056728281003828573)
XLA Ops:
  6.5 0.0 copy-start.4
  6.6 0.0 all-gather.3.cloned.1.call-start
  6.6 2.8 %take_windows.1.rest_0_ = bf16[2,2,128,128]{3,2,1,0:T(8,128)(2,1)} custom-call(s32[2,2]{1,0:T(2,128)} %pos_ref.1, f32[2,768,768]{2,1,0:T(8,128)} %bitcast.11), custom_call_target="tpu_custom_call" | custom-call | tf_op jit(solution)/shard_map/take_windows/pallas_call | solution.py:69
  9.4 4.0 %collective-permute-start.2 = (bf16[2,2,128,128]{3,2,1,0:T(8,128)(2,1)}, bf16[2,2,128,128]{3,2,1,0:T(8,128)(2,1)S(1)}, u32[]{:S(2)}, u32[]{:S(2)}) collective-permute-start(bf16[2,2,128,128]{3,2,1,0:T(8,128)(2,1)} %take_windows.1.rest_0_), channel_id=1, source_target_pairs={{0,24},{8,16},{16,8},{24,0},{1,25},{9,17},{17,9},{25,1},{2,26},{10... | collective-permute-start | bytes 393224 | tf_op jit(solution)/shard_map/ppermute | solution.py:247
  13.3 0.5 collective-permute-start.1
  13.9 0.1 collective-permute-start
  14.0 0.0 copy-done.6
  14.0 0.2 cosine_bitcast_fusion
  14.3 3.3 %collective-permute-done.2.rest_3_ = bf16[2,2,128,128]{3,2,1,0:T(8,128)(2,1)S(1)} collective-permute-done((bf16[2,2,128,128]{3,2,1,0:T(8,128)(2,1)}, bf16[2,2,128,128]{3,2,1,0:T(8,128)(2,1)S(1)}, u32[]{:S(2)}, u32[]{:S(2)}) %collective-permute-start.2) | collective-permute-done | bytes 131104 | tf_op jit(solution)/shard_map/ppermute | solution.py:247
  17.6 2.3 %collective-permute-done.1.rest_2_ = bf16[2,2,128,128]{3,2,1,0:T(8,128)(2,1)S(1)} collective-permute-done((bf16[2,2,128,128]{3,2,1,0:T(8,128)(2,1)}, bf16[2,2,128,128]{3,2,1,0:T(8,128)(2,1)S(1)}, u32[]{:S(2)}, u32[]{:S(2)}) %collective-permute-start.1) | collective-permute-done | bytes 131104 | tf_op jit(solution)/shard_map/ppermute | solution.py:247
  19.9 0.2 collective-permute-done.rest_1_
  20.1 0.0 copy-done.1
  20.1 0.0 copy-done.2
  20.1 0.0 copy-done.5
  20.1 0.0 copy-done.4
  20.1 0.0 copy-start.3
  20.1 0.9 %copy-done.3 = bf16[2,2,128,128]{3,2,1,0:T(8,128)(2,1)S(1)} copy-done((bf16[2,2,128,128]{3,2,1,0:T(8,128)(2,1)S(1)}, bf16[2,2,128,128]{3,2,1,0:T(8,128)(2,1)}, u32[]{:S(2)}) %copy-start.3) | copy-done | bytes 131096
  21.0 10.2 %run_waves.1 = bf16[2,2,128,128]{3,2,1,0:T(8,128)(2,1)} custom-call(s32[1]{0:T(128)} %bitcast.3.meta_ref, f32[2,128,128]{2,1,0:T(8,128)S(1)} %copy-done.4, f32[2,128,128]{2,1,0:T(8,128)S(1)} %pad_maximum_fusion.kern_ref, f32[2,128,128]{2,1,0:T(8,128)S(1)} %copy-done.5, bf16[2,256,768]{2,1,0:T(8,128)(2,1)S(1)} %copy-done.2, ...), custom_call_target="tpu_custom_call" | custom-call | tf_op jit(solution)/shard_map/run_waves/pallas_call | solution.py:179
  31.3 0.0 all-gather.3.cloned.1.call-update
  31.3 0.0 copy-done.7
  31.3 12.0 %all-gather = s32[8,2,2]{2,1,0:T(2,128)S(1)} all-gather(s32[1,2,2]{2,1,0:T(2,128)S(1)} %bitcast.12), channel_id=1, replica_groups=mesh['depth'=4,'dp'=8] {'dp'}, dimensions={0}, use_global_device_ids=true | all-gather | bytes 144 | tf_op jit(solution)/shard_map/all_gather | solution.py:243
  43.3 10.7 %all-gather.3.cloned.1.call-done.terms_ref = bf16[16,2,128,128]{3,2,1,0:T(8,128)(2,1)} async-done(((bf16[2,2,128,128]{3,2,1,0:T(8,128)(2,1)}), bf16[16,2,128,128]{3,2,1,0:T(8,128)(2,1)}) %all-gather.3.cloned.1.call-update) | async-done | bytes 1048592 | tf_op jit(solution)/shard_map/all_gather | solution.py:251
  54.0 1.2 %copy-done = bf16[16,2,128,128]{3,2,1,0:T(8,128)(2,1)S(1)} copy-done((bf16[16,2,128,128]{3,2,1,0:T(8,128)(2,1)S(1)}, bf16[16,2,128,128]{3,2,1,0:T(8,128)(2,1)}, u32[]{:S(2)}) %copy-start) | copy-done | bytes 1048600
  55.2 2.6 %place_windows.1 = f32[2,96,768]{2,1,0:T(8,128)} custom-call(s32[16,2]{1,0:T(8,128)S(1)} %bitcast.10, s32[1]{0:T(128)} %bitcast.2.meta_ref, bf16[16,2,128,128]{3,2,1,0:T(8,128)(2,1)S(1)} %copy-done), custom_call_target="tpu_custom_call" | custom-call | tf_op jit(solution)/shard_map/place_windows/pallas_call | solution.py:225
  (7 shorter events, 0.0 us)
Async XLA Ops:
  6.5 13.6 %copy-start.1 = (bf16[2,768,256]{2,1,0:T(8,128)(2,1)S(1)}, bf16[2,768,256]{2,1,0:T(8,128)(2,1)}, u32[]{:S(2)}) copy-start(bf16[2,768,256]{2,1,0:T(8,128)(2,1)} %constant.13.clone.right_ref) | copy-start | bytes 2359300
  6.5 13.6 %copy-start.2 = (bf16[2,256,768]{2,1,0:T(8,128)(2,1)S(1)}, bf16[2,256,768]{2,1,0:T(8,128)(2,1)}, u32[]{:S(2)}) copy-start(bf16[2,256,768]{2,1,0:T(8,128)(2,1)} %constant.12.clone.left_ref) | copy-start | bytes 2359300
  6.5 24.7 %copy-start.7 = (s32[2,2]{1,0:T(2,128)S(1)}, s32[2,2]{1,0:T(2,128)}, u32[]{:S(2)}) copy-start(s32[2,2]{1,0:T(2,128)} %pos_ref.1) | copy-start | bytes 52
  6.5 7.5 %copy-start.6 = (f32[128,128]{1,0:T(8,128)S(1)}, f32[128,128]{1,0:T(8,128)}, u32[]{:S(2)}) copy-start(f32[128,128]{1,0:T(8,128)} %param.10) | copy-start | bytes 196612
  6.5 13.6 %copy-start.5 = (f32[2,128,128]{2,1,0:T(8,128)S(1)}, f32[2,128,128]{2,1,0:T(8,128)}, u32[]{:S(2)}) copy-start(f32[2,128,128]{2,1,0:T(8,128)} %meas_ref.1) | copy-start | bytes 393220
  6.5 13.6 %copy-start.4 = (f32[2,128,128]{2,1,0:T(8,128)S(1)}, f32[2,128,128]{2,1,0:T(8,128)}, u32[]{:S(2)}) copy-start(f32[2,128,128]{2,1,0:T(8,128)} %probe_ref.1) | copy-start | bytes 393220
  6.6 47.4 %all-gather.3.cloned.1.call-start = ((), (), s32[]{:S(2)}) async-start(), calls=%async_computation | async-start | bytes 1179648 | tf_op jit(solution)/shard_map/all_gather | solution.py:251
  9.4 8.2 %collective-permute-start.2 = (bf16[2,2,128,128]{3,2,1,0:T(8,128)(2,1)}, bf16[2,2,128,128]{3,2,1,0:T(8,128)(2,1)S(1)}, u32[]{:S(2)}, u32[]{:S(2)}) collective-permute-start(bf16[2,2,128,128]{3,2,1,0:T(8,128)(2,1)} %take_windows.1.rest_0_), channel_id=1, source_target_pairs={{0,24},{8,16},{16,8},{24,0},{1,25},{9,17},{17,9},{25,1},{2,26},{10... | collective-permute-start | bytes 393224 | tf_op jit(solution)/shard_map/ppermute | solution.py:247
  13.3 6.5 %collective-permute-start.1 = (bf16[2,2,128,128]{3,2,1,0:T(8,128)(2,1)}, bf16[2,2,128,128]{3,2,1,0:T(8,128)(2,1)S(1)}, u32[]{:S(2)}, u32[]{:S(2)}) collective-permute-start(bf16[2,2,128,128]{3,2,1,0:T(8,128)(2,1)} %take_windows.1.rest_0_), channel_id=1, source_target_pairs={{0,16},{8,24},{16,0},{24,8},{1,17},{9,25},{17,1},{25,9},{2,18},{10... | collective-permute-start | bytes 393224 | tf_op jit(solution)/shard_map/ppermute | solution.py:247
  13.9 6.3 %collective-permute-start = (bf16[2,2,128,128]{3,2,1,0:T(8,128)(2,1)}, bf16[2,2,128,128]{3,2,1,0:T(8,128)(2,1)S(1)}, u32[]{:S(2)}, u32[]{:S(2)}) collective-permute-start(bf16[2,2,128,128]{3,2,1,0:T(8,128)(2,1)} %take_windows.1.rest_0_), channel_id=1, source_target_pairs={{0,8},{8,0},{16,24},{24,16},{1,9},{9,1},{17,25},{25,17},{2,10},{10... | collective-permute-start | bytes 393224 | tf_op jit(solution)/shard_map/ppermute | solution.py:247
  20.1 0.9 %copy-start.3 = (bf16[2,2,128,128]{3,2,1,0:T(8,128)(2,1)S(1)}, bf16[2,2,128,128]{3,2,1,0:T(8,128)(2,1)}, u32[]{:S(2)}) copy-start(bf16[2,2,128,128]{3,2,1,0:T(8,128)(2,1)} %take_windows.1.rest_0_) | copy-start | bytes 393220
  54.0 1.2 %copy-start = (bf16[16,2,128,128]{3,2,1,0:T(8,128)(2,1)S(1)}, bf16[16,2,128,128]{3,2,1,0:T(8,128)(2,1)}, u32[]{:S(2)}) copy-start(bf16[16,2,128,128]{3,2,1,0:T(8,128)(2,1)} %all-gather.3.cloned.1.call-done.terms_ref) | copy-start | bytes 3145732
Sparse Core Ops, SparseCore 0:
  31.4 22.5 all-gather.2

commit v2 on v1

--- a/solution.py
+++ b/solution.py
@@ -92,7 +92,7 @@
     return a[0] * b[0] + a[1] * b[1], a[0] * b[1] - a[1] * b[0]
 
 
-def wave_kernel(meta_ref, probe_ref, kern_ref, meas_ref, left_ref, right_ref, *rest):
+def wave_kernel(meta_ref, pos_ref, probe_ref, kern_ref, meas_ref, left_ref, right_ref, *rest):
     t_refs, (out_ref, waves) = rest[:-2], rest[-2:]
     slices = len(t_refs)
     count, _, window, _ = out_ref.shape
@@ -104,27 +104,31 @@
 
         return tuple(x.astype(f32) for x in lax.switch(own ^ k, [pick(m) for m in range(slices)]))
 
-    def rows(fields, sign):
+    def rows(fields, sign, exact):
         x = jnp.concatenate(
             [jnp.concatenate([f[0], f[1]], axis=0) for f in fields], axis=1
         )
-        high, low = split(x)
-        y = jnp.dot(
-            left_ref[sign], jnp.concatenate([high, low, high], axis=0), preferred_element_type=f32
-        )
+        if exact:
+            high, low = split(x)
+            x = jnp.concatenate([high, low, high], axis=0)
+        else:
+            x = x.astype(bf16)
+        y = jnp.dot(left_ref[sign, :, : x.shape[0]], x, preferred_element_type=f32)
         return [
             (y[:window, p * window : (p + 1) * window], y[window:, p * window : (p + 1) * window])
             for p in range(len(fields))
         ]
 
-    def cols(fields, sign):
+    def cols(fields, sign, exact):
         x = jnp.concatenate(
             [jnp.concatenate([f[0], f[1]], axis=1) for f in fields], axis=0
         )
-        high, low = split(x)
-        y = jnp.dot(
-            jnp.concatenate([high, low, high], axis=1), right_ref[sign], preferred_element_type=f32
-        )
+        if exact:
+            high, low = split(x)
+            x = jnp.concatenate([high, low, high], axis=1)
+        else:
+            x = x.astype(bf16)
+        y = jnp.dot(x, right_ref[sign, : x.shape[1]], preferred_element_type=f32)
         return [
             (y[p * window : (p + 1) * window, :window], y[p * window : (p + 1) * window, window:])
             for p in range(len(fields))
@@ -132,8 +136,8 @@
 
     plus, minus = 0, 1
 
-    def transform(fields, sign):
-        return cols(rows(fields, sign), sign)
+    def transform(fields, sign, exact=True):
+        return cols(rows(fields, sign, exact), sign, exact)
 
     kern = (kern_ref[0], kern_ref[1])
     probe = (probe_ref[0], probe_ref[1])
@@ -156,7 +160,7 @@
         scale = 2.0 * (re * re + im * im - meas_ref[p])
         return scale * re, scale * im
 
-    returned = transform([source(p) for p in range(count)], plus)
+    returned = transform([source(p) for p in range(count)], plus, False)
     for k in reversed(range(slices)):
 
         @pl.when(own == k)
@@ -168,35 +172,37 @@
 
         if k > 0:
             chi = [cmul_conj(t_of(k, p), returned[p]) for p in range(count)]
-            spectrum = transform(chi, minus)
-            returned = transform([cmul_conj(kern, s) for s in spectrum], plus)
-
-
-def run_waves(depth_index, probe, kern, measured, gathered):
+            spectrum = transform(chi, minus, False)
+            returned = transform([cmul_conj(kern, s) for s in spectrum], plus, False)
+
+
+def run_waves(depth_index, positions, probe, kern, measured, gathered):
     count, _, window, _ = gathered[0].shape
     left, right = dft_matrices(window)
+    smem = pl.BlockSpec(memory_space=pltpu.SMEM)
     vmem = pl.BlockSpec(memory_space=pltpu.VMEM)
     return pl.pallas_call(
         wave_kernel,
         out_shape=jax.ShapeDtypeStruct((count, 2, window, window), bf16),
-        in_specs=[pl.BlockSpec(memory_space=pltpu.SMEM)] + [vmem] * (5 + len(gathered)),
+        in_specs=[smem, smem] + [vmem] * (5 + len(gathered)),
         out_specs=vmem,
         scratch_shapes=[pltpu.VMEM((count, 2, window, window), f32)],
         compiler_params=pltpu.CompilerParams(vmem_limit_bytes=32 * 1024 * 1024),
         name="run_waves",
-    )(depth_index, probe, kern, measured, jnp.asarray(left), jnp.asarray(right), *gathered)
-
-
-def place_kernel(pos_ref, meta_ref, terms_ref, out_ref, canvas):
-    count, _, window, _ = terms_ref.shape
+    )(depth_index, positions, probe, kern, measured, jnp.asarray(left), jnp.asarray(right), *gathered)
+
+
+def place_kernel(pos_ref, meta_ref, *rest):
+    terms_refs, (out_ref, canvas) = rest[:-2], rest[-2:]
+    count, _, window, _ = terms_refs[0].shape
     _, stripe, cols = out_ref.shape
     wide = window + 128
     canvas[:, window : window + stripe, :] = jnp.zeros((2, stripe, canvas.shape[2]), f32)
     first_row = meta_ref[0] * stripe
 
-    def body(p, carry):
-        row = pos_ref[p, 0] - first_row + window
-        col = pos_ref[p, 1]
+    def body(p, terms_ref, base):
+        row = pos_ref[base + p, 0] - first_row + window
+        col = pos_ref[base + p, 1]
         row_base = pl.multiple_of(row // 8 * 8, 8)
         col_base = pl.multiple_of(col // 128 * 128, 128)
 
@@ -211,26 +217,34 @@
                 at = (part, pl.ds(row_base, window + 8), pl.ds(col_base, wide))
                 canvas[at] = canvas[at] + block
 
-        return carry
-
-    lax.fori_loop(0, count, body, 0)
+    for source, terms_ref in enumerate(terms_refs):
+        for p in range(count):
+            body(p, terms_ref, source * count)
     out_ref[...] = canvas[:, window : window + stripe, :cols]
 
 
 def place_windows(positions, dp_index, terms, stripe, cols):
-    window = terms.shape[-1]
+    window = terms[0].shape[-1]
     vmem = pl.BlockSpec(memory_space=pltpu.VMEM)
     smem = pl.BlockSpec(memory_space=pltpu.SMEM)
     tall = window + (stripe + 7) // 8 * 8 + window + 8
     return pl.pallas_call(
         place_kernel,
         out_shape=jax.ShapeDtypeStruct((2, stripe, cols), f32),
-        in_specs=[smem, smem, vmem],
+        in_specs=[smem, smem] + [vmem] * len(terms),
         out_specs=vmem,
         scratch_shapes=[pltpu.VMEM((2, tall, cols + 128), f32)],
         compiler_params=pltpu.CompilerParams(vmem_limit_bytes=40 * 1024 * 1024),
         name="place_windows",
-    )(positions, dp_index, terms)
+    )(positions, dp_index, *terms)
+
+
+def swap(block, axis, distance):
+    return lax.ppermute(block, axis, [(i, i ^ distance) for i in range(lax.axis_size(axis))])
+
+
+def spread(block, axis):
+    return [block] + [swap(block, axis, m) for m in range(2, lax.axis_size(axis), 2)]
 
 
 def on_device(object_slices, positions, probe_field, propagator_phase, measured):
@@ -240,15 +254,14 @@
     window = probe_field.shape[-1]
     rows, cols = object_slices.shape[-2:]
     stripe = rows // lax.axis_size("dp")
-    all_positions = lax.all_gather(positions, "dp", axis=0, tiled=True)
+    all_positions = jnp.concatenate(spread(positions, "dp"))
+    all_positions = jnp.concatenate([all_positions, swap(all_positions, "dp", 1)])
     kern = jnp.stack([jnp.cos(propagator_phase), jnp.sin(propagator_phase)])
     own = take_windows(object_slices[0], positions, window)
-    gathered = [own] + [
-        lax.ppermute(own, "depth", [(i, i ^ m) for i in range(depth_count)])
-        for m in range(1, depth_count)
-    ]
-    terms = run_waves(depth_index, probe_field, kern, measured, gathered)
-    all_terms = lax.all_gather(terms, "dp", axis=0, tiled=True)
+    gathered = [own] + [swap(own, "depth", m) for m in range(1, depth_count)]
+    terms = run_waves(depth_index, all_positions, probe_field, kern, measured, gathered)
+    all_terms = spread(terms, "dp")
+    all_terms += [swap(x, "dp", 1) for x in all_terms]
     return place_windows(all_positions, dp_index, all_terms, stripe, cols)[None]
 
 

time: 64.9 us -> 45.4 us (0.70)
  between operations: 13.5 us -> 0.11 us
  blocking collectives: 12 us -> 0 us
  starting transfers between devices: 4.64 us -> 14.4 us
  Pallas kernels: 15.6 us -> 13.4 us
  local copies, waits for them, and re-layouts: 2.38 us -> 1.18 us
  waiting for transfers between devices: 16.6 us -> 15.9 us
    all_gather x1 -> x0, blocking collectives: 12 us -> none  [on_device(): all_positions = lax.all_gather(positions, 'dp', axis=0, tiled=True)]
    all_gather x1 -> x0, waiting for transfers between devices: 10.7 us -> none  [on_device(): all_terms = lax.all_gather(terms, 'dp', axis=0, tiled=True)]
    ppermute x3 -> x14, waiting for transfers between devices: 5.85 us -> 15.9 us  [swap(): lax.ppermute(block, axis, [(i, i ^ distance) for i in range(lax.axis_size...]
    ppermute x3 -> x14, starting transfers between devices: 4.6 us -> 14.4 us  [swap(): lax.ppermute(block, axis, [(i, i ^ distance) for i in range(lax.axis_size...]
    pallas_call x1, Pallas kernels: 10.2 us -> 8.34 us  [run_waves(): pl.pallas_call(wave_kernel, out_shape=jax.ShapeDtypeStruct((count, 2, win...]
    unnamed x16 -> x14, local copies, waits for them, and re-layouts: 2.15 us -> 0.92 us
  transfers between devices with their start and end apart: 4 -> 14, of which waited for: 4 -> 8; matrix products, arithmetic and copies ran while one was open for 0% -> 1% of each run, Pallas kernels for 0% -> 6%
where the time goes in v2:
time: 45.4 us; the launch traced here: 45 us
  waiting for transfers between devices  15.9 us (35%)
  starting transfers between devices  14.4 us (32%)
  Pallas kernels  13.4 us (30%)
  local copies, waits for them, and re-layouts  1.18 us (3%)
    ppermute x14, waiting for transfers between devices, swap(): lax.ppermute(block, axis, [(i, i ^ distance) for i in range(lax.axis_size...  15.9 us
    ppermute x14, starting transfers between devices, swap(): lax.ppermute(block, axis, [(i, i ^ distance) for i in range(lax.axis_size...  14.4 us
    pallas_call x1, Pallas kernels, run_waves(): pl.pallas_call(wave_kernel, out_shape=jax.ShapeDtypeStruct((count, 2, win...  8.34 us
    pallas_call x1, Pallas kernels, take_windows(): pl.pallas_call(window_kernel, out_shape=jax.ShapeDtypeStruct((count, 2, w...  2.71 us
    pallas_call x1, Pallas kernels, place_windows(): pl.pallas_call(place_kernel, out_shape=jax.ShapeDtypeStruct((2, stripe, c...  2.33 us
    unnamed x14, local copies, waits for them, and re-layouts  0.92 us
  transfers between devices with their start and end apart: 14, of which 8 were waited for; matrix products, arithmetic and copies ran while one was open for 1% of the time, Pallas kernels for 6%

profile of v2, /device:TPU:0, one launch (start us, length us, event | category | flops | bytes accessed | tf_op | source)
XLA Modules:
  0.0 45.0 jit_solution(18137350282789687035)
XLA Ops:
  0.0 5.1 %collective-permute-start.2 = (s32[2,2]{1,0:T(2,128)}, s32[2,2]{1,0:T(2,128)S(1)}, u32[]{:S(2)}, u32[]{:S(2)}) collective-permute-start(s32[2,2]{1,0:T(2,128)} %pos_ref.1), channel_id=1, source_target_pairs={{0,6},{1,7},{2,4},{3,5},{4,2},{5,3},{6,0},{7,1},{8,14},{9,15},{10,... | collective-permute-start | bytes 56 | tf_op jit(solution)/shard_map/ppermute | solution.py:243
  5.2 2.7 %take_windows.1.rest_0_ = bf16[2,2,128,128]{3,2,1,0:T(8,128)(2,1)} custom-call(s32[2,2]{1,0:T(2,128)} %pos_ref.1, f32[2,768,768]{2,1,0:T(8,128)} %bitcast.8), custom_call_target="tpu_custom_call" | custom-call | tf_op jit(solution)/shard_map/take_windows/pallas_call | solution.py:69
  7.9 2.5 %collective-permute-start.6 = (bf16[2,2,128,128]{3,2,1,0:T(8,128)(2,1)}, bf16[2,2,128,128]{3,2,1,0:T(8,128)(2,1)S(1)}, u32[]{:S(2)}, u32[]{:S(2)}) collective-permute-start(bf16[2,2,128,128]{3,2,1,0:T(8,128)(2,1)} %take_windows.1.rest_0_), channel_id=1, source_target_pairs={{0,24},{8,16},{16,8},{24,0},{1,25},{9,17},{17,9},{25,1},{2,26},{10... | collective-permute-start | bytes 393224 | tf_op jit(solution)/shard_map/ppermute | solution.py:243
  10.4 0.5 %collective-permute-start.5 = (bf16[2,2,128,128]{3,2,1,0:T(8,128)(2,1)}, bf16[2,2,128,128]{3,2,1,0:T(8,128)(2,1)S(1)}, u32[]{:S(2)}, u32[]{:S(2)}) collective-permute-start(bf16[2,2,128,128]{3,2,1,0:T(8,128)(2,1)} %take_windows.1.rest_0_), channel_id=1, source_target_pairs={{0,16},{8,24},{16,0},{24,8},{1,17},{9,25},{17,1},{25,9},{2,18},{10... | collective-permute-start | bytes 393224 | tf_op jit(solution)/shard_map/ppermute | solution.py:243
  10.9 0.5 %collective-permute-start.4 = (bf16[2,2,128,128]{3,2,1,0:T(8,128)(2,1)}, bf16[2,2,128,128]{3,2,1,0:T(8,128)(2,1)S(1)}, u32[]{:S(2)}, u32[]{:S(2)}) collective-permute-start(bf16[2,2,128,128]{3,2,1,0:T(8,128)(2,1)} %take_windows.1.rest_0_), channel_id=1, source_target_pairs={{0,8},{8,0},{16,24},{24,16},{1,9},{9,1},{17,25},{25,17},{2,10},{10... | collective-permute-start | bytes 393224 | tf_op jit(solution)/shard_map/ppermute | solution.py:243
  11.4 0.2 cosine_bitcast_fusion
  11.7 0.7 %collective-permute-start = (s32[2,2]{1,0:T(2,128)S(1)}, s32[2,2]{1,0:T(2,128)S(1)}, u32[]{:S(2)}, u32[]{:S(2)}) collective-permute-start(s32[2,2]{1,0:T(2,128)S(1)} %copy-done.6), channel_id=1, source_target_pairs={{0,2},{1,3},{2,0},{3,1},{4,6},{5,7},{6,4},{7,5},{8,10},{9,11},{10,... | collective-permute-start | bytes 56 | tf_op jit(solution)/shard_map/ppermute | solution.py:243
  12.4 3.0 %collective-permute-done = s32[2,2]{1,0:T(2,128)S(1)} collective-permute-done((s32[2,2]{1,0:T(2,128)S(1)}, s32[2,2]{1,0:T(2,128)S(1)}, u32[]{:S(2)}, u32[]{:S(2)}) %collective-permute-start) | collective-permute-done | bytes 48 | tf_op jit(solution)/shard_map/ppermute | solution.py:243
  15.4 0.1 collective-permute-start.3
  15.4 1.2 %collective-permute-done.3 = s32[8,2]{1,0:T(8,128)S(1)} collective-permute-done((s32[8,2]{1,0:T(8,128)S(1)}, s32[8,2]{1,0:T(8,128)S(1)}, u32[]{:S(2)}, u32[]{:S(2)}) %collective-permute-start.3) | collective-permute-done | bytes 96 | tf_op jit(solution)/shard_map/ppermute | solution.py:243
  16.6 0.2 collective-permute-done.5.rest_2_
  16.8 0.1 collective-permute-done.4.rest_1_
  16.9 0.0 copy-start.2
  16.9 0.9 %copy-done.2 = bf16[2,2,128,128]{3,2,1,0:T(8,128)(2,1)S(1)} copy-done((bf16[2,2,128,128]{3,2,1,0:T(8,128)(2,1)S(1)}, bf16[2,2,128,128]{3,2,1,0:T(8,128)(2,1)}, u32[]{:S(2)}) %copy-start.2) | copy-done | bytes 131096
  17.8 8.3 %run_waves.1.rest_0_ = bf16[2,2,128,128]{3,2,1,0:T(8,128)(2,1)S(1)} custom-call(s32[1]{0:T(128)} %bitcast.1.meta_ref, s32[16,2]{1,0:T(8,128)S(1)} %concatenate.8.pos_ref, f32[2,128,128]{2,1,0:T(8,128)S(1)} %copy-done.3, f32[2,128,128]{2,1,0:T(8,128)S(1)} %pad_maximum_fusion.kern_ref, f32[2,128,128]{2,1,0:T(8,128)S(1)} %copy-done.4, ...), custom_call_target="tpu_custom_call" | custom-call | tf_op jit(solution)/shard_map/run_waves/pallas_call | solution.py:184
  26.2 2.2 %collective-permute-start.9 = (bf16[2,2,128,128]{3,2,1,0:T(8,128)(2,1)S(1)}, bf16[2,2,128,128]{3,2,1,0:T(8,128)(2,1)S(1)}, u32[]{:S(2)}, u32[]{:S(2)}) collective-permute-start(bf16[2,2,128,128]{3,2,1,0:T(8,128)(2,1)S(1)} %run_waves.1.rest_0_), channel_id=1, source_target_pairs={{0,6},{1,7},{2,4},{3,5},{4,2},{5,3},{6,0},{7,1},{8,14},{9,15},{10,... | collective-permute-start | bytes 393224 | tf_op jit(solution)/shard_map/ppermute | solution.py:243
  28.3 0.6 %collective-permute-start.8 = (bf16[2,2,128,128]{3,2,1,0:T(8,128)(2,1)S(1)}, bf16[2,2,128,128]{3,2,1,0:T(8,128)(2,1)S(1)}, u32[]{:S(2)}, u32[]{:S(2)}) collective-permute-start(bf16[2,2,128,128]{3,2,1,0:T(8,128)(2,1)S(1)} %run_waves.1.rest_0_), channel_id=1, source_target_pairs={{0,4},{1,5},{2,6},{3,7},{4,0},{5,1},{6,2},{7,3},{8,12},{9,13},{10,... | collective-permute-start | bytes 393224 | tf_op jit(solution)/shard_map/ppermute | solution.py:243
  29.0 1.6 %collective-permute-start.7 = (bf16[2,2,128,128]{3,2,1,0:T(8,128)(2,1)S(1)}, bf16[2,2,128,128]{3,2,1,0:T(8,128)(2,1)S(1)}, u32[]{:S(2)}, u32[]{:S(2)}) collective-permute-start(bf16[2,2,128,128]{3,2,1,0:T(8,128)(2,1)S(1)} %run_waves.1.rest_0_), channel_id=1, source_target_pairs={{0,2},{1,3},{2,0},{3,1},{4,6},{5,7},{6,4},{7,5},{8,10},{9,11},{10,... | collective-permute-start | bytes 393224 | tf_op jit(solution)/shard_map/ppermute | solution.py:243
  30.6 3.8 %collective-permute-done.9.rest_3_ = bf16[2,2,128,128]{3,2,1,0:T(8,128)(2,1)S(1)} collective-permute-done((bf16[2,2,128,128]{3,2,1,0:T(8,128)(2,1)S(1)}, bf16[2,2,128,128]{3,2,1,0:T(8,128)(2,1)S(1)}, u32[]{:S(2)}, u32[]{:S(2)}) %collective-permute-start.9) | collective-permute-done | bytes 131104 | tf_op jit(solution)/shard_map/ppermute | solution.py:243
  34.5 6.7 %collective-permute-done.8.rest_2_ = bf16[2,2,128,128]{3,2,1,0:T(8,128)(2,1)S(1)} collective-permute-done((bf16[2,2,128,128]{3,2,1,0:T(8,128)(2,1)S(1)}, bf16[2,2,128,128]{3,2,1,0:T(8,128)(2,1)S(1)}, u32[]{:S(2)}, u32[]{:S(2)}) %collective-permute-start.8) | collective-permute-done | bytes 131104 | tf_op jit(solution)/shard_map/ppermute | solution.py:243
  41.2 0.5 %collective-permute-start.11 = (bf16[2,2,128,128]{3,2,1,0:T(8,128)(2,1)S(1)}, bf16[2,2,128,128]{3,2,1,0:T(8,128)(2,1)S(1)}, u32[]{:S(2)}, u32[]{:S(2)}) collective-permute-start(bf16[2,2,128,128]{3,2,1,0:T(8,128)(2,1)S(1)} %collective-permute-done.7.rest_1_), channel_id=1, source_target_pairs={{0,1},{1,0},{2,3},{3,2},{4,5},{5,4},{6,7},{7,6},{8,9},{9,8},{10,11... | collective-permute-start | bytes 393224 | tf_op jit(solution)/shard_map/ppermute | solution.py:243
  41.7 0.8 %collective-permute-done.12.rest_6_ = bf16[2,2,128,128]{3,2,1,0:T(8,128)(2,1)S(1)} collective-permute-done((bf16[2,2,128,128]{3,2,1,0:T(8,128)(2,1)S(1)}, bf16[2,2,128,128]{3,2,1,0:T(8,128)(2,1)S(1)}, u32[]{:S(2)}, u32[]{:S(2)}) %collective-permute-start.12) | collective-permute-done | bytes 131104 | tf_op jit(solution)/shard_map/ppermute | solution.py:243
  42.5 0.2 collective-permute-done.11.rest_5_
  42.7 2.3 %place_windows.1 = f32[2,96,768]{2,1,0:T(8,128)} custom-call(s32[16,2]{1,0:T(8,128)S(1)} %concatenate.8.pos_ref, s32[1]{0:T(128)} %bitcast.meta_ref, bf16[2,2,128,128]{3,2,1,0:T(8,128)(2,1)S(1)} %run_waves.1.rest_0_, bf16[2,2,128,128]{3,2,1,0:T(8,128)(2,1)S(1)} %collective-permute-done.7.rest_1_, ...), custom_call_target="tpu_custom_call" | custom-call | tf_op jit(solution)/shard_map/place_windows/pallas_call | solution.py:231
  (25 shorter events, 0.1 us)
Async XLA Ops:
  0.0 16.9 %copy-start = (bf16[2,768,256]{2,1,0:T(8,128)(2,1)S(1)}, bf16[2,768,256]{2,1,0:T(8,128)(2,1)}, u32[]{:S(2)}) copy-start(bf16[2,768,256]{2,1,0:T(8,128)(2,1)} %constant.13.clone.right_ref) | copy-start | bytes 2359300
  0.0 16.9 %copy-start.1 = (bf16[2,256,768]{2,1,0:T(8,128)(2,1)S(1)}, bf16[2,256,768]{2,1,0:T(8,128)(2,1)}, u32[]{:S(2)}) copy-start(bf16[2,256,768]{2,1,0:T(8,128)(2,1)} %constant.12.clone.left_ref) | copy-start | bytes 2359300
  0.0 11.7 %copy-start.6 = (s32[2,2]{1,0:T(2,128)S(1)}, s32[2,2]{1,0:T(2,128)}, u32[]{:S(2)}) copy-start(s32[2,2]{1,0:T(2,128)} %pos_ref.1) | copy-start | bytes 52
  0.0 11.4 %copy-start.5 = (f32[128,128]{1,0:T(8,128)S(1)}, f32[128,128]{1,0:T(8,128)}, u32[]{:S(2)}) copy-start(f32[128,128]{1,0:T(8,128)} %param.10) | copy-start | bytes 196612
  0.0 16.9 %copy-start.4 = (f32[2,128,128]{2,1,0:T(8,128)S(1)}, f32[2,128,128]{2,1,0:T(8,128)}, u32[]{:S(2)}) copy-start(f32[2,128,128]{2,1,0:T(8,128)} %meas_ref.1) | copy-start | bytes 393220
  0.0 16.9 %copy-start.3 = (f32[2,128,128]{2,1,0:T(8,128)S(1)}, f32[2,128,128]{2,1,0:T(8,128)}, u32[]{:S(2)}) copy-start(f32[2,128,128]{2,1,0:T(8,128)} %probe_ref.1) | copy-start | bytes 393220
  0.0 11.7 %collective-permute-start.2 = (s32[2,2]{1,0:T(2,128)}, s32[2,2]{1,0:T(2,128)S(1)}, u32[]{:S(2)}, u32[]{:S(2)}) collective-permute-start(s32[2,2]{1,0:T(2,128)} %pos_ref.1), channel_id=1, source_target_pairs={{0,6},{1,7},{2,4},{3,5},{4,2},{5,3},{6,0},{7,1},{8,14},{9,15},{10,... | collective-permute-start | bytes 56 | tf_op jit(solution)/shard_map/ppermute | solution.py:243
  5.2 7.2 %collective-permute-start.1 = (s32[2,2]{1,0:T(2,128)}, s32[2,2]{1,0:T(2,128)S(1)}, u32[]{:S(2)}, u32[]{:S(2)}) collective-permute-start(s32[2,2]{1,0:T(2,128)} %pos_ref.1), channel_id=1, source_target_pairs={{0,4},{1,5},{2,6},{3,7},{4,0},{5,1},{6,2},{7,3},{8,12},{9,13},{10,... | collective-permute-start | bytes 56 | tf_op jit(solution)/shard_map/ppermute | solution.py:243
  7.9 8.7 %collective-permute-start.6 = (bf16[2,2,128,128]{3,2,1,0:T(8,128)(2,1)}, bf16[2,2,128,128]{3,2,1,0:T(8,128)(2,1)S(1)}, u32[]{:S(2)}, u32[]{:S(2)}) collective-permute-start(bf16[2,2,128,128]{3,2,1,0:T(8,128)(2,1)} %take_windows.1.rest_0_), channel_id=1, source_target_pairs={{0,24},{8,16},{16,8},{24,0},{1,25},{9,17},{17,9},{25,1},{2,26},{10... | collective-permute-start | bytes 393224 | tf_op jit(solution)/shard_map/ppermute | solution.py:243
  10.4 6.4 %collective-permute-start.5 = (bf16[2,2,128,128]{3,2,1,0:T(8,128)(2,1)}, bf16[2,2,128,128]{3,2,1,0:T(8,128)(2,1)S(1)}, u32[]{:S(2)}, u32[]{:S(2)}) collective-permute-start(bf16[2,2,128,128]{3,2,1,0:T(8,128)(2,1)} %take_windows.1.rest_0_), channel_id=1, source_target_pairs={{0,16},{8,24},{16,0},{24,8},{1,17},{9,25},{17,1},{25,9},{2,18},{10... | collective-permute-start | bytes 393224 | tf_op jit(solution)/shard_map/ppermute | solution.py:243
  10.9 6.0 %collective-permute-start.4 = (bf16[2,2,128,128]{3,2,1,0:T(8,128)(2,1)}, bf16[2,2,128,128]{3,2,1,0:T(8,128)(2,1)S(1)}, u32[]{:S(2)}, u32[]{:S(2)}) collective-permute-start(bf16[2,2,128,128]{3,2,1,0:T(8,128)(2,1)} %take_windows.1.rest_0_), channel_id=1, source_target_pairs={{0,8},{8,0},{16,24},{24,16},{1,9},{9,1},{17,25},{25,17},{2,10},{10... | collective-permute-start | bytes 393224 | tf_op jit(solution)/shard_map/ppermute | solution.py:243
  11.7 3.6 %collective-permute-start = (s32[2,2]{1,0:T(2,128)S(1)}, s32[2,2]{1,0:T(2,128)S(1)}, u32[]{:S(2)}, u32[]{:S(2)}) collective-permute-start(s32[2,2]{1,0:T(2,128)S(1)} %copy-done.6), channel_id=1, source_target_pairs={{0,2},{1,3},{2,0},{3,1},{4,6},{5,7},{6,4},{7,5},{8,10},{9,11},{10,... | collective-permute-start | bytes 56 | tf_op jit(solution)/shard_map/ppermute | solution.py:243
  15.4 1.2 %collective-permute-start.3 = (s32[8,2]{1,0:T(8,128)S(1)}, s32[8,2]{1,0:T(8,128)S(1)}, u32[]{:S(2)}, u32[]{:S(2)}) collective-permute-start(s32[8,2]{1,0:T(8,128)S(1)} %pad_add_fusion), channel_id=1, source_target_pairs={{0,1},{1,0},{2,3},{3,2},{4,5},{5,4},{6,7},{7,6},{8,9},{9,8},{10,11... | collective-permute-start | bytes 200 | tf_op jit(solution)/shard_map/ppermute | solution.py:243
  16.9 0.9 %copy-start.2 = (bf16[2,2,128,128]{3,2,1,0:T(8,128)(2,1)S(1)}, bf16[2,2,128,128]{3,2,1,0:T(8,128)(2,1)}, u32[]{:S(2)}) copy-start(bf16[2,2,128,128]{3,2,1,0:T(8,128)(2,1)} %take_windows.1.rest_0_) | copy-start | bytes 393220
  26.2 8.3 %collective-permute-start.9 = (bf16[2,2,128,128]{3,2,1,0:T(8,128)(2,1)S(1)}, bf16[2,2,128,128]{3,2,1,0:T(8,128)(2,1)S(1)}, u32[]{:S(2)}, u32[]{:S(2)}) collective-permute-start(bf16[2,2,128,128]{3,2,1,0:T(8,128)(2,1)S(1)} %run_waves.1.rest_0_), channel_id=1, source_target_pairs={{0,6},{1,7},{2,4},{3,5},{4,2},{5,3},{6,0},{7,1},{8,14},{9,15},{10,... | collective-permute-start | bytes 393224 | tf_op jit(solution)/shard_map/ppermute | solution.py:243
  28.3 12.8 %collective-permute-start.8 = (bf16[2,2,128,128]{3,2,1,0:T(8,128)(2,1)S(1)}, bf16[2,2,128,128]{3,2,1,0:T(8,128)(2,1)S(1)}, u32[]{:S(2)}, u32[]{:S(2)}) collective-permute-start(bf16[2,2,128,128]{3,2,1,0:T(8,128)(2,1)S(1)} %run_waves.1.rest_0_), channel_id=1, source_target_pairs={{0,4},{1,5},{2,6},{3,7},{4,0},{5,1},{6,2},{7,3},{8,12},{9,13},{10,... | collective-permute-start | bytes 393224 | tf_op jit(solution)/shard_map/ppermute | solution.py:243
  29.0 12.2 %collective-permute-start.7 = (bf16[2,2,128,128]{3,2,1,0:T(8,128)(2,1)S(1)}, bf16[2,2,128,128]{3,2,1,0:T(8,128)(2,1)S(1)}, u32[]{:S(2)}, u32[]{:S(2)}) collective-permute-start(bf16[2,2,128,128]{3,2,1,0:T(8,128)(2,1)S(1)} %run_waves.1.rest_0_), channel_id=1, source_target_pairs={{0,2},{1,3},{2,0},{3,1},{4,6},{5,7},{6,4},{7,5},{8,10},{9,11},{10,... | collective-permute-start | bytes 393224 | tf_op jit(solution)/shard_map/ppermute | solution.py:243
  30.6 11.1 %collective-permute-start.10 = (bf16[2,2,128,128]{3,2,1,0:T(8,128)(2,1)S(1)}, bf16[2,2,128,128]{3,2,1,0:T(8,128)(2,1)S(1)}, u32[]{:S(2)}, u32[]{:S(2)}) collective-permute-start(bf16[2,2,128,128]{3,2,1,0:T(8,128)(2,1)S(1)} %run_waves.1.rest_0_), channel_id=1, source_target_pairs={{0,1},{1,0},{2,3},{3,2},{4,5},{5,4},{6,7},{7,6},{8,9},{9,8},{10,11... | collective-permute-start | bytes 393224 | tf_op jit(solution)/shard_map/ppermute | solution.py:243
  34.5 7.2 %collective-permute-start.13 = (bf16[2,2,128,128]{3,2,1,0:T(8,128)(2,1)S(1)}, bf16[2,2,128,128]{3,2,1,0:T(8,128)(2,1)S(1)}, u32[]{:S(2)}, u32[]{:S(2)}) collective-permute-start(bf16[2,2,128,128]{3,2,1,0:T(8,128)(2,1)S(1)} %collective-permute-done.9.rest_3_), channel_id=1, source_target_pairs={{0,1},{1,0},{2,3},{3,2},{4,5},{5,4},{6,7},{7,6},{8,9},{9,8},{10,11... | collective-permute-start | bytes 393224 | tf_op jit(solution)/shard_map/ppermute | solution.py:243
  41.1 1.3 %collective-permute-start.12 = (bf16[2,2,128,128]{3,2,1,0:T(8,128)(2,1)S(1)}, bf16[2,2,128,128]{3,2,1,0:T(8,128)(2,1)S(1)}, u32[]{:S(2)}, u32[]{:S(2)}) collective-permute-start(bf16[2,2,128,128]{3,2,1,0:T(8,128)(2,1)S(1)} %collective-permute-done.8.rest_2_), channel_id=1, source_target_pairs={{0,1},{1,0},{2,3},{3,2},{4,5},{5,4},{6,7},{7,6},{8,9},{9,8},{10,11... | collective-permute-start | bytes 393224 | tf_op jit(solution)/shard_map/ppermute | solution.py:243
  41.2 1.5 %collective-permute-start.11 = (bf16[2,2,128,128]{3,2,1,0:T(8,128)(2,1)S(1)}, bf16[2,2,128,128]{3,2,1,0:T(8,128)(2,1)S(1)}, u32[]{:S(2)}, u32[]{:S(2)}) collective-permute-start(bf16[2,2,128,128]{3,2,1,0:T(8,128)(2,1)S(1)} %collective-permute-done.7.rest_1_), channel_id=1, source_target_pairs={{0,1},{1,0},{2,3},{3,2},{4,5},{5,4},{6,7},{7,6},{8,9},{9,8},{10,11... | collective-permute-start | bytes 393224 | tf_op jit(solution)/shard_map/ppermute | solution.py:243

commit v3 on v1

v3 whole, which is shorter than its diff:
```python
import functools
import math

import jax
import jax.numpy as jnp
import numpy as np
from jax import lax
from jax.experimental import pallas as pl
from jax.experimental.pallas import tpu as pltpu
from jax.sharding import PartitionSpec as P

grad_scale = 0.03125
f32 = jnp.float32
bf16 = jnp.bfloat16


def dft_matrices(size):
    k = np.arange(size)
    angles = 2.0 * np.pi * ((k[:, None] * k[None, :]) % size) / size
    c = np.cos(angles) / math.sqrt(size)
    s = np.sin(angles) / math.sqrt(size)
    plus = np.block([[c, s], [-s, c]]).astype(np.float32)
    minus = np.block([[c, -s], [s, c]]).astype(np.float32)
    parts = []
    for full in (plus, minus):
        high = full.astype(bf16)
        low = (full - high.astype(np.float32)).astype(bf16)
        parts.append((high, low))
    (ph, plo), (mh, mlo) = parts
    right = np.stack([np.concatenate([ph, ph, plo], 0), np.concatenate([mh, mh, mlo], 0)])
    left = np.stack([np.concatenate([mh, mh, mlo], 1), np.concatenate([ph, ph, plo], 1)])
    return left, right


def indices(clusters):
    dp_index = lax.axis_index("dp")
    return lax.axis_index("depth"), lax.div(dp_index, lax.axis_size("dp") // clusters), dp_index


def window_kernel(obj_ref, *rest):
    buf, sems = rest[-2:]
    depth = buf.shape[0]
    clusters = len(rest) - 3 - depth
    pos_refs = rest[:clusters]
    out_refs = rest[clusters : clusters + depth]
    table_ref = rest[clusters + depth]
    own, cluster, _ = indices(clusters)
    per_home = depth // clusters
    window = out_refs[0].shape[-1]
    rows, cols = obj_ref.shape[-2:]
    tall, wide = buf.shape[-2:]

    for home in range(clusters):
        for q in range(per_home):
            for axis in range(2):
                value = pos_refs[0][q, axis]
                for m in range(1, clusters):
                    value = jnp.where(home ^ cluster == m, pos_refs[m][q, axis], value)
                table_ref[home * per_home + q, axis] = value

    def corner(m):
        at = own ^ m
        row, col = table_ref[at, 0], table_ref[at, 1]
        row_base = pl.multiple_of(jnp.minimum(row >> 3, (rows - tall) // 8) * 8, 8)
        col_base = pl.multiple_of(jnp.minimum(col >> 7, (cols - wide) // 128) * 128, 128)
        return row_base, col_base, row - row_base, col - col_base

    def copy(m):
        row_base, col_base, _, _ = corner(m)
        return pltpu.make_async_copy(
            obj_ref.at[:, pl.ds(row_base, tall), pl.ds(col_base, wide)], buf.at[m], sems.at[m]
        )

    for m in range(depth):
        copy(m).start()
    for m in range(depth):
        copy(m).wait()
        _, _, row_off, col_off = corner(m)
        lift = jnp.where(row_off == 0, 0, tall - row_off)
        shift = jnp.where(col_off == 0, 0, wide - col_off)
        for part in range(2):
            block = pltpu.roll(buf[m, part], shift, 1)[:, :window]
            block = pltpu.roll(block, lift, 0)[:window]
            out_refs[m][part] = block.astype(bf16)


def take_windows(obj, positions, window, depth):
    tall, wide = window + 8, window + 128
    smem = pl.BlockSpec(memory_space=pltpu.SMEM)
    vmem = pl.BlockSpec(memory_space=pltpu.VMEM)
    out = pl.pallas_call(
        window_kernel,
        out_shape=[jax.ShapeDtypeStruct((2, window, window), bf16)] * depth
        + [jax.ShapeDtypeStruct((depth, 2), jnp.int32)],
        in_specs=[pl.BlockSpec(memory_space=pl.ANY)] + [smem] * len(positions),
        out_specs=[vmem] * depth + [smem],
        scratch_shapes=[
            pltpu.VMEM((depth, 2, tall, wide), f32),
            pltpu.SemaphoreType.DMA((depth,)),
        ],
        name="take_windows",
    )(obj, *positions)
    return list(out[:depth]), out[depth]


def split(x):
    high = x.astype(bf16)
    return high, (x - high.astype(f32)).astype(bf16)


def cmul(a, b):
    return a[0] * b[0] - a[1] * b[1], a[0] * b[1] + a[1] * b[0]


def cmul_conj(a, b):
    return a[0] * b[0] + a[1] * b[1], a[0] * b[1] - a[1] * b[0]


def wave_kernel(slices, probe_ref, kern_ref, left_ref, right_ref, *rest):
    t_refs, rest = rest[:slices], rest[slices:]
    meas_refs = rest[: -slices - 3]
    out_refs = rest[-slices - 3 : -3]
    trans, terms, meas = rest[-3:]
    own, cluster, _ = indices(len(meas_refs))
    per_home = slices // len(meas_refs)
    window = probe_ref.shape[-1]

    for m in range(slices):
        trans[own ^ m] = t_refs[m][...]
    home = lax.div(own, per_home)
    for m, meas_ref in enumerate(meas_refs):

        @pl.when(home ^ cluster == m)
        def _():
            meas[...] = meas_ref[lax.rem(own, per_home)]

    def t_of(k):
        return trans[k, 0].astype(f32), trans[k, 1].astype(f32)

    def passes(x, axis, exact):
        if not exact:
            return x.astype(bf16)
        high, low = split(x)
        return jnp.concatenate([high, low, high], axis=axis)

    def rows(field, sign, exact):
        x = passes(jnp.concatenate(field, axis=0), 0, exact)
        y = jnp.dot(left_ref[sign, :, : x.shape[0]], x, preferred_element_type=f32)
        return y[:window], y[window:]

    def cols(field, sign, exact):
        x = passes(jnp.concatenate(field, axis=1), 1, exact)
        y = jnp.dot(x, right_ref[sign, : x.shape[1]], preferred_element_type=f32)
        return y[:, :window], y[:, window:]

    plus, minus = 0, 1

    def transform(field, sign, exact):
        return cols(rows(field, sign, exact), sign, exact)

    kern = (kern_ref[0], kern_ref[1])
    psi = (probe_ref[0], probe_ref[1])
    kept = []
    for k in range(slices):
        kept.append(psi)
        spectrum = transform(cmul(t_of(k), psi), minus, True)
        if k < slices - 1:
            psi = transform(cmul(kern, spectrum), plus, True)

    re, im = spectrum
    scale = 2.0 * (re * re + im * im - meas[...])
    returned = transform((scale * re, scale * im), plus, False)
    for k in reversed(range(slices)):
        re, im = cmul_conj(kept[k], returned)
        terms[own ^ k, 0] = (re * grad_scale).astype(bf16)
        terms[own ^ k, 1] = (im * grad_scale).astype(bf16)
        if k > 0:
            spectrum = transform(cmul_conj(t_of(k), returned), minus, False)
            returned = transform(cmul_conj(kern, spectrum), plus, False)
    for m in range(slices):
        out_refs[m][...] = terms[m]


def run_waves(probe, kern, windows, measured):
    slices = len(windows)
    window = probe.shape[-1]
    left, right = dft_matrices(window)
    vmem = pl.BlockSpec(memory_space=pltpu.VMEM)
    return pl.pallas_call(
        functools.partial(wave_kernel, slices),
        out_shape=[jax.ShapeDtypeStruct((2, window, window), bf16)] * slices,
        in_specs=[vmem] * (4 + slices + len(measured)),
        out_specs=[vmem] * slices,
        scratch_shapes=[
            pltpu.VMEM((slices, 2, window, window), bf16),
            pltpu.VMEM((slices, 2, window, window), bf16),
            pltpu.VMEM((window, window), f32),
        ],
        compiler_params=pltpu.CompilerParams(vmem_limit_bytes=40 * 1024 * 1024),
        name="run_waves",
    )(probe, kern, jnp.asarray(left), jnp.asarray(right), *windows, *measured)


def place_kernel(depth, *rest):
    out_ref, canvas = rest[-2:]
    groups = (len(rest) - 2) // (depth + 1)
    table_refs, terms_refs = rest[:groups], rest[groups:-2]
    _, stripe, cols = out_ref.shape
    window = terms_refs[0].shape[-1]
    wide = window + 128
    own, _, dp_index = indices(1)
    first_row = dp_index * stripe
    canvas[:, window : window + stripe, :] = jnp.zeros((2, stripe, canvas.shape[2]), f32)
    for group in range(groups):
        for m in range(depth):
            terms_ref = terms_refs[group * depth + m]
            row = table_refs[group][own ^ m, 0] - first_row + window
            col = table_refs[group][own ^ m, 1]
            row_base = pl.multiple_of((row >> 3) << 3, 8)
            col_base = pl.multiple_of((col >> 7) << 7, 128)

            @pl.when((row > 0) & (row < window + stripe))
            def _():
                for part in range(2):
                    block = terms_ref[part].astype(f32)
                    block = jnp.concatenate([block, jnp.zeros((8, window), f32)], axis=0)
                    block = pltpu.roll(block, row - row_base, 0)
                    block = jnp.concatenate([block, jnp.zeros((window + 8, 128), f32)], axis=1)
                    block = pltpu.roll(block, col - col_base, 1)
                    at = (part, pl.ds(row_base, window + 8), pl.ds(col_base, wide))
                    canvas[at] = canvas[at] + block

    out_ref[...] = canvas[:, window : window + stripe, :cols]


def place_windows(tables, terms, depth, stripe, cols):
    window = terms[0].shape[-1]
    vmem = pl.BlockSpec(memory_space=pltpu.VMEM)
    smem = pl.BlockSpec(memory_space=pltpu.SMEM)
    tall = window + (stripe + 7) // 8 * 8 + window + 8
    return pl.pallas_call(
        functools.partial(place_kernel, depth),
        out_shape=jax.ShapeDtypeStruct((2, stripe, cols), f32),
        in_specs=[smem] * len(tables) + [vmem] * len(terms),
        out_specs=vmem,
        scratch_shapes=[pltpu.VMEM((2, tall, cols + 128), f32)],
        compiler_params=pltpu.CompilerParams(vmem_limit_bytes=40 * 1024 * 1024),
        name="place_windows",
    )(*tables, *terms)


def swap(block, depth_distance, dp_distance):
    depth, dp = lax.axis_size("depth"), lax.axis_size("dp")
    route = [
        (d * dp + j, (d ^ depth_distance) * dp + (j ^ dp_distance))
        for d in range(depth)
        for j in range(dp)
    ]
    return lax.ppermute(block, ("depth", "dp"), route)


def on_device(object_slices, positions, probe_field, propagator_phase, measured):
    depth, dp = lax.axis_size("depth"), lax.axis_size("dp")
    clusters = depth // positions.shape[0]
    members = dp // clusters
    window = probe_field.shape[-1]
    rows, cols = object_slices.shape[-2:]
    homes = range(1, clusters)
    all_homes = [positions] + [swap(positions, 0, m * members) for m in homes]
    windows, table = take_windows(object_slices[0], all_homes, window, depth)
    windows = [windows[0]] + [swap(windows[m], m, 0) for m in range(1, depth)]
    targets = [measured] + [swap(measured, 0, m * members) for m in homes]
    kern = jnp.stack([jnp.cos(propagator_phase), jnp.sin(propagator_phase)])
    terms = run_waves(probe_field, kern, windows, targets)

    tables = [table] + [swap(table, 0, i) for i in range(1, members)]
    near = []
    for i in range(0, members, 2):
        near.append([terms[m] if m == i == 0 else swap(terms[m], m, i) for m in range(depth)])
    spread = []
    for i in range(members):
        group = near[i // 2]
        spread += group if i % 2 == 0 else [swap(x, 0, 1) for x in group]
    return place_windows(tables, spread, depth, rows // dp, cols)[None]


def solution(mesh):
    placed = (P("depth", None, None, None), P("dp", None), P(), P(), P("dp", None, None))
    return jax.shard_map(
        on_device,
        mesh=mesh,
        in_specs=placed,
        out_specs=P("depth", None, "dp", None),
        check_vma=False,
    )
```

time: 64.9 us -> 43.7 us (0.67)
  the two profiles are of different devices: /device:TPU:0 before, /device:TPU:17 now
where the time goes in v3:
time: 43.7 us; the launch traced here: 43.4 us
  starting transfers between devices  28.2 us (65%)
  Pallas kernels  10.6 us (24%)
  local copies, waits for them, and re-layouts  3.17 us (7%)
  waiting for transfers between devices  1.31 us (3%)
    ppermute x23, starting transfers between devices, swap(): return lax.ppermute(block, ('depth', 'dp'), route)  28.2 us
    pallas_call x1, Pallas kernels, run_waves(): pl.pallas_call(functools.partial(wave_kernel, slices), out_shape=[jax.Sha...  5.44 us
    pallas_call x1, Pallas kernels, take_windows(): pl.pallas_call(window_kernel, out_shape=[jax.ShapeDtypeStruct((2, window,...  2.93 us
    pallas_call x1, Pallas kernels, place_windows(): pl.pallas_call(functools.partial(place_kernel, depth), out_shape=jax.Shap...  2.24 us
    unnamed x14, local copies, waits for them, and re-layouts  2.09 us
    ppermute x23, waiting for transfers between devices, swap(): return lax.ppermute(block, ('depth', 'dp'), route)  1.31 us
    another operation x1, local copies, waits for them, and re-layouts, on_device(): kern = jnp.stack([jnp.cos(propagator_phase), jnp.sin(propagator_phase)])  1.08 us
  transfers between devices with their start and end apart: 23, of which 5 were waited for; matrix products, arithmetic and copies ran while one was open for 3% of the time, Pallas kernels for 19%

profile of v3, /device:TPU:17, one launch (start us, length us, event | category | flops | bytes accessed | tf_op | source)
XLA Modules:
  0.0 43.4 jit_solution(5199859823557370692)
XLA Ops:
  0.1 2.3 %collective-permute-start.7 = (f32[2,128,128]{2,1,0:T(8,128)}, f32[2,128,128]{2,1,0:T(8,128)S(1)}, u32[]{:S(2)}, u32[]{:S(2)}) collective-permute-start(f32[2,128,128]{2,1,0:T(8,128)} %rest_4_.1), channel_id=1, source_target_pairs={{0,4},{1,5},{2,6},{3,7},{4,0},{5,1},{6,2},{7,3},{8,12},{9,13},{10,... | collective-permute-start | bytes 393224 | tf_op jit(solution)/shard_map/ppermute | solution.py:259
  2.5 1.1 %cosine_bitcast_fusion = (f32[1,128,128]{2,1,0:T(8,128)S(1)}, f32[1,128,128]{2,1,0:T(8,128)S(1)}) fusion(f32[128,128]{1,0:T(8,128)} %param.10), kind=kLoop, calls=%fused_computation.2 | loop fusion | bytes 196608 | tf_op jit(solution)/shard_map/stack | solution.py:273
  3.6 0.6 %copy-done.6 = s32[2,2]{1,0:T(2,128)} copy-done((s32[2,2]{1,0:T(2,128)}, s32[2,2]{1,0:T(2,128)S(1)}, u32[]{:S(2)}) %copy-start.6) | copy-done | bytes 40
  4.2 2.9 %take_windows.1 = (bf16[2,128,128]{2,1,0:T(8,128)(2,1)}, bf16[2,128,128]{2,1,0:T(8,128)(2,1)}, bf16[2,128,128]{2,1,0:T(8,128)(2,1)}, bf16[2,128,128]{2,1,0:T(8,128)(2,1)}, s32[4,2]{1,0:T(4,128)}) custom-call(f32[2,768,768]{2,1,0:T(8,128)} %bitcast.6, s32[2,2]{1,0:T(2,128)} %rest_0_.1, s32[2,2]{1,0:T(2,128)} %copy-done.6), custom_call_target="tpu_custom_call" | custom-call | tf_op jit(solution)/shard_map/take_windows/pallas_call | solution.py:91
  7.1 1.3 %collective-permute-start.4 = (bf16[2,128,128]{2,1,0:T(8,128)(2,1)}, bf16[2,128,128]{2,1,0:T(8,128)(2,1)S(1)}, u32[]{:S(2)}, u32[]{:S(2)}) collective-permute-start(bf16[2,128,128]{2,1,0:T(8,128)(2,1)} %get-tuple-element.16), channel_id=1, source_target_pairs={{0,8},{1,9},{2,10},{3,11},{4,12},{5,13},{6,14},{7,15},{8,0},{9,1},... | collective-permute-start | bytes 196616 | tf_op jit(solution)/shard_map/ppermute | solution.py:259
  8.4 1.2 %collective-permute-start.5 = (bf16[2,128,128]{2,1,0:T(8,128)(2,1)}, bf16[2,128,128]{2,1,0:T(8,128)(2,1)S(1)}, u32[]{:S(2)}, u32[]{:S(2)}) collective-permute-start(bf16[2,128,128]{2,1,0:T(8,128)(2,1)} %get-tuple-element.17), channel_id=1, source_target_pairs={{0,16},{1,17},{2,18},{3,19},{4,20},{5,21},{6,22},{7,23},{8,24},{9,... | collective-permute-start | bytes 196616 | tf_op jit(solution)/shard_map/ppermute | solution.py:259
  9.8 5.7 %collective-permute-start.3 = (s32[4,2]{1,0:T(4,128)}, s32[4,2]{1,0:T(4,128)S(1)}, u32[]{:S(2)}, u32[]{:S(2)}) collective-permute-start(s32[4,2]{1,0:T(4,128)} %get-tuple-element.14.rest_0_), channel_id=1, source_target_pairs={{0,3},{1,2},{2,1},{3,0},{4,7},{5,6},{6,5},{7,4},{8,11},{9,10},{10,... | collective-permute-start | bytes 104 | tf_op jit(solution)/shard_map/ppermute | solution.py:259
  15.5 1.3 %collective-permute-start.1 = (s32[4,2]{1,0:T(4,128)}, s32[4,2]{1,0:T(4,128)S(1)}, u32[]{:S(2)}, u32[]{:S(2)}) collective-permute-start(s32[4,2]{1,0:T(4,128)} %get-tuple-element.14.rest_0_), channel_id=1, source_target_pairs={{0,1},{1,0},{2,3},{3,2},{4,5},{5,4},{6,7},{7,6},{8,9},{9,8},{10,11... | collective-permute-start | bytes 104 | tf_op jit(solution)/shard_map/ppermute | solution.py:259
  16.9 0.8 %copy-done.4 = bf16[2,128,128]{2,1,0:T(8,128)(2,1)S(1)} copy-done((bf16[2,128,128]{2,1,0:T(8,128)(2,1)S(1)}, bf16[2,128,128]{2,1,0:T(8,128)(2,1)}, u32[]{:S(2)}) %copy-start.4) | copy-done | bytes 65560
  17.7 5.4 %run_waves.1 = (bf16[2,128,128]{2,1,0:T(8,128)(2,1)S(1)}, bf16[2,128,128]{2,1,0:T(8,128)(2,1)S(1)}, bf16[2,128,128]{2,1,0:T(8,128)(2,1)S(1)}, bf16[2,128,128]{2,1,0:T(8,128)(2,1)S(1)}) custom-call(f32[2,128,128]{2,1,0:T(8,128)S(1)} %copy-done.2, f32[2,128,128]{2,1,0:T(8,128)S(1)} %pad_maximum_fusion.kern_ref, bf16[2,256,768]{2,1,0:T(8,128)(2,1)S(1)} %copy-done.1, ...), custom_call_target="tpu_custom_call" | custom-call | tf_op jit(solution)/shard_map/run_waves/pallas_call | solution.py:189
  23.1 1.2 %collective-permute-start.16 = (bf16[2,128,128]{2,1,0:T(8,128)(2,1)S(1)}, bf16[2,128,128]{2,1,0:T(8,128)(2,1)S(1)}, u32[]{:S(2)}, u32[]{:S(2)}) collective-permute-start(bf16[2,128,128]{2,1,0:T(8,128)(2,1)S(1)} %get-tuple-element.20), channel_id=1, source_target_pairs={{0,10},{1,11},{2,8},{3,9},{4,14},{5,15},{6,12},{7,13},{8,2},{9,3},... | collective-permute-start | bytes 196616 | tf_op jit(solution)/shard_map/ppermute | solution.py:259
  24.4 1.2 %collective-permute-start.8 = (bf16[2,128,128]{2,1,0:T(8,128)(2,1)S(1)}, bf16[2,128,128]{2,1,0:T(8,128)(2,1)S(1)}, u32[]{:S(2)}, u32[]{:S(2)}) collective-permute-start(bf16[2,128,128]{2,1,0:T(8,128)(2,1)S(1)} %get-tuple-element.20), channel_id=1, source_target_pairs={{0,8},{1,9},{2,10},{3,11},{4,12},{5,13},{6,14},{7,15},{8,0},{9,1},... | collective-permute-start | bytes 196616 | tf_op jit(solution)/shard_map/ppermute | solution.py:259
  25.6 1.2 %collective-permute-start.17 = (bf16[2,128,128]{2,1,0:T(8,128)(2,1)S(1)}, bf16[2,128,128]{2,1,0:T(8,128)(2,1)S(1)}, u32[]{:S(2)}, u32[]{:S(2)}) collective-permute-start(bf16[2,128,128]{2,1,0:T(8,128)(2,1)S(1)} %get-tuple-element.21), channel_id=1, source_target_pairs={{0,18},{1,19},{2,16},{3,17},{4,22},{5,23},{6,20},{7,21},{8,26},{9,... | collective-permute-start | bytes 196616 | tf_op jit(solution)/shard_map/ppermute | solution.py:259
  27.1 2.1 %collective-permute-start.18 = (bf16[2,128,128]{2,1,0:T(8,128)(2,1)S(1)}, bf16[2,128,128]{2,1,0:T(8,128)(2,1)S(1)}, u32[]{:S(2)}, u32[]{:S(2)}) collective-permute-start(bf16[2,128,128]{2,1,0:T(8,128)(2,1)S(1)} %get-tuple-element.22), channel_id=1, source_target_pairs={{0,26},{1,27},{2,24},{3,25},{4,30},{5,31},{6,28},{7,29},{8,18},{9,... | collective-permute-start | bytes 196616 | tf_op jit(solution)/shard_map/ppermute | solution.py:259
  29.2 1.2 %collective-permute-start.10 = (bf16[2,128,128]{2,1,0:T(8,128)(2,1)S(1)}, bf16[2,128,128]{2,1,0:T(8,128)(2,1)S(1)}, u32[]{:S(2)}, u32[]{:S(2)}) collective-permute-start(bf16[2,128,128]{2,1,0:T(8,128)(2,1)S(1)} %get-tuple-element.22), channel_id=1, source_target_pairs={{0,24},{1,25},{2,26},{3,27},{4,28},{5,29},{6,30},{7,31},{8,16},{9,... | collective-permute-start | bytes 196616 | tf_op jit(solution)/shard_map/ppermute | solution.py:259
  30.6 3.9 %collective-permute-start.11 = (bf16[2,128,128]{2,1,0:T(8,128)(2,1)S(1)}, bf16[2,128,128]{2,1,0:T(8,128)(2,1)S(1)}, u32[]{:S(2)}, u32[]{:S(2)}) collective-permute-start(bf16[2,128,128]{2,1,0:T(8,128)(2,1)S(1)} %get-tuple-element.19.rest_4_), channel_id=1, source_target_pairs={{0,1},{1,0},{2,3},{3,2},{4,5},{5,4},{6,7},{7,6},{8,9},{9,8},{10,11... | collective-permute-start | bytes 196616 | tf_op jit(solution)/shard_map/ppermute | solution.py:259
  34.5 0.4 collective-permute-start.20
  35.0 0.8 %collective-permute-start.12 = (bf16[2,128,128]{2,1,0:T(8,128)(2,1)S(1)}, bf16[2,128,128]{2,1,0:T(8,128)(2,1)S(1)}, u32[]{:S(2)}, u32[]{:S(2)}) collective-permute-start(bf16[2,128,128]{2,1,0:T(8,128)(2,1)S(1)} %collective-permute-done.8.rest_5_), channel_id=1, source_target_pairs={{0,1},{1,0},{2,3},{3,2},{4,5},{5,4},{6,7},{7,6},{8,9},{9,8},{10,11... | collective-permute-start | bytes 196616 | tf_op jit(solution)/shard_map/ppermute | solution.py:259
  35.8 1.4 %collective-permute-start.21 = (bf16[2,128,128]{2,1,0:T(8,128)(2,1)S(1)}, bf16[2,128,128]{2,1,0:T(8,128)(2,1)S(1)}, u32[]{:S(2)}, u32[]{:S(2)}) collective-permute-start(bf16[2,128,128]{2,1,0:T(8,128)(2,1)S(1)} %collective-permute-done.17.rest_14_), channel_id=1, source_target_pairs={{0,1},{1,0},{2,3},{3,2},{4,5},{5,4},{6,7},{7,6},{8,9},{9,8},{10,11... | collective-permute-start | bytes 196616 | tf_op jit(solution)/shard_map/ppermute | solution.py:259
  37.2 1.6 %collective-permute-start.13 = (bf16[2,128,128]{2,1,0:T(8,128)(2,1)S(1)}, bf16[2,128,128]{2,1,0:T(8,128)(2,1)S(1)}, u32[]{:S(2)}, u32[]{:S(2)}) collective-permute-start(bf16[2,128,128]{2,1,0:T(8,128)(2,1)S(1)} %collective-permute-done.9.rest_6_), channel_id=1, source_target_pairs={{0,1},{1,0},{2,3},{3,2},{4,5},{5,4},{6,7},{7,6},{8,9},{9,8},{10,11... | collective-permute-start | bytes 196616 | tf_op jit(solution)/shard_map/ppermute | solution.py:259
  38.7 0.5 %collective-permute-start.14 = (bf16[2,128,128]{2,1,0:T(8,128)(2,1)S(1)}, bf16[2,128,128]{2,1,0:T(8,128)(2,1)S(1)}, u32[]{:S(2)}, u32[]{:S(2)}) collective-permute-start(bf16[2,128,128]{2,1,0:T(8,128)(2,1)S(1)} %collective-permute-done.10.rest_7_), channel_id=1, source_target_pairs={{0,1},{1,0},{2,3},{3,2},{4,5},{5,4},{6,7},{7,6},{8,9},{9,8},{10,11... | collective-permute-start | bytes 196616 | tf_op jit(solution)/shard_map/ppermute | solution.py:259
  39.6 0.4 collective-permute-done.22.rest_19_
  40.5 0.7 %copy-done.5 = s32[4,2]{1,0:T(4,128)S(1)} copy-done((s32[4,2]{1,0:T(4,128)S(1)}, s32[4,2]{1,0:T(4,128)}, u32[]{:S(2)}) %copy-start.5) | copy-done | bytes 56
  41.2 2.2 %place_windows.1 = f32[2,96,768]{2,1,0:T(8,128)} custom-call(s32[4,2]{1,0:T(4,128)S(1)} %copy-done.5, s32[4,2]{1,0:T(4,128)S(1)} %collective-permute-done.1.rest_1_, s32[4,2]{1,0:T(4,128)S(1)} %collective-permute-done.2.rest_2_, s32[4,2]{1,0:T(4,128)S(1)} %collective-permute-done.3.rest_3_, bf16[2,128,128]{2,1,0:T(8,128)(2,1)S(1)} %get-tuple-element.19.rest_4_, ...), custom_call_target="tpu_custom_call" | custom-call | tf_op jit(solution)/shard_map/place_windows/pallas_call | solution.py:241
  (41 shorter events, 1.8 us)
Async XLA Ops:
  0.0 16.9 %copy-start.2 = (f32[2,128,128]{2,1,0:T(8,128)S(1)}, f32[2,128,128]{2,1,0:T(8,128)}, u32[]{:S(2)}) copy-start(f32[2,128,128]{2,1,0:T(8,128)} %probe_ref.1) | copy-start | bytes 393220
  0.0 3.6 %collective-permute-start = (s32[2,2]{1,0:T(2,128)}, s32[2,2]{1,0:T(2,128)S(1)}, u32[]{:S(2)}, u32[]{:S(2)}) collective-permute-start(s32[2,2]{1,0:T(2,128)} %rest_0_.1), channel_id=1, source_target_pairs={{0,4},{1,5},{2,6},{3,7},{4,0},{5,1},{6,2},{7,3},{8,12},{9,13},{10,... | collective-permute-start | bytes 56 | tf_op jit(solution)/shard_map/ppermute | solution.py:259
  0.1 16.7 %collective-permute-start.7 = (f32[2,128,128]{2,1,0:T(8,128)}, f32[2,128,128]{2,1,0:T(8,128)S(1)}, u32[]{:S(2)}, u32[]{:S(2)}) collective-permute-start(f32[2,128,128]{2,1,0:T(8,128)} %rest_4_.1), channel_id=1, source_target_pairs={{0,4},{1,5},{2,6},{3,7},{4,0},{5,1},{6,2},{7,3},{8,12},{9,13},{10,... | collective-permute-start | bytes 393224 | tf_op jit(solution)/shard_map/ppermute | solution.py:259
  7.1 8.4 %collective-permute-start.4 = (bf16[2,128,128]{2,1,0:T(8,128)(2,1)}, bf16[2,128,128]{2,1,0:T(8,128)(2,1)S(1)}, u32[]{:S(2)}, u32[]{:S(2)}) collective-permute-start(bf16[2,128,128]{2,1,0:T(8,128)(2,1)} %get-tuple-element.16), channel_id=1, source_target_pairs={{0,8},{1,9},{2,10},{3,11},{4,12},{5,13},{6,14},{7,15},{8,0},{9,1},... | collective-permute-start | bytes 196616 | tf_op jit(solution)/shard_map/ppermute | solution.py:259
  8.4 7.1 %collective-permute-start.5 = (bf16[2,128,128]{2,1,0:T(8,128)(2,1)}, bf16[2,128,128]{2,1,0:T(8,128)(2,1)S(1)}, u32[]{:S(2)}, u32[]{:S(2)}) collective-permute-start(bf16[2,128,128]{2,1,0:T(8,128)(2,1)} %get-tuple-element.17), channel_id=1, source_target_pairs={{0,16},{1,17},{2,18},{3,19},{4,20},{5,21},{6,22},{7,23},{8,24},{9,... | collective-permute-start | bytes 196616 | tf_op jit(solution)/shard_map/ppermute | solution.py:259
  9.6 7.2 %collective-permute-start.6 = (bf16[2,128,128]{2,1,0:T(8,128)(2,1)}, bf16[2,128,128]{2,1,0:T(8,128)(2,1)S(1)}, u32[]{:S(2)}, u32[]{:S(2)}) collective-permute-start(bf16[2,128,128]{2,1,0:T(8,128)(2,1)} %get-tuple-element.18), channel_id=1, source_target_pairs={{0,24},{1,25},{2,26},{3,27},{4,28},{5,29},{6,30},{7,31},{8,16},{9,... | collective-permute-start | bytes 196616 | tf_op jit(solution)/shard_map/ppermute | solution.py:259
  9.8 15.8 %collective-permute-start.3 = (s32[4,2]{1,0:T(4,128)}, s32[4,2]{1,0:T(4,128)S(1)}, u32[]{:S(2)}, u32[]{:S(2)}) collective-permute-start(s32[4,2]{1,0:T(4,128)} %get-tuple-element.14.rest_0_), channel_id=1, source_target_pairs={{0,3},{1,2},{2,1},{3,0},{4,7},{5,6},{6,5},{7,4},{8,11},{9,10},{10,... | collective-permute-start | bytes 104 | tf_op jit(solution)/shard_map/ppermute | solution.py:259
  15.5 11.3 %collective-permute-start.2 = (s32[4,2]{1,0:T(4,128)}, s32[4,2]{1,0:T(4,128)S(1)}, u32[]{:S(2)}, u32[]{:S(2)}) collective-permute-start(s32[4,2]{1,0:T(4,128)} %get-tuple-element.14.rest_0_), channel_id=1, source_target_pairs={{0,2},{1,3},{2,0},{3,1},{4,6},{5,7},{6,4},{7,5},{8,10},{9,11},{10,... | collective-permute-start | bytes 104 | tf_op jit(solution)/shard_map/ppermute | solution.py:259
  15.5 11.5 %collective-permute-start.1 = (s32[4,2]{1,0:T(4,128)}, s32[4,2]{1,0:T(4,128)S(1)}, u32[]{:S(2)}, u32[]{:S(2)}) collective-permute-start(s32[4,2]{1,0:T(4,128)} %get-tuple-element.14.rest_0_), channel_id=1, source_target_pairs={{0,1},{1,0},{2,3},{3,2},{4,5},{5,4},{6,7},{7,6},{8,9},{9,8},{10,11... | collective-permute-start | bytes 104 | tf_op jit(solution)/shard_map/ppermute | solution.py:259
  23.1 6.0 %collective-permute-start.16 = (bf16[2,128,128]{2,1,0:T(8,128)(2,1)S(1)}, bf16[2,128,128]{2,1,0:T(8,128)(2,1)S(1)}, u32[]{:S(2)}, u32[]{:S(2)}) collective-permute-start(bf16[2,128,128]{2,1,0:T(8,128)(2,1)S(1)} %get-tuple-element.20), channel_id=1, source_target_pairs={{0,10},{1,11},{2,8},{3,9},{4,14},{5,15},{6,12},{7,13},{8,2},{9,3},... | collective-permute-start | bytes 196616 | tf_op jit(solution)/shard_map/ppermute | solution.py:259
  24.4 6.0 %collective-permute-start.8 = (bf16[2,128,128]{2,1,0:T(8,128)(2,1)S(1)}, bf16[2,128,128]{2,1,0:T(8,128)(2,1)S(1)}, u32[]{:S(2)}, u32[]{:S(2)}) collective-permute-start(bf16[2,128,128]{2,1,0:T(8,128)(2,1)S(1)} %get-tuple-element.20), channel_id=1, source_target_pairs={{0,8},{1,9},{2,10},{3,11},{4,12},{5,13},{6,14},{7,15},{8,0},{9,1},... | collective-permute-start | bytes 196616 | tf_op jit(solution)/shard_map/ppermute | solution.py:259
  25.6 5.0 %collective-permute-start.17 = (bf16[2,128,128]{2,1,0:T(8,128)(2,1)S(1)}, bf16[2,128,128]{2,1,0:T(8,128)(2,1)S(1)}, u32[]{:S(2)}, u32[]{:S(2)}) collective-permute-start(bf16[2,128,128]{2,1,0:T(8,128)(2,1)S(1)} %get-tuple-element.21), channel_id=1, source_target_pairs={{0,18},{1,19},{2,16},{3,17},{4,22},{5,23},{6,20},{7,21},{8,26},{9,... | collective-permute-start | bytes 196616 | tf_op jit(solution)/shard_map/ppermute | solution.py:259
  26.8 7.7 %collective-permute-start.9 = (bf16[2,128,128]{2,1,0:T(8,128)(2,1)S(1)}, bf16[2,128,128]{2,1,0:T(8,128)(2,1)S(1)}, u32[]{:S(2)}, u32[]{:S(2)}) collective-permute-start(bf16[2,128,128]{2,1,0:T(8,128)(2,1)S(1)} %get-tuple-element.21), channel_id=1, source_target_pairs={{0,16},{1,17},{2,18},{3,19},{4,20},{5,21},{6,22},{7,23},{8,24},{9,... | collective-permute-start | bytes 196616 | tf_op jit(solution)/shard_map/ppermute | solution.py:259
  27.1 7.9 %collective-permute-start.18 = (bf16[2,128,128]{2,1,0:T(8,128)(2,1)S(1)}, bf16[2,128,128]{2,1,0:T(8,128)(2,1)S(1)}, u32[]{:S(2)}, u32[]{:S(2)}) collective-permute-start(bf16[2,128,128]{2,1,0:T(8,128)(2,1)S(1)} %get-tuple-element.22), channel_id=1, source_target_pairs={{0,26},{1,27},{2,24},{3,25},{4,30},{5,31},{6,28},{7,29},{8,18},{9,... | collective-permute-start | bytes 196616 | tf_op jit(solution)/shard_map/ppermute | solution.py:259
  29.2 6.6 %collective-permute-start.10 = (bf16[2,128,128]{2,1,0:T(8,128)(2,1)S(1)}, bf16[2,128,128]{2,1,0:T(8,128)(2,1)S(1)}, u32[]{:S(2)}, u32[]{:S(2)}) collective-permute-start(bf16[2,128,128]{2,1,0:T(8,128)(2,1)S(1)} %get-tuple-element.22), channel_id=1, source_target_pairs={{0,24},{1,25},{2,26},{3,27},{4,28},{5,29},{6,30},{7,31},{8,16},{9,... | collective-permute-start | bytes 196616 | tf_op jit(solution)/shard_map/ppermute | solution.py:259
  30.4 6.8 %collective-permute-start.15 = (bf16[2,128,128]{2,1,0:T(8,128)(2,1)S(1)}, bf16[2,128,128]{2,1,0:T(8,128)(2,1)S(1)}, u32[]{:S(2)}, u32[]{:S(2)}) collective-permute-start(bf16[2,128,128]{2,1,0:T(8,128)(2,1)S(1)} %get-tuple-element.19.rest_4_), channel_id=1, source_target_pairs={{0,2},{1,3},{2,0},{3,1},{4,6},{5,7},{6,4},{7,5},{8,10},{9,11},{10,... | collective-permute-start | bytes 196616 | tf_op jit(solution)/shard_map/ppermute | solution.py:259
  30.6 8.1 %collective-permute-start.11 = (bf16[2,128,128]{2,1,0:T(8,128)(2,1)S(1)}, bf16[2,128,128]{2,1,0:T(8,128)(2,1)S(1)}, u32[]{:S(2)}, u32[]{:S(2)}) collective-permute-start(bf16[2,128,128]{2,1,0:T(8,128)(2,1)S(1)} %get-tuple-element.19.rest_4_), channel_id=1, source_target_pairs={{0,1},{1,0},{2,3},{3,2},{4,5},{5,4},{6,7},{7,6},{8,9},{9,8},{10,11... | collective-permute-start | bytes 196616 | tf_op jit(solution)/shard_map/ppermute | solution.py:259
  34.5 4.2 %collective-permute-start.20 = (bf16[2,128,128]{2,1,0:T(8,128)(2,1)S(1)}, bf16[2,128,128]{2,1,0:T(8,128)(2,1)S(1)}, u32[]{:S(2)}, u32[]{:S(2)}) collective-permute-start(bf16[2,128,128]{2,1,0:T(8,128)(2,1)S(1)} %collective-permute-done.16.rest_13_), channel_id=1, source_target_pairs={{0,1},{1,0},{2,3},{3,2},{4,5},{5,4},{6,7},{7,6},{8,9},{9,8},{10,11... | collective-permute-start | bytes 196616 | tf_op jit(solution)/shard_map/ppermute | solution.py:259
  35.0 4.3 %collective-permute-start.12 = (bf16[2,128,128]{2,1,0:T(8,128)(2,1)S(1)}, bf16[2,128,128]{2,1,0:T(8,128)(2,1)S(1)}, u32[]{:S(2)}, u32[]{:S(2)}) collective-permute-start(bf16[2,128,128]{2,1,0:T(8,128)(2,1)S(1)} %collective-permute-done.8.rest_5_), channel_id=1, source_target_pairs={{0,1},{1,0},{2,3},{3,2},{4,5},{5,4},{6,7},{7,6},{8,9},{9,8},{10,11... | collective-permute-start | bytes 196616 | tf_op jit(solution)/shard_map/ppermute | solution.py:259
  35.8 3.5 %collective-permute-start.21 = (bf16[2,128,128]{2,1,0:T(8,128)(2,1)S(1)}, bf16[2,128,128]{2,1,0:T(8,128)(2,1)S(1)}, u32[]{:S(2)}, u32[]{:S(2)}) collective-permute-start(bf16[2,128,128]{2,1,0:T(8,128)(2,1)S(1)} %collective-permute-done.17.rest_14_), channel_id=1, source_target_pairs={{0,1},{1,0},{2,3},{3,2},{4,5},{5,4},{6,7},{7,6},{8,9},{9,8},{10,11... | collective-permute-start | bytes 196616 | tf_op jit(solution)/shard_map/ppermute | solution.py:259
  37.2 2.5 %collective-permute-start.13 = (bf16[2,128,128]{2,1,0:T(8,128)(2,1)S(1)}, bf16[2,128,128]{2,1,0:T(8,128)(2,1)S(1)}, u32[]{:S(2)}, u32[]{:S(2)}) collective-permute-start(bf16[2,128,128]{2,1,0:T(8,128)(2,1)S(1)} %collective-permute-done.9.rest_6_), channel_id=1, source_target_pairs={{0,1},{1,0},{2,3},{3,2},{4,5},{5,4},{6,7},{7,6},{8,9},{9,8},{10,11... | collective-permute-start | bytes 196616 | tf_op jit(solution)/shard_map/ppermute | solution.py:259
  38.7 1.3 %collective-permute-start.22 = (bf16[2,128,128]{2,1,0:T(8,128)(2,1)S(1)}, bf16[2,128,128]{2,1,0:T(8,128)(2,1)S(1)}, u32[]{:S(2)}, u32[]{:S(2)}) collective-permute-start(bf16[2,128,128]{2,1,0:T(8,128)(2,1)S(1)} %collective-permute-done.18.rest_15_), channel_id=1, source_target_pairs={{0,1},{1,0},{2,3},{3,2},{4,5},{5,4},{6,7},{7,6},{8,9},{9,8},{10,11... | collective-permute-start | bytes 196616 | tf_op jit(solution)/shard_map/ppermute | solution.py:259
  38.7 1.4 %collective-permute-start.14 = (bf16[2,128,128]{2,1,0:T(8,128)(2,1)S(1)}, bf16[2,128,128]{2,1,0:T(8,128)(2,1)S(1)}, u32[]{:S(2)}, u32[]{:S(2)}) collective-permute-start(bf16[2,128,128]{2,1,0:T(8,128)(2,1)S(1)} %collective-permute-done.10.rest_7_), channel_id=1, source_target_pairs={{0,1},{1,0},{2,3},{3,2},{4,5},{5,4},{6,7},{7,6},{8,9},{9,8},{10,11... | collective-permute-start | bytes 196616 | tf_op jit(solution)/shard_map/ppermute | solution.py:259
  39.3 1.3 %collective-permute-start.19 = (bf16[2,128,128]{2,1,0:T(8,128)(2,1)S(1)}, bf16[2,128,128]{2,1,0:T(8,128)(2,1)S(1)}, u32[]{:S(2)}, u32[]{:S(2)}) collective-permute-start(bf16[2,128,128]{2,1,0:T(8,128)(2,1)S(1)} %collective-permute-done.15.rest_12_), channel_id=1, source_target_pairs={{0,1},{1,0},{2,3},{3,2},{4,5},{5,4},{6,7},{7,6},{8,9},{9,8},{10,11... | collective-permute-start | bytes 196616 | tf_op jit(solution)/shard_map/ppermute | solution.py:259
  (6 other events, 52.6 us)

commit v4 on v3

v4 whole, which is shorter than its diff:
```python
import functools
import math

import jax
import jax.numpy as jnp
import numpy as np
from jax import lax
from jax.experimental import pallas as pl
from jax.experimental.pallas import tpu as pltpu
from jax.sharding import PartitionSpec as P

grad_scale = 0.03125
f32 = jnp.float32
bf16 = jnp.bfloat16


def dft_matrices(size):
    k = np.arange(size)
    angles = 2.0 * np.pi * ((k[:, None] * k[None, :]) % size) / size
    c = np.cos(angles) / math.sqrt(size)
    s = np.sin(angles) / math.sqrt(size)
    plus = np.block([[c, s], [-s, c]]).astype(np.float32)
    minus = np.block([[c, -s], [s, c]]).astype(np.float32)
    parts = []
    for full in (plus, minus):
        high = full.astype(bf16)
        low = (full - high.astype(np.float32)).astype(bf16)
        parts.append((high, low))
    (ph, plo), (mh, mlo) = parts
    right = np.stack([np.concatenate([ph, ph, plo], 0), np.concatenate([mh, mh, mlo], 0)])
    left = np.stack([np.concatenate([mh, mh, mlo], 1), np.concatenate([ph, ph, plo], 1)])
    return left, right


def taken_by(d, i, members, dp, positions):
    per_home = positions // dp
    home = lax.div(d, per_home) * members + i
    return home * per_home + lax.rem(d, per_home)


def window_kernel(members, pos_ref, obj_ref, phase_ref, out_ref, kern_ref, buf, sems):
    depth, _, window, _ = out_ref.shape
    rows, cols = obj_ref.shape[-2:]
    tall, wide = buf.shape[-2:]
    lane = lax.rem(lax.axis_index("dp"), members)

    def corner(d):
        at = taken_by(d, lane, members, lax.axis_size("dp"), pos_ref.shape[0])
        row, col = pos_ref[at, 0], pos_ref[at, 1]
        row_base = pl.multiple_of(jnp.minimum(row >> 3, (rows - tall) // 8) * 8, 8)
        col_base = pl.multiple_of(jnp.minimum(col >> 7, (cols - wide) // 128) * 128, 128)
        return row_base, col_base, row - row_base, col - col_base

    def copy(d):
        row_base, col_base, _, _ = corner(d)
        return pltpu.make_async_copy(
            obj_ref.at[:, pl.ds(row_base, tall), pl.ds(col_base, wide)], buf.at[d], sems.at[d]
        )

    for d in range(depth):
        copy(d).start()
    kern_ref[0] = jnp.cos(phase_ref[...])
    kern_ref[1] = jnp.sin(phase_ref[...])
    for d in range(depth):
        copy(d).wait()
        _, _, row_off, col_off = corner(d)
        lift = jnp.where(row_off == 0, 0, tall - row_off)
        shift = jnp.where(col_off == 0, 0, wide - col_off)
        for part in range(2):
            block = pltpu.roll(buf[d, part], shift, 1)[:, :window]
            block = pltpu.roll(block, lift, 0)[:window]
            out_ref[d, part] = block.astype(bf16)


def take_windows(all_positions, obj, phase, depth, members):
    window = phase.shape[-1]
    tall, wide = window + 8, window + 128
    vmem = pl.BlockSpec(memory_space=pltpu.VMEM)
    return pl.pallas_call(
        functools.partial(window_kernel, members),
        out_shape=[
            jax.ShapeDtypeStruct((depth, 2, window, window), bf16),
            jax.ShapeDtypeStruct((2, window, window), f32),
        ],
        in_specs=[
            pl.BlockSpec(memory_space=pltpu.SMEM),
            pl.BlockSpec(memory_space=pl.ANY),
            vmem,
        ],
        out_specs=[vmem, vmem],
        scratch_shapes=[
            pltpu.VMEM((depth, 2, tall, wide), f32),
            pltpu.SemaphoreType.DMA((depth,)),
        ],
        name="take_windows",
    )(all_positions, obj, phase)


def split(x):
    high = x.astype(bf16)
    return high, (x - high.astype(f32)).astype(bf16)


def cmul(a, b):
    return a[0] * b[0] - a[1] * b[1], a[0] * b[1] + a[1] * b[0]


def cmul_conj(a, b):
    return a[0] * b[0] + a[1] * b[1], a[0] * b[1] - a[1] * b[0]


def wave_kernel(members, probe_ref, kern_ref, left_ref, right_ref, t_ref, *rest):
    meas_refs, (out_ref, meas) = rest[:-2], rest[-2:]
    slices = t_ref.shape[0]
    copies = out_ref.shape[0] // slices
    window = probe_ref.shape[-1]
    per_home = slices // len(meas_refs)
    own, cluster = lax.axis_index("depth"), lax.div(lax.axis_index("dp"), members)
    home = lax.div(own, per_home)
    for m, meas_ref in enumerate(meas_refs):

        @pl.when(home ^ cluster == m)
        def _():
            meas[...] = meas_ref[lax.rem(own, per_home)]

    def t_of(k):
        return t_ref[k, 0].astype(f32), t_ref[k, 1].astype(f32)

    def passes(x, axis, exact):
        if not exact:
            return x.astype(bf16)
        high, low = split(x)
        return jnp.concatenate([high, low, high], axis=axis)

    def rows(field, sign, exact):
        x = passes(jnp.concatenate(field, axis=0), 0, exact)
        y = jnp.dot(left_ref[sign, :, : x.shape[0]], x, preferred_element_type=f32)
        return y[:window], y[window:]

    def cols(field, sign, exact):
        x = passes(jnp.concatenate(field, axis=1), 1, exact)
        y = jnp.dot(x, right_ref[sign, : x.shape[1]], preferred_element_type=f32)
        return y[:, :window], y[:, window:]

    plus, minus = 0, 1

    def transform(field, sign, exact):
        return cols(rows(field, sign, exact), sign, exact)

    kern = (kern_ref[0], kern_ref[1])
    psi = (probe_ref[0], probe_ref[1])
    kept = []
    for k in range(slices):
        kept.append(psi)
        spectrum = transform(cmul(t_of(k), psi), minus, True)
        if k < slices - 1:
            psi = transform(cmul(kern, spectrum), plus, True)

    re, im = spectrum
    scale = 2.0 * (re * re + im * im - meas[...])
    returned = transform((scale * re, scale * im), plus, False)
    for k in reversed(range(slices)):
        re, im = cmul_conj(kept[k], returned)
        term = (re * grad_scale).astype(bf16), (im * grad_scale).astype(bf16)
        for n in range(copies):
            for part in range(2):
                out_ref[k * copies + n, part] = term[part]
        if k > 0:
            spectrum = transform(cmul_conj(t_of(k), returned), minus, False)
            returned = transform(cmul_conj(kern, spectrum), plus, False)


def run_waves(probe, kern, windows, measured, members):
    slices = windows.shape[0]
    window = probe.shape[-1]
    left, right = dft_matrices(window)
    vmem = pl.BlockSpec(memory_space=pltpu.VMEM)
    return pl.pallas_call(
        functools.partial(wave_kernel, members),
        out_shape=jax.ShapeDtypeStruct((slices * members // 2, 2, window, window), bf16),
        in_specs=[vmem] * (5 + len(measured)),
        out_specs=vmem,
        scratch_shapes=[pltpu.VMEM((window, window), f32)],
        compiler_params=pltpu.CompilerParams(vmem_limit_bytes=40 * 1024 * 1024),
        name="run_waves",
    )(probe, kern, jnp.asarray(left), jnp.asarray(right), windows, *measured)


def place_kernel(members, pos_ref, *rest):
    terms_refs, (out_ref, canvas) = rest[:2], rest[2:]
    _, stripe, cols = out_ref.shape
    count, _, window, _ = terms_refs[0].shape
    pairs = members // 2
    wide = window + 128
    dp_index = lax.axis_index("dp")
    first_row = dp_index * stripe
    canvas[:, window : window + stripe, :] = jnp.zeros((2, stripe, canvas.shape[2]), f32)
    for other, terms_ref in enumerate(terms_refs):
        for n in range(count):
            i = n % pairs * 2 + (dp_index + other) % 2
            at = taken_by(n // pairs, i, members, lax.axis_size("dp"), pos_ref.shape[0])
            row = pos_ref[at, 0] - first_row + window
            col = pos_ref[at, 1]
            row_base = pl.multiple_of((row >> 3) << 3, 8)
            col_base = pl.multiple_of((col >> 7) << 7, 128)

            @pl.when((row > 0) & (row < window + stripe))
            def _():
                for part in range(2):
                    block = terms_ref[n, part].astype(f32)
                    block = jnp.concatenate([block, jnp.zeros((8, window), f32)], axis=0)
                    block = pltpu.roll(block, row - row_base, 0)
                    block = jnp.concatenate([block, jnp.zeros((window + 8, 128), f32)], axis=1)
                    block = pltpu.roll(block, col - col_base, 1)
                    put = (part, pl.ds(row_base, window + 8), pl.ds(col_base, wide))
                    canvas[put] = canvas[put] + block

    out_ref[...] = canvas[:, window : window + stripe, :cols]


def place_windows(positions, own, other, members, stripe, cols):
    window = own.shape[-1]
    vmem = pl.BlockSpec(memory_space=pltpu.VMEM)
    tall = window + (stripe + 7) // 8 * 8 + window + 8
    return pl.pallas_call(
        functools.partial(place_kernel, members),
        out_shape=jax.ShapeDtypeStruct((2, stripe, cols), f32),
        in_specs=[pl.BlockSpec(memory_space=pltpu.SMEM), vmem, vmem],
        out_specs=vmem,
        scratch_shapes=[pltpu.VMEM((2, tall, cols + 128), f32)],
        compiler_params=pltpu.CompilerParams(vmem_limit_bytes=40 * 1024 * 1024),
        name="place_windows",
    )(positions, own, other)


def swap(block, distance):
    return lax.ppermute(block, "dp", [(j, j ^ distance) for j in range(lax.axis_size("dp"))])


def on_device(object_slices, positions, probe_field, propagator_phase, measured):
    depth, dp = lax.axis_size("depth"), lax.axis_size("dp")
    clusters = depth // positions.shape[0]
    members = dp // clusters
    rows, cols = object_slices.shape[-2:]

    all_positions = lax.all_to_all(jnp.tile(positions, (dp, 1)), "dp", 0, 0, tiled=True)
    windows, kern = take_windows(all_positions, object_slices[0], propagator_phase, depth, members)
    windows = lax.all_to_all(windows, "depth", 0, 0, tiled=True)
    targets = [measured] + [swap(measured, m * members) for m in range(1, clusters)]
    terms = run_waves(probe_field, kern, windows, targets, members)

    groups = [
        [d * dp + w * members + i for d in range(depth) for i in range(core, members, 2)]
        for w in range(clusters)
        for core in range(2)
    ]
    terms = lax.all_to_all(terms, ("depth", "dp"), 0, 0, axis_index_groups=groups, tiled=True)
    return place_windows(all_positions, terms, swap(terms, 1), members, rows // dp, cols)[None]


def solution(mesh):
    placed = (P("depth", None, None, None), P("dp", None), P(), P(), P("dp", None, None))
    return jax.shard_map(
        on_device,
        mesh=mesh,
        in_specs=placed,
        out_specs=P("depth", None, "dp", None),
        check_vma=False,
    )
```

time: 43.7 us -> 53.2 us (1.22)
  the two profiles are of different devices: /device:TPU:17 before, /device:TPU:0 now
where the time goes in v4:
time: 53.2 us; the launch traced here: 52.8 us
  blocking collectives  25.1 us (47%)
  Pallas kernels  10.7 us (20%)
  waiting for transfers between devices  10 us (19%)
  starting transfers between devices  4.28 us (8%)
  local copies, waits for them, and re-layouts  2.54 us (5%)
    all_to_all x1, blocking collectives, on_device(): lax.all_to_all(terms, ('depth', 'dp'), 0, 0, axis_index_groups=groups, ti...  13.4 us
    all_to_all x1, blocking collectives, on_device(): lax.all_to_all(jnp.tile(positions, (dp, 1)), 'dp', 0, 0, tiled=True)  11.7 us
    ppermute x2, waiting for transfers between devices, swap(): lax.ppermute(block, 'dp', [(j, j ^ distance) for j in range(lax.axis_size...  10 us
    pallas_call x1, Pallas kernels, run_waves(): pl.pallas_call(functools.partial(wave_kernel, members), out_shape=jax.Sha...  5.38 us
    all_to_all x1, starting transfers between devices, on_device(): windows = lax.all_to_all(windows, 'depth', 0, 0, tiled=True)  3.73 us
    pallas_call x1, Pallas kernels, take_windows(): pl.pallas_call(functools.partial(window_kernel, members), out_shape=[jax....  3.21 us
    pallas_call x1, Pallas kernels, place_windows(): pl.pallas_call(functools.partial(place_kernel, members), out_shape=jax.Sh...  2.13 us
    unnamed x13, local copies, waits for them, and re-layouts  1.81 us
  transfers between devices with their start and end apart: 3, of which 2 were waited for; matrix products, arithmetic and copies ran while one was open for 0% of the time, Pallas kernels for 0%

profile of v4, /device:TPU:0, one launch (start us, length us, event | category | flops | bytes accessed | tf_op | source)
XLA Modules:
  0.0 52.8 jit_solution(9815366992628269862)
XLA Ops:
  0.0 0.0 copy-start
  0.0 0.0 copy-start.1
  0.0 0.0 copy-start.3
  0.0 0.0 copy-start.2
  0.0 0.9 %copy.14 = s32[2,2]{0,1:T(2,128)S(1)} copy(s32[2,2]{1,0:T(2,128)} %param.8) | data formatting | bytes 32 | tf_op args[1]
  0.9 11.7 %all_to_all.18 = s32[8,2,2]{1,2,0:T(2,128)S(1)} all-to-all(s32[8,2,2]{1,2,0:T(2,128)S(1)} %tile.2), channel_id=1, replica_groups=mesh['depth'=4,'dp'=8] {'dp'}, dimensions={0} | all-to-all | bytes 256 | tf_op jit(solution)/shard_map/all_to_all | solution.py:246
  12.6 0.7 %copy.18 = s32[8,2,2]{2,1,0:T(2,128)} copy(s32[8,2,2]{1,2,0:T(2,128)S(1)} %all_to_all.18) | data formatting | bytes 256 | tf_op jit(solution)/shard_map/all_to_all | solution.py:246
  13.4 3.2 %take_windows.1 = (bf16[4,2,128,128]{3,2,1,0:T(8,128)(2,1)}, f32[2,128,128]{2,1,0:T(8,128)}) custom-call(s32[16,2]{1,0:T(8,128)} %bitcast.3, f32[2,768,768]{2,1,0:T(8,128)} %bitcast.5, f32[128,128]{1,0:T(8,128)} %phase_ref.1), custom_call_target="tpu_custom_call" | custom-call | tf_op jit(solution)/shard_map/take_windows/pallas_call | solution.py:79
  16.6 3.7 %all-to-all-start.1 = ((bf16[4,2,128,128]{3,2,1,0:T(8,128)(2,1)}), bf16[4,2,128,128]{3,2,1,0:T(8,128)(2,1)S(1)}, u32[]{:S(2)}, u32[]{:S(2)}) async-start(bf16[4,2,128,128]{3,2,1,0:T(8,128)(2,1)} %get-tuple-element.8), calls=%async_computation.1 | async-start | bytes 524288 | tf_op jit(solution)/shard_map/all_to_all | solution.py:248
  20.3 0.0 copy-done.3
  20.3 0.6 %collective-permute-start = (f32[2,128,128]{2,1,0:T(8,128)S(1)}, f32[2,128,128]{2,1,0:T(8,128)S(1)}, u32[]{:S(2)}, u32[]{:S(2)}) collective-permute-start(f32[2,128,128]{2,1,0:T(8,128)S(1)} %copy-done.3), channel_id=1, source_target_pairs={{0,4},{1,5},{2,6},{3,7},{4,0},{5,1},{6,2},{7,3},{8,12},{9,13},{10,... | collective-permute-start | bytes 393224 | tf_op jit(solution)/shard_map/ppermute | solution.py:237
  20.9 8.1 %collective-permute-done.rest_1_ = f32[2,128,128]{2,1,0:T(8,128)S(1)} collective-permute-done((f32[2,128,128]{2,1,0:T(8,128)S(1)}, f32[2,128,128]{2,1,0:T(8,128)S(1)}, u32[]{:S(2)}, u32[]{:S(2)}) %collective-permute-start) | collective-permute-done | bytes 131104 | tf_op jit(solution)/shard_map/ppermute | solution.py:237
  29.0 0.0 all-to-all-done.1.t_ref
  29.0 0.0 copy-done
  29.0 0.0 copy-done.1
  29.0 0.0 copy-done.2
  29.0 0.0 copy-start.4
  29.0 0.9 %copy-done.4 = f32[2,128,128]{2,1,0:T(8,128)S(1)} copy-done((f32[2,128,128]{2,1,0:T(8,128)S(1)}, f32[2,128,128]{2,1,0:T(8,128)}, u32[]{:S(2)}) %copy-start.4) | copy-done | bytes 131096
  29.9 5.4 %run_waves.1 = bf16[8,2,128,128]{3,2,1,0:T(8,128)(2,1)S(1)} custom-call(f32[2,128,128]{2,1,0:T(8,128)S(1)} %copy-done.2, f32[2,128,128]{2,1,0:T(8,128)S(1)} %copy-done.4, bf16[2,256,768]{2,1,0:T(8,128)(2,1)S(1)} %copy-done.1, bf16[2,768,256]{2,1,0:T(8,128)(2,1)S(1)} %copy-done, bf16[4,2,128,128]{3,2,1,0:T(8,128)(2,1)S(1)} %all-to-all-done.1.t_ref, ...), custom_call_target="tpu_custom_call" | custom-call | tf_op jit(solution)/shard_map/run_waves/pallas_call | solution.py:178
  35.3 13.4 %all_to_all.19.rest_0_ = bf16[8,2,128,128]{3,2,1,0:T(8,128)(2,1)S(1)} all-to-all(bf16[8,2,128,128]{3,2,1,0:T(8,128)(2,1)S(1)} %run_waves.1), channel_id=1, replica_groups={{0,2,8,10,16,18,24,26},{1,3,9,11,17,19,25,27},{4,6,12,14,20,22,28,30},{..., dimensions={0} | all-to-all | bytes 1048576 | tf_op jit(solution)/shard_map/all_to_all | solution.py:257
  48.7 0.0 collective-permute-start.1
  48.7 1.9 %collective-permute-done.1.rest_1_ = bf16[8,2,128,128]{3,2,1,0:T(8,128)(2,1)S(1)} collective-permute-done((bf16[8,2,128,128]{3,2,1,0:T(8,128)(2,1)S(1)}, bf16[8,2,128,128]{3,2,1,0:T(8,128)(2,1)S(1)}, u32[]{:S(2)}, u32[]{:S(2)}) %collective-permute-start.1) | collective-permute-done | bytes 524320 | tf_op jit(solution)/shard_map/ppermute | solution.py:237
  50.6 0.0 copy-done.5
  50.6 2.1 %place_windows.1 = f32[2,96,768]{2,1,0:T(8,128)} custom-call(s32[16,2]{1,0:T(8,128)S(1)} %bitcast.4, bf16[8,2,128,128]{3,2,1,0:T(8,128)(2,1)S(1)} %all_to_all.19.rest_0_, bf16[8,2,128,128]{3,2,1,0:T(8,128)(2,1)S(1)} %collective-permute-done.1.rest_1_), custom_call_target="tpu_custom_call" | custom-call | tf_op jit(solution)/shard_map/place_windows/pallas_call | solution.py:225
  (2 shorter events, 0.0 us)
Async XLA Ops:
  0.0 29.0 %copy-start = (bf16[2,768,256]{2,1,0:T(8,128)(2,1)S(1)}, bf16[2,768,256]{2,1,0:T(8,128)(2,1)}, u32[]{:S(2)}) copy-start(bf16[2,768,256]{2,1,0:T(8,128)(2,1)} %constant.5.clone.right_ref) | copy-start | bytes 2359300
  0.0 29.0 %copy-start.1 = (bf16[2,256,768]{2,1,0:T(8,128)(2,1)S(1)}, bf16[2,256,768]{2,1,0:T(8,128)(2,1)}, u32[]{:S(2)}) copy-start(bf16[2,256,768]{2,1,0:T(8,128)(2,1)} %constant.4.clone.left_ref) | copy-start | bytes 2359300
  0.0 20.3 %copy-start.3 = (f32[2,128,128]{2,1,0:T(8,128)S(1)}, f32[2,128,128]{2,1,0:T(8,128)}, u32[]{:S(2)}) copy-start(f32[2,128,128]{2,1,0:T(8,128)} %rest_0_.1) | copy-start | bytes 393220
  0.0 29.0 %copy-start.2 = (f32[2,128,128]{2,1,0:T(8,128)S(1)}, f32[2,128,128]{2,1,0:T(8,128)}, u32[]{:S(2)}) copy-start(f32[2,128,128]{2,1,0:T(8,128)} %probe_ref.1) | copy-start | bytes 393220
  13.4 37.3 %copy-start.5 = (s32[8,2,2]{2,1,0:T(2,128)S(1)}, s32[8,2,2]{2,1,0:T(2,128)}, u32[]{:S(2)}) copy-start(s32[8,2,2]{2,1,0:T(2,128)} %copy.18) | copy-start | bytes 388
  16.6 12.4 %all-to-all-start.1 = ((bf16[4,2,128,128]{3,2,1,0:T(8,128)(2,1)}), bf16[4,2,128,128]{3,2,1,0:T(8,128)(2,1)S(1)}, u32[]{:S(2)}, u32[]{:S(2)}) async-start(bf16[4,2,128,128]{3,2,1,0:T(8,128)(2,1)} %get-tuple-element.8), calls=%async_computation.1 | async-start | bytes 524288 | tf_op jit(solution)/shard_map/all_to_all | solution.py:248
  20.3 8.7 %collective-permute-start = (f32[2,128,128]{2,1,0:T(8,128)S(1)}, f32[2,128,128]{2,1,0:T(8,128)S(1)}, u32[]{:S(2)}, u32[]{:S(2)}) collective-permute-start(f32[2,128,128]{2,1,0:T(8,128)S(1)} %copy-done.3), channel_id=1, source_target_pairs={{0,4},{1,5},{2,6},{3,7},{4,0},{5,1},{6,2},{7,3},{8,12},{9,13},{10,... | collective-permute-start | bytes 393224 | tf_op jit(solution)/shard_map/ppermute | solution.py:237
  29.0 0.9 %copy-start.4 = (f32[2,128,128]{2,1,0:T(8,128)S(1)}, f32[2,128,128]{2,1,0:T(8,128)}, u32[]{:S(2)}) copy-start(f32[2,128,128]{2,1,0:T(8,128)} %get-tuple-element.7.kern_ref) | copy-start | bytes 393220
  48.7 1.9 %collective-permute-start.1 = (bf16[8,2,128,128]{3,2,1,0:T(8,128)(2,1)S(1)}, bf16[8,2,128,128]{3,2,1,0:T(8,128)(2,1)S(1)}, u32[]{:S(2)}, u32[]{:S(2)}) collective-permute-start(bf16[8,2,128,128]{3,2,1,0:T(8,128)(2,1)S(1)} %all_to_all.19.rest_0_), channel_id=1, source_target_pairs={{0,1},{1,0},{2,3},{3,2},{4,5},{5,4},{6,7},{7,6},{8,9},{9,8},{10,11... | collective-permute-start | bytes 1572872 | tf_op jit(solution)/shard_map/ppermute | solution.py:237

commit v5 on v3

v5 whole, which is shorter than its diff:
```python
import functools
import math

import jax
import jax.numpy as jnp
import numpy as np
from jax import lax
from jax.experimental import pallas as pl
from jax.experimental.pallas import tpu as pltpu
from jax.sharding import PartitionSpec as P

grad_scale = 0.03125
f32 = jnp.float32
bf16 = jnp.bfloat16


def dft_matrices(size):
    k = np.arange(size)
    angles = 2.0 * np.pi * ((k[:, None] * k[None, :]) % size) / size
    c = np.cos(angles) / math.sqrt(size)
    s = np.sin(angles) / math.sqrt(size)
    plus = np.block([[c, s], [-s, c]]).astype(np.float32)
    minus = np.block([[c, -s], [s, c]]).astype(np.float32)
    parts = []
    for full in (plus, minus):
        high = full.astype(bf16)
        low = (full - high.astype(np.float32)).astype(bf16)
        parts.append((high, low))
    (ph, plo), (mh, mlo) = parts
    right = np.stack([np.concatenate([ph, ph, plo], 0), np.concatenate([mh, mh, mlo], 0)])
    left = np.stack([np.concatenate([mh, mh, mlo], 1), np.concatenate([ph, ph, plo], 1)])
    return left, right


def indices(clusters):
    dp_index = lax.axis_index("dp")
    return lax.axis_index("depth"), lax.div(dp_index, lax.axis_size("dp") // clusters), dp_index


def window_kernel(obj_ref, phase_ref, *rest):
    buf, sems = rest[-2:]
    depth = buf.shape[0]
    clusters = len(rest) - 4 - depth
    pos_refs = rest[:clusters]
    out_refs = rest[clusters : clusters + depth]
    table_ref, kern_ref = rest[clusters + depth : -2]
    own, cluster, _ = indices(clusters)
    per_home = depth // clusters
    window = out_refs[0].shape[-1]
    rows, cols = obj_ref.shape[-2:]
    tall, wide = buf.shape[-2:]

    for home in range(clusters):
        for q in range(per_home):
            for axis in range(2):
                value = pos_refs[0][q, axis]
                for m in range(1, clusters):
                    value = jnp.where(home ^ cluster == m, pos_refs[m][q, axis], value)
                table_ref[home * per_home + q, axis] = value

    def corner(m):
        at = own ^ m
        row, col = table_ref[at, 0], table_ref[at, 1]
        row_base = pl.multiple_of(jnp.minimum(row >> 3, (rows - tall) // 8) * 8, 8)
        col_base = pl.multiple_of(jnp.minimum(col >> 7, (cols - wide) // 128) * 128, 128)
        return row_base, col_base, row - row_base, col - col_base

    def copy(m):
        row_base, col_base, _, _ = corner(m)
        return pltpu.make_async_copy(
            obj_ref.at[:, pl.ds(row_base, tall), pl.ds(col_base, wide)], buf.at[m], sems.at[m]
        )

    for m in range(depth):
        copy(m).start()
    kern_ref[0] = jnp.cos(phase_ref[...])
    kern_ref[1] = jnp.sin(phase_ref[...])
    for m in range(depth):
        copy(m).wait()
        _, _, row_off, col_off = corner(m)
        lift = jnp.where(row_off == 0, 0, tall - row_off)
        shift = jnp.where(col_off == 0, 0, wide - col_off)
        for part in range(2):
            block = pltpu.roll(buf[m, part], shift, 1)[:, :window]
            block = pltpu.roll(block, lift, 0)[:window]
            out_refs[m][part] = block.astype(bf16)


def take_windows(obj, phase, positions, depth):
    window = phase.shape[-1]
    tall, wide = window + 8, window + 128
    smem = pl.BlockSpec(memory_space=pltpu.SMEM)
    vmem = pl.BlockSpec(memory_space=pltpu.VMEM)
    out = pl.pallas_call(
        window_kernel,
        out_shape=[jax.ShapeDtypeStruct((2, window, window), bf16)] * depth
        + [
            jax.ShapeDtypeStruct((depth, 2), jnp.int32),
            jax.ShapeDtypeStruct((2, window, window), f32),
        ],
        in_specs=[pl.BlockSpec(memory_space=pl.ANY), vmem] + [smem] * len(positions),
        out_specs=[vmem] * depth + [smem, vmem],
        scratch_shapes=[
            pltpu.VMEM((depth, 2, tall, wide), f32),
            pltpu.SemaphoreType.DMA((depth,)),
        ],
        name="take_windows",
    )(obj, phase, *positions)
    return list(out[:depth]), out[depth], out[depth + 1]


def split(x):
    high = x.astype(bf16)
    return high, (x - high.astype(f32)).astype(bf16)


def cmul(a, b):
    return a[0] * b[0] - a[1] * b[1], a[0] * b[1] + a[1] * b[0]


def cmul_conj(a, b):
    return a[0] * b[0] + a[1] * b[1], a[0] * b[1] - a[1] * b[0]


def wave_kernel(slices, clusters, probe_ref, kern_ref, left_ref, right_ref, *rest):
    t_refs, rest = rest[:slices], rest[slices:]
    meas_refs = rest[:clusters]
    out_ref, trans, meas = rest[-3:]
    own, cluster, _ = indices(clusters)
    per_home = slices // clusters
    window = probe_ref.shape[-1]

    for m in range(slices):
        trans[own ^ m] = t_refs[m][...]
    home = lax.div(own, per_home)
    for m, meas_ref in enumerate(meas_refs):

        @pl.when(home ^ cluster == m)
        def _():
            meas[...] = meas_ref[lax.rem(own, per_home)]

    def t_of(k):
        return trans[k, 0].astype(f32), trans[k, 1].astype(f32)

    def passes(x, axis, exact):
        if not exact:
            return x.astype(bf16)
        high, low = split(x)
        return jnp.concatenate([high, low, high], axis=axis)

    def rows(field, sign, exact):
        x = passes(jnp.concatenate(field, axis=0), 0, exact)
        y = jnp.dot(left_ref[sign, :, : x.shape[0]], x, preferred_element_type=f32)
        return y[:window], y[window:]

    def cols(field, sign, exact):
        x = passes(jnp.concatenate(field, axis=1), 1, exact)
        y = jnp.dot(x, right_ref[sign, : x.shape[1]], preferred_element_type=f32)
        return y[:, :window], y[:, window:]

    plus, minus = 0, 1

    def transform(field, sign, exact):
        return cols(rows(field, sign, exact), sign, exact)

    kern = (kern_ref[0], kern_ref[1])
    psi = (probe_ref[0], probe_ref[1])
    kept = []
    for k in range(slices):
        kept.append(psi)
        spectrum = transform(cmul(t_of(k), psi), minus, True)
        if k < slices - 1:
            psi = transform(cmul(kern, spectrum), plus, True)

    re, im = spectrum
    scale = 2.0 * (re * re + im * im - meas[...])
    returned = transform((scale * re, scale * im), plus, False)
    for k in reversed(range(slices)):
        re, im = cmul_conj(kept[k], returned)
        out_ref[own ^ k, 0] = (re * grad_scale).astype(bf16)
        out_ref[own ^ k, 1] = (im * grad_scale).astype(bf16)
        if k > 0:
            spectrum = transform(cmul_conj(t_of(k), returned), minus, False)
            returned = transform(cmul_conj(kern, spectrum), plus, False)


def run_waves(probe, kern, windows, measured, tables):
    slices = len(windows)
    window = probe.shape[-1]
    left, right = dft_matrices(window)
    vmem = pl.BlockSpec(memory_space=pltpu.VMEM)
    smem = pl.BlockSpec(memory_space=pltpu.SMEM)
    return pl.pallas_call(
        functools.partial(wave_kernel, slices, len(measured)),
        out_shape=jax.ShapeDtypeStruct((slices, 2, window, window), bf16),
        in_specs=[vmem] * (4 + slices + len(measured)) + [smem] * len(tables),
        out_specs=vmem,
        scratch_shapes=[
            pltpu.VMEM((slices, 2, window, window), bf16),
            pltpu.VMEM((window, window), f32),
        ],
        compiler_params=pltpu.CompilerParams(vmem_limit_bytes=40 * 1024 * 1024),
        name="run_waves",
    )(probe, kern, jnp.asarray(left), jnp.asarray(right), *windows, *measured, *tables)


def pack_kernel(own_ref, other_ref, *out_refs):
    for m, out_ref in enumerate(out_refs):
        out_ref[0] = own_ref[m]
        out_ref[1] = other_ref[m]


def pack(own, other):
    vmem = pl.BlockSpec(memory_space=pltpu.VMEM)
    return pl.pallas_call(
        pack_kernel,
        out_shape=[jax.ShapeDtypeStruct((2,) + own.shape[1:], own.dtype)] * own.shape[0],
        in_specs=[vmem, vmem],
        out_specs=[vmem] * own.shape[0],
        name="pack_terms",
    )(own, other)


def place_kernel(depth, planes, *rest):
    out_ref, canvas = rest[-2:]
    table_refs = rest[: 2 * planes]
    own_block, *blocks = rest[2 * planes : -2]
    _, stripe, cols = out_ref.shape
    window = own_block.shape[-1]
    wide = window + 128
    own, dp_index = lax.axis_index("depth"), lax.axis_index("dp")
    core = lax.rem(dp_index, 2)
    first_row = dp_index * stripe
    canvas[:, window : window + stripe, :] = jnp.zeros((2, stripe, canvas.shape[2]), f32)

    def place(block_ref, n, at, valid):
        row, col = at
        row = row - first_row + window
        row_base = pl.multiple_of((row >> 3) << 3, 8)
        col_base = pl.multiple_of((col >> 7) << 7, 128)

        @pl.when((row > 0) & (row < window + stripe) & valid)
        def _():
            for part in range(2):
                block = block_ref[n, part].astype(f32)
                block = jnp.concatenate([block, jnp.zeros((8, window), f32)], axis=0)
                block = pltpu.roll(block, row - row_base, 0)
                block = jnp.concatenate([block, jnp.zeros((window + 8, 128), f32)], axis=1)
                block = pltpu.roll(block, col - col_base, 1)
                put = (part, pl.ds(row_base, window + 8), pl.ds(col_base, wide))
                canvas[put] = canvas[put] + block

    def position(plane, other, d):
        return [table_refs[2 * plane + other][d, axis] for axis in range(2)]

    for n in range(2):
        place(own_block, n, position(0, n, own), True)
    for held in range(2):
        for r in range(planes // 2):
            for m in range(depth):
                block_ref = blocks[(held * (planes // 2) + r) * depth + m]
                for n in range(2):
                    choice = []
                    for h in range(2):
                        first = position(2 * r + h, held ^ n, own ^ m)
                        choice.append(first)
                    by = core ^ held
                    at = [jnp.where(by == 0, choice[0][axis], choice[1][axis]) for axis in range(2)]
                    place(block_ref, n, at, (by == 1) if r == m == 0 else True)

    out_ref[...] = canvas[:, window : window + stripe, :cols]


def place_windows(tables, own_block, blocks, depth, stripe, cols):
    window = own_block.shape[-1]
    vmem = pl.BlockSpec(memory_space=pltpu.VMEM)
    smem = pl.BlockSpec(memory_space=pltpu.SMEM)
    tall = window + (stripe + 7) // 8 * 8 + window + 8
    return pl.pallas_call(
        functools.partial(place_kernel, depth, len(tables) // 2),
        out_shape=jax.ShapeDtypeStruct((2, stripe, cols), f32),
        in_specs=[smem] * len(tables) + [vmem] * (1 + len(blocks)),
        out_specs=vmem,
        scratch_shapes=[pltpu.VMEM((2, tall, cols + 128), f32)],
        compiler_params=pltpu.CompilerParams(vmem_limit_bytes=48 * 1024 * 1024),
        name="place_windows",
    )(*tables, own_block, *blocks)


def swap(block, depth_distance, dp_distances):
    depth, dp = lax.axis_size("depth"), lax.axis_size("dp")
    route = [
        (d * dp + j, (d ^ depth_distance) * dp + (j ^ dp_distances[j % 2]))
        for d in range(depth)
        for j in range(dp)
        if depth_distance or dp_distances[j % 2]
    ]
    return lax.ppermute(block, ("depth", "dp"), route)


def on_device(object_slices, positions, probe_field, propagator_phase, measured):
    depth, dp = lax.axis_size("depth"), lax.axis_size("dp")
    clusters = depth // positions.shape[0]
    members = dp // clusters
    planes = members // 2
    rows, cols = object_slices.shape[-2:]
    across = (1, 1)

    homes = [(m * members, m * members) for m in range(1, clusters)]
    all_homes = [positions] + [swap(positions, 0, home) for home in homes]
    windows, table, kern = take_windows(object_slices[0], propagator_phase, all_homes, depth)
    windows = [windows[0]] + [swap(windows[m], m, (0, 0)) for m in range(1, depth)]
    late, kern = lax.optimization_barrier((measured, kern))
    targets = [measured] + [swap(late, 0, home) for home in homes]
    tables = []
    for plane in range(planes):
        near = swap(table, 0, (2 * plane, 2 * plane)) if plane else table
        tables += [near, swap(near, 0, across)]
    terms = run_waves(probe_field, kern, windows, targets, tables)

    packed = pack(terms, swap(terms, 0, across))
    arrived = [
        swap(packed[m], m, (4 * r, 4 * r + 2)) for r in range(planes // 2) for m in range(depth)
    ]
    passed = [swap(block, 0, across) for block in arrived]
    out = place_windows(tables, packed[0], arrived + passed, depth, rows // dp, cols)
    return out[None]


def solution(mesh):
    placed = (P("depth", None, None, None), P("dp", None), P(), P(), P("dp", None, None))
    return jax.shard_map(
        on_device,
        mesh=mesh,
        in_specs=placed,
        out_specs=P("depth", None, "dp", None),
        check_vma=False,
    )
```

time: 43.7 us -> 52.1 us (1.19)
  the two profiles are of different devices: /device:TPU:17 before, /device:TPU:0 now
where the time goes in v5:
time: 52.1 us; the launch traced here: 51.7 us
  starting transfers between devices  17.6 us (34%)
  waiting for transfers between devices  15.4 us (30%)
  Pallas kernels  13.2 us (25%)
  local copies, waits for them, and re-layouts  5.32 us (10%)
    ppermute x17, starting transfers between devices, swap(): return lax.ppermute(block, ('depth', 'dp'), route)  17.6 us
    ppermute x17, waiting for transfers between devices, swap(): return lax.ppermute(block, ('depth', 'dp'), route)  15.4 us
    pallas_call x1, Pallas kernels, run_waves(): pl.pallas_call(functools.partial(wave_kernel, slices, len(measured)), out...  6.09 us
    unnamed x24, local copies, waits for them, and re-layouts  5.32 us
    pallas_call x1, Pallas kernels, take_windows(): pl.pallas_call(window_kernel, out_shape=[jax.ShapeDtypeStruct((2, window,...  3.13 us
    pallas_call x1, Pallas kernels, place_windows(): pl.pallas_call(functools.partial(place_kernel, depth, len(tables) // 2),...  2.16 us
    pallas_call x1, Pallas kernels, pack(): pl.pallas_call(pack_kernel, out_shape=[jax.ShapeDtypeStruct((2,) + own.sh...  1.86 us
  transfers between devices with their start and end apart: 17, of which 10 were waited for; matrix products, arithmetic and copies ran while one was open for 0% of the time, Pallas kernels for 0%

profile of v5, /device:TPU:0, one launch (start us, length us, event | category | flops | bytes accessed | tf_op | source)
XLA Modules:
  0.0 51.7 jit_solution(9001661540576980757)
XLA Ops:
  0.0 4.1 %collective-permute-start = (s32[2,2]{1,0:T(2,128)}, s32[2,2]{1,0:T(2,128)S(1)}, u32[]{:S(2)}, u32[]{:S(2)}) collective-permute-start(s32[2,2]{1,0:T(2,128)} %rest_0_.1), channel_id=1, source_target_pairs={{0,4},{1,5},{2,6},{3,7},{4,0},{5,1},{6,2},{7,3},{8,12},{9,13},{10,... | collective-permute-start | bytes 56 | tf_op jit(solution)/shard_map/ppermute | solution.py:298
  4.1 1.8 %collective-permute-done.rest_1_ = s32[2,2]{1,0:T(2,128)S(1)} collective-permute-done((s32[2,2]{1,0:T(2,128)}, s32[2,2]{1,0:T(2,128)S(1)}, u32[]{:S(2)}, u32[]{:S(2)}) %collective-permute-start) | collective-permute-done | bytes 48 | tf_op jit(solution)/shard_map/ppermute | solution.py:298
  6.5 3.1 %take_windows.1 = (bf16[2,128,128]{2,1,0:T(8,128)(2,1)}, bf16[2,128,128]{2,1,0:T(8,128)(2,1)}, bf16[2,128,128]{2,1,0:T(8,128)(2,1)}, bf16[2,128,128]{2,1,0:T(8,1...) custom-call(f32[2,768,768]{2,1,0:T(8,128)} %bitcast.2, f32[128,128]{1,0:T(8,128)} %phase_ref.1, s32[2,2]{1,0:T(2,128)} %rest_0_.1, ...), custom_call_target="tpu_custom_call" | custom-call | tf_op jit(solution)/shard_map/take_windows/pallas_call | solution.py:94
  9.6 3.0 %collective-permute-start.7 = (f32[2,128,128]{2,1,0:T(8,128)S(1)}, f32[2,128,128]{2,1,0:T(8,128)S(1)}, u32[]{:S(2)}, u32[]{:S(2)}) collective-permute-start(f32[2,128,128]{2,1,0:T(8,128)S(1)} %copy-done.4), channel_id=1, source_target_pairs={{0,4},{1,5},{2,6},{3,7},{4,0},{5,1},{6,2},{7,3},{8,12},{9,13},{10,... | collective-permute-start | bytes 393224 | tf_op jit(solution)/shard_map/ppermute | solution.py:298
  12.6 1.5 %collective-permute-start.4 = (bf16[2,128,128]{2,1,0:T(8,128)(2,1)}, bf16[2,128,128]{2,1,0:T(8,128)(2,1)S(1)}, u32[]{:S(2)}, u32[]{:S(2)}) collective-permute-start(bf16[2,128,128]{2,1,0:T(8,128)(2,1)} %get-tuple-element.21), channel_id=1, source_target_pairs={{0,8},{1,9},{2,10},{3,11},{4,12},{5,13},{6,14},{7,15},{8,0},{9,1},... | collective-permute-start | bytes 196616 | tf_op jit(solution)/shard_map/ppermute | solution.py:298
  14.1 1.5 %collective-permute-start.5 = (bf16[2,128,128]{2,1,0:T(8,128)(2,1)}, bf16[2,128,128]{2,1,0:T(8,128)(2,1)S(1)}, u32[]{:S(2)}, u32[]{:S(2)}) collective-permute-start(bf16[2,128,128]{2,1,0:T(8,128)(2,1)} %get-tuple-element.22), channel_id=1, source_target_pairs={{0,16},{1,17},{2,18},{3,19},{4,20},{5,21},{6,22},{7,23},{8,24},{9,... | collective-permute-start | bytes 196616 | tf_op jit(solution)/shard_map/ppermute | solution.py:298
  16.1 1.6 %collective-permute-start.2 = (s32[4,2]{1,0:T(4,128)}, s32[4,2]{1,0:T(4,128)S(1)}, u32[]{:S(2)}, u32[]{:S(2)}) collective-permute-start(s32[4,2]{1,0:T(4,128)} %get-tuple-element.17.rest_6_.rest_0_), channel_id=1, source_target_pairs={{0,2},{1,3},{2,0},{3,1},{4,6},{5,7},{6,4},{7,5},{8,10},{9,11},{10,... | collective-permute-start | bytes 104 | tf_op jit(solution)/shard_map/ppermute | solution.py:298
  17.7 2.2 %collective-permute-done.2.rest_8_.rest_2_ = s32[4,2]{1,0:T(4,128)S(1)} collective-permute-done((s32[4,2]{1,0:T(4,128)}, s32[4,2]{1,0:T(4,128)S(1)}, u32[]{:S(2)}, u32[]{:S(2)}) %collective-permute-start.2) | collective-permute-done | bytes 64 | tf_op jit(solution)/shard_map/ppermute | solution.py:298
  19.9 1.4 %collective-permute-done.1.rest_7_.rest_1_ = s32[4,2]{1,0:T(4,128)S(1)} collective-permute-done((s32[4,2]{1,0:T(4,128)}, s32[4,2]{1,0:T(4,128)S(1)}, u32[]{:S(2)}, u32[]{:S(2)}) %collective-permute-start.1) | collective-permute-done | bytes 64 | tf_op jit(solution)/shard_map/ppermute | solution.py:298
  21.4 1.0 %collective-permute-done.3.rest_9_.rest_3_ = s32[4,2]{1,0:T(4,128)S(1)} collective-permute-done((s32[4,2]{1,0:T(4,128)S(1)}, s32[4,2]{1,0:T(4,128)S(1)}, u32[]{:S(2)}, u32[]{:S(2)}) %collective-permute-start.3) | collective-permute-done | bytes 64 | tf_op jit(solution)/shard_map/ppermute | solution.py:298
  22.5 0.9 %copy-done.6 = f32[2,128,128]{2,1,0:T(8,128)S(1)} copy-done((f32[2,128,128]{2,1,0:T(8,128)S(1)}, f32[2,128,128]{2,1,0:T(8,128)}, u32[]{:S(2)}) %copy-start.6) | copy-done | bytes 131096
  23.4 0.8 %copy-done.7 = bf16[2,128,128]{2,1,0:T(8,128)(2,1)S(1)} copy-done((bf16[2,128,128]{2,1,0:T(8,128)(2,1)S(1)}, bf16[2,128,128]{2,1,0:T(8,128)(2,1)}, u32[]{:S(2)}) %copy-start.7) | copy-done | bytes 65560
  24.2 0.7 %copy-done.8 = s32[4,2]{1,0:T(4,128)S(1)} copy-done((s32[4,2]{1,0:T(4,128)S(1)}, s32[4,2]{1,0:T(4,128)}, u32[]{:S(2)}) %copy-start.8) | copy-done | bytes 56
  24.9 6.1 %run_waves.1.own_ref = bf16[4,2,128,128]{3,2,1,0:T(8,128)(2,1)S(1)} custom-call(f32[2,128,128]{2,1,0:T(8,128)S(1)} %copy-done.3, f32[2,128,128]{2,1,0:T(8,128)S(1)} %copy-done.6, bf16[2,256,768]{2,1,0:T(8,128)(2,1)S(1)} %copy-done.2, bf16[2,768,256]{2,1,0:T(8,128)(2,1)S(1)} %copy-done.1, bf16[2,128,128]{2,1,0:T(8,128)(2,1)S(1)} %copy-done.7, ...), custom_call_target="tpu_custom_call" | custom-call | tf_op jit(solution)/shard_map/run_waves/pallas_call | solution.py:193
  31.2 1.4 %collective-permute-done.8.other_ref = bf16[4,2,128,128]{3,2,1,0:T(8,128)(2,1)S(1)} collective-permute-done((bf16[4,2,128,128]{3,2,1,0:T(8,128)(2,1)S(1)}, bf16[4,2,128,128]{3,2,1,0:T(8,128)(2,1)S(1)}, u32[]{:S(2)}, u32[]{:S(2)}) %collective-permute-start.8) | collective-permute-done | bytes 262176 | tf_op jit(solution)/shard_map/ppermute | solution.py:298
  32.6 0.7 %copy-done.10 = bf16[4,2,128,128]{3,2,1,0:T(8,128)(2,1)} copy-done((bf16[4,2,128,128]{3,2,1,0:T(8,128)(2,1)}, bf16[4,2,128,128]{3,2,1,0:T(8,128)(2,1)S(1)}, u32[]{:S(2)}) %copy-start.10) | copy-done | bytes 262168
  33.3 1.9 %pack_terms.1 = (bf16[2,2,128,128]{3,2,1,0:T(8,128)(2,1)}, bf16[2,2,128,128]{3,2,1,0:T(8,128)(2,1)}, bf16[2,2,128,128]{3,2,1,0:T(8,128)(2,1)}, bf16[2,2,128,128]{3,2,1,0:T(8,128)(2,1)}) custom-call(bf16[4,2,128,128]{3,2,1,0:T(8,128)(2,1)} %copy-done, bf16[4,2,128,128]{3,2,1,0:T(8,128)(2,1)} %copy-done.10), custom_call_target="tpu_custom_call" | custom-call | tf_op jit(solution)/shard_map/pack_terms/pallas_call | solution.py:215
  35.2 1.5 %collective-permute-start.10 = (bf16[2,2,128,128]{3,2,1,0:T(8,128)(2,1)}, bf16[2,2,128,128]{3,2,1,0:T(8,128)(2,1)S(1)}, u32[]{:S(2)}, u32[]{:S(2)}) collective-permute-start(bf16[2,2,128,128]{3,2,1,0:T(8,128)(2,1)} %get-tuple-element.26), channel_id=1, source_target_pairs={{0,8},{1,11},{2,10},{3,9},{4,12},{5,15},{6,14},{7,13},{8,0},{9,3},... | collective-permute-start | bytes 393224 | tf_op jit(solution)/shard_map/ppermute | solution.py:298
  36.6 1.5 %collective-permute-start.11 = (bf16[2,2,128,128]{3,2,1,0:T(8,128)(2,1)}, bf16[2,2,128,128]{3,2,1,0:T(8,128)(2,1)S(1)}, u32[]{:S(2)}, u32[]{:S(2)}) collective-permute-start(bf16[2,2,128,128]{3,2,1,0:T(8,128)(2,1)} %get-tuple-element.27), channel_id=1, source_target_pairs={{0,16},{1,19},{2,18},{3,17},{4,20},{5,23},{6,22},{7,21},{8,24},{9,... | collective-permute-start | bytes 393224 | tf_op jit(solution)/shard_map/ppermute | solution.py:298
  39.3 2.4 %collective-permute-done.10.rest_6_ = bf16[2,2,128,128]{3,2,1,0:T(8,128)(2,1)S(1)} collective-permute-done((bf16[2,2,128,128]{3,2,1,0:T(8,128)(2,1)}, bf16[2,2,128,128]{3,2,1,0:T(8,128)(2,1)S(1)}, u32[]{:S(2)}, u32[]{:S(2)}) %collective-permute-start.10) | collective-permute-done | bytes 131104 | tf_op jit(solution)/shard_map/ppermute | solution.py:298
  42.0 4.0 %collective-permute-done.11.rest_7_ = bf16[2,2,128,128]{3,2,1,0:T(8,128)(2,1)S(1)} collective-permute-done((bf16[2,2,128,128]{3,2,1,0:T(8,128)(2,1)}, bf16[2,2,128,128]{3,2,1,0:T(8,128)(2,1)S(1)}, u32[]{:S(2)}, u32[]{:S(2)}) %collective-permute-start.11) | collective-permute-done | bytes 131104 | tf_op jit(solution)/shard_map/ppermute | solution.py:298
  46.6 0.8 %collective-permute-done.15.rest_11_ = bf16[2,2,128,128]{3,2,1,0:T(8,128)(2,1)S(1)} collective-permute-done((bf16[2,2,128,128]{3,2,1,0:T(8,128)(2,1)S(1)}, bf16[2,2,128,128]{3,2,1,0:T(8,128)(2,1)S(1)}, u32[]{:S(2)}, u32[]{:S(2)}) %collective-permute-start.15) | collective-permute-done | bytes 131104 | tf_op jit(solution)/shard_map/ppermute | solution.py:298
  47.9 0.9 %copy-done.5 = bf16[2,2,128,128]{3,2,1,0:T(8,128)(2,1)S(1)} copy-done((bf16[2,2,128,128]{3,2,1,0:T(8,128)(2,1)S(1)}, bf16[2,2,128,128]{3,2,1,0:T(8,128)(2,1)}, u32[]{:S(2)}) %copy-start.5) | copy-done | bytes 131096
  49.5 2.2 %place_windows.1 = f32[2,96,768]{2,1,0:T(8,128)} custom-call(s32[4,2]{1,0:T(4,128)S(1)} %copy-done.9, s32[4,2]{1,0:T(4,128)S(1)} %collective-permute-done.1.rest_7_.rest_1_, s32[4,2]{1,0:T(4,128)S(1)} %collective-permute-done.2.rest_8_.rest_2_, s32[4,2]{1,0:T(4,128)S(1)} %collective-permute-done.3.rest_9_.rest_3_, bf16[2,2,128,128]{3,2,1,0:T(8,128)(2,1)S(1)} %copy-done.5, ...), custom_call_target="tpu_custom_call" | custom-call | tf_op jit(solution)/shard_map/place_windows/pallas_call | solution.py:279
  (38 shorter events, 4.7 us)
Async XLA Ops:
  0.0 22.4 %copy-start.1 = (bf16[2,768,256]{2,1,0:T(8,128)(2,1)S(1)}, bf16[2,768,256]{2,1,0:T(8,128)(2,1)}, u32[]{:S(2)}) copy-start(bf16[2,768,256]{2,1,0:T(8,128)(2,1)} %constant.5.clone.right_ref) | copy-start | bytes 2359300
  0.0 22.4 %copy-start.2 = (bf16[2,256,768]{2,1,0:T(8,128)(2,1)S(1)}, bf16[2,256,768]{2,1,0:T(8,128)(2,1)}, u32[]{:S(2)}) copy-start(bf16[2,256,768]{2,1,0:T(8,128)(2,1)} %constant.4.clone.left_ref) | copy-start | bytes 2359300
  0.0 9.6 %copy-start.4 = (f32[2,128,128]{2,1,0:T(8,128)S(1)}, f32[2,128,128]{2,1,0:T(8,128)}, u32[]{:S(2)}) copy-start(f32[2,128,128]{2,1,0:T(8,128)} %rest_4_.1) | copy-start | bytes 393220
  0.0 22.4 %copy-start.3 = (f32[2,128,128]{2,1,0:T(8,128)S(1)}, f32[2,128,128]{2,1,0:T(8,128)}, u32[]{:S(2)}) copy-start(f32[2,128,128]{2,1,0:T(8,128)} %probe_ref.1) | copy-start | bytes 393220
  0.0 5.9 %collective-permute-start = (s32[2,2]{1,0:T(2,128)}, s32[2,2]{1,0:T(2,128)S(1)}, u32[]{:S(2)}, u32[]{:S(2)}) collective-permute-start(s32[2,2]{1,0:T(2,128)} %rest_0_.1), channel_id=1, source_target_pairs={{0,4},{1,5},{2,6},{3,7},{4,0},{5,1},{6,2},{7,3},{8,12},{9,13},{10,... | collective-permute-start | bytes 56 | tf_op jit(solution)/shard_map/ppermute | solution.py:298
  9.6 12.8 %collective-permute-start.7 = (f32[2,128,128]{2,1,0:T(8,128)S(1)}, f32[2,128,128]{2,1,0:T(8,128)S(1)}, u32[]{:S(2)}, u32[]{:S(2)}) collective-permute-start(f32[2,128,128]{2,1,0:T(8,128)S(1)} %copy-done.4), channel_id=1, source_target_pairs={{0,4},{1,5},{2,6},{3,7},{4,0},{5,1},{6,2},{7,3},{8,12},{9,13},{10,... | collective-permute-start | bytes 393224 | tf_op jit(solution)/shard_map/ppermute | solution.py:298
  12.6 9.8 %collective-permute-start.4 = (bf16[2,128,128]{2,1,0:T(8,128)(2,1)}, bf16[2,128,128]{2,1,0:T(8,128)(2,1)S(1)}, u32[]{:S(2)}, u32[]{:S(2)}) collective-permute-start(bf16[2,128,128]{2,1,0:T(8,128)(2,1)} %get-tuple-element.21), channel_id=1, source_target_pairs={{0,8},{1,9},{2,10},{3,11},{4,12},{5,13},{6,14},{7,15},{8,0},{9,1},... | collective-permute-start | bytes 196616 | tf_op jit(solution)/shard_map/ppermute | solution.py:298
  14.1 8.3 %collective-permute-start.5 = (bf16[2,128,128]{2,1,0:T(8,128)(2,1)}, bf16[2,128,128]{2,1,0:T(8,128)(2,1)S(1)}, u32[]{:S(2)}, u32[]{:S(2)}) collective-permute-start(bf16[2,128,128]{2,1,0:T(8,128)(2,1)} %get-tuple-element.22), channel_id=1, source_target_pairs={{0,16},{1,17},{2,18},{3,19},{4,20},{5,21},{6,22},{7,23},{8,24},{9,... | collective-permute-start | bytes 196616 | tf_op jit(solution)/shard_map/ppermute | solution.py:298
  15.6 6.8 %collective-permute-start.6 = (bf16[2,128,128]{2,1,0:T(8,128)(2,1)}, bf16[2,128,128]{2,1,0:T(8,128)(2,1)S(1)}, u32[]{:S(2)}, u32[]{:S(2)}) collective-permute-start(bf16[2,128,128]{2,1,0:T(8,128)(2,1)} %get-tuple-element.23), channel_id=1, source_target_pairs={{0,24},{1,25},{2,26},{3,27},{4,28},{5,29},{6,30},{7,31},{8,16},{9,... | collective-permute-start | bytes 196616 | tf_op jit(solution)/shard_map/ppermute | solution.py:298
  16.1 3.8 %collective-permute-start.2 = (s32[4,2]{1,0:T(4,128)}, s32[4,2]{1,0:T(4,128)S(1)}, u32[]{:S(2)}, u32[]{:S(2)}) collective-permute-start(s32[4,2]{1,0:T(4,128)} %get-tuple-element.17.rest_6_.rest_0_), channel_id=1, source_target_pairs={{0,2},{1,3},{2,0},{3,1},{4,6},{5,7},{6,4},{7,5},{8,10},{9,11},{10,... | collective-permute-start | bytes 104 | tf_op jit(solution)/shard_map/ppermute | solution.py:298
  19.9 1.4 %collective-permute-start.1 = (s32[4,2]{1,0:T(4,128)}, s32[4,2]{1,0:T(4,128)S(1)}, u32[]{:S(2)}, u32[]{:S(2)}) collective-permute-start(s32[4,2]{1,0:T(4,128)} %get-tuple-element.17.rest_6_.rest_0_), channel_id=1, source_target_pairs={{0,1},{1,0},{2,3},{3,2},{4,5},{5,4},{6,7},{7,6},{8,9},{9,8},{10,11... | collective-permute-start | bytes 104 | tf_op jit(solution)/shard_map/ppermute | solution.py:298
  21.3 1.2 %collective-permute-start.3 = (s32[4,2]{1,0:T(4,128)S(1)}, s32[4,2]{1,0:T(4,128)S(1)}, u32[]{:S(2)}, u32[]{:S(2)}) collective-permute-start(s32[4,2]{1,0:T(4,128)S(1)} %collective-permute-done.2.rest_8_.rest_2_), channel_id=1, source_target_pairs={{0,1},{1,0},{2,3},{3,2},{4,5},{5,4},{6,7},{7,6},{8,9},{9,8},{10,11... | collective-permute-start | bytes 104 | tf_op jit(solution)/shard_map/ppermute | solution.py:298
  22.5 0.9 %copy-start.6 = (f32[2,128,128]{2,1,0:T(8,128)S(1)}, f32[2,128,128]{2,1,0:T(8,128)}, u32[]{:S(2)}) copy-start(f32[2,128,128]{2,1,0:T(8,128)} %get-tuple-element.19.kern_ref) | copy-start | bytes 393220
  31.0 1.6 %copy-start = (bf16[4,2,128,128]{3,2,1,0:T(8,128)(2,1)}, bf16[4,2,128,128]{3,2,1,0:T(8,128)(2,1)S(1)}, u32[]{:S(2)}) copy-start(bf16[4,2,128,128]{3,2,1,0:T(8,128)(2,1)S(1)} %run_waves.1.own_ref) | copy-start | bytes 786436
  31.0 1.6 %collective-permute-start.8 = (bf16[4,2,128,128]{3,2,1,0:T(8,128)(2,1)S(1)}, bf16[4,2,128,128]{3,2,1,0:T(8,128)(2,1)S(1)}, u32[]{:S(2)}, u32[]{:S(2)}) collective-permute-start(bf16[4,2,128,128]{3,2,1,0:T(8,128)(2,1)S(1)} %run_waves.1.own_ref), channel_id=1, source_target_pairs={{0,1},{1,0},{2,3},{3,2},{4,5},{5,4},{6,7},{7,6},{8,9},{9,8},{10,11... | collective-permute-start | bytes 786440 | tf_op jit(solution)/shard_map/ppermute | solution.py:298
  35.2 6.6 %collective-permute-start.10 = (bf16[2,2,128,128]{3,2,1,0:T(8,128)(2,1)}, bf16[2,2,128,128]{3,2,1,0:T(8,128)(2,1)S(1)}, u32[]{:S(2)}, u32[]{:S(2)}) collective-permute-start(bf16[2,2,128,128]{3,2,1,0:T(8,128)(2,1)} %get-tuple-element.26), channel_id=1, source_target_pairs={{0,8},{1,11},{2,10},{3,9},{4,12},{5,15},{6,14},{7,13},{8,0},{9,3},... | collective-permute-start | bytes 393224 | tf_op jit(solution)/shard_map/ppermute | solution.py:298
  36.6 9.4 %collective-permute-start.11 = (bf16[2,2,128,128]{3,2,1,0:T(8,128)(2,1)}, bf16[2,2,128,128]{3,2,1,0:T(8,128)(2,1)S(1)}, u32[]{:S(2)}, u32[]{:S(2)}) collective-permute-start(bf16[2,2,128,128]{3,2,1,0:T(8,128)(2,1)} %get-tuple-element.27), channel_id=1, source_target_pairs={{0,16},{1,19},{2,18},{3,17},{4,20},{5,23},{6,22},{7,21},{8,24},{9,... | collective-permute-start | bytes 393224 | tf_op jit(solution)/shard_map/ppermute | solution.py:298
  38.2 7.9 %collective-permute-start.12 = (bf16[2,2,128,128]{3,2,1,0:T(8,128)(2,1)}, bf16[2,2,128,128]{3,2,1,0:T(8,128)(2,1)S(1)}, u32[]{:S(2)}, u32[]{:S(2)}) collective-permute-start(bf16[2,2,128,128]{3,2,1,0:T(8,128)(2,1)} %get-tuple-element.28), channel_id=1, source_target_pairs={{0,24},{1,27},{2,26},{3,25},{4,28},{5,31},{6,30},{7,29},{8,16},{9,... | collective-permute-start | bytes 393224 | tf_op jit(solution)/shard_map/ppermute | solution.py:298
  38.7 7.9 %collective-permute-start.9 = (bf16[2,2,128,128]{3,2,1,0:T(8,128)(2,1)}, bf16[2,2,128,128]{3,2,1,0:T(8,128)(2,1)S(1)}, u32[]{:S(2)}, u32[]{:S(2)}) collective-permute-start(bf16[2,2,128,128]{3,2,1,0:T(8,128)(2,1)} %get-tuple-element.25.rest_4_), channel_id=1, source_target_pairs={{1,3},{3,1},{5,7},{7,5},{9,11},{11,9},{13,15},{15,13},{17,19},{19,... | collective-permute-start | bytes 393224 | tf_op jit(solution)/shard_map/ppermute | solution.py:298
  41.8 4.9 %collective-permute-start.14 = (bf16[2,2,128,128]{3,2,1,0:T(8,128)(2,1)S(1)}, bf16[2,2,128,128]{3,2,1,0:T(8,128)(2,1)S(1)}, u32[]{:S(2)}, u32[]{:S(2)}) collective-permute-start(bf16[2,2,128,128]{3,2,1,0:T(8,128)(2,1)S(1)} %collective-permute-done.10.rest_6_), channel_id=1, source_target_pairs={{0,1},{1,0},{2,3},{3,2},{4,5},{5,4},{6,7},{7,6},{8,9},{9,8},{10,11... | collective-permute-start | bytes 393224 | tf_op jit(solution)/shard_map/ppermute | solution.py:298
  46.0 1.3 %collective-permute-start.15 = (bf16[2,2,128,128]{3,2,1,0:T(8,128)(2,1)S(1)}, bf16[2,2,128,128]{3,2,1,0:T(8,128)(2,1)S(1)}, u32[]{:S(2)}, u32[]{:S(2)}) collective-permute-start(bf16[2,2,128,128]{3,2,1,0:T(8,128)(2,1)S(1)} %collective-permute-done.11.rest_7_), channel_id=1, source_target_pairs={{0,1},{1,0},{2,3},{3,2},{4,5},{5,4},{6,7},{7,6},{8,9},{9,8},{10,11... | collective-permute-start | bytes 393224 | tf_op jit(solution)/shard_map/ppermute | solution.py:298
  46.0 1.5 %collective-permute-start.16 = (bf16[2,2,128,128]{3,2,1,0:T(8,128)(2,1)S(1)}, bf16[2,2,128,128]{3,2,1,0:T(8,128)(2,1)S(1)}, u32[]{:S(2)}, u32[]{:S(2)}) collective-permute-start(bf16[2,2,128,128]{3,2,1,0:T(8,128)(2,1)S(1)} %collective-permute-done.12.rest_8_), channel_id=1, source_target_pairs={{0,1},{1,0},{2,3},{3,2},{4,5},{5,4},{6,7},{7,6},{8,9},{9,8},{10,11... | collective-permute-start | bytes 393224 | tf_op jit(solution)/shard_map/ppermute | solution.py:298
  46.6 1.3 %collective-permute-start.13 = (bf16[2,2,128,128]{3,2,1,0:T(8,128)(2,1)S(1)}, bf16[2,2,128,128]{3,2,1,0:T(8,128)(2,1)S(1)}, u32[]{:S(2)}, u32[]{:S(2)}) collective-permute-start(bf16[2,2,128,128]{3,2,1,0:T(8,128)(2,1)S(1)} %collective-permute-done.9.rest_5_), channel_id=1, source_target_pairs={{0,1},{1,0},{2,3},{3,2},{4,5},{5,4},{6,7},{7,6},{8,9},{9,8},{10,11... | collective-permute-start | bytes 393224 | tf_op jit(solution)/shard_map/ppermute | solution.py:298
  47.9 0.9 %copy-start.5 = (bf16[2,2,128,128]{3,2,1,0:T(8,128)(2,1)S(1)}, bf16[2,2,128,128]{3,2,1,0:T(8,128)(2,1)}, u32[]{:S(2)}) copy-start(bf16[2,2,128,128]{3,2,1,0:T(8,128)(2,1)} %get-tuple-element.25.rest_4_) | copy-start | bytes 393220
  (5 other events, 3.5 us)

commit v6 on v3

v6 whole, which is shorter than its diff:
```python
import functools
import math

import jax
import jax.numpy as jnp
import numpy as np
from jax import lax
from jax.experimental import pallas as pl
from jax.experimental.pallas import tpu as pltpu
from jax.sharding import PartitionSpec as P

grad_scale = 0.03125
f32 = jnp.float32
bf16 = jnp.bfloat16


def dft_matrices(size):
    k = np.arange(size)
    angles = 2.0 * np.pi * ((k[:, None] * k[None, :]) % size) / size
    c = np.cos(angles) / math.sqrt(size)
    s = np.sin(angles) / math.sqrt(size)
    plus = np.block([[c, s], [-s, c]]).astype(np.float32)
    minus = np.block([[c, -s], [s, c]]).astype(np.float32)
    parts = []
    for full in (plus, minus):
        high = full.astype(bf16)
        low = (full - high.astype(np.float32)).astype(bf16)
        parts.append((high, low))
    (ph, plo), (mh, mlo) = parts
    right = np.stack([np.concatenate([ph, ph, plo], 0), np.concatenate([mh, mh, mlo], 0)])
    left = np.stack([np.concatenate([mh, mh, mlo], 1), np.concatenate([ph, ph, plo], 1)])
    return left, right


code_rows = 16


def window_kernel(members, obj_ref, *rest):
    table, buf, table_sems, sems = rest[-4:]
    clusters, count = buf.shape[:2]
    pos_refs, out_refs, code_ref = rest[:clusters], rest[clusters:-5], rest[-5]
    window = out_refs[0].shape[-1]
    rows, cols = obj_ref.shape[-2:]
    tall, wide = buf.shape[-2:]
    cluster = lax.div(lax.axis_index("dp"), members)
    home = lax.div(lax.axis_index("depth"), 2)

    fetches = [
        pltpu.make_async_copy(pos_refs[m], table.at[m], table_sems.at[m]) for m in range(clusters)
    ]
    for fetch in fetches:
        fetch.start()
    for fetch in fetches:
        fetch.wait()

    def corner(m, p):
        at = home ^ cluster ^ m
        row, col = table[at, p, 0], table[at, p, 1]
        row_base = pl.multiple_of(jnp.minimum(row >> 3, (rows - tall) // 8) * 8, 8)
        col_base = pl.multiple_of(jnp.minimum(col >> 7, (cols - wide) // 128) * 128, 128)
        return row_base, col_base, row - row_base, col - col_base

    def copy(m, p):
        row_base, col_base, _, _ = corner(m, p)
        return pltpu.make_async_copy(
            obj_ref.at[:, pl.ds(row_base, tall), pl.ds(col_base, wide)], buf.at[m, p], sems.at[m, p]
        )

    order = [(m, p) for m in reversed(range(clusters)) for p in range(count)]
    for m, p in order:
        copy(m, p).start()
    line = lax.broadcasted_iota(jnp.int32, (code_rows, window), 0)
    for p in range(count):
        row, col = table[home ^ cluster, p, 0], table[home ^ cluster, p, 1]
        code = jnp.where(line == 0, row >> 3, jnp.where(line == 1, row & 7, 0))
        code = jnp.where(line == 2, col >> 3, jnp.where(line == 3, col & 7, code))
        code_ref[p] = code.astype(f32).astype(bf16)
    for m, p in order:
        copy(m, p).wait()
        _, _, row_off, col_off = corner(m, p)
        lift = jnp.where(row_off == 0, 0, tall - row_off)
        shift = jnp.where(col_off == 0, 0, wide - col_off)
        for part in range(2):
            block = pltpu.roll(buf[m, p, part], shift, 1)[:, :window]
            block = pltpu.roll(block, lift, 0)[:window]
            out_refs[m][p, part] = block.astype(bf16)


def take_windows(obj, positions, window, members):
    clusters, count = len(positions), positions[0].shape[0]
    tall, wide = window + 8, window + 128
    any_space = pl.BlockSpec(memory_space=pl.ANY)
    vmem = pl.BlockSpec(memory_space=pltpu.VMEM)
    out = pl.pallas_call(
        functools.partial(window_kernel, members),
        out_shape=[jax.ShapeDtypeStruct((count, 2, window, window), bf16)] * clusters
        + [jax.ShapeDtypeStruct((count, code_rows, window), bf16)],
        in_specs=[any_space] * (1 + clusters),
        out_specs=[vmem] * (clusters + 1),
        scratch_shapes=[
            pltpu.SMEM((clusters, count, 2), jnp.int32),
            pltpu.VMEM((clusters, count, 2, tall, wide), f32),
            pltpu.SemaphoreType.DMA((clusters,)),
            pltpu.SemaphoreType.DMA((clusters, count)),
        ],
        compiler_params=pltpu.CompilerParams(vmem_limit_bytes=24 * 1024 * 1024),
        name="take_windows",
    )(obj, *positions)
    return out[:clusters], out[clusters]


def split(x):
    high = x.astype(bf16)
    return high, (x - high.astype(f32)).astype(bf16)


def cmul(a, b):
    return a[0] * b[0] - a[1] * b[1], a[0] * b[1] + a[1] * b[0]


def cmul_conj(a, b):
    return a[0] * b[0] + a[1] * b[1], a[0] * b[1] - a[1] * b[0]


def wave_kernel(members, clusters, probe_ref, kern_ref, left_ref, right_ref, code_ref, *rest):
    trans, terms, meas = rest[-3:]
    slices, count, _, _, window = trans.shape
    meas_refs, t_refs, out_refs = rest[:clusters], rest[clusters : clusters + slices], rest[clusters + slices : -3]
    own, cluster = lax.axis_index("depth"), lax.div(lax.axis_index("dp"), members)
    everyone = range(count)

    for m in range(slices):
        trans[own ^ m] = t_refs[m][...]
    for m, meas_ref in enumerate(meas_refs):

        @pl.when(lax.div(own, 2) ^ cluster == m)
        def _():
            meas[...] = meas_ref[...]

    def t_of(k, p):
        return trans[k, p, 0].astype(f32), trans[k, p, 1].astype(f32)

    def passes(x, axis, exact):
        if not exact:
            return x.astype(bf16)
        high, low = split(x)
        return jnp.concatenate([high, low, high], axis=axis)

    def rows(fields, sign, exact):
        x = jnp.concatenate([jnp.concatenate(f, axis=0) for f in fields], axis=1)
        x = passes(x, 0, exact)
        y = jnp.dot(left_ref[sign, :, : x.shape[0]], x, preferred_element_type=f32)
        cut = [y[:, p * window : (p + 1) * window] for p in everyone]
        return [(c[:window], c[window:]) for c in cut]

    def cols(fields, sign, exact):
        x = jnp.concatenate([jnp.concatenate(f, axis=1) for f in fields], axis=0)
        x = passes(x, 1, exact)
        y = jnp.dot(x, right_ref[sign, : x.shape[1]], preferred_element_type=f32)
        cut = [y[p * window : (p + 1) * window] for p in everyone]
        return [(c[:, :window], c[:, window:]) for c in cut]

    plus, minus = 0, 1

    def transform(fields, sign, exact):
        return cols(rows(fields, sign, exact), sign, exact)

    kern = (kern_ref[0], kern_ref[1])
    psi = [(probe_ref[0], probe_ref[1])] * count
    kept = []
    for k in range(slices):
        kept.append(psi)
        spectrum = transform([cmul(t_of(k, p), psi[p]) for p in everyone], minus, True)
        if k < slices - 1:
            psi = transform([cmul(kern, s) for s in spectrum], plus, True)

    def source(p):
        re, im = spectrum[p]
        scale = 2.0 * (re * re + im * im - meas[p])
        return scale * re, scale * im

    returned = transform([source(p) for p in everyone], plus, False)
    for k in reversed(range(slices)):
        for p in everyone:
            re, im = cmul_conj(kept[k][p], returned[p])
            terms[own ^ k, p, :window] = (re * grad_scale).astype(bf16)
            terms[own ^ k, p, window:] = (im * grad_scale).astype(bf16)
        if k > 0:
            chi = [cmul_conj(t_of(k, p), returned[p]) for p in everyone]
            spectrum = transform(chi, minus, False)
            returned = transform([cmul_conj(kern, s) for s in spectrum], plus, False)
    for n, out_ref in enumerate(out_refs):
        out_ref[:, : 2 * window] = terms[2 * n]
        out_ref[:, 2 * window :] = code_ref[...]


def run_waves(probe, kern, code, measured, windows, members):
    slices, count, window = len(windows), code.shape[0], code.shape[-1]
    left, right = dft_matrices(window)
    vmem = pl.BlockSpec(memory_space=pltpu.VMEM)
    block = jax.ShapeDtypeStruct((count, 2 * window + code_rows, window), bf16)
    return pl.pallas_call(
        functools.partial(wave_kernel, members, len(measured)),
        out_shape=[block] * (slices // 2),
        in_specs=[vmem] * (5 + len(measured) + slices),
        out_specs=[vmem] * (slices // 2),
        scratch_shapes=[
            pltpu.VMEM((slices, count, 2, window, window), bf16),
            pltpu.VMEM((slices, count, 2 * window, window), bf16),
            pltpu.VMEM((count, window, window), f32),
        ],
        compiler_params=pltpu.CompilerParams(vmem_limit_bytes=40 * 1024 * 1024),
        name="run_waves",
    )(probe, kern, jnp.asarray(left), jnp.asarray(right), code, *measured, *windows)


def place_kernel(*refs):
    block_refs, (out_ref, canvas) = refs[:-2], refs[-2:]
    _, stripe, cols = out_ref.shape
    count, _, window = block_refs[0].shape
    wide = window + 128
    first_row = lax.axis_index("dp") * stripe
    canvas[:, window : window + stripe, :] = jnp.zeros((2, stripe, canvas.shape[2]), f32)
    corners = []
    for block_ref in block_refs:
        for p in range(count):
            code = block_ref[p, 2 * window :].astype(f32)
            row = (8.0 * code[0:1] + code[1:2]).astype(jnp.int32)
            col = (8.0 * code[2:3] + code[3:4]).astype(jnp.int32)
            corners.append((row[0, 0], col[0, 0]))
    for n, (row, col) in enumerate(corners):
        block_ref, p = block_refs[n // count], n % count
        row = row - first_row + window
        row_base = pl.multiple_of((row >> 3) << 3, 8)
        col_base = pl.multiple_of((col >> 7) << 7, 128)

        @pl.when((row > 0) & (row < window + stripe))
        def _():
            for part in range(2):
                block = block_ref[p, part * window : (part + 1) * window].astype(f32)
                block = jnp.concatenate([block, jnp.zeros((8, window), f32)], axis=0)
                block = pltpu.roll(block, row - row_base, 0)
                block = jnp.concatenate([block, jnp.zeros((window + 8, 128), f32)], axis=1)
                block = pltpu.roll(block, col - col_base, 1)
                put = (part, pl.ds(row_base, window + 8), pl.ds(col_base, wide))
                canvas[put] = canvas[put] + block

    out_ref[...] = canvas[:, window : window + stripe, :cols]


def place_windows(blocks, stripe, cols):
    window = blocks[0].shape[-1]
    vmem = pl.BlockSpec(memory_space=pltpu.VMEM)
    tall = window + (stripe + 7) // 8 * 8 + window + 8
    return pl.pallas_call(
        place_kernel,
        out_shape=jax.ShapeDtypeStruct((2, stripe, cols), f32),
        in_specs=[vmem] * len(blocks),
        out_specs=vmem,
        scratch_shapes=[pltpu.VMEM((2, tall, cols + 128), f32)],
        compiler_params=pltpu.CompilerParams(vmem_limit_bytes=48 * 1024 * 1024),
        name="place_windows",
    )(*blocks)


def swap(block, depth_distance, dp_distance):
    depth, dp = lax.axis_size("depth"), lax.axis_size("dp")
    route = [
        (d * dp + j, (d ^ depth_distance) * dp + (j ^ dp_distance))
        for d in range(depth)
        for j in range(dp)
    ]
    return lax.ppermute(block, ("depth", "dp"), route)


def on_device(object_slices, positions, probe_field, propagator_phase, measured):
    depth, dp = lax.axis_size("depth"), lax.axis_size("dp")
    clusters = depth // 2
    members = dp // clusters
    rows, cols = object_slices.shape[-2:]
    window = probe_field.shape[-1]

    homes = [m * members for m in range(1, clusters)]
    all_positions = [positions] + [swap(positions, 0, home) for home in homes]
    windows, code = take_windows(object_slices[0], all_positions, window, members)
    measured, phase, code = lax.optimization_barrier((measured, propagator_phase, code))
    windows = [windows[0]] + [swap(windows[m // 2], m, 0) for m in range(1, depth)]
    targets = [measured] + [swap(measured, 0, home) for home in homes]
    kern = jnp.stack([jnp.cos(phase), jnp.sin(phase)])
    terms = run_waves(probe_field, kern, code, targets, windows, members)

    blocks = [
        swap(terms[m // 2], m, plane) if m or plane else terms[0]
        for plane in range(0, members, 2)
        for m in range(0, depth, 2)
    ]
    blocks += [swap(block, 0, 1) for block in blocks]
    return place_windows(blocks, rows // dp, cols)[None]


def solution(mesh):
    placed = (P("depth", None, None, None), P("dp", None), P(), P(), P("dp", None, None))
    return jax.shard_map(
        on_device,
        mesh=mesh,
        in_specs=placed,
        out_specs=P("depth", None, "dp", None),
        check_vma=False,
    )
```

time: 43.7 us -> 39.5 us (0.904)
  the two profiles are of different devices: /device:TPU:17 before, /device:TPU:0 now
where the time goes in v6:
time: 39.5 us; the launch traced here: 39.2 us
  starting transfers between devices  14.1 us (36%)
  waiting for transfers between devices  11.9 us (30%)
  Pallas kernels  9.86 us (25%)
  local copies, waits for them, and re-layouts  3.27 us (8%)
    ppermute x12, starting transfers between devices, swap(): return lax.ppermute(block, ('depth', 'dp'), route)  14.1 us
    ppermute x12, waiting for transfers between devices, swap(): return lax.ppermute(block, ('depth', 'dp'), route)  11.9 us
    pallas_call x1, Pallas kernels, run_waves(): pl.pallas_call(functools.partial(wave_kernel, members, len(measured)), ou...  7.06 us
    unnamed x14, local copies, waits for them, and re-layouts  3.03 us
    pallas_call x1, Pallas kernels, place_windows(): pl.pallas_call(place_kernel, out_shape=jax.ShapeDtypeStruct((2, stripe, c...  1.48 us
    pallas_call x1, Pallas kernels, take_windows(): pl.pallas_call(functools.partial(window_kernel, members), out_shape=[jax....  1.31 us
  transfers between devices with their start and end apart: 12, of which 8 were waited for; matrix products, arithmetic and copies ran while one was open for 1% of the time, Pallas kernels for 0%

profile of v6, /device:TPU:0, one launch (start us, length us, event | category | flops | bytes accessed | tf_op | source)
XLA Modules:
  0.0 39.2 jit_solution(9624450903527940270)
XLA Ops:
  0.0 4.0 %collective-permute-start = (s32[2,2]{1,0:T(2,128)}, s32[2,2]{1,0:T(2,128)S(1)}, u32[]{:S(2)}, u32[]{:S(2)}) collective-permute-start(s32[2,2]{1,0:T(2,128)} %rest_0_.1), channel_id=1, source_target_pairs={{0,4},{1,5},{2,6},{3,7},{4,0},{5,1},{6,2},{7,3},{8,12},{9,13},{10,... | collective-permute-start | bytes 56 | tf_op jit(solution)/shard_map/ppermute | solution.py:273
  4.0 1.8 %collective-permute-done.rest_1_ = s32[2,2]{1,0:T(2,128)S(1)} collective-permute-done((s32[2,2]{1,0:T(2,128)}, s32[2,2]{1,0:T(2,128)S(1)}, u32[]{:S(2)}, u32[]{:S(2)}) %collective-permute-start) | collective-permute-done | bytes 48 | tf_op jit(solution)/shard_map/ppermute | solution.py:273
  5.8 2.3 %copy-done = f32[1,2,768,768]{3,2,1,0:T(8,128)S(1)} copy-done((f32[1,2,768,768]{3,2,1,0:T(8,128)S(1)}, f32[1,2,768,768]{3,2,1,0:T(8,128)}, u32[]{:S(2)}) %copy-start) | copy-done | bytes 4718616
  8.1 0.7 %copy-done.5 = s32[2,2]{1,0:T(2,128)S(1)} copy-done((s32[2,2]{1,0:T(2,128)S(1)}, s32[2,2]{1,0:T(2,128)}, u32[]{:S(2)}) %copy-start.5) | copy-done | bytes 40
  8.8 1.3 %take_windows.1 = (bf16[2,2,128,128]{3,2,1,0:T(8,128)(2,1)S(1)}, bf16[2,2,128,128]{3,2,1,0:T(8,128)(2,1)S(1)}, bf16[2,16,128]{2,1,0:T(8,128)(2,1)S(1)}) custom-call(f32[2,768,768]{2,1,0:T(8,128)S(1)} %bitcast.6, s32[2,2]{1,0:T(2,128)S(1)} %copy-done.5, s32[2,2]{1,0:T(2,128)S(1)} %collective-permute-done.rest_1_), custom_call_target="tpu_custom_call" | custom-call | tf_op jit(solution)/shard_map/take_windows/pallas_call | solution.py:94
  10.2 2.8 %collective-permute-start.4 = (bf16[2,2,128,128]{3,2,1,0:T(8,128)(2,1)S(1)}, bf16[2,2,128,128]{3,2,1,0:T(8,128)(2,1)S(1)}, u32[]{:S(2)}, u32[]{:S(2)}) collective-permute-start(bf16[2,2,128,128]{3,2,1,0:T(8,128)(2,1)S(1)} %get-tuple-element.18), channel_id=1, source_target_pairs={{0,24},{1,25},{2,26},{3,27},{4,28},{5,29},{6,30},{7,31},{8,16},{9,... | collective-permute-start | bytes 393224 | tf_op jit(solution)/shard_map/ppermute | solution.py:273
  13.0 0.5 %collective-permute-start.3 = (bf16[2,2,128,128]{3,2,1,0:T(8,128)(2,1)S(1)}, bf16[2,2,128,128]{3,2,1,0:T(8,128)(2,1)S(1)}, u32[]{:S(2)}, u32[]{:S(2)}) collective-permute-start(bf16[2,2,128,128]{3,2,1,0:T(8,128)(2,1)S(1)} %get-tuple-element.18), channel_id=1, source_target_pairs={{0,16},{1,17},{2,18},{3,19},{4,20},{5,21},{6,22},{7,23},{8,24},{9,... | collective-permute-start | bytes 393224 | tf_op jit(solution)/shard_map/ppermute | solution.py:273
  13.5 2.6 %collective-permute-start.1 = (f32[2,128,128]{2,1,0:T(8,128)S(1)}, f32[2,128,128]{2,1,0:T(8,128)S(1)}, u32[]{:S(2)}, u32[]{:S(2)}) collective-permute-start(f32[2,128,128]{2,1,0:T(8,128)S(1)} %copy-done.4), channel_id=1, source_target_pairs={{0,4},{1,5},{2,6},{3,7},{4,0},{5,1},{6,2},{7,3},{8,12},{9,13},{10,... | collective-permute-start | bytes 393224 | tf_op jit(solution)/shard_map/ppermute | solution.py:273
  16.1 0.5 %collective-permute-start.2 = (bf16[2,2,128,128]{3,2,1,0:T(8,128)(2,1)S(1)}, bf16[2,2,128,128]{3,2,1,0:T(8,128)(2,1)S(1)}, u32[]{:S(2)}, u32[]{:S(2)}) collective-permute-start(bf16[2,2,128,128]{3,2,1,0:T(8,128)(2,1)S(1)} %get-tuple-element.17.rest_2_), channel_id=1, source_target_pairs={{0,8},{1,9},{2,10},{3,11},{4,12},{5,13},{6,14},{7,15},{8,0},{9,1},... | collective-permute-start | bytes 393224 | tf_op jit(solution)/shard_map/ppermute | solution.py:273
  16.6 0.2 cosine_bitcast_fusion
  16.9 3.9 %collective-permute-done.1.rest_1_ = f32[2,128,128]{2,1,0:T(8,128)S(1)} collective-permute-done((f32[2,128,128]{2,1,0:T(8,128)S(1)}, f32[2,128,128]{2,1,0:T(8,128)S(1)}, u32[]{:S(2)}, u32[]{:S(2)}) %collective-permute-start.1) | collective-permute-done | bytes 131104 | tf_op jit(solution)/shard_map/ppermute | solution.py:273
  20.8 0.3 collective-permute-done.2.rest_3_
  21.1 0.0 collective-permute-done.4.rest_5_
  21.1 7.1 %run_waves.1 = (bf16[2,272,128]{2,1,0:T(8,128)(2,1)S(1)}, bf16[2,272,128]{2,1,0:T(8,128)(2,1)S(1)}) custom-call(f32[2,128,128]{2,1,0:T(8,128)S(1)} %copy-done.3, f32[2,128,128]{2,1,0:T(8,128)S(1)} %pad_maximum_fusion.kern_ref, bf16[2,256,768]{2,1,0:T(8,128)(2,1)S(1)} %copy-done.2, bf16[2,768,256]{2,1,0:T(8,128)(2,1)S(1)} %copy-done.1, ...), custom_call_target="tpu_custom_call" | custom-call | tf_op jit(solution)/shard_map/run_waves/pallas_call | solution.py:202
  28.2 2.6 %collective-permute-start.7 = (bf16[2,272,128]{2,1,0:T(8,128)(2,1)S(1)}, bf16[2,272,128]{2,1,0:T(8,128)(2,1)S(1)}, u32[]{:S(2)}, u32[]{:S(2)}) collective-permute-start(bf16[2,272,128]{2,1,0:T(8,128)(2,1)S(1)} %get-tuple-element.20), channel_id=1, source_target_pairs={{0,18},{1,19},{2,16},{3,17},{4,22},{5,23},{6,20},{7,21},{8,26},{9,... | collective-permute-start | bytes 417800 | tf_op jit(solution)/shard_map/ppermute | solution.py:273
  30.8 0.5 %collective-permute-start.5 = (bf16[2,272,128]{2,1,0:T(8,128)(2,1)S(1)}, bf16[2,272,128]{2,1,0:T(8,128)(2,1)S(1)}, u32[]{:S(2)}, u32[]{:S(2)}) collective-permute-start(bf16[2,272,128]{2,1,0:T(8,128)(2,1)S(1)} %get-tuple-element.20), channel_id=1, source_target_pairs={{0,16},{1,17},{2,18},{3,19},{4,20},{5,21},{6,22},{7,23},{8,24},{9,... | collective-permute-start | bytes 417800 | tf_op jit(solution)/shard_map/ppermute | solution.py:273
  31.3 0.4 %collective-permute-start.6 = (bf16[2,272,128]{2,1,0:T(8,128)(2,1)S(1)}, bf16[2,272,128]{2,1,0:T(8,128)(2,1)S(1)}, u32[]{:S(2)}, u32[]{:S(2)}) collective-permute-start(bf16[2,272,128]{2,1,0:T(8,128)(2,1)S(1)} %get-tuple-element.19.refs_0_), channel_id=1, source_target_pairs={{0,2},{1,3},{2,0},{3,1},{4,6},{5,7},{6,4},{7,5},{8,10},{9,11},{10,... | collective-permute-start | bytes 417800 | tf_op jit(solution)/shard_map/ppermute | solution.py:273
  31.7 2.5 %collective-permute-done.7.refs_3_ = bf16[2,272,128]{2,1,0:T(8,128)(2,1)S(1)} collective-permute-done((bf16[2,272,128]{2,1,0:T(8,128)(2,1)S(1)}, bf16[2,272,128]{2,1,0:T(8,128)(2,1)S(1)}, u32[]{:S(2)}, u32[]{:S(2)}) %collective-permute-start.7) | collective-permute-done | bytes 139296 | tf_op jit(solution)/shard_map/ppermute | solution.py:273
  34.2 1.6 %collective-permute-done.5.refs_1_ = bf16[2,272,128]{2,1,0:T(8,128)(2,1)S(1)} collective-permute-done((bf16[2,272,128]{2,1,0:T(8,128)(2,1)S(1)}, bf16[2,272,128]{2,1,0:T(8,128)(2,1)S(1)}, u32[]{:S(2)}, u32[]{:S(2)}) %collective-permute-start.5) | collective-permute-done | bytes 139296 | tf_op jit(solution)/shard_map/ppermute | solution.py:273
  35.8 0.5 %collective-permute-done.6.refs_2_ = bf16[2,272,128]{2,1,0:T(8,128)(2,1)S(1)} collective-permute-done((bf16[2,272,128]{2,1,0:T(8,128)(2,1)S(1)}, bf16[2,272,128]{2,1,0:T(8,128)(2,1)S(1)}, u32[]{:S(2)}, u32[]{:S(2)}) %collective-permute-start.6) | collective-permute-done | bytes 139296 | tf_op jit(solution)/shard_map/ppermute | solution.py:273
  36.3 0.0 collective-permute-start.10
  36.3 0.8 %collective-permute-done.9.refs_5_ = bf16[2,272,128]{2,1,0:T(8,128)(2,1)S(1)} collective-permute-done((bf16[2,272,128]{2,1,0:T(8,128)(2,1)S(1)}, bf16[2,272,128]{2,1,0:T(8,128)(2,1)S(1)}, u32[]{:S(2)}, u32[]{:S(2)}) %collective-permute-start.9) | collective-permute-done | bytes 139296 | tf_op jit(solution)/shard_map/ppermute | solution.py:273
  37.2 0.5 %collective-permute-done.10.refs_6_ = bf16[2,272,128]{2,1,0:T(8,128)(2,1)S(1)} collective-permute-done((bf16[2,272,128]{2,1,0:T(8,128)(2,1)S(1)}, bf16[2,272,128]{2,1,0:T(8,128)(2,1)S(1)}, u32[]{:S(2)}, u32[]{:S(2)}) %collective-permute-start.10) | collective-permute-done | bytes 139296 | tf_op jit(solution)/shard_map/ppermute | solution.py:273
  37.7 1.5 %place_windows.1 = f32[2,96,768]{2,1,0:T(8,128)} custom-call(bf16[2,272,128]{2,1,0:T(8,128)(2,1)S(1)} %get-tuple-element.19.refs_0_, bf16[2,272,128]{2,1,0:T(8,128)(2,1)S(1)} %collective-permute-done.5.refs_1_, bf16[2,272,128]{2,1,0:T(8,128)(2,1)S(1)} %collective-permute-done.6.refs_2_, bf16[2,272,128]{2,1,0:T(8,128)(2,1)S(1)} %collective-permute-done.7.refs_3_, ...), custom_call_target="tpu_custom_call" | custom-call | tf_op jit(solution)/shard_map/place_windows/pallas_call | solution.py:255
  (19 shorter events, 0.0 us)
Async XLA Ops:
  0.0 5.8 %collective-permute-start = (s32[2,2]{1,0:T(2,128)}, s32[2,2]{1,0:T(2,128)S(1)}, u32[]{:S(2)}, u32[]{:S(2)}) collective-permute-start(s32[2,2]{1,0:T(2,128)} %rest_0_.1), channel_id=1, source_target_pairs={{0,4},{1,5},{2,6},{3,7},{4,0},{5,1},{6,2},{7,3},{8,12},{9,13},{10,... | collective-permute-start | bytes 56 | tf_op jit(solution)/shard_map/ppermute | solution.py:273
  5.8 2.3 %copy-start = (f32[1,2,768,768]{3,2,1,0:T(8,128)S(1)}, f32[1,2,768,768]{3,2,1,0:T(8,128)}, u32[]{:S(2)}) copy-start(f32[1,2,768,768]{3,2,1,0:T(8,128)} %param.7) | copy-start | bytes 14155780
  8.1 0.7 %copy-start.5 = (s32[2,2]{1,0:T(2,128)S(1)}, s32[2,2]{1,0:T(2,128)}, u32[]{:S(2)}) copy-start(s32[2,2]{1,0:T(2,128)} %rest_0_.1) | copy-start | bytes 52
  8.8 4.7 %copy-start.4 = (f32[2,128,128]{2,1,0:T(8,128)S(1)}, f32[2,128,128]{2,1,0:T(8,128)}, u32[]{:S(2)}) copy-start(f32[2,128,128]{2,1,0:T(8,128)} %rest_0_.2) | copy-start | bytes 393220
  8.8 7.8 %copy-start.6 = (f32[128,128]{1,0:T(8,128)S(1)}, f32[128,128]{1,0:T(8,128)}, u32[]{:S(2)}) copy-start(f32[128,128]{1,0:T(8,128)} %param.10) | copy-start | bytes 196612
  8.8 12.3 %copy-start.1 = (bf16[2,768,256]{2,1,0:T(8,128)(2,1)S(1)}, bf16[2,768,256]{2,1,0:T(8,128)(2,1)}, u32[]{:S(2)}) copy-start(bf16[2,768,256]{2,1,0:T(8,128)(2,1)} %constant.5.clone.right_ref) | copy-start | bytes 2359300
  8.8 12.3 %copy-start.2 = (bf16[2,256,768]{2,1,0:T(8,128)(2,1)S(1)}, bf16[2,256,768]{2,1,0:T(8,128)(2,1)}, u32[]{:S(2)}) copy-start(bf16[2,256,768]{2,1,0:T(8,128)(2,1)} %constant.4.clone.left_ref) | copy-start | bytes 2359300
  8.8 12.3 %copy-start.3 = (f32[2,128,128]{2,1,0:T(8,128)S(1)}, f32[2,128,128]{2,1,0:T(8,128)}, u32[]{:S(2)}) copy-start(f32[2,128,128]{2,1,0:T(8,128)} %probe_ref.1) | copy-start | bytes 393220
  10.2 10.9 %collective-permute-start.4 = (bf16[2,2,128,128]{3,2,1,0:T(8,128)(2,1)S(1)}, bf16[2,2,128,128]{3,2,1,0:T(8,128)(2,1)S(1)}, u32[]{:S(2)}, u32[]{:S(2)}) collective-permute-start(bf16[2,2,128,128]{3,2,1,0:T(8,128)(2,1)S(1)} %get-tuple-element.18), channel_id=1, source_target_pairs={{0,24},{1,25},{2,26},{3,27},{4,28},{5,29},{6,30},{7,31},{8,16},{9,... | collective-permute-start | bytes 393224 | tf_op jit(solution)/shard_map/ppermute | solution.py:273
  13.0 8.1 %collective-permute-start.3 = (bf16[2,2,128,128]{3,2,1,0:T(8,128)(2,1)S(1)}, bf16[2,2,128,128]{3,2,1,0:T(8,128)(2,1)S(1)}, u32[]{:S(2)}, u32[]{:S(2)}) collective-permute-start(bf16[2,2,128,128]{3,2,1,0:T(8,128)(2,1)S(1)} %get-tuple-element.18), channel_id=1, source_target_pairs={{0,16},{1,17},{2,18},{3,19},{4,20},{5,21},{6,22},{7,23},{8,24},{9,... | collective-permute-start | bytes 393224 | tf_op jit(solution)/shard_map/ppermute | solution.py:273
  13.5 7.3 %collective-permute-start.1 = (f32[2,128,128]{2,1,0:T(8,128)S(1)}, f32[2,128,128]{2,1,0:T(8,128)S(1)}, u32[]{:S(2)}, u32[]{:S(2)}) collective-permute-start(f32[2,128,128]{2,1,0:T(8,128)S(1)} %copy-done.4), channel_id=1, source_target_pairs={{0,4},{1,5},{2,6},{3,7},{4,0},{5,1},{6,2},{7,3},{8,12},{9,13},{10,... | collective-permute-start | bytes 393224 | tf_op jit(solution)/shard_map/ppermute | solution.py:273
  16.1 5.0 %collective-permute-start.2 = (bf16[2,2,128,128]{3,2,1,0:T(8,128)(2,1)S(1)}, bf16[2,2,128,128]{3,2,1,0:T(8,128)(2,1)S(1)}, u32[]{:S(2)}, u32[]{:S(2)}) collective-permute-start(bf16[2,2,128,128]{3,2,1,0:T(8,128)(2,1)S(1)} %get-tuple-element.17.rest_2_), channel_id=1, source_target_pairs={{0,8},{1,9},{2,10},{3,11},{4,12},{5,13},{6,14},{7,15},{8,0},{9,1},... | collective-permute-start | bytes 393224 | tf_op jit(solution)/shard_map/ppermute | solution.py:273
  28.2 6.1 %collective-permute-start.7 = (bf16[2,272,128]{2,1,0:T(8,128)(2,1)S(1)}, bf16[2,272,128]{2,1,0:T(8,128)(2,1)S(1)}, u32[]{:S(2)}, u32[]{:S(2)}) collective-permute-start(bf16[2,272,128]{2,1,0:T(8,128)(2,1)S(1)} %get-tuple-element.20), channel_id=1, source_target_pairs={{0,18},{1,19},{2,16},{3,17},{4,22},{5,23},{6,20},{7,21},{8,26},{9,... | collective-permute-start | bytes 417800 | tf_op jit(solution)/shard_map/ppermute | solution.py:273
  30.8 5.1 %collective-permute-start.5 = (bf16[2,272,128]{2,1,0:T(8,128)(2,1)S(1)}, bf16[2,272,128]{2,1,0:T(8,128)(2,1)S(1)}, u32[]{:S(2)}, u32[]{:S(2)}) collective-permute-start(bf16[2,272,128]{2,1,0:T(8,128)(2,1)S(1)} %get-tuple-element.20), channel_id=1, source_target_pairs={{0,16},{1,17},{2,18},{3,19},{4,20},{5,21},{6,22},{7,23},{8,24},{9,... | collective-permute-start | bytes 417800 | tf_op jit(solution)/shard_map/ppermute | solution.py:273
  31.3 5.1 %collective-permute-start.6 = (bf16[2,272,128]{2,1,0:T(8,128)(2,1)S(1)}, bf16[2,272,128]{2,1,0:T(8,128)(2,1)S(1)}, u32[]{:S(2)}, u32[]{:S(2)}) collective-permute-start(bf16[2,272,128]{2,1,0:T(8,128)(2,1)S(1)} %get-tuple-element.19.refs_0_), channel_id=1, source_target_pairs={{0,2},{1,3},{2,0},{3,1},{4,6},{5,7},{6,4},{7,5},{8,10},{9,11},{10,... | collective-permute-start | bytes 417800 | tf_op jit(solution)/shard_map/ppermute | solution.py:273
  31.7 4.6 %collective-permute-start.8 = (bf16[2,272,128]{2,1,0:T(8,128)(2,1)S(1)}, bf16[2,272,128]{2,1,0:T(8,128)(2,1)S(1)}, u32[]{:S(2)}, u32[]{:S(2)}) collective-permute-start(bf16[2,272,128]{2,1,0:T(8,128)(2,1)S(1)} %get-tuple-element.19.refs_0_), channel_id=1, source_target_pairs={{0,1},{1,0},{2,3},{3,2},{4,5},{5,4},{6,7},{7,6},{8,9},{9,8},{10,11... | collective-permute-start | bytes 417800 | tf_op jit(solution)/shard_map/ppermute | solution.py:273
  34.2 2.1 %collective-permute-start.11 = (bf16[2,272,128]{2,1,0:T(8,128)(2,1)S(1)}, bf16[2,272,128]{2,1,0:T(8,128)(2,1)S(1)}, u32[]{:S(2)}, u32[]{:S(2)}) collective-permute-start(bf16[2,272,128]{2,1,0:T(8,128)(2,1)S(1)} %collective-permute-done.7.refs_3_), channel_id=1, source_target_pairs={{0,1},{1,0},{2,3},{3,2},{4,5},{5,4},{6,7},{7,6},{8,9},{9,8},{10,11... | collective-permute-start | bytes 417800 | tf_op jit(solution)/shard_map/ppermute | solution.py:273
  35.8 1.4 %collective-permute-start.9 = (bf16[2,272,128]{2,1,0:T(8,128)(2,1)S(1)}, bf16[2,272,128]{2,1,0:T(8,128)(2,1)S(1)}, u32[]{:S(2)}, u32[]{:S(2)}) collective-permute-start(bf16[2,272,128]{2,1,0:T(8,128)(2,1)S(1)} %collective-permute-done.5.refs_1_), channel_id=1, source_target_pairs={{0,1},{1,0},{2,3},{3,2},{4,5},{5,4},{6,7},{7,6},{8,9},{9,8},{10,11... | collective-permute-start | bytes 417800 | tf_op jit(solution)/shard_map/ppermute | solution.py:273
  36.3 1.4 %collective-permute-start.10 = (bf16[2,272,128]{2,1,0:T(8,128)(2,1)S(1)}, bf16[2,272,128]{2,1,0:T(8,128)(2,1)S(1)}, u32[]{:S(2)}, u32[]{:S(2)}) collective-permute-start(bf16[2,272,128]{2,1,0:T(8,128)(2,1)S(1)} %collective-permute-done.6.refs_2_), channel_id=1, source_target_pairs={{0,1},{1,0},{2,3},{3,2},{4,5},{5,4},{6,7},{7,6},{8,9},{9,8},{10,11... | collective-permute-start | bytes 417800 | tf_op jit(solution)/shard_map/ppermute | solution.py:273

commit v7 on v6

--- a/solution.py
+++ b/solution.py
@@ -35,21 +35,45 @@
 code_rows = 16
 
 
+def fetch_kernel(obj_ref, out_ref, sem):
+    copy = pltpu.make_async_copy(obj_ref, out_ref, sem)
+    copy.start()
+    copy.wait()
+
+
+def fetch(obj):
+    size = 4 * math.prod(obj.shape)
+    return pl.pallas_call(
+        fetch_kernel,
+        out_shape=jax.ShapeDtypeStruct(obj.shape, obj.dtype),
+        in_specs=[pl.BlockSpec(memory_space=pltpu.HBM)],
+        out_specs=pl.BlockSpec(memory_space=pltpu.VMEM),
+        scratch_shapes=[pltpu.SemaphoreType.DMA],
+        compiler_params=pltpu.CompilerParams(vmem_limit_bytes=16 * 1024 * 1024),
+        cost_estimate=pl.CostEstimate(flops=0, bytes_accessed=2 * size, transcendentals=0),
+        name="fetch_slice",
+    )(obj)
+
+
 def window_kernel(members, obj_ref, *rest):
-    table, buf, table_sems, sems = rest[-4:]
-    clusters, count = buf.shape[:2]
-    pos_refs, out_refs, code_ref = rest[:clusters], rest[clusters:-5], rest[-5]
+    table, table_sems = rest[-2:]
+    clusters, count = table.shape[:2]
+    pos_refs, out_refs, code_ref = rest[:clusters], rest[clusters:-3], rest[-3]
     window = out_refs[0].shape[-1]
     rows, cols = obj_ref.shape[-2:]
-    tall, wide = buf.shape[-2:]
+    tall, wide = window + 8, window + 128
     cluster = lax.div(lax.axis_index("dp"), members)
     home = lax.div(lax.axis_index("depth"), 2)
 
     fetches = [
-        pltpu.make_async_copy(pos_refs[m], table.at[m], table_sems.at[m]) for m in range(clusters)
+        pltpu.make_async_copy(pos_refs[m], table.at[m], table_sems.at[m])
+        for m in range(1, clusters)
     ]
     for fetch in fetches:
         fetch.start()
+    for p in range(count):
+        for axis in range(2):
+            table[0, p, axis] = pos_refs[0][p, axis]
     for fetch in fetches:
         fetch.wait()
 
@@ -60,50 +84,40 @@
         col_base = pl.multiple_of(jnp.minimum(col >> 7, (cols - wide) // 128) * 128, 128)
         return row_base, col_base, row - row_base, col - col_base
 
-    def copy(m, p):
-        row_base, col_base, _, _ = corner(m, p)
-        return pltpu.make_async_copy(
-            obj_ref.at[:, pl.ds(row_base, tall), pl.ds(col_base, wide)], buf.at[m, p], sems.at[m, p]
-        )
-
-    order = [(m, p) for m in reversed(range(clusters)) for p in range(count)]
-    for m, p in order:
-        copy(m, p).start()
     line = lax.broadcasted_iota(jnp.int32, (code_rows, window), 0)
     for p in range(count):
         row, col = table[home ^ cluster, p, 0], table[home ^ cluster, p, 1]
         code = jnp.where(line == 0, row >> 3, jnp.where(line == 1, row & 7, 0))
         code = jnp.where(line == 2, col >> 3, jnp.where(line == 3, col & 7, code))
         code_ref[p] = code.astype(f32).astype(bf16)
-    for m, p in order:
-        copy(m, p).wait()
-        _, _, row_off, col_off = corner(m, p)
-        lift = jnp.where(row_off == 0, 0, tall - row_off)
-        shift = jnp.where(col_off == 0, 0, wide - col_off)
-        for part in range(2):
-            block = pltpu.roll(buf[m, p, part], shift, 1)[:, :window]
-            block = pltpu.roll(block, lift, 0)[:window]
-            out_refs[m][p, part] = block.astype(bf16)
+    for m in reversed(range(clusters)):
+        for p in range(count):
+            row_base, col_base, row_off, col_off = corner(m, p)
+            lift = jnp.where(row_off == 0, 0, tall - row_off)
+            shift = jnp.where(col_off == 0, 0, wide - col_off)
+            for part in range(2):
+                block = obj_ref[part, pl.ds(row_base, tall), pl.ds(col_base, wide)]
+                block = pltpu.roll(block, shift, 1)[:, :window]
+                block = pltpu.roll(block, lift, 0)[:window]
+                out_refs[m][p, part] = block.astype(bf16)
 
 
 def take_windows(obj, positions, window, members):
     clusters, count = len(positions), positions[0].shape[0]
-    tall, wide = window + 8, window + 128
     any_space = pl.BlockSpec(memory_space=pl.ANY)
+    smem = pl.BlockSpec(memory_space=pltpu.SMEM)
     vmem = pl.BlockSpec(memory_space=pltpu.VMEM)
     out = pl.pallas_call(
         functools.partial(window_kernel, members),
         out_shape=[jax.ShapeDtypeStruct((count, 2, window, window), bf16)] * clusters
         + [jax.ShapeDtypeStruct((count, code_rows, window), bf16)],
-        in_specs=[any_space] * (1 + clusters),
+        in_specs=[vmem, smem] + [any_space] * (clusters - 1),
         out_specs=[vmem] * (clusters + 1),
         scratch_shapes=[
             pltpu.SMEM((clusters, count, 2), jnp.int32),
-            pltpu.VMEM((clusters, count, 2, tall, wide), f32),
             pltpu.SemaphoreType.DMA((clusters,)),
-            pltpu.SemaphoreType.DMA((clusters, count)),
         ],
-        compiler_params=pltpu.CompilerParams(vmem_limit_bytes=24 * 1024 * 1024),
+        compiler_params=pltpu.CompilerParams(vmem_limit_bytes=16 * 1024 * 1024),
         name="take_windows",
     )(obj, *positions)
     return out[:clusters], out[clusters]
@@ -282,8 +296,8 @@
 
     homes = [m * members for m in range(1, clusters)]
     all_positions = [positions] + [swap(positions, 0, home) for home in homes]
-    windows, code = take_windows(object_slices[0], all_positions, window, members)
-    measured, phase, code = lax.optimization_barrier((measured, propagator_phase, code))
+    windows, code = take_windows(fetch(object_slices[0]), all_positions, window, members)
+    phase, code = lax.optimization_barrier((propagator_phase, code))
     windows = [windows[0]] + [swap(windows[m // 2], m, 0) for m in range(1, depth)]
     targets = [measured] + [swap(measured, 0, home) for home in homes]
     kern = jnp.stack([jnp.cos(phase), jnp.sin(phase)])

time: 39.5 us -> 37 us (0.937)
  starting transfers between devices: 14.1 us -> 11.2 us
  Pallas kernels: 9.86 us -> 10.5 us
  waiting for transfers between devices: 11.9 us -> 12.3 us
    ppermute x12, starting transfers between devices: 14.1 us -> 11.2 us  [swap(): return lax.ppermute(block, ('depth', 'dp'), route)]
    ppermute x12, waiting for transfers between devices: 11.9 us -> 12.3 us  [swap(): return lax.ppermute(block, ('depth', 'dp'), route)]
  transfers between devices with their start and end apart: 12 -> 12, of which waited for: 8 -> 6; matrix products, arithmetic and copies ran while one was open for 1% -> 1% of each run, Pallas kernels for 0% -> 5%
where the time goes in v7:
time: 37 us; the launch traced here: 36.9 us
  waiting for transfers between devices  12.3 us (33%)
  starting transfers between devices  11.2 us (30%)
  Pallas kernels  10.5 us (28%)
  local copies, waits for them, and re-layouts  2.88 us (8%)
    ppermute x12, waiting for transfers between devices, swap(): return lax.ppermute(block, ('depth', 'dp'), route)  12.3 us
    ppermute x12, starting transfers between devices, swap(): return lax.ppermute(block, ('depth', 'dp'), route)  11.2 us
    pallas_call x1, Pallas kernels, run_waves(): pl.pallas_call(functools.partial(wave_kernel, members, len(measured)), ou...  7.06 us
    unnamed x14, local copies, waits for them, and re-layouts  2.64 us
    pallas_call x1, Pallas kernels, place_windows(): pl.pallas_call(place_kernel, out_shape=jax.ShapeDtypeStruct((2, stripe, c...  1.61 us
    pallas_call x1, Pallas kernels, take_windows(): pl.pallas_call(functools.partial(window_kernel, members), out_shape=[jax....  1.45 us
  transfers between devices with their start and end apart: 12, of which 6 were waited for; matrix products, arithmetic and copies ran while one was open for 1% of the time, Pallas kernels for 5%

profile of v7, /device:TPU:0, one launch (start us, length us, event | category | flops | bytes accessed | tf_op | source)
XLA Modules:
  0.0 36.9 jit_solution(9138176946480152559)
XLA Ops:
  0.0 4.0 %collective-permute-start = (s32[2,2]{1,0:T(2,128)}, s32[2,2]{1,0:T(2,128)S(1)}, u32[]{:S(2)}, u32[]{:S(2)}) collective-permute-start(s32[2,2]{1,0:T(2,128)} %rest_0_.2), channel_id=1, source_target_pairs={{0,4},{1,5},{2,6},{3,7},{4,0},{5,1},{6,2},{7,3},{8,12},{9,13},{10,... | collective-permute-start | bytes 56 | tf_op jit(solution)/shard_map/ppermute | solution.py:287
  4.0 0.0 collective-permute-start.1
  4.1 2.3 %copy-done = f32[1,2,768,768]{3,2,1,0:T(8,128)S(1)} copy-done((f32[1,2,768,768]{3,2,1,0:T(8,128)S(1)}, f32[1,2,768,768]{3,2,1,0:T(8,128)}, u32[]{:S(2)}) %copy-start) | copy-done | bytes 4718616
  6.4 0.3 fetch_slice.1.obj_ref
  6.8 0.0 copy-start.1
  6.8 0.0 copy-start.2
  6.8 0.0 copy-start.3
  6.8 0.3 copy-done.5
  7.1 1.5 %take_windows.1 = (bf16[2,2,128,128]{3,2,1,0:T(8,128)(2,1)S(1)}, bf16[2,2,128,128]{3,2,1,0:T(8,128)(2,1)S(1)}, bf16[2,16,128]{2,1,0:T(8,128)(2,1)S(1)}) custom-call(f32[2,768,768]{2,1,0:T(8,128)S(1)} %fetch_slice.1.obj_ref, s32[2,2]{1,0:T(2,128)S(1)} %copy-done.5, s32[2,2]{1,0:T(2,128)S(1)} %collective-permute-done.rest_1_), custom_call_target="tpu_custom_call" | custom-call | tf_op jit(solution)/shard_map/take_windows/pallas_call | solution.py:110
  8.5 1.9 %collective-permute-start.3 = (bf16[2,2,128,128]{3,2,1,0:T(8,128)(2,1)S(1)}, bf16[2,2,128,128]{3,2,1,0:T(8,128)(2,1)S(1)}, u32[]{:S(2)}, u32[]{:S(2)}) collective-permute-start(bf16[2,2,128,128]{3,2,1,0:T(8,128)(2,1)S(1)} %get-tuple-element.16), channel_id=1, source_target_pairs={{0,16},{1,17},{2,18},{3,19},{4,20},{5,21},{6,22},{7,23},{8,24},{9,... | collective-permute-start | bytes 393224 | tf_op jit(solution)/shard_map/ppermute | solution.py:287
  10.4 1.4 %collective-permute-start.4 = (bf16[2,2,128,128]{3,2,1,0:T(8,128)(2,1)S(1)}, bf16[2,2,128,128]{3,2,1,0:T(8,128)(2,1)S(1)}, u32[]{:S(2)}, u32[]{:S(2)}) collective-permute-start(bf16[2,2,128,128]{3,2,1,0:T(8,128)(2,1)S(1)} %get-tuple-element.16), channel_id=1, source_target_pairs={{0,24},{1,25},{2,26},{3,27},{4,28},{5,29},{6,30},{7,31},{8,16},{9,... | collective-permute-start | bytes 393224 | tf_op jit(solution)/shard_map/ppermute | solution.py:287
  11.9 0.2 collective-permute-start.2
  12.1 0.2 cosine_bitcast_fusion
  12.4 0.5 %collective-permute-done.1.rest_1_ = f32[2,128,128]{2,1,0:T(8,128)S(1)} collective-permute-done((f32[2,128,128]{2,1,0:T(8,128)}, f32[2,128,128]{2,1,0:T(8,128)S(1)}, u32[]{:S(2)}, u32[]{:S(2)}) %collective-permute-start.1) | collective-permute-done | bytes 131104 | tf_op jit(solution)/shard_map/ppermute | solution.py:287
  12.9 4.7 %collective-permute-done.2.rest_3_ = bf16[2,2,128,128]{3,2,1,0:T(8,128)(2,1)S(1)} collective-permute-done((bf16[2,2,128,128]{3,2,1,0:T(8,128)(2,1)S(1)}, bf16[2,2,128,128]{3,2,1,0:T(8,128)(2,1)S(1)}, u32[]{:S(2)}, u32[]{:S(2)}) %collective-permute-start.2) | collective-permute-done | bytes 131104 | tf_op jit(solution)/shard_map/ppermute | solution.py:287
  17.7 7.1 %run_waves.1 = (bf16[2,272,128]{2,1,0:T(8,128)(2,1)S(1)}, bf16[2,272,128]{2,1,0:T(8,128)(2,1)S(1)}) custom-call(f32[2,128,128]{2,1,0:T(8,128)S(1)} %copy-done.3, f32[2,128,128]{2,1,0:T(8,128)S(1)} %pad_maximum_fusion.kern_ref, bf16[2,256,768]{2,1,0:T(8,128)(2,1)S(1)} %copy-done.1, bf16[2,768,256]{2,1,0:T(8,128)(2,1)S(1)} %copy-done.2, ...), custom_call_target="tpu_custom_call" | custom-call | tf_op jit(solution)/shard_map/run_waves/pallas_call | solution.py:216
  24.7 1.7 %collective-permute-start.6 = (bf16[2,272,128]{2,1,0:T(8,128)(2,1)S(1)}, bf16[2,272,128]{2,1,0:T(8,128)(2,1)S(1)}, u32[]{:S(2)}, u32[]{:S(2)}) collective-permute-start(bf16[2,272,128]{2,1,0:T(8,128)(2,1)S(1)} %get-tuple-element.17.refs_0_), channel_id=1, source_target_pairs={{0,2},{1,3},{2,0},{3,1},{4,6},{5,7},{6,4},{7,5},{8,10},{9,11},{10,... | collective-permute-start | bytes 417800 | tf_op jit(solution)/shard_map/ppermute | solution.py:287
  26.4 1.4 %collective-permute-start.7 = (bf16[2,272,128]{2,1,0:T(8,128)(2,1)S(1)}, bf16[2,272,128]{2,1,0:T(8,128)(2,1)S(1)}, u32[]{:S(2)}, u32[]{:S(2)}) collective-permute-start(bf16[2,272,128]{2,1,0:T(8,128)(2,1)S(1)} %get-tuple-element.18), channel_id=1, source_target_pairs={{0,18},{1,19},{2,16},{3,17},{4,22},{5,23},{6,20},{7,21},{8,26},{9,... | collective-permute-start | bytes 417800 | tf_op jit(solution)/shard_map/ppermute | solution.py:287
  27.8 0.5 %collective-permute-start.5 = (bf16[2,272,128]{2,1,0:T(8,128)(2,1)S(1)}, bf16[2,272,128]{2,1,0:T(8,128)(2,1)S(1)}, u32[]{:S(2)}, u32[]{:S(2)}) collective-permute-start(bf16[2,272,128]{2,1,0:T(8,128)(2,1)S(1)} %get-tuple-element.18), channel_id=1, source_target_pairs={{0,16},{1,17},{2,18},{3,19},{4,20},{5,21},{6,22},{7,23},{8,24},{9,... | collective-permute-start | bytes 417800 | tf_op jit(solution)/shard_map/ppermute | solution.py:287
  28.3 2.5 %collective-permute-done.6.refs_2_ = bf16[2,272,128]{2,1,0:T(8,128)(2,1)S(1)} collective-permute-done((bf16[2,272,128]{2,1,0:T(8,128)(2,1)S(1)}, bf16[2,272,128]{2,1,0:T(8,128)(2,1)S(1)}, u32[]{:S(2)}, u32[]{:S(2)}) %collective-permute-start.6) | collective-permute-done | bytes 139296 | tf_op jit(solution)/shard_map/ppermute | solution.py:287
  30.8 1.8 %collective-permute-done.7.refs_3_ = bf16[2,272,128]{2,1,0:T(8,128)(2,1)S(1)} collective-permute-done((bf16[2,272,128]{2,1,0:T(8,128)(2,1)S(1)}, bf16[2,272,128]{2,1,0:T(8,128)(2,1)S(1)}, u32[]{:S(2)}, u32[]{:S(2)}) %collective-permute-start.7) | collective-permute-done | bytes 139296 | tf_op jit(solution)/shard_map/ppermute | solution.py:287
  32.6 1.4 %collective-permute-done.5.refs_1_ = bf16[2,272,128]{2,1,0:T(8,128)(2,1)S(1)} collective-permute-done((bf16[2,272,128]{2,1,0:T(8,128)(2,1)S(1)}, bf16[2,272,128]{2,1,0:T(8,128)(2,1)S(1)}, u32[]{:S(2)}, u32[]{:S(2)}) %collective-permute-start.5) | collective-permute-done | bytes 139296 | tf_op jit(solution)/shard_map/ppermute | solution.py:287
  34.0 1.3 %collective-permute-done.9.refs_5_ = bf16[2,272,128]{2,1,0:T(8,128)(2,1)S(1)} collective-permute-done((bf16[2,272,128]{2,1,0:T(8,128)(2,1)S(1)}, bf16[2,272,128]{2,1,0:T(8,128)(2,1)S(1)}, u32[]{:S(2)}, u32[]{:S(2)}) %collective-permute-start.9) | collective-permute-done | bytes 139296 | tf_op jit(solution)/shard_map/ppermute | solution.py:287
  35.3 1.6 %place_windows.1 = f32[2,96,768]{2,1,0:T(8,128)} custom-call(bf16[2,272,128]{2,1,0:T(8,128)(2,1)S(1)} %get-tuple-element.17.refs_0_, bf16[2,272,128]{2,1,0:T(8,128)(2,1)S(1)} %collective-permute-done.5.refs_1_, bf16[2,272,128]{2,1,0:T(8,128)(2,1)S(1)} %collective-permute-done.6.refs_2_, bf16[2,272,128]{2,1,0:T(8,128)(2,1)S(1)} %collective-permute-done.7.refs_3_, ...), custom_call_target="tpu_custom_call" | custom-call | tf_op jit(solution)/shard_map/place_windows/pallas_call | solution.py:269
  (20 shorter events, 0.1 us)
Async XLA Ops:
  0.0 6.8 %collective-permute-start = (s32[2,2]{1,0:T(2,128)}, s32[2,2]{1,0:T(2,128)S(1)}, u32[]{:S(2)}, u32[]{:S(2)}) collective-permute-start(s32[2,2]{1,0:T(2,128)} %rest_0_.2), channel_id=1, source_target_pairs={{0,4},{1,5},{2,6},{3,7},{4,0},{5,1},{6,2},{7,3},{8,12},{9,13},{10,... | collective-permute-start | bytes 56 | tf_op jit(solution)/shard_map/ppermute | solution.py:287
  4.0 8.9 %collective-permute-start.1 = (f32[2,128,128]{2,1,0:T(8,128)}, f32[2,128,128]{2,1,0:T(8,128)S(1)}, u32[]{:S(2)}, u32[]{:S(2)}) collective-permute-start(f32[2,128,128]{2,1,0:T(8,128)} %rest_0_.3), channel_id=1, source_target_pairs={{0,4},{1,5},{2,6},{3,7},{4,0},{5,1},{6,2},{7,3},{8,12},{9,13},{10,... | collective-permute-start | bytes 393224 | tf_op jit(solution)/shard_map/ppermute | solution.py:287
  4.1 2.3 %copy-start = (f32[1,2,768,768]{3,2,1,0:T(8,128)S(1)}, f32[1,2,768,768]{3,2,1,0:T(8,128)}, u32[]{:S(2)}) copy-start(f32[1,2,768,768]{3,2,1,0:T(8,128)} %param.7) | copy-start | bytes 14155780
  6.4 0.7 %copy-start.5 = (s32[2,2]{1,0:T(2,128)S(1)}, s32[2,2]{1,0:T(2,128)}, u32[]{:S(2)}) copy-start(s32[2,2]{1,0:T(2,128)} %rest_0_.2) | copy-start | bytes 52
  6.7 5.4 %copy-start.6 = (f32[128,128]{1,0:T(8,128)S(1)}, f32[128,128]{1,0:T(8,128)}, u32[]{:S(2)}) copy-start(f32[128,128]{1,0:T(8,128)} %param.10) | copy-start | bytes 196612
  6.8 10.9 %copy-start.1 = (bf16[2,256,768]{2,1,0:T(8,128)(2,1)S(1)}, bf16[2,256,768]{2,1,0:T(8,128)(2,1)}, u32[]{:S(2)}) copy-start(bf16[2,256,768]{2,1,0:T(8,128)(2,1)} %constant.4.clone.left_ref) | copy-start | bytes 2359300
  6.8 10.9 %copy-start.2 = (bf16[2,768,256]{2,1,0:T(8,128)(2,1)S(1)}, bf16[2,768,256]{2,1,0:T(8,128)(2,1)}, u32[]{:S(2)}) copy-start(bf16[2,768,256]{2,1,0:T(8,128)(2,1)} %constant.5.clone.right_ref) | copy-start | bytes 2359300
  6.8 10.9 %copy-start.3 = (f32[2,128,128]{2,1,0:T(8,128)S(1)}, f32[2,128,128]{2,1,0:T(8,128)}, u32[]{:S(2)}) copy-start(f32[2,128,128]{2,1,0:T(8,128)} %probe_ref.1) | copy-start | bytes 393220
  6.8 10.9 %copy-start.4 = (f32[2,128,128]{2,1,0:T(8,128)S(1)}, f32[2,128,128]{2,1,0:T(8,128)}, u32[]{:S(2)}) copy-start(f32[2,128,128]{2,1,0:T(8,128)} %rest_0_.3) | copy-start | bytes 393220
  8.5 9.1 %collective-permute-start.3 = (bf16[2,2,128,128]{3,2,1,0:T(8,128)(2,1)S(1)}, bf16[2,2,128,128]{3,2,1,0:T(8,128)(2,1)S(1)}, u32[]{:S(2)}, u32[]{:S(2)}) collective-permute-start(bf16[2,2,128,128]{3,2,1,0:T(8,128)(2,1)S(1)} %get-tuple-element.16), channel_id=1, source_target_pairs={{0,16},{1,17},{2,18},{3,19},{4,20},{5,21},{6,22},{7,23},{8,24},{9,... | collective-permute-start | bytes 393224 | tf_op jit(solution)/shard_map/ppermute | solution.py:287
  10.4 7.2 %collective-permute-start.4 = (bf16[2,2,128,128]{3,2,1,0:T(8,128)(2,1)S(1)}, bf16[2,2,128,128]{3,2,1,0:T(8,128)(2,1)S(1)}, u32[]{:S(2)}, u32[]{:S(2)}) collective-permute-start(bf16[2,2,128,128]{3,2,1,0:T(8,128)(2,1)S(1)} %get-tuple-element.16), channel_id=1, source_target_pairs={{0,24},{1,25},{2,26},{3,27},{4,28},{5,29},{6,30},{7,31},{8,16},{9,... | collective-permute-start | bytes 393224 | tf_op jit(solution)/shard_map/ppermute | solution.py:287
  11.9 5.7 %collective-permute-start.2 = (bf16[2,2,128,128]{3,2,1,0:T(8,128)(2,1)S(1)}, bf16[2,2,128,128]{3,2,1,0:T(8,128)(2,1)S(1)}, u32[]{:S(2)}, u32[]{:S(2)}) collective-permute-start(bf16[2,2,128,128]{3,2,1,0:T(8,128)(2,1)S(1)} %get-tuple-element.15.rest_2_), channel_id=1, source_target_pairs={{0,8},{1,9},{2,10},{3,11},{4,12},{5,13},{6,14},{7,15},{8,0},{9,1},... | collective-permute-start | bytes 393224 | tf_op jit(solution)/shard_map/ppermute | solution.py:287
  24.7 6.0 %collective-permute-start.6 = (bf16[2,272,128]{2,1,0:T(8,128)(2,1)S(1)}, bf16[2,272,128]{2,1,0:T(8,128)(2,1)S(1)}, u32[]{:S(2)}, u32[]{:S(2)}) collective-permute-start(bf16[2,272,128]{2,1,0:T(8,128)(2,1)S(1)} %get-tuple-element.17.refs_0_), channel_id=1, source_target_pairs={{0,2},{1,3},{2,0},{3,1},{4,6},{5,7},{6,4},{7,5},{8,10},{9,11},{10,... | collective-permute-start | bytes 417800 | tf_op jit(solution)/shard_map/ppermute | solution.py:287
  26.4 6.2 %collective-permute-start.7 = (bf16[2,272,128]{2,1,0:T(8,128)(2,1)S(1)}, bf16[2,272,128]{2,1,0:T(8,128)(2,1)S(1)}, u32[]{:S(2)}, u32[]{:S(2)}) collective-permute-start(bf16[2,272,128]{2,1,0:T(8,128)(2,1)S(1)} %get-tuple-element.18), channel_id=1, source_target_pairs={{0,18},{1,19},{2,16},{3,17},{4,22},{5,23},{6,20},{7,21},{8,26},{9,... | collective-permute-start | bytes 417800 | tf_op jit(solution)/shard_map/ppermute | solution.py:287
  27.8 6.2 %collective-permute-start.5 = (bf16[2,272,128]{2,1,0:T(8,128)(2,1)S(1)}, bf16[2,272,128]{2,1,0:T(8,128)(2,1)S(1)}, u32[]{:S(2)}, u32[]{:S(2)}) collective-permute-start(bf16[2,272,128]{2,1,0:T(8,128)(2,1)S(1)} %get-tuple-element.18), channel_id=1, source_target_pairs={{0,16},{1,17},{2,18},{3,19},{4,20},{5,21},{6,22},{7,23},{8,24},{9,... | collective-permute-start | bytes 417800 | tf_op jit(solution)/shard_map/ppermute | solution.py:287
  28.3 5.7 %collective-permute-start.8 = (bf16[2,272,128]{2,1,0:T(8,128)(2,1)S(1)}, bf16[2,272,128]{2,1,0:T(8,128)(2,1)S(1)}, u32[]{:S(2)}, u32[]{:S(2)}) collective-permute-start(bf16[2,272,128]{2,1,0:T(8,128)(2,1)S(1)} %get-tuple-element.17.refs_0_), channel_id=1, source_target_pairs={{0,1},{1,0},{2,3},{3,2},{4,5},{5,4},{6,7},{7,6},{8,9},{9,8},{10,11... | collective-permute-start | bytes 417800 | tf_op jit(solution)/shard_map/ppermute | solution.py:287
  30.8 3.2 %collective-permute-start.10 = (bf16[2,272,128]{2,1,0:T(8,128)(2,1)S(1)}, bf16[2,272,128]{2,1,0:T(8,128)(2,1)S(1)}, u32[]{:S(2)}, u32[]{:S(2)}) collective-permute-start(bf16[2,272,128]{2,1,0:T(8,128)(2,1)S(1)} %collective-permute-done.6.refs_2_), channel_id=1, source_target_pairs={{0,1},{1,0},{2,3},{3,2},{4,5},{5,4},{6,7},{7,6},{8,9},{9,8},{10,11... | collective-permute-start | bytes 417800 | tf_op jit(solution)/shard_map/ppermute | solution.py:287
  32.6 1.4 %collective-permute-start.11 = (bf16[2,272,128]{2,1,0:T(8,128)(2,1)S(1)}, bf16[2,272,128]{2,1,0:T(8,128)(2,1)S(1)}, u32[]{:S(2)}, u32[]{:S(2)}) collective-permute-start(bf16[2,272,128]{2,1,0:T(8,128)(2,1)S(1)} %collective-permute-done.7.refs_3_), channel_id=1, source_target_pairs={{0,1},{1,0},{2,3},{3,2},{4,5},{5,4},{6,7},{7,6},{8,9},{9,8},{10,11... | collective-permute-start | bytes 417800 | tf_op jit(solution)/shard_map/ppermute | solution.py:287
  34.0 1.4 %collective-permute-start.9 = (bf16[2,272,128]{2,1,0:T(8,128)(2,1)S(1)}, bf16[2,272,128]{2,1,0:T(8,128)(2,1)S(1)}, u32[]{:S(2)}, u32[]{:S(2)}) collective-permute-start(bf16[2,272,128]{2,1,0:T(8,128)(2,1)S(1)} %collective-permute-done.5.refs_1_), channel_id=1, source_target_pairs={{0,1},{1,0},{2,3},{3,2},{4,5},{5,4},{6,7},{7,6},{8,9},{9,8},{10,11... | collective-permute-start | bytes 417800 | tf_op jit(solution)/shard_map/ppermute | solution.py:287

commit v8 on v7

--- a/solution.py
+++ b/solution.py
@@ -35,24 +35,29 @@
 code_rows = 16
 
 
-def fetch_kernel(obj_ref, out_ref, sem):
+def fetch_kernel(obj_ref, meas_ref, out_ref, rounded_ref, sem):
     copy = pltpu.make_async_copy(obj_ref, out_ref, sem)
     copy.start()
+    rounded_ref[...] = meas_ref[...].astype(bf16)
     copy.wait()
 
 
-def fetch(obj):
+def fetch(obj, measured):
+    vmem = pl.BlockSpec(memory_space=pltpu.VMEM)
     size = 4 * math.prod(obj.shape)
     return pl.pallas_call(
         fetch_kernel,
-        out_shape=jax.ShapeDtypeStruct(obj.shape, obj.dtype),
-        in_specs=[pl.BlockSpec(memory_space=pltpu.HBM)],
-        out_specs=pl.BlockSpec(memory_space=pltpu.VMEM),
+        out_shape=[
+            jax.ShapeDtypeStruct(obj.shape, obj.dtype),
+            jax.ShapeDtypeStruct(measured.shape, bf16),
+        ],
+        in_specs=[pl.BlockSpec(memory_space=pltpu.HBM), vmem],
+        out_specs=[vmem, vmem],
         scratch_shapes=[pltpu.SemaphoreType.DMA],
         compiler_params=pltpu.CompilerParams(vmem_limit_bytes=16 * 1024 * 1024),
         cost_estimate=pl.CostEstimate(flops=0, bytes_accessed=2 * size, transcendentals=0),
         name="fetch_slice",
-    )(obj)
+    )(obj, measured)
 
 
 def window_kernel(members, obj_ref, *rest):
@@ -149,7 +154,7 @@
 
         @pl.when(lax.div(own, 2) ^ cluster == m)
         def _():
-            meas[...] = meas_ref[...]
+            meas[...] = meas_ref[...].astype(f32)
 
     def t_of(k, p):
         return trans[k, p, 0].astype(f32), trans[k, p, 1].astype(f32)
@@ -296,11 +301,13 @@
 
     homes = [m * members for m in range(1, clusters)]
     all_positions = [positions] + [swap(positions, 0, home) for home in homes]
-    windows, code = take_windows(fetch(object_slices[0]), all_positions, window, members)
+    obj, measured = fetch(object_slices[0], measured)
+    windows, code = take_windows(obj, all_positions, window, members)
     phase, code = lax.optimization_barrier((propagator_phase, code))
     windows = [windows[0]] + [swap(windows[m // 2], m, 0) for m in range(1, depth)]
+    kern = jnp.stack([jnp.cos(phase), jnp.sin(phase)])
+    kern, measured = lax.optimization_barrier((kern, measured))
     targets = [measured] + [swap(measured, 0, home) for home in homes]
-    kern = jnp.stack([jnp.cos(phase), jnp.sin(phase)])
     terms = run_waves(probe_field, kern, code, targets, windows, members)
 
     blocks = [

time: 37 us -> 37.6 us (1.016)
  starting transfers between devices: 11.2 us -> 12.8 us
  waiting for transfers between devices: 12.3 us -> 10.8 us
  local copies, waits for them, and re-layouts: 2.88 us -> 3.5 us
    ppermute x12, starting transfers between devices: 11.2 us -> 12.8 us  [swap(): return lax.ppermute(block, ('depth', 'dp'), route)]
    ppermute x12, waiting for transfers between devices: 12.3 us -> 10.8 us  [swap(): return lax.ppermute(block, ('depth', 'dp'), route)]
    unnamed x14, local copies, waits for them, and re-layouts: 2.64 us -> 3.26 us
  transfers between devices with their start and end apart: 12 -> 12, of which waited for: 6 -> 6; matrix products, arithmetic and copies ran while one was open for 1% -> 1% of each run, Pallas kernels for 5% -> 1%
where the time goes in v8:
time: 37.6 us; the launch traced here: 37.5 us
  starting transfers between devices  12.8 us (34%)
  waiting for transfers between devices  10.8 us (29%)
  Pallas kernels  10.3 us (27%)
  local copies, waits for them, and re-layouts  3.5 us (9%)
    ppermute x12, starting transfers between devices, swap(): return lax.ppermute(block, ('depth', 'dp'), route)  12.8 us
    ppermute x12, waiting for transfers between devices, swap(): return lax.ppermute(block, ('depth', 'dp'), route)  10.8 us
    pallas_call x1, Pallas kernels, run_waves(): pl.pallas_call(functools.partial(wave_kernel, members, len(measured)), ou...  7.07 us
    unnamed x14, local copies, waits for them, and re-layouts  3.26 us
    pallas_call x1, Pallas kernels, place_windows(): pl.pallas_call(place_kernel, out_shape=jax.ShapeDtypeStruct((2, stripe, c...  1.48 us
    pallas_call x1, Pallas kernels, take_windows(): pl.pallas_call(functools.partial(window_kernel, members), out_shape=[jax....  1.45 us
  transfers between devices with their start and end apart: 12, of which 6 were waited for; matrix products, arithmetic and copies ran while one was open for 1% of the time, Pallas kernels for 1%

profile of v8, /device:TPU:0, one launch (start us, length us, event | category | flops | bytes accessed | tf_op | source)
XLA Modules:
  0.0 37.5 jit_solution(4345494351074139425)
XLA Ops:
  0.0 4.0 %collective-permute-start = (s32[2,2]{1,0:T(2,128)}, s32[2,2]{1,0:T(2,128)S(1)}, u32[]{:S(2)}, u32[]{:S(2)}) collective-permute-start(s32[2,2]{1,0:T(2,128)} %rest_0_.1), channel_id=1, source_target_pairs={{0,4},{1,5},{2,6},{3,7},{4,0},{5,1},{6,2},{7,3},{8,12},{9,13},{10,... | collective-permute-start | bytes 56 | tf_op jit(solution)/shard_map/ppermute | solution.py:292
  4.0 2.3 %copy-done = f32[1,2,768,768]{3,2,1,0:T(8,128)S(1)} copy-done((f32[1,2,768,768]{3,2,1,0:T(8,128)S(1)}, f32[1,2,768,768]{3,2,1,0:T(8,128)}, u32[]{:S(2)}) %copy-start) | copy-done | bytes 4718616
  6.4 0.9 %copy-done.3 = f32[2,128,128]{2,1,0:T(8,128)S(1)} copy-done((f32[2,128,128]{2,1,0:T(8,128)S(1)}, f32[2,128,128]{2,1,0:T(8,128)}, u32[]{:S(2)}) %copy-start.3) | copy-done | bytes 131096
  7.3 0.3 fetch_slice.1
  7.6 0.0 collective-permute-done.rest_1_
  7.7 1.5 %take_windows.1 = (bf16[2,2,128,128]{3,2,1,0:T(8,128)(2,1)S(1)}, bf16[2,2,128,128]{3,2,1,0:T(8,128)(2,1)S(1)}, bf16[2,16,128]{2,1,0:T(8,128)(2,1)S(1)}) custom-call(f32[2,768,768]{2,1,0:T(8,128)S(1)} %get-tuple-element.16.obj_ref, s32[2,2]{1,0:T(2,128)S(1)} %copy-done.5, s32[2,2]{1,0:T(2,128)S(1)} %collective-permute-done.rest_1_), custom_call_target="tpu_custom_call" | custom-call | tf_op jit(solution)/shard_map/take_windows/pallas_call | solution.py:115
  9.1 2.5 %collective-permute-start.4 = (bf16[2,2,128,128]{3,2,1,0:T(8,128)(2,1)S(1)}, bf16[2,2,128,128]{3,2,1,0:T(8,128)(2,1)S(1)}, u32[]{:S(2)}, u32[]{:S(2)}) collective-permute-start(bf16[2,2,128,128]{3,2,1,0:T(8,128)(2,1)S(1)} %get-tuple-element.24), channel_id=1, source_target_pairs={{0,24},{1,25},{2,26},{3,27},{4,28},{5,29},{6,30},{7,31},{8,16},{9,... | collective-permute-start | bytes 393224 | tf_op jit(solution)/shard_map/ppermute | solution.py:292
  11.6 0.5 %collective-permute-start.3 = (bf16[2,2,128,128]{3,2,1,0:T(8,128)(2,1)S(1)}, bf16[2,2,128,128]{3,2,1,0:T(8,128)(2,1)S(1)}, u32[]{:S(2)}, u32[]{:S(2)}) collective-permute-start(bf16[2,2,128,128]{3,2,1,0:T(8,128)(2,1)S(1)} %get-tuple-element.24), channel_id=1, source_target_pairs={{0,16},{1,17},{2,18},{3,19},{4,20},{5,21},{6,22},{7,23},{8,24},{9,... | collective-permute-start | bytes 393224 | tf_op jit(solution)/shard_map/ppermute | solution.py:292
  12.1 0.2 cosine_bitcast_fusion
  12.4 0.6 %collective-permute-start.2 = (bf16[2,2,128,128]{3,2,1,0:T(8,128)(2,1)S(1)}, bf16[2,2,128,128]{3,2,1,0:T(8,128)(2,1)S(1)}, u32[]{:S(2)}, u32[]{:S(2)}) collective-permute-start(bf16[2,2,128,128]{3,2,1,0:T(8,128)(2,1)S(1)} %get-tuple-element.23.rest_2_), channel_id=1, source_target_pairs={{0,8},{1,9},{2,10},{3,11},{4,12},{5,13},{6,14},{7,15},{8,0},{9,1},... | collective-permute-start | bytes 393224 | tf_op jit(solution)/shard_map/ppermute | solution.py:292
  13.0 1.1 %collective-permute-start.1 = (bf16[2,128,128]{2,1,0:T(8,128)(2,1)S(1)}, bf16[2,128,128]{2,1,0:T(8,128)(2,1)S(1)}, u32[]{:S(2)}, u32[]{:S(2)}) collective-permute-start(bf16[2,128,128]{2,1,0:T(8,128)(2,1)S(1)} %get-tuple-element.22.rest_0_), channel_id=1, source_target_pairs={{0,4},{1,5},{2,6},{3,7},{4,0},{5,1},{6,2},{7,3},{8,12},{9,13},{10,... | collective-permute-start | bytes 196616 | tf_op jit(solution)/shard_map/ppermute | solution.py:292
  14.1 4.1 %collective-permute-done.1.rest_1_ = bf16[2,128,128]{2,1,0:T(8,128)(2,1)S(1)} collective-permute-done((bf16[2,128,128]{2,1,0:T(8,128)(2,1)S(1)}, bf16[2,128,128]{2,1,0:T(8,128)(2,1)S(1)}, u32[]{:S(2)}, u32[]{:S(2)}) %collective-permute-start.1) | collective-permute-done | bytes 65568 | tf_op jit(solution)/shard_map/ppermute | solution.py:292
  18.2 0.0 collective-permute-done.2.rest_3_
  18.3 7.1 %run_waves.1 = (bf16[2,272,128]{2,1,0:T(8,128)(2,1)S(1)}, bf16[2,272,128]{2,1,0:T(8,128)(2,1)S(1)}) custom-call(f32[2,128,128]{2,1,0:T(8,128)S(1)} %copy-done.4, f32[2,128,128]{2,1,0:T(8,128)S(1)} %pad_maximum_fusion.kern_ref, bf16[2,256,768]{2,1,0:T(8,128)(2,1)S(1)} %copy-done.2, bf16[2,768,256]{2,1,0:T(8,128)(2,1)S(1)} %copy-done.1, ...), custom_call_target="tpu_custom_call" | custom-call | tf_op jit(solution)/shard_map/run_waves/pallas_call | solution.py:221
  25.3 2.6 %collective-permute-start.7 = (bf16[2,272,128]{2,1,0:T(8,128)(2,1)S(1)}, bf16[2,272,128]{2,1,0:T(8,128)(2,1)S(1)}, u32[]{:S(2)}, u32[]{:S(2)}) collective-permute-start(bf16[2,272,128]{2,1,0:T(8,128)(2,1)S(1)} %get-tuple-element.26), channel_id=1, source_target_pairs={{0,18},{1,19},{2,16},{3,17},{4,22},{5,23},{6,20},{7,21},{8,26},{9,... | collective-permute-start | bytes 417800 | tf_op jit(solution)/shard_map/ppermute | solution.py:292
  27.9 0.5 %collective-permute-start.5 = (bf16[2,272,128]{2,1,0:T(8,128)(2,1)S(1)}, bf16[2,272,128]{2,1,0:T(8,128)(2,1)S(1)}, u32[]{:S(2)}, u32[]{:S(2)}) collective-permute-start(bf16[2,272,128]{2,1,0:T(8,128)(2,1)S(1)} %get-tuple-element.26), channel_id=1, source_target_pairs={{0,16},{1,17},{2,18},{3,19},{4,20},{5,21},{6,22},{7,23},{8,24},{9,... | collective-permute-start | bytes 417800 | tf_op jit(solution)/shard_map/ppermute | solution.py:292
  28.4 0.4 %collective-permute-start.6 = (bf16[2,272,128]{2,1,0:T(8,128)(2,1)S(1)}, bf16[2,272,128]{2,1,0:T(8,128)(2,1)S(1)}, u32[]{:S(2)}, u32[]{:S(2)}) collective-permute-start(bf16[2,272,128]{2,1,0:T(8,128)(2,1)S(1)} %get-tuple-element.25.refs_0_), channel_id=1, source_target_pairs={{0,2},{1,3},{2,0},{3,1},{4,6},{5,7},{6,4},{7,5},{8,10},{9,11},{10,... | collective-permute-start | bytes 417800 | tf_op jit(solution)/shard_map/ppermute | solution.py:292
  28.9 3.2 %collective-permute-done.7.refs_3_ = bf16[2,272,128]{2,1,0:T(8,128)(2,1)S(1)} collective-permute-done((bf16[2,272,128]{2,1,0:T(8,128)(2,1)S(1)}, bf16[2,272,128]{2,1,0:T(8,128)(2,1)S(1)}, u32[]{:S(2)}, u32[]{:S(2)}) %collective-permute-start.7) | collective-permute-done | bytes 139296 | tf_op jit(solution)/shard_map/ppermute | solution.py:292
  32.0 2.4 %collective-permute-done.5.refs_1_ = bf16[2,272,128]{2,1,0:T(8,128)(2,1)S(1)} collective-permute-done((bf16[2,272,128]{2,1,0:T(8,128)(2,1)S(1)}, bf16[2,272,128]{2,1,0:T(8,128)(2,1)S(1)}, u32[]{:S(2)}, u32[]{:S(2)}) %collective-permute-start.5) | collective-permute-done | bytes 139296 | tf_op jit(solution)/shard_map/ppermute | solution.py:292
  34.4 0.1 collective-permute-done.6.refs_2_
  34.5 0.4 %collective-permute-start.10 = (bf16[2,272,128]{2,1,0:T(8,128)(2,1)S(1)}, bf16[2,272,128]{2,1,0:T(8,128)(2,1)S(1)}, u32[]{:S(2)}, u32[]{:S(2)}) collective-permute-start(bf16[2,272,128]{2,1,0:T(8,128)(2,1)S(1)} %collective-permute-done.6.refs_2_), channel_id=1, source_target_pairs={{0,1},{1,0},{2,3},{3,2},{4,5},{5,4},{6,7},{7,6},{8,9},{9,8},{10,11... | collective-permute-start | bytes 417800 | tf_op jit(solution)/shard_map/ppermute | solution.py:292
  34.9 0.8 %collective-permute-done.9.refs_5_ = bf16[2,272,128]{2,1,0:T(8,128)(2,1)S(1)} collective-permute-done((bf16[2,272,128]{2,1,0:T(8,128)(2,1)S(1)}, bf16[2,272,128]{2,1,0:T(8,128)(2,1)S(1)}, u32[]{:S(2)}, u32[]{:S(2)}) %collective-permute-start.9) | collective-permute-done | bytes 139296 | tf_op jit(solution)/shard_map/ppermute | solution.py:292
  35.8 0.2 collective-permute-done.10.refs_6_
  36.0 1.5 %place_windows.1 = f32[2,96,768]{2,1,0:T(8,128)} custom-call(bf16[2,272,128]{2,1,0:T(8,128)(2,1)S(1)} %get-tuple-element.25.refs_0_, bf16[2,272,128]{2,1,0:T(8,128)(2,1)S(1)} %collective-permute-done.5.refs_1_, bf16[2,272,128]{2,1,0:T(8,128)(2,1)S(1)} %collective-permute-done.6.refs_2_, bf16[2,272,128]{2,1,0:T(8,128)(2,1)S(1)} %collective-permute-done.7.refs_3_, ...), custom_call_target="tpu_custom_call" | custom-call | tf_op jit(solution)/shard_map/place_windows/pallas_call | solution.py:274
  (20 shorter events, 0.0 us)
Async XLA Ops:
  0.0 7.6 %copy-start.5 = (s32[2,2]{1,0:T(2,128)S(1)}, s32[2,2]{1,0:T(2,128)}, u32[]{:S(2)}) copy-start(s32[2,2]{1,0:T(2,128)} %rest_0_.1) | copy-start | bytes 52
  0.0 7.6 %collective-permute-start = (s32[2,2]{1,0:T(2,128)}, s32[2,2]{1,0:T(2,128)S(1)}, u32[]{:S(2)}, u32[]{:S(2)}) collective-permute-start(s32[2,2]{1,0:T(2,128)} %rest_0_.1), channel_id=1, source_target_pairs={{0,4},{1,5},{2,6},{3,7},{4,0},{5,1},{6,2},{7,3},{8,12},{9,13},{10,... | collective-permute-start | bytes 56 | tf_op jit(solution)/shard_map/ppermute | solution.py:292
  4.0 2.3 %copy-start = (f32[1,2,768,768]{3,2,1,0:T(8,128)S(1)}, f32[1,2,768,768]{3,2,1,0:T(8,128)}, u32[]{:S(2)}) copy-start(f32[1,2,768,768]{3,2,1,0:T(8,128)} %param.7) | copy-start | bytes 14155780
  6.4 0.9 %copy-start.3 = (f32[2,128,128]{2,1,0:T(8,128)S(1)}, f32[2,128,128]{2,1,0:T(8,128)}, u32[]{:S(2)}) copy-start(f32[2,128,128]{2,1,0:T(8,128)} %meas_ref.1) | copy-start | bytes 393220
  7.3 4.9 %copy-start.6 = (f32[128,128]{1,0:T(8,128)S(1)}, f32[128,128]{1,0:T(8,128)}, u32[]{:S(2)}) copy-start(f32[128,128]{1,0:T(8,128)} %param.10) | copy-start | bytes 196612
  7.3 11.0 %copy-start.1 = (bf16[2,768,256]{2,1,0:T(8,128)(2,1)S(1)}, bf16[2,768,256]{2,1,0:T(8,128)(2,1)}, u32[]{:S(2)}) copy-start(bf16[2,768,256]{2,1,0:T(8,128)(2,1)} %constant.5.clone.right_ref) | copy-start | bytes 2359300
  7.3 11.0 %copy-start.2 = (bf16[2,256,768]{2,1,0:T(8,128)(2,1)S(1)}, bf16[2,256,768]{2,1,0:T(8,128)(2,1)}, u32[]{:S(2)}) copy-start(bf16[2,256,768]{2,1,0:T(8,128)(2,1)} %constant.4.clone.left_ref) | copy-start | bytes 2359300
  7.3 11.0 %copy-start.4 = (f32[2,128,128]{2,1,0:T(8,128)S(1)}, f32[2,128,128]{2,1,0:T(8,128)}, u32[]{:S(2)}) copy-start(f32[2,128,128]{2,1,0:T(8,128)} %probe_ref.1) | copy-start | bytes 393220
  9.1 9.1 %collective-permute-start.4 = (bf16[2,2,128,128]{3,2,1,0:T(8,128)(2,1)S(1)}, bf16[2,2,128,128]{3,2,1,0:T(8,128)(2,1)S(1)}, u32[]{:S(2)}, u32[]{:S(2)}) collective-permute-start(bf16[2,2,128,128]{3,2,1,0:T(8,128)(2,1)S(1)} %get-tuple-element.24), channel_id=1, source_target_pairs={{0,24},{1,25},{2,26},{3,27},{4,28},{5,29},{6,30},{7,31},{8,16},{9,... | collective-permute-start | bytes 393224 | tf_op jit(solution)/shard_map/ppermute | solution.py:292
  11.6 6.6 %collective-permute-start.3 = (bf16[2,2,128,128]{3,2,1,0:T(8,128)(2,1)S(1)}, bf16[2,2,128,128]{3,2,1,0:T(8,128)(2,1)S(1)}, u32[]{:S(2)}, u32[]{:S(2)}) collective-permute-start(bf16[2,2,128,128]{3,2,1,0:T(8,128)(2,1)S(1)} %get-tuple-element.24), channel_id=1, source_target_pairs={{0,16},{1,17},{2,18},{3,19},{4,20},{5,21},{6,22},{7,23},{8,24},{9,... | collective-permute-start | bytes 393224 | tf_op jit(solution)/shard_map/ppermute | solution.py:292
  12.4 5.8 %collective-permute-start.2 = (bf16[2,2,128,128]{3,2,1,0:T(8,128)(2,1)S(1)}, bf16[2,2,128,128]{3,2,1,0:T(8,128)(2,1)S(1)}, u32[]{:S(2)}, u32[]{:S(2)}) collective-permute-start(bf16[2,2,128,128]{3,2,1,0:T(8,128)(2,1)S(1)} %get-tuple-element.23.rest_2_), channel_id=1, source_target_pairs={{0,8},{1,9},{2,10},{3,11},{4,12},{5,13},{6,14},{7,15},{8,0},{9,1},... | collective-permute-start | bytes 393224 | tf_op jit(solution)/shard_map/ppermute | solution.py:292
  13.0 5.2 %collective-permute-start.1 = (bf16[2,128,128]{2,1,0:T(8,128)(2,1)S(1)}, bf16[2,128,128]{2,1,0:T(8,128)(2,1)S(1)}, u32[]{:S(2)}, u32[]{:S(2)}) collective-permute-start(bf16[2,128,128]{2,1,0:T(8,128)(2,1)S(1)} %get-tuple-element.22.rest_0_), channel_id=1, source_target_pairs={{0,4},{1,5},{2,6},{3,7},{4,0},{5,1},{6,2},{7,3},{8,12},{9,13},{10,... | collective-permute-start | bytes 196616 | tf_op jit(solution)/shard_map/ppermute | solution.py:292
  25.3 6.7 %collective-permute-start.7 = (bf16[2,272,128]{2,1,0:T(8,128)(2,1)S(1)}, bf16[2,272,128]{2,1,0:T(8,128)(2,1)S(1)}, u32[]{:S(2)}, u32[]{:S(2)}) collective-permute-start(bf16[2,272,128]{2,1,0:T(8,128)(2,1)S(1)} %get-tuple-element.26), channel_id=1, source_target_pairs={{0,18},{1,19},{2,16},{3,17},{4,22},{5,23},{6,20},{7,21},{8,26},{9,... | collective-permute-start | bytes 417800 | tf_op jit(solution)/shard_map/ppermute | solution.py:292
  27.9 6.5 %collective-permute-start.5 = (bf16[2,272,128]{2,1,0:T(8,128)(2,1)S(1)}, bf16[2,272,128]{2,1,0:T(8,128)(2,1)S(1)}, u32[]{:S(2)}, u32[]{:S(2)}) collective-permute-start(bf16[2,272,128]{2,1,0:T(8,128)(2,1)S(1)} %get-tuple-element.26), channel_id=1, source_target_pairs={{0,16},{1,17},{2,18},{3,19},{4,20},{5,21},{6,22},{7,23},{8,24},{9,... | collective-permute-start | bytes 417800 | tf_op jit(solution)/shard_map/ppermute | solution.py:292
  28.4 6.1 %collective-permute-start.6 = (bf16[2,272,128]{2,1,0:T(8,128)(2,1)S(1)}, bf16[2,272,128]{2,1,0:T(8,128)(2,1)S(1)}, u32[]{:S(2)}, u32[]{:S(2)}) collective-permute-start(bf16[2,272,128]{2,1,0:T(8,128)(2,1)S(1)} %get-tuple-element.25.refs_0_), channel_id=1, source_target_pairs={{0,2},{1,3},{2,0},{3,1},{4,6},{5,7},{6,4},{7,5},{8,10},{9,11},{10,... | collective-permute-start | bytes 417800 | tf_op jit(solution)/shard_map/ppermute | solution.py:292
  28.9 6.0 %collective-permute-start.8 = (bf16[2,272,128]{2,1,0:T(8,128)(2,1)S(1)}, bf16[2,272,128]{2,1,0:T(8,128)(2,1)S(1)}, u32[]{:S(2)}, u32[]{:S(2)}) collective-permute-start(bf16[2,272,128]{2,1,0:T(8,128)(2,1)S(1)} %get-tuple-element.25.refs_0_), channel_id=1, source_target_pairs={{0,1},{1,0},{2,3},{3,2},{4,5},{5,4},{6,7},{7,6},{8,9},{9,8},{10,11... | collective-permute-start | bytes 417800 | tf_op jit(solution)/shard_map/ppermute | solution.py:292
  32.0 2.9 %collective-permute-start.11 = (bf16[2,272,128]{2,1,0:T(8,128)(2,1)S(1)}, bf16[2,272,128]{2,1,0:T(8,128)(2,1)S(1)}, u32[]{:S(2)}, u32[]{:S(2)}) collective-permute-start(bf16[2,272,128]{2,1,0:T(8,128)(2,1)S(1)} %collective-permute-done.7.refs_3_), channel_id=1, source_target_pairs={{0,1},{1,0},{2,3},{3,2},{4,5},{5,4},{6,7},{7,6},{8,9},{9,8},{10,11... | collective-permute-start | bytes 417800 | tf_op jit(solution)/shard_map/ppermute | solution.py:292
  34.4 1.4 %collective-permute-start.9 = (bf16[2,272,128]{2,1,0:T(8,128)(2,1)S(1)}, bf16[2,272,128]{2,1,0:T(8,128)(2,1)S(1)}, u32[]{:S(2)}, u32[]{:S(2)}) collective-permute-start(bf16[2,272,128]{2,1,0:T(8,128)(2,1)S(1)} %collective-permute-done.5.refs_1_), channel_id=1, source_target_pairs={{0,1},{1,0},{2,3},{3,2},{4,5},{5,4},{6,7},{7,6},{8,9},{9,8},{10,11... | collective-permute-start | bytes 417800 | tf_op jit(solution)/shard_map/ppermute | solution.py:292
  34.5 1.5 %collective-permute-start.10 = (bf16[2,272,128]{2,1,0:T(8,128)(2,1)S(1)}, bf16[2,272,128]{2,1,0:T(8,128)(2,1)S(1)}, u32[]{:S(2)}, u32[]{:S(2)}) collective-permute-start(bf16[2,272,128]{2,1,0:T(8,128)(2,1)S(1)} %collective-permute-done.6.refs_2_), channel_id=1, source_target_pairs={{0,1},{1,0},{2,3},{3,2},{4,5},{5,4},{6,7},{7,6},{8,9},{9,8},{10,11... | collective-permute-start | bytes 417800 | tf_op jit(solution)/shard_map/ppermute | solution.py:292

commit v9 on v7

--- a/solution.py
+++ b/solution.py
@@ -28,8 +28,9 @@
         parts.append((high, low))
     (ph, plo), (mh, mlo) = parts
     right = np.stack([np.concatenate([ph, ph, plo], 0), np.concatenate([mh, mh, mlo], 0)])
-    left = np.stack([np.concatenate([mh, mh, mlo], 1), np.concatenate([ph, ph, plo], 1)])
-    return left, right
+    left = np.stack([mh, ph])
+    thin = np.concatenate([minus[:, :size] for minus in (mh, mh, mlo)], 1)
+    return jnp.asarray(thin), jnp.asarray(left), jnp.asarray(right)
 
 
 code_rows = 16
@@ -136,96 +137,117 @@
     return a[0] * b[0] + a[1] * b[1], a[0] * b[1] - a[1] * b[0]
 
 
-def wave_kernel(members, clusters, probe_ref, kern_ref, left_ref, right_ref, code_ref, *rest):
-    trans, terms, meas = rest[-3:]
-    slices, count, _, _, window = trans.shape
-    meas_refs, t_refs, out_refs = rest[:clusters], rest[clusters : clusters + slices], rest[clusters + slices : -3]
+def transform(field, sign, tables, exact):
+    thin_ref, left_ref, right_ref = tables
+    re, im = field
+    size = re.shape[0]
+    if exact:
+        high, low = split(jnp.concatenate([re, im], axis=1))
+        x = jnp.concatenate([high, low, high], axis=0)
+        y = jnp.dot(thin_ref[...], x, preferred_element_type=f32)
+        cr, ci, sr, si = y[:size, :size], y[:size, size:], y[size:, :size], y[size:, size:]
+        re, im = (cr - si, ci + sr) if sign == 0 else (cr + si, ci - sr)
+        high, low = split(jnp.concatenate([re, im], axis=1))
+        x = jnp.concatenate([high, low, high], axis=1)
+        y = jnp.dot(x, right_ref[sign], preferred_element_type=f32)
+    else:
+        x = jnp.concatenate([re, im], axis=0).astype(bf16)
+        y = jnp.dot(left_ref[sign], x, preferred_element_type=f32)
+        x = jnp.concatenate([y[:size], y[size:]], axis=1).astype(bf16)
+        y = jnp.dot(x, right_ref[sign, : 2 * size], preferred_element_type=f32)
+    return y[:, :size], y[:, size:]
+
+
+def forward_kernel(probe_ref, kern_ref, *rest):
+    tables, t_refs, (trans, waves) = rest[:3], rest[3:-2], rest[-2:]
+    slices, count = trans.shape[:2]
+    own = lax.axis_index("depth")
+    everyone = range(count)
+    for m in range(slices):
+        trans[own ^ m] = t_refs[m][...]
+    kern = (kern_ref[0], kern_ref[1])
+    psi = [(probe_ref[0], probe_ref[1])] * count
+    for k in range(slices):
+        field = [cmul((trans[k, p, 0].astype(f32), trans[k, p, 1].astype(f32)), psi[p]) for p in everyone]
+        psi = [transform(f, 1, tables, True) for f in field]
+        if k < slices - 1:
+            psi = [transform(cmul(kern, s), 0, tables, True) for s in psi]
+        for p in everyone:
+            waves[k, p, 0] = psi[p][0]
+            waves[k, p, 1] = psi[p][1]
+
+
+def backward_kernel(members, clusters, probe_ref, kern_ref, code_ref, trans, waves, *rest):
+    tables, meas_refs, out_refs, (terms, meas) = rest[:3], rest[3 : 3 + clusters], rest[3 + clusters : -2], rest[-2:]
+    slices, count, _, window, _ = trans.shape
     own, cluster = lax.axis_index("depth"), lax.div(lax.axis_index("dp"), members)
     everyone = range(count)
-
-    for m in range(slices):
-        trans[own ^ m] = t_refs[m][...]
     for m, meas_ref in enumerate(meas_refs):
 
         @pl.when(lax.div(own, 2) ^ cluster == m)
         def _():
             meas[...] = meas_ref[...]
 
-    def t_of(k, p):
-        return trans[k, p, 0].astype(f32), trans[k, p, 1].astype(f32)
-
-    def passes(x, axis, exact):
-        if not exact:
-            return x.astype(bf16)
-        high, low = split(x)
-        return jnp.concatenate([high, low, high], axis=axis)
-
-    def rows(fields, sign, exact):
-        x = jnp.concatenate([jnp.concatenate(f, axis=0) for f in fields], axis=1)
-        x = passes(x, 0, exact)
-        y = jnp.dot(left_ref[sign, :, : x.shape[0]], x, preferred_element_type=f32)
-        cut = [y[:, p * window : (p + 1) * window] for p in everyone]
-        return [(c[:window], c[window:]) for c in cut]
-
-    def cols(fields, sign, exact):
-        x = jnp.concatenate([jnp.concatenate(f, axis=1) for f in fields], axis=0)
-        x = passes(x, 1, exact)
-        y = jnp.dot(x, right_ref[sign, : x.shape[1]], preferred_element_type=f32)
-        cut = [y[p * window : (p + 1) * window] for p in everyone]
-        return [(c[:, :window], c[:, window:]) for c in cut]
-
-    plus, minus = 0, 1
-
-    def transform(fields, sign, exact):
-        return cols(rows(fields, sign, exact), sign, exact)
-
     kern = (kern_ref[0], kern_ref[1])
-    psi = [(probe_ref[0], probe_ref[1])] * count
-    kept = []
-    for k in range(slices):
-        kept.append(psi)
-        spectrum = transform([cmul(t_of(k, p), psi[p]) for p in everyone], minus, True)
-        if k < slices - 1:
-            psi = transform([cmul(kern, s) for s in spectrum], plus, True)
 
     def source(p):
-        re, im = spectrum[p]
+        re, im = waves[slices - 1, p, 0], waves[slices - 1, p, 1]
         scale = 2.0 * (re * re + im * im - meas[p])
         return scale * re, scale * im
 
-    returned = transform([source(p) for p in everyone], plus, False)
+    returned = [transform(source(p), 0, tables, False) for p in everyone]
     for k in reversed(range(slices)):
         for p in everyone:
-            re, im = cmul_conj(kept[k][p], returned[p])
+            wave = (waves[k - 1, p, 0], waves[k - 1, p, 1]) if k else (probe_ref[0], probe_ref[1])
+            re, im = cmul_conj(wave, returned[p])
             terms[own ^ k, p, :window] = (re * grad_scale).astype(bf16)
             terms[own ^ k, p, window:] = (im * grad_scale).astype(bf16)
         if k > 0:
-            chi = [cmul_conj(t_of(k, p), returned[p]) for p in everyone]
-            spectrum = transform(chi, minus, False)
-            returned = transform([cmul_conj(kern, s) for s in spectrum], plus, False)
+            chi = [
+                cmul_conj((trans[k, p, 0].astype(f32), trans[k, p, 1].astype(f32)), returned[p])
+                for p in everyone
+            ]
+            chi = [transform(c, 1, tables, False) for c in chi]
+            returned = [transform(cmul_conj(kern, c), 0, tables, False) for c in chi]
     for n, out_ref in enumerate(out_refs):
         out_ref[:, : 2 * window] = terms[2 * n]
         out_ref[:, 2 * window :] = code_ref[...]
 
 
-def run_waves(probe, kern, code, measured, windows, members):
-    slices, count, window = len(windows), code.shape[0], code.shape[-1]
-    left, right = dft_matrices(window)
-    vmem = pl.BlockSpec(memory_space=pltpu.VMEM)
+limit = pltpu.CompilerParams(vmem_limit_bytes=32 * 1024 * 1024)
+vmem = pl.BlockSpec(memory_space=pltpu.VMEM)
+
+
+def run_forward(probe, kern, tables, windows):
+    slices, shape = len(windows), windows[0].shape
+    return pl.pallas_call(
+        forward_kernel,
+        out_shape=[
+            jax.ShapeDtypeStruct((slices,) + shape, bf16),
+            jax.ShapeDtypeStruct((slices,) + shape, f32),
+        ],
+        in_specs=[vmem] * (5 + slices),
+        out_specs=[vmem, vmem],
+        compiler_params=limit,
+        name="run_forward",
+    )(probe, kern, *tables, *windows)
+
+
+def run_backward(probe, kern, code, trans, waves, tables, measured, members):
+    slices, count, _, window, _ = trans.shape
     block = jax.ShapeDtypeStruct((count, 2 * window + code_rows, window), bf16)
     return pl.pallas_call(
-        functools.partial(wave_kernel, members, len(measured)),
+        functools.partial(backward_kernel, members, len(measured)),
         out_shape=[block] * (slices // 2),
-        in_specs=[vmem] * (5 + len(measured) + slices),
+        in_specs=[vmem] * (8 + len(measured)),
         out_specs=[vmem] * (slices // 2),
         scratch_shapes=[
-            pltpu.VMEM((slices, count, 2, window, window), bf16),
             pltpu.VMEM((slices, count, 2 * window, window), bf16),
             pltpu.VMEM((count, window, window), f32),
         ],
-        compiler_params=pltpu.CompilerParams(vmem_limit_bytes=40 * 1024 * 1024),
-        name="run_waves",
-    )(probe, kern, jnp.asarray(left), jnp.asarray(right), code, *measured, *windows)
+        compiler_params=limit,
+        name="run_backward",
+    )(probe, kern, code, trans, waves, *tables, *measured)
 
 
 def place_kernel(*refs):
@@ -299,9 +321,12 @@
     windows, code = take_windows(fetch(object_slices[0]), all_positions, window, members)
     phase, code = lax.optimization_barrier((propagator_phase, code))
     windows = [windows[0]] + [swap(windows[m // 2], m, 0) for m in range(1, depth)]
-    targets = [measured] + [swap(measured, 0, home) for home in homes]
     kern = jnp.stack([jnp.cos(phase), jnp.sin(phase)])
-    terms = run_waves(probe_field, kern, code, targets, windows, members)
+    kern, late = lax.optimization_barrier((kern, measured))
+    targets = [measured] + [swap(late, 0, home) for home in homes]
+    tables = dft_matrices(window)
+    trans, waves = run_forward(probe_field, kern, tables, windows)
+    terms = run_backward(probe_field, kern, code, trans, waves, tables, targets, members)
 
     blocks = [
         swap(terms[m // 2], m, plane) if m or plane else terms[0]

time: 37 us -> 37.6 us (1.016)
  starting transfers between devices: 11.2 us -> 13.4 us
  waiting for transfers between devices: 12.3 us -> 10.2 us
    ppermute x12, starting transfers between devices: 11.2 us -> 13.4 us  [swap(): return lax.ppermute(block, ('depth', 'dp'), route)]
    ppermute x12, waiting for transfers between devices: 12.3 us -> 10.2 us  [swap(): return lax.ppermute(block, ('depth', 'dp'), route)]
    pallas_call x1 -> x2, Pallas kernels: 7.06 us -> 7.6 us  [the longest x1 4.75 us: run_forward(): pl.pallas_call(forward_kernel, out_shape=[jax.ShapeDtypeStruct((slices,)...]
    unnamed x14 -> x16, local copies, waits for them, and re-layouts: 2.64 us -> 2.64 us
  transfers between devices with their start and end apart: 12 -> 12, of which waited for: 6 -> 6; matrix products, arithmetic and copies ran while one was open for 1% -> 1% of each run, Pallas kernels for 5% -> 14%
where the time goes in v9:
time: 37.6 us; the launch traced here: 37.3 us
  starting transfers between devices  13.4 us (36%)
  Pallas kernels  10.7 us (28%)
  waiting for transfers between devices  10.2 us (27%)
  local copies, waits for them, and re-layouts  2.88 us (8%)
    ppermute x12, starting transfers between devices, swap(): return lax.ppermute(block, ('depth', 'dp'), route)  13.4 us
    ppermute x12, waiting for transfers between devices, swap(): return lax.ppermute(block, ('depth', 'dp'), route)  10.2 us
    pallas_call x1, Pallas kernels, run_forward(): pl.pallas_call(forward_kernel, out_shape=[jax.ShapeDtypeStruct((slices,)...  4.75 us
    pallas_call x1, Pallas kernels, run_backward(): pl.pallas_call(functools.partial(backward_kernel, members, len(measured))...  2.85 us
    unnamed x16, local copies, waits for them, and re-layouts  2.64 us
    pallas_call x1, Pallas kernels, take_windows(): pl.pallas_call(functools.partial(window_kernel, members), out_shape=[jax....  1.45 us
    pallas_call x1, Pallas kernels, place_windows(): pl.pallas_call(place_kernel, out_shape=jax.ShapeDtypeStruct((2, stripe, c...  1.35 us
  transfers between devices with their start and end apart: 12, of which 6 were waited for; matrix products, arithmetic and copies ran while one was open for 1% of the time, Pallas kernels for 14%

profile of v9, /device:TPU:0, one launch (start us, length us, event | category | flops | bytes accessed | tf_op | source)
XLA Modules:
  0.0 37.3 jit_solution(14945291008813471973)
XLA Ops:
  0.0 4.0 %collective-permute-start = (s32[2,2]{1,0:T(2,128)}, s32[2,2]{1,0:T(2,128)S(1)}, u32[]{:S(2)}, u32[]{:S(2)}) collective-permute-start(s32[2,2]{1,0:T(2,128)} %rest_0_.3), channel_id=1, source_target_pairs={{0,4},{1,5},{2,6},{3,7},{4,0},{5,1},{6,2},{7,3},{8,12},{9,13},{10,... | collective-permute-start | bytes 56 | tf_op jit(solution)/shard_map/ppermute | solution.py:309
  4.0 2.3 %copy-done = f32[1,2,768,768]{3,2,1,0:T(8,128)S(1)} copy-done((f32[1,2,768,768]{3,2,1,0:T(8,128)S(1)}, f32[1,2,768,768]{3,2,1,0:T(8,128)}, u32[]{:S(2)}) %copy-start) | copy-done | bytes 4718616
  6.4 0.3 fetch_slice.1.obj_ref
  6.8 0.3 copy-done.6
  7.1 1.5 %take_windows.1 = (bf16[2,2,128,128]{3,2,1,0:T(8,128)(2,1)S(1)}, bf16[2,2,128,128]{3,2,1,0:T(8,128)(2,1)S(1)}, bf16[2,16,128]{2,1,0:T(8,128)(2,1)S(1)}) custom-call(f32[2,768,768]{2,1,0:T(8,128)S(1)} %fetch_slice.1.obj_ref, s32[2,2]{1,0:T(2,128)S(1)} %copy-done.6, s32[2,2]{1,0:T(2,128)S(1)} %collective-permute-done.rest_1_), custom_call_target="tpu_custom_call" | custom-call | tf_op jit(solution)/shard_map/take_windows/pallas_call | solution.py:111
  8.5 2.5 %collective-permute-start.3 = (bf16[2,2,128,128]{3,2,1,0:T(8,128)(2,1)S(1)}, bf16[2,2,128,128]{3,2,1,0:T(8,128)(2,1)S(1)}, u32[]{:S(2)}, u32[]{:S(2)}) collective-permute-start(bf16[2,2,128,128]{3,2,1,0:T(8,128)(2,1)S(1)} %get-tuple-element.21), channel_id=1, source_target_pairs={{0,24},{1,25},{2,26},{3,27},{4,28},{5,29},{6,30},{7,31},{8,16},{9,... | collective-permute-start | bytes 393224 | tf_op jit(solution)/shard_map/ppermute | solution.py:309
  11.0 0.5 %collective-permute-start.2 = (bf16[2,2,128,128]{3,2,1,0:T(8,128)(2,1)S(1)}, bf16[2,2,128,128]{3,2,1,0:T(8,128)(2,1)S(1)}, u32[]{:S(2)}, u32[]{:S(2)}) collective-permute-start(bf16[2,2,128,128]{3,2,1,0:T(8,128)(2,1)S(1)} %get-tuple-element.21), channel_id=1, source_target_pairs={{0,16},{1,17},{2,18},{3,19},{4,20},{5,21},{6,22},{7,23},{8,24},{9,... | collective-permute-start | bytes 393224 | tf_op jit(solution)/shard_map/ppermute | solution.py:309
  11.5 0.2 cosine_bitcast_fusion
  11.8 0.6 %collective-permute-start.1 = (bf16[2,2,128,128]{3,2,1,0:T(8,128)(2,1)S(1)}, bf16[2,2,128,128]{3,2,1,0:T(8,128)(2,1)S(1)}, u32[]{:S(2)}, u32[]{:S(2)}) collective-permute-start(bf16[2,2,128,128]{3,2,1,0:T(8,128)(2,1)S(1)} %get-tuple-element.20.rest_3_), channel_id=1, source_target_pairs={{0,8},{1,9},{2,10},{3,11},{4,12},{5,13},{6,14},{7,15},{8,0},{9,1},... | collective-permute-start | bytes 393224 | tf_op jit(solution)/shard_map/ppermute | solution.py:309
  12.4 1.7 %collective-permute-start.4 = (f32[2,128,128]{2,1,0:T(8,128)S(1)}, f32[2,128,128]{2,1,0:T(8,128)S(1)}, u32[]{:S(2)}, u32[]{:S(2)}) collective-permute-start(f32[2,128,128]{2,1,0:T(8,128)S(1)} %copy-done.5), channel_id=1, source_target_pairs={{0,4},{1,5},{2,6},{3,7},{4,0},{5,1},{6,2},{7,3},{8,12},{9,13},{10,... | collective-permute-start | bytes 393224 | tf_op jit(solution)/shard_map/ppermute | solution.py:309
  14.1 3.2 %collective-permute-done.1.rest_4_ = bf16[2,2,128,128]{3,2,1,0:T(8,128)(2,1)S(1)} collective-permute-done((bf16[2,2,128,128]{3,2,1,0:T(8,128)(2,1)S(1)}, bf16[2,2,128,128]{3,2,1,0:T(8,128)(2,1)S(1)}, u32[]{:S(2)}, u32[]{:S(2)}) %collective-permute-start.1) | collective-permute-done | bytes 131104 | tf_op jit(solution)/shard_map/ppermute | solution.py:309
  17.4 4.8 %run_forward.1 = (bf16[4,2,2,128,128]{4,3,2,1,0:T(8,128)(2,1)S(1)}, f32[4,2,2,128,128]{4,3,2,1,0:T(8,128)S(1)}) custom-call(f32[2,128,128]{2,1,0:T(8,128)S(1)} %copy-done.4, f32[2,128,128]{2,1,0:T(8,128)S(1)} %pad_maximum_fusion.kern_ref, bf16[256,384]{1,0:T(8,128)(2,1)S(1)} %copy-done.3, bf16[2,256,256]{2,1,0:T(8,128)(2,1)S(1)} %copy-done.2, ...), custom_call_target="tpu_custom_call" | custom-call | tf_op jit(solution)/shard_map/run_forward/pallas_call | solution.py:223
  22.1 2.8 %run_backward.1 = (bf16[2,272,128]{2,1,0:T(8,128)(2,1)S(1)}, bf16[2,272,128]{2,1,0:T(8,128)(2,1)S(1)}) custom-call(f32[2,128,128]{2,1,0:T(8,128)S(1)} %copy-done.4, f32[2,128,128]{2,1,0:T(8,128)S(1)} %pad_maximum_fusion.kern_ref, bf16[2,16,128]{2,1,0:T(8,128)(2,1)S(1)} %get-tuple-element.19.code_ref, ...), custom_call_target="tpu_custom_call" | custom-call | tf_op jit(solution)/shard_map/run_backward/pallas_call | solution.py:239
  25.0 2.5 %collective-permute-start.7 = (bf16[2,272,128]{2,1,0:T(8,128)(2,1)S(1)}, bf16[2,272,128]{2,1,0:T(8,128)(2,1)S(1)}, u32[]{:S(2)}, u32[]{:S(2)}) collective-permute-start(bf16[2,272,128]{2,1,0:T(8,128)(2,1)S(1)} %get-tuple-element.26), channel_id=1, source_target_pairs={{0,18},{1,19},{2,16},{3,17},{4,22},{5,23},{6,20},{7,21},{8,26},{9,... | collective-permute-start | bytes 417800 | tf_op jit(solution)/shard_map/ppermute | solution.py:309
  27.5 0.6 %collective-permute-start.5 = (bf16[2,272,128]{2,1,0:T(8,128)(2,1)S(1)}, bf16[2,272,128]{2,1,0:T(8,128)(2,1)S(1)}, u32[]{:S(2)}, u32[]{:S(2)}) collective-permute-start(bf16[2,272,128]{2,1,0:T(8,128)(2,1)S(1)} %get-tuple-element.26), channel_id=1, source_target_pairs={{0,16},{1,17},{2,18},{3,19},{4,20},{5,21},{6,22},{7,23},{8,24},{9,... | collective-permute-start | bytes 417800 | tf_op jit(solution)/shard_map/ppermute | solution.py:309
  28.1 0.4 %collective-permute-start.6 = (bf16[2,272,128]{2,1,0:T(8,128)(2,1)S(1)}, bf16[2,272,128]{2,1,0:T(8,128)(2,1)S(1)}, u32[]{:S(2)}, u32[]{:S(2)}) collective-permute-start(bf16[2,272,128]{2,1,0:T(8,128)(2,1)S(1)} %get-tuple-element.25.refs_0_), channel_id=1, source_target_pairs={{0,2},{1,3},{2,0},{3,1},{4,6},{5,7},{6,4},{7,5},{8,10},{9,11},{10,... | collective-permute-start | bytes 417800 | tf_op jit(solution)/shard_map/ppermute | solution.py:309
  28.5 3.2 %collective-permute-done.7.refs_3_ = bf16[2,272,128]{2,1,0:T(8,128)(2,1)S(1)} collective-permute-done((bf16[2,272,128]{2,1,0:T(8,128)(2,1)S(1)}, bf16[2,272,128]{2,1,0:T(8,128)(2,1)S(1)}, u32[]{:S(2)}, u32[]{:S(2)}) %collective-permute-start.7) | collective-permute-done | bytes 139296 | tf_op jit(solution)/shard_map/ppermute | solution.py:309
  31.7 2.6 %collective-permute-done.5.refs_1_ = bf16[2,272,128]{2,1,0:T(8,128)(2,1)S(1)} collective-permute-done((bf16[2,272,128]{2,1,0:T(8,128)(2,1)S(1)}, bf16[2,272,128]{2,1,0:T(8,128)(2,1)S(1)}, u32[]{:S(2)}, u32[]{:S(2)}) %collective-permute-start.5) | collective-permute-done | bytes 139296 | tf_op jit(solution)/shard_map/ppermute | solution.py:309
  34.4 0.0 collective-permute-start.9
  34.4 0.1 collective-permute-done.6.refs_2_
  34.5 0.4 %collective-permute-start.10 = (bf16[2,272,128]{2,1,0:T(8,128)(2,1)S(1)}, bf16[2,272,128]{2,1,0:T(8,128)(2,1)S(1)}, u32[]{:S(2)}, u32[]{:S(2)}) collective-permute-start(bf16[2,272,128]{2,1,0:T(8,128)(2,1)S(1)} %collective-permute-done.6.refs_2_), channel_id=1, source_target_pairs={{0,1},{1,0},{2,3},{3,2},{4,5},{5,4},{6,7},{7,6},{8,9},{9,8},{10,11... | collective-permute-start | bytes 417800 | tf_op jit(solution)/shard_map/ppermute | solution.py:309
  34.9 0.8 %collective-permute-done.9.refs_5_ = bf16[2,272,128]{2,1,0:T(8,128)(2,1)S(1)} collective-permute-done((bf16[2,272,128]{2,1,0:T(8,128)(2,1)S(1)}, bf16[2,272,128]{2,1,0:T(8,128)(2,1)S(1)}, u32[]{:S(2)}, u32[]{:S(2)}) %collective-permute-start.9) | collective-permute-done | bytes 139296 | tf_op jit(solution)/shard_map/ppermute | solution.py:309
  35.7 0.2 collective-permute-done.10.refs_6_
  35.9 1.3 %place_windows.1 = f32[2,96,768]{2,1,0:T(8,128)} custom-call(bf16[2,272,128]{2,1,0:T(8,128)(2,1)S(1)} %get-tuple-element.25.refs_0_, bf16[2,272,128]{2,1,0:T(8,128)(2,1)S(1)} %collective-permute-done.5.refs_1_, bf16[2,272,128]{2,1,0:T(8,128)(2,1)S(1)} %collective-permute-done.6.refs_2_, bf16[2,272,128]{2,1,0:T(8,128)(2,1)S(1)} %collective-permute-done.7.refs_3_, ...), custom_call_target="tpu_custom_call" | custom-call | tf_op jit(solution)/shard_map/place_windows/pallas_call | solution.py:291
  (23 shorter events, 0.1 us)
Async XLA Ops:
  0.0 6.8 %collective-permute-start = (s32[2,2]{1,0:T(2,128)}, s32[2,2]{1,0:T(2,128)S(1)}, u32[]{:S(2)}, u32[]{:S(2)}) collective-permute-start(s32[2,2]{1,0:T(2,128)} %rest_0_.3), channel_id=1, source_target_pairs={{0,4},{1,5},{2,6},{3,7},{4,0},{5,1},{6,2},{7,3},{8,12},{9,13},{10,... | collective-permute-start | bytes 56 | tf_op jit(solution)/shard_map/ppermute | solution.py:309
  4.0 2.3 %copy-start = (f32[1,2,768,768]{3,2,1,0:T(8,128)S(1)}, f32[1,2,768,768]{3,2,1,0:T(8,128)}, u32[]{:S(2)}) copy-start(f32[1,2,768,768]{3,2,1,0:T(8,128)} %param.8) | copy-start | bytes 14155780
  6.4 0.7 %copy-start.6 = (s32[2,2]{1,0:T(2,128)S(1)}, s32[2,2]{1,0:T(2,128)}, u32[]{:S(2)}) copy-start(s32[2,2]{1,0:T(2,128)} %rest_0_.3) | copy-start | bytes 52
  6.7 4.8 %copy-start.7 = (f32[128,128]{1,0:T(8,128)S(1)}, f32[128,128]{1,0:T(8,128)}, u32[]{:S(2)}) copy-start(f32[128,128]{1,0:T(8,128)} %param.11) | copy-start | bytes 196612
  6.7 5.7 %copy-start.5 = (f32[2,128,128]{2,1,0:T(8,128)S(1)}, f32[2,128,128]{2,1,0:T(8,128)}, u32[]{:S(2)}) copy-start(f32[2,128,128]{2,1,0:T(8,128)} %rest_3_.1) | copy-start | bytes 393220
  6.7 10.6 %copy-start.1 = (bf16[2,768,256]{2,1,0:T(8,128)(2,1)S(1)}, bf16[2,768,256]{2,1,0:T(8,128)(2,1)}, u32[]{:S(2)}) copy-start(bf16[2,768,256]{2,1,0:T(8,128)(2,1)} %constant.8.clone.rest_2_) | copy-start | bytes 2359300
  6.7 10.6 %copy-start.2 = (bf16[2,256,256]{2,1,0:T(8,128)(2,1)S(1)}, bf16[2,256,256]{2,1,0:T(8,128)(2,1)}, u32[]{:S(2)}) copy-start(bf16[2,256,256]{2,1,0:T(8,128)(2,1)} %constant.7.clone.rest_1_) | copy-start | bytes 786436
  6.8 10.6 %copy-start.3 = (bf16[256,384]{1,0:T(8,128)(2,1)S(1)}, bf16[256,384]{1,0:T(8,128)(2,1)}, u32[]{:S(2)}) copy-start(bf16[256,384]{1,0:T(8,128)(2,1)} %constant.6.clone.rest_0_) | copy-start | bytes 589828
  6.8 10.6 %copy-start.4 = (f32[2,128,128]{2,1,0:T(8,128)S(1)}, f32[2,128,128]{2,1,0:T(8,128)}, u32[]{:S(2)}) copy-start(f32[2,128,128]{2,1,0:T(8,128)} %probe_ref.3) | copy-start | bytes 393220
  8.5 8.8 %collective-permute-start.3 = (bf16[2,2,128,128]{3,2,1,0:T(8,128)(2,1)S(1)}, bf16[2,2,128,128]{3,2,1,0:T(8,128)(2,1)S(1)}, u32[]{:S(2)}, u32[]{:S(2)}) collective-permute-start(bf16[2,2,128,128]{3,2,1,0:T(8,128)(2,1)S(1)} %get-tuple-element.21), channel_id=1, source_target_pairs={{0,24},{1,25},{2,26},{3,27},{4,28},{5,29},{6,30},{7,31},{8,16},{9,... | collective-permute-start | bytes 393224 | tf_op jit(solution)/shard_map/ppermute | solution.py:309
  11.0 6.3 %collective-permute-start.2 = (bf16[2,2,128,128]{3,2,1,0:T(8,128)(2,1)S(1)}, bf16[2,2,128,128]{3,2,1,0:T(8,128)(2,1)S(1)}, u32[]{:S(2)}, u32[]{:S(2)}) collective-permute-start(bf16[2,2,128,128]{3,2,1,0:T(8,128)(2,1)S(1)} %get-tuple-element.21), channel_id=1, source_target_pairs={{0,16},{1,17},{2,18},{3,19},{4,20},{5,21},{6,22},{7,23},{8,24},{9,... | collective-permute-start | bytes 393224 | tf_op jit(solution)/shard_map/ppermute | solution.py:309
  11.8 5.5 %collective-permute-start.1 = (bf16[2,2,128,128]{3,2,1,0:T(8,128)(2,1)S(1)}, bf16[2,2,128,128]{3,2,1,0:T(8,128)(2,1)S(1)}, u32[]{:S(2)}, u32[]{:S(2)}) collective-permute-start(bf16[2,2,128,128]{3,2,1,0:T(8,128)(2,1)S(1)} %get-tuple-element.20.rest_3_), channel_id=1, source_target_pairs={{0,8},{1,9},{2,10},{3,11},{4,12},{5,13},{6,14},{7,15},{8,0},{9,1},... | collective-permute-start | bytes 393224 | tf_op jit(solution)/shard_map/ppermute | solution.py:309
  12.4 9.7 %collective-permute-start.4 = (f32[2,128,128]{2,1,0:T(8,128)S(1)}, f32[2,128,128]{2,1,0:T(8,128)S(1)}, u32[]{:S(2)}, u32[]{:S(2)}) collective-permute-start(f32[2,128,128]{2,1,0:T(8,128)S(1)} %copy-done.5), channel_id=1, source_target_pairs={{0,4},{1,5},{2,6},{3,7},{4,0},{5,1},{6,2},{7,3},{8,12},{9,13},{10,... | collective-permute-start | bytes 393224 | tf_op jit(solution)/shard_map/ppermute | solution.py:309
  25.0 6.7 %collective-permute-start.7 = (bf16[2,272,128]{2,1,0:T(8,128)(2,1)S(1)}, bf16[2,272,128]{2,1,0:T(8,128)(2,1)S(1)}, u32[]{:S(2)}, u32[]{:S(2)}) collective-permute-start(bf16[2,272,128]{2,1,0:T(8,128)(2,1)S(1)} %get-tuple-element.26), channel_id=1, source_target_pairs={{0,18},{1,19},{2,16},{3,17},{4,22},{5,23},{6,20},{7,21},{8,26},{9,... | collective-permute-start | bytes 417800 | tf_op jit(solution)/shard_map/ppermute | solution.py:309
  27.5 6.9 %collective-permute-start.5 = (bf16[2,272,128]{2,1,0:T(8,128)(2,1)S(1)}, bf16[2,272,128]{2,1,0:T(8,128)(2,1)S(1)}, u32[]{:S(2)}, u32[]{:S(2)}) collective-permute-start(bf16[2,272,128]{2,1,0:T(8,128)(2,1)S(1)} %get-tuple-element.26), channel_id=1, source_target_pairs={{0,16},{1,17},{2,18},{3,19},{4,20},{5,21},{6,22},{7,23},{8,24},{9,... | collective-permute-start | bytes 417800 | tf_op jit(solution)/shard_map/ppermute | solution.py:309
  28.1 6.4 %collective-permute-start.6 = (bf16[2,272,128]{2,1,0:T(8,128)(2,1)S(1)}, bf16[2,272,128]{2,1,0:T(8,128)(2,1)S(1)}, u32[]{:S(2)}, u32[]{:S(2)}) collective-permute-start(bf16[2,272,128]{2,1,0:T(8,128)(2,1)S(1)} %get-tuple-element.25.refs_0_), channel_id=1, source_target_pairs={{0,2},{1,3},{2,0},{3,1},{4,6},{5,7},{6,4},{7,5},{8,10},{9,11},{10,... | collective-permute-start | bytes 417800 | tf_op jit(solution)/shard_map/ppermute | solution.py:309
  28.5 6.4 %collective-permute-start.8 = (bf16[2,272,128]{2,1,0:T(8,128)(2,1)S(1)}, bf16[2,272,128]{2,1,0:T(8,128)(2,1)S(1)}, u32[]{:S(2)}, u32[]{:S(2)}) collective-permute-start(bf16[2,272,128]{2,1,0:T(8,128)(2,1)S(1)} %get-tuple-element.25.refs_0_), channel_id=1, source_target_pairs={{0,1},{1,0},{2,3},{3,2},{4,5},{5,4},{6,7},{7,6},{8,9},{9,8},{10,11... | collective-permute-start | bytes 417800 | tf_op jit(solution)/shard_map/ppermute | solution.py:309
  31.7 3.2 %collective-permute-start.11 = (bf16[2,272,128]{2,1,0:T(8,128)(2,1)S(1)}, bf16[2,272,128]{2,1,0:T(8,128)(2,1)S(1)}, u32[]{:S(2)}, u32[]{:S(2)}) collective-permute-start(bf16[2,272,128]{2,1,0:T(8,128)(2,1)S(1)} %collective-permute-done.7.refs_3_), channel_id=1, source_target_pairs={{0,1},{1,0},{2,3},{3,2},{4,5},{5,4},{6,7},{7,6},{8,9},{9,8},{10,11... | collective-permute-start | bytes 417800 | tf_op jit(solution)/shard_map/ppermute | solution.py:309
  34.4 1.4 %collective-permute-start.9 = (bf16[2,272,128]{2,1,0:T(8,128)(2,1)S(1)}, bf16[2,272,128]{2,1,0:T(8,128)(2,1)S(1)}, u32[]{:S(2)}, u32[]{:S(2)}) collective-permute-start(bf16[2,272,128]{2,1,0:T(8,128)(2,1)S(1)} %collective-permute-done.5.refs_1_), channel_id=1, source_target_pairs={{0,1},{1,0},{2,3},{3,2},{4,5},{5,4},{6,7},{7,6},{8,9},{9,8},{10,11... | collective-permute-start | bytes 417800 | tf_op jit(solution)/shard_map/ppermute | solution.py:309
  34.5 1.4 %collective-permute-start.10 = (bf16[2,272,128]{2,1,0:T(8,128)(2,1)S(1)}, bf16[2,272,128]{2,1,0:T(8,128)(2,1)S(1)}, u32[]{:S(2)}, u32[]{:S(2)}) collective-permute-start(bf16[2,272,128]{2,1,0:T(8,128)(2,1)S(1)} %collective-permute-done.6.refs_2_), channel_id=1, source_target_pairs={{0,1},{1,0},{2,3},{3,2},{4,5},{5,4},{6,7},{7,6},{8,9},{9,8},{10,11... | collective-permute-start | bytes 417800 | tf_op jit(solution)/shard_map/ppermute | solution.py:309

commit v10 on v9

--- a/solution.py
+++ b/solution.py
@@ -28,99 +28,105 @@
         parts.append((high, low))
     (ph, plo), (mh, mlo) = parts
     right = np.stack([np.concatenate([ph, ph, plo], 0), np.concatenate([mh, mh, mlo], 0)])
-    left = np.stack([mh, ph])
-    thin = np.concatenate([minus[:, :size] for minus in (mh, mh, mlo)], 1)
-    return jnp.asarray(thin), jnp.asarray(left), jnp.asarray(right)
+    left = np.stack([np.concatenate([mh, mh, mlo], 1), np.concatenate([ph, ph, plo], 1)])
+    return jnp.asarray(left), jnp.asarray(right)
 
 
 code_rows = 16
 
-
-def fetch_kernel(obj_ref, out_ref, sem):
-    copy = pltpu.make_async_copy(obj_ref, out_ref, sem)
-    copy.start()
-    copy.wait()
-
-
-def fetch(obj):
-    size = 4 * math.prod(obj.shape)
+small = pltpu.CompilerParams(vmem_limit_bytes=16 * 1024 * 1024)
+limit = pltpu.CompilerParams(vmem_limit_bytes=32 * 1024 * 1024)
+vmem = pl.BlockSpec(memory_space=pltpu.VMEM)
+smem = pl.BlockSpec(memory_space=pltpu.SMEM)
+
+
+def cut(obj_ref, row, col, out_ref, window):
+    rows, cols = obj_ref.shape[-2:]
+    tall, wide = window + 8, window + 128
+    row_base = pl.multiple_of(jnp.minimum(row >> 3, (rows - tall) // 8) * 8, 8)
+    col_base = pl.multiple_of(jnp.minimum(col >> 7, (cols - wide) // 128) * 128, 128)
+    lift = jnp.where(row == row_base, 0, tall - (row - row_base))
+    shift = jnp.where(col == col_base, 0, wide - (col - col_base))
+    for part in range(2):
+        block = obj_ref[part, pl.ds(row_base, tall), pl.ds(col_base, wide)]
+        block = pltpu.roll(block, shift, 1)[:, :window]
+        block = pltpu.roll(block, lift, 0)[:window]
+        out_ref[part] = block.astype(bf16)
+
+
+def near_kernel(pos_ref, obj_ref, out_ref):
+    for p in range(out_ref.shape[0]):
+        cut(obj_ref, pos_ref[p, 0], pos_ref[p, 1], out_ref.at[p], out_ref.shape[-1])
+
+
+def near_windows(obj, positions, window):
     return pl.pallas_call(
-        fetch_kernel,
-        out_shape=jax.ShapeDtypeStruct(obj.shape, obj.dtype),
-        in_specs=[pl.BlockSpec(memory_space=pltpu.HBM)],
-        out_specs=pl.BlockSpec(memory_space=pltpu.VMEM),
-        scratch_shapes=[pltpu.SemaphoreType.DMA],
-        compiler_params=pltpu.CompilerParams(vmem_limit_bytes=16 * 1024 * 1024),
-        cost_estimate=pl.CostEstimate(flops=0, bytes_accessed=2 * size, transcendentals=0),
-        name="fetch_slice",
-    )(obj)
-
-
-def window_kernel(members, obj_ref, *rest):
+        near_kernel,
+        out_shape=jax.ShapeDtypeStruct((positions.shape[0], 2, window, window), bf16),
+        in_specs=[smem, vmem],
+        out_specs=vmem,
+        compiler_params=small,
+        cost_estimate=pl.CostEstimate(flops=0, bytes_accessed=4 * math.prod(obj.shape), transcendentals=0),
+        name="near_windows",
+    )(positions, obj)
+
+
+def far_kernel(members, obj_ref, near_ref, *rest):
     table, table_sems = rest[-2:]
     clusters, count = table.shape[:2]
     pos_refs, out_refs, code_ref = rest[:clusters], rest[clusters:-3], rest[-3]
-    window = out_refs[0].shape[-1]
-    rows, cols = obj_ref.shape[-2:]
-    tall, wide = window + 8, window + 128
+    window = near_ref.shape[-1]
     cluster = lax.div(lax.axis_index("dp"), members)
     home = lax.div(lax.axis_index("depth"), 2)
 
-    fetches = [
+    arrivals = [
         pltpu.make_async_copy(pos_refs[m], table.at[m], table_sems.at[m])
         for m in range(1, clusters)
     ]
-    for fetch in fetches:
-        fetch.start()
+    for arrival in arrivals:
+        arrival.start()
     for p in range(count):
         for axis in range(2):
             table[0, p, axis] = pos_refs[0][p, axis]
-    for fetch in fetches:
-        fetch.wait()
-
-    def corner(m, p):
-        at = home ^ cluster ^ m
-        row, col = table[at, p, 0], table[at, p, 1]
-        row_base = pl.multiple_of(jnp.minimum(row >> 3, (rows - tall) // 8) * 8, 8)
-        col_base = pl.multiple_of(jnp.minimum(col >> 7, (cols - wide) // 128) * 128, 128)
-        return row_base, col_base, row - row_base, col - col_base
-
+    for m in range(clusters):
+
+        @pl.when(home ^ cluster == m)
+        def _():
+            out_refs[m][...] = near_ref[...]
+
+    for arrival in arrivals:
+        arrival.wait()
     line = lax.broadcasted_iota(jnp.int32, (code_rows, window), 0)
     for p in range(count):
         row, col = table[home ^ cluster, p, 0], table[home ^ cluster, p, 1]
         code = jnp.where(line == 0, row >> 3, jnp.where(line == 1, row & 7, 0))
         code = jnp.where(line == 2, col >> 3, jnp.where(line == 3, col & 7, code))
         code_ref[p] = code.astype(f32).astype(bf16)
-    for m in reversed(range(clusters)):
-        for p in range(count):
-            row_base, col_base, row_off, col_off = corner(m, p)
-            lift = jnp.where(row_off == 0, 0, tall - row_off)
-            shift = jnp.where(col_off == 0, 0, wide - col_off)
-            for part in range(2):
-                block = obj_ref[part, pl.ds(row_base, tall), pl.ds(col_base, wide)]
-                block = pltpu.roll(block, shift, 1)[:, :window]
-                block = pltpu.roll(block, lift, 0)[:window]
-                out_refs[m][p, part] = block.astype(bf16)
+    for m in range(clusters):
+        at = home ^ cluster ^ m
+
+        @pl.when(at > 0)
+        def _():
+            for p in range(count):
+                cut(obj_ref, table[at, p, 0], table[at, p, 1], out_refs[m].at[p], window)
 
 
 def take_windows(obj, positions, window, members):
     clusters, count = len(positions), positions[0].shape[0]
-    any_space = pl.BlockSpec(memory_space=pl.ANY)
-    smem = pl.BlockSpec(memory_space=pltpu.SMEM)
-    vmem = pl.BlockSpec(memory_space=pltpu.VMEM)
+    near = near_windows(obj, positions[0], window)
     out = pl.pallas_call(
-        functools.partial(window_kernel, members),
-        out_shape=[jax.ShapeDtypeStruct((count, 2, window, window), bf16)] * clusters
+        functools.partial(far_kernel, members),
+        out_shape=[jax.ShapeDtypeStruct(near.shape, bf16)] * clusters
         + [jax.ShapeDtypeStruct((count, code_rows, window), bf16)],
-        in_specs=[vmem, smem] + [any_space] * (clusters - 1),
+        in_specs=[vmem, vmem, smem] + [pl.BlockSpec(memory_space=pl.ANY)] * (clusters - 1),
         out_specs=[vmem] * (clusters + 1),
         scratch_shapes=[
             pltpu.SMEM((clusters, count, 2), jnp.int32),
             pltpu.SemaphoreType.DMA((clusters,)),
         ],
-        compiler_params=pltpu.CompilerParams(vmem_limit_bytes=16 * 1024 * 1024),
-        name="take_windows",
-    )(obj, *positions)
+        compiler_params=small,
+        name="far_windows",
+    )(obj, near, *positions)
     return out[:clusters], out[clusters]
 
 
@@ -137,29 +143,28 @@
     return a[0] * b[0] + a[1] * b[1], a[0] * b[1] - a[1] * b[0]
 
 
-def transform(field, sign, tables, exact):
-    thin_ref, left_ref, right_ref = tables
-    re, im = field
-    size = re.shape[0]
-    if exact:
-        high, low = split(jnp.concatenate([re, im], axis=1))
-        x = jnp.concatenate([high, low, high], axis=0)
-        y = jnp.dot(thin_ref[...], x, preferred_element_type=f32)
-        cr, ci, sr, si = y[:size, :size], y[:size, size:], y[size:, :size], y[size:, size:]
-        re, im = (cr - si, ci + sr) if sign == 0 else (cr + si, ci - sr)
-        high, low = split(jnp.concatenate([re, im], axis=1))
-        x = jnp.concatenate([high, low, high], axis=1)
-        y = jnp.dot(x, right_ref[sign], preferred_element_type=f32)
-    else:
-        x = jnp.concatenate([re, im], axis=0).astype(bf16)
-        y = jnp.dot(left_ref[sign], x, preferred_element_type=f32)
-        x = jnp.concatenate([y[:size], y[size:]], axis=1).astype(bf16)
-        y = jnp.dot(x, right_ref[sign, : 2 * size], preferred_element_type=f32)
-    return y[:, :size], y[:, size:]
+def transform(fields, sign, tables, exact):
+    left_ref, right_ref = tables
+    size = fields[0][0].shape[0]
+
+    def passes(x, axis):
+        if not exact:
+            return x.astype(bf16)
+        high, low = split(x)
+        return jnp.concatenate([high, low, high], axis=axis)
+
+    x = passes(jnp.concatenate([jnp.concatenate(f, axis=0) for f in fields], axis=1), 0)
+    y = jnp.dot(left_ref[sign, :, : x.shape[0]], x, preferred_element_type=f32)
+    fields = [y[:, n * size : (n + 1) * size] for n in range(len(fields))]
+    fields = [jnp.concatenate([f[:size], f[size:]], axis=1) for f in fields]
+    x = passes(jnp.concatenate(fields, axis=0), 1)
+    y = jnp.dot(x, right_ref[sign, : x.shape[1]], preferred_element_type=f32)
+    fields = [y[n * size : (n + 1) * size] for n in range(len(fields))]
+    return [(f[:, :size], f[:, size:]) for f in fields]
 
 
 def forward_kernel(probe_ref, kern_ref, *rest):
-    tables, t_refs, (trans, waves) = rest[:3], rest[3:-2], rest[-2:]
+    tables, t_refs, (trans, waves) = rest[:2], rest[2:-2], rest[-2:]
     slices, count = trans.shape[:2]
     own = lax.axis_index("depth")
     everyone = range(count)
@@ -169,16 +174,17 @@
     psi = [(probe_ref[0], probe_ref[1])] * count
     for k in range(slices):
         field = [cmul((trans[k, p, 0].astype(f32), trans[k, p, 1].astype(f32)), psi[p]) for p in everyone]
-        psi = [transform(f, 1, tables, True) for f in field]
+        psi = transform(field, 1, tables, True)
         if k < slices - 1:
-            psi = [transform(cmul(kern, s), 0, tables, True) for s in psi]
+            psi = transform([cmul(kern, s) for s in psi], 0, tables, True)
         for p in everyone:
             waves[k, p, 0] = psi[p][0]
             waves[k, p, 1] = psi[p][1]
 
 
 def backward_kernel(members, clusters, probe_ref, kern_ref, code_ref, trans, waves, *rest):
-    tables, meas_refs, out_refs, (terms, meas) = rest[:3], rest[3 : 3 + clusters], rest[3 + clusters : -2], rest[-2:]
+    tables, meas_refs = rest[:2], rest[2 : 2 + clusters]
+    out_refs, (terms, meas) = rest[2 + clusters : -2], rest[-2:]
     slices, count, _, window, _ = trans.shape
     own, cluster = lax.axis_index("depth"), lax.div(lax.axis_index("dp"), members)
     everyone = range(count)
@@ -195,7 +201,7 @@
         scale = 2.0 * (re * re + im * im - meas[p])
         return scale * re, scale * im
 
-    returned = [transform(source(p), 0, tables, False) for p in everyone]
+    returned = transform([source(p) for p in everyone], 0, tables, False)
     for k in reversed(range(slices)):
         for p in everyone:
             wave = (waves[k - 1, p, 0], waves[k - 1, p, 1]) if k else (probe_ref[0], probe_ref[1])
@@ -207,15 +213,11 @@
                 cmul_conj((trans[k, p, 0].astype(f32), trans[k, p, 1].astype(f32)), returned[p])
                 for p in everyone
             ]
-            chi = [transform(c, 1, tables, False) for c in chi]
-            returned = [transform(cmul_conj(kern, c), 0, tables, False) for c in chi]
+            chi = transform(chi, 1, tables, False)
+            returned = transform([cmul_conj(kern, c) for c in chi], 0, tables, False)
     for n, out_ref in enumerate(out_refs):
         out_ref[:, : 2 * window] = terms[2 * n]
         out_ref[:, 2 * window :] = code_ref[...]
-
-
-limit = pltpu.CompilerParams(vmem_limit_bytes=32 * 1024 * 1024)
-vmem = pl.BlockSpec(memory_space=pltpu.VMEM)
 
 
 def run_forward(probe, kern, tables, windows):
@@ -226,7 +228,7 @@
             jax.ShapeDtypeStruct((slices,) + shape, bf16),
             jax.ShapeDtypeStruct((slices,) + shape, f32),
         ],
-        in_specs=[vmem] * (5 + slices),
+        in_specs=[vmem] * (4 + slices),
         out_specs=[vmem, vmem],
         compiler_params=limit,
         name="run_forward",
@@ -239,7 +241,7 @@
     return pl.pallas_call(
         functools.partial(backward_kernel, members, len(measured)),
         out_shape=[block] * (slices // 2),
-        in_specs=[vmem] * (8 + len(measured)),
+        in_specs=[vmem] * (7 + len(measured)),
         out_specs=[vmem] * (slices // 2),
         scratch_shapes=[
             pltpu.VMEM((slices, count, 2 * window, window), bf16),
@@ -318,7 +320,7 @@
 
     homes = [m * members for m in range(1, clusters)]
     all_positions = [positions] + [swap(positions, 0, home) for home in homes]
-    windows, code = take_windows(fetch(object_slices[0]), all_positions, window, members)
+    windows, code = take_windows(object_slices[0], all_positions, window, members)
     phase, code = lax.optimization_barrier((propagator_phase, code))
     windows = [windows[0]] + [swap(windows[m // 2], m, 0) for m in range(1, depth)]
     kern = jnp.stack([jnp.cos(phase), jnp.sin(phase)])

time: 37.6 us -> 37.7 us (level)
  starting transfers between devices: 13.4 us -> 12.1 us
  waiting for transfers between devices: 10.2 us -> 11.2 us
  local copies, waits for them, and re-layouts: 2.88 us -> 3.27 us
    ppermute x12, starting transfers between devices: 13.4 us -> 12.1 us  [swap(): return lax.ppermute(block, ('depth', 'dp'), route)]
    ppermute x12, waiting for transfers between devices: 10.2 us -> 11.2 us  [swap(): return lax.ppermute(block, ('depth', 'dp'), route)]
    unnamed x16 -> x14, local copies, waits for them, and re-layouts: 2.64 us -> 3.03 us
  transfers between devices with their start and end apart: 12 -> 12, of which waited for: 6 -> 5; matrix products, arithmetic and copies ran while one was open for 1% -> 1% of each run, Pallas kernels for 14% -> 14%
where the time goes in v10:
time: 37.7 us; the launch traced here: 37.3 us
  starting transfers between devices  12.1 us (32%)
  waiting for transfers between devices  11.2 us (30%)
  Pallas kernels  10.6 us (28%)
  local copies, waits for them, and re-layouts  3.27 us (9%)
    ppermute x12, starting transfers between devices, swap(): return lax.ppermute(block, ('depth', 'dp'), route)  12.1 us
    ppermute x12, waiting for transfers between devices, swap(): return lax.ppermute(block, ('depth', 'dp'), route)  11.2 us
    pallas_call x1, Pallas kernels, run_forward(): pl.pallas_call(forward_kernel, out_shape=[jax.ShapeDtypeStruct((slices,)...  4.48 us
    unnamed x14, local copies, waits for them, and re-layouts  3.03 us
    pallas_call x1, Pallas kernels, run_backward(): pl.pallas_call(functools.partial(backward_kernel, members, len(measured))...  2.66 us
    pallas_call x1, Pallas kernels, place_windows(): pl.pallas_call(place_kernel, out_shape=jax.ShapeDtypeStruct((2, stripe, c...  1.35 us
    pallas_call x1, Pallas kernels, take_windows(): pl.pallas_call(functools.partial(far_kernel, members), out_shape=[jax.Sha...  1.33 us
  transfers between devices with their start and end apart: 12, of which 5 were waited for; matrix products, arithmetic and copies ran while one was open for 1% of the time, Pallas kernels for 14%

profile of v10, /device:TPU:0, one launch (start us, length us, event | category | flops | bytes accessed | tf_op | source)
XLA Modules:
  0.0 37.3 jit_solution(3882222185239636373)
XLA Ops:
  0.0 4.0 %collective-permute-start = (s32[2,2]{1,0:T(2,128)}, s32[2,2]{1,0:T(2,128)S(1)}, u32[]{:S(2)}, u32[]{:S(2)}) collective-permute-start(s32[2,2]{1,0:T(2,128)} %rest_0_.3), channel_id=1, source_target_pairs={{0,4},{1,5},{2,6},{3,7},{4,0},{5,1},{6,2},{7,3},{8,12},{9,13},{10,... | collective-permute-start | bytes 56 | tf_op jit(solution)/shard_map/ppermute | solution.py:311
  4.0 2.3 %copy-done = f32[1,2,768,768]{3,2,1,0:T(8,128)S(1)} copy-done((f32[1,2,768,768]{3,2,1,0:T(8,128)S(1)}, f32[1,2,768,768]{3,2,1,0:T(8,128)}, u32[]{:S(2)}) %copy-start) | copy-done | bytes 4718616
  6.4 0.7 %copy-done.5 = s32[2,2]{1,0:T(2,128)S(1)} copy-done((s32[2,2]{1,0:T(2,128)S(1)}, s32[2,2]{1,0:T(2,128)}, u32[]{:S(2)}) %copy-start.5) | copy-done | bytes 40
  7.1 0.7 %near_windows.1.near_ref = bf16[2,2,128,128]{3,2,1,0:T(8,128)(2,1)S(1)} custom-call(s32[2,2]{1,0:T(2,128)S(1)} %copy-done.5, f32[2,768,768]{2,1,0:T(8,128)S(1)} %bitcast.6), custom_call_target="tpu_custom_call" | custom-call | bytes 4718592 | tf_op jit(solution)/shard_map/near_windows/pallas_call | solution.py:63
  7.8 1.3 %far_windows.1 = (bf16[2,2,128,128]{3,2,1,0:T(8,128)(2,1)S(1)}, bf16[2,2,128,128]{3,2,1,0:T(8,128)(2,1)S(1)}, bf16[2,16,128]{2,1,0:T(8,128)(2,1)S(1)}) custom-call(f32[2,768,768]{2,1,0:T(8,128)S(1)} %bitcast.7, bf16[2,2,128,128]{3,2,1,0:T(8,128)(2,1)S(1)} %near_windows.1.near_ref, s32[2,2]{1,0:T(2,128)S(1)} %copy-done.5, s32[2,2]{1,0:T(2,128)S(1)} %collective-permute-done.rest_1_), custom_call_target="tpu_custom_call" | custom-call | tf_op jit(solution)/shard_map/far_windows/pallas_call | solution.py:117
  9.2 1.6 %collective-permute-start.2 = (bf16[2,2,128,128]{3,2,1,0:T(8,128)(2,1)S(1)}, bf16[2,2,128,128]{3,2,1,0:T(8,128)(2,1)S(1)}, u32[]{:S(2)}, u32[]{:S(2)}) collective-permute-start(bf16[2,2,128,128]{3,2,1,0:T(8,128)(2,1)S(1)} %get-tuple-element.21), channel_id=1, source_target_pairs={{0,16},{1,17},{2,18},{3,19},{4,20},{5,21},{6,22},{7,23},{8,24},{9,... | collective-permute-start | bytes 393224 | tf_op jit(solution)/shard_map/ppermute | solution.py:311
  10.8 1.4 %collective-permute-start.3 = (bf16[2,2,128,128]{3,2,1,0:T(8,128)(2,1)S(1)}, bf16[2,2,128,128]{3,2,1,0:T(8,128)(2,1)S(1)}, u32[]{:S(2)}, u32[]{:S(2)}) collective-permute-start(bf16[2,2,128,128]{3,2,1,0:T(8,128)(2,1)S(1)} %get-tuple-element.21), channel_id=1, source_target_pairs={{0,24},{1,25},{2,26},{3,27},{4,28},{5,29},{6,30},{7,31},{8,16},{9,... | collective-permute-start | bytes 393224 | tf_op jit(solution)/shard_map/ppermute | solution.py:311
  12.2 0.2 cosine_bitcast_fusion
  12.4 0.6 %collective-permute-start.1 = (bf16[2,2,128,128]{3,2,1,0:T(8,128)(2,1)S(1)}, bf16[2,2,128,128]{3,2,1,0:T(8,128)(2,1)S(1)}, u32[]{:S(2)}, u32[]{:S(2)}) collective-permute-start(bf16[2,2,128,128]{3,2,1,0:T(8,128)(2,1)S(1)} %get-tuple-element.20.rest_2_), channel_id=1, source_target_pairs={{0,8},{1,9},{2,10},{3,11},{4,12},{5,13},{6,14},{7,15},{8,0},{9,1},... | collective-permute-start | bytes 393224 | tf_op jit(solution)/shard_map/ppermute | solution.py:311
  13.1 0.9 %collective-permute-start.4 = (f32[2,128,128]{2,1,0:T(8,128)S(1)}, f32[2,128,128]{2,1,0:T(8,128)S(1)}, u32[]{:S(2)}, u32[]{:S(2)}) collective-permute-start(f32[2,128,128]{2,1,0:T(8,128)S(1)} %copy-done.4), channel_id=1, source_target_pairs={{0,4},{1,5},{2,6},{3,7},{4,0},{5,1},{6,2},{7,3},{8,12},{9,13},{10,... | collective-permute-start | bytes 393224 | tf_op jit(solution)/shard_map/ppermute | solution.py:311
  14.0 4.3 %collective-permute-done.1.rest_3_ = bf16[2,2,128,128]{3,2,1,0:T(8,128)(2,1)S(1)} collective-permute-done((bf16[2,2,128,128]{3,2,1,0:T(8,128)(2,1)S(1)}, bf16[2,2,128,128]{3,2,1,0:T(8,128)(2,1)S(1)}, u32[]{:S(2)}, u32[]{:S(2)}) %collective-permute-start.1) | collective-permute-done | bytes 131104 | tf_op jit(solution)/shard_map/ppermute | solution.py:311
  18.3 4.5 %run_forward.1 = (bf16[4,2,2,128,128]{4,3,2,1,0:T(8,128)(2,1)S(1)}, f32[4,2,2,128,128]{4,3,2,1,0:T(8,128)S(1)}) custom-call(f32[2,128,128]{2,1,0:T(8,128)S(1)} %copy-done.3, f32[2,128,128]{2,1,0:T(8,128)S(1)} %pad_maximum_fusion.kern_ref, bf16[2,256,768]{2,1,0:T(8,128)(2,1)S(1)} %copy-done.1, bf16[2,768,256]{2,1,0:T(8,128)(2,1)S(1)} %copy-done.2, ...), custom_call_target="tpu_custom_call" | custom-call | tf_op jit(solution)/shard_map/run_forward/pallas_call | solution.py:225
  22.8 0.0 collective-permute-done.4.rest_3_
  22.8 2.7 %run_backward.1 = (bf16[2,272,128]{2,1,0:T(8,128)(2,1)S(1)}, bf16[2,272,128]{2,1,0:T(8,128)(2,1)S(1)}) custom-call(f32[2,128,128]{2,1,0:T(8,128)S(1)} %copy-done.3, f32[2,128,128]{2,1,0:T(8,128)S(1)} %pad_maximum_fusion.kern_ref, bf16[2,16,128]{2,1,0:T(8,128)(2,1)S(1)} %get-tuple-element.19.code_ref, ...), custom_call_target="tpu_custom_call" | custom-call | tf_op jit(solution)/shard_map/run_backward/pallas_call | solution.py:241
  25.5 1.6 %collective-permute-start.5 = (bf16[2,272,128]{2,1,0:T(8,128)(2,1)S(1)}, bf16[2,272,128]{2,1,0:T(8,128)(2,1)S(1)}, u32[]{:S(2)}, u32[]{:S(2)}) collective-permute-start(bf16[2,272,128]{2,1,0:T(8,128)(2,1)S(1)} %get-tuple-element.26), channel_id=1, source_target_pairs={{0,16},{1,17},{2,18},{3,19},{4,20},{5,21},{6,22},{7,23},{8,24},{9,... | collective-permute-start | bytes 417800 | tf_op jit(solution)/shard_map/ppermute | solution.py:311
  27.1 1.6 %collective-permute-start.6 = (bf16[2,272,128]{2,1,0:T(8,128)(2,1)S(1)}, bf16[2,272,128]{2,1,0:T(8,128)(2,1)S(1)}, u32[]{:S(2)}, u32[]{:S(2)}) collective-permute-start(bf16[2,272,128]{2,1,0:T(8,128)(2,1)S(1)} %get-tuple-element.25.refs_0_), channel_id=1, source_target_pairs={{0,2},{1,3},{2,0},{3,1},{4,6},{5,7},{6,4},{7,5},{8,10},{9,11},{10,... | collective-permute-start | bytes 417800 | tf_op jit(solution)/shard_map/ppermute | solution.py:311
  28.7 0.4 %collective-permute-start.7 = (bf16[2,272,128]{2,1,0:T(8,128)(2,1)S(1)}, bf16[2,272,128]{2,1,0:T(8,128)(2,1)S(1)}, u32[]{:S(2)}, u32[]{:S(2)}) collective-permute-start(bf16[2,272,128]{2,1,0:T(8,128)(2,1)S(1)} %get-tuple-element.26), channel_id=1, source_target_pairs={{0,18},{1,19},{2,16},{3,17},{4,22},{5,23},{6,20},{7,21},{8,26},{9,... | collective-permute-start | bytes 417800 | tf_op jit(solution)/shard_map/ppermute | solution.py:311
  29.1 2.5 %collective-permute-done.5.refs_1_ = bf16[2,272,128]{2,1,0:T(8,128)(2,1)S(1)} collective-permute-done((bf16[2,272,128]{2,1,0:T(8,128)(2,1)S(1)}, bf16[2,272,128]{2,1,0:T(8,128)(2,1)S(1)}, u32[]{:S(2)}, u32[]{:S(2)}) %collective-permute-start.5) | collective-permute-done | bytes 139296 | tf_op jit(solution)/shard_map/ppermute | solution.py:311
  31.5 0.9 %collective-permute-done.6.refs_2_ = bf16[2,272,128]{2,1,0:T(8,128)(2,1)S(1)} collective-permute-done((bf16[2,272,128]{2,1,0:T(8,128)(2,1)S(1)}, bf16[2,272,128]{2,1,0:T(8,128)(2,1)S(1)}, u32[]{:S(2)}, u32[]{:S(2)}) %collective-permute-start.6) | collective-permute-done | bytes 139296 | tf_op jit(solution)/shard_map/ppermute | solution.py:311
  32.4 0.0 collective-permute-start.10
  32.5 2.2 %collective-permute-done.7.refs_3_ = bf16[2,272,128]{2,1,0:T(8,128)(2,1)S(1)} collective-permute-done((bf16[2,272,128]{2,1,0:T(8,128)(2,1)S(1)}, bf16[2,272,128]{2,1,0:T(8,128)(2,1)S(1)}, u32[]{:S(2)}, u32[]{:S(2)}) %collective-permute-start.7) | collective-permute-done | bytes 139296 | tf_op jit(solution)/shard_map/ppermute | solution.py:311
  34.6 0.0 collective-permute-done.9.refs_5_
  34.6 1.3 %collective-permute-done.11.refs_7_ = bf16[2,272,128]{2,1,0:T(8,128)(2,1)S(1)} collective-permute-done((bf16[2,272,128]{2,1,0:T(8,128)(2,1)S(1)}, bf16[2,272,128]{2,1,0:T(8,128)(2,1)S(1)}, u32[]{:S(2)}, u32[]{:S(2)}) %collective-permute-start.11) | collective-permute-done | bytes 139296 | tf_op jit(solution)/shard_map/ppermute | solution.py:311
  36.0 1.4 %place_windows.1 = f32[2,96,768]{2,1,0:T(8,128)} custom-call(bf16[2,272,128]{2,1,0:T(8,128)(2,1)S(1)} %get-tuple-element.25.refs_0_, bf16[2,272,128]{2,1,0:T(8,128)(2,1)S(1)} %collective-permute-done.5.refs_1_, bf16[2,272,128]{2,1,0:T(8,128)(2,1)S(1)} %collective-permute-done.6.refs_2_, bf16[2,272,128]{2,1,0:T(8,128)(2,1)S(1)} %collective-permute-done.7.refs_3_, ...), custom_call_target="tpu_custom_call" | custom-call | tf_op jit(solution)/shard_map/place_windows/pallas_call | solution.py:293
  (21 shorter events, 0.1 us)
Async XLA Ops:
  0.0 7.8 %collective-permute-start = (s32[2,2]{1,0:T(2,128)}, s32[2,2]{1,0:T(2,128)S(1)}, u32[]{:S(2)}, u32[]{:S(2)}) collective-permute-start(s32[2,2]{1,0:T(2,128)} %rest_0_.3), channel_id=1, source_target_pairs={{0,4},{1,5},{2,6},{3,7},{4,0},{5,1},{6,2},{7,3},{8,12},{9,13},{10,... | collective-permute-start | bytes 56 | tf_op jit(solution)/shard_map/ppermute | solution.py:311
  4.0 2.3 %copy-start = (f32[1,2,768,768]{3,2,1,0:T(8,128)S(1)}, f32[1,2,768,768]{3,2,1,0:T(8,128)}, u32[]{:S(2)}) copy-start(f32[1,2,768,768]{3,2,1,0:T(8,128)} %param.7) | copy-start | bytes 14155780
  6.4 0.7 %copy-start.5 = (s32[2,2]{1,0:T(2,128)S(1)}, s32[2,2]{1,0:T(2,128)}, u32[]{:S(2)}) copy-start(s32[2,2]{1,0:T(2,128)} %rest_0_.3) | copy-start | bytes 52
  7.1 5.1 %copy-start.6 = (f32[128,128]{1,0:T(8,128)S(1)}, f32[128,128]{1,0:T(8,128)}, u32[]{:S(2)}) copy-start(f32[128,128]{1,0:T(8,128)} %param.10) | copy-start | bytes 196612
  7.1 6.0 %copy-start.4 = (f32[2,128,128]{2,1,0:T(8,128)S(1)}, f32[2,128,128]{2,1,0:T(8,128)}, u32[]{:S(2)}) copy-start(f32[2,128,128]{2,1,0:T(8,128)} %rest_2_.1) | copy-start | bytes 393220
  7.1 11.3 %copy-start.1 = (bf16[2,256,768]{2,1,0:T(8,128)(2,1)S(1)}, bf16[2,256,768]{2,1,0:T(8,128)(2,1)}, u32[]{:S(2)}) copy-start(bf16[2,256,768]{2,1,0:T(8,128)(2,1)} %constant.4.clone.rest_0_) | copy-start | bytes 2359300
  7.1 11.3 %copy-start.2 = (bf16[2,768,256]{2,1,0:T(8,128)(2,1)S(1)}, bf16[2,768,256]{2,1,0:T(8,128)(2,1)}, u32[]{:S(2)}) copy-start(bf16[2,768,256]{2,1,0:T(8,128)(2,1)} %constant.5.clone.rest_1_) | copy-start | bytes 2359300
  7.1 11.3 %copy-start.3 = (f32[2,128,128]{2,1,0:T(8,128)S(1)}, f32[2,128,128]{2,1,0:T(8,128)}, u32[]{:S(2)}) copy-start(f32[2,128,128]{2,1,0:T(8,128)} %probe_ref.3) | copy-start | bytes 393220
  9.2 9.1 %collective-permute-start.2 = (bf16[2,2,128,128]{3,2,1,0:T(8,128)(2,1)S(1)}, bf16[2,2,128,128]{3,2,1,0:T(8,128)(2,1)S(1)}, u32[]{:S(2)}, u32[]{:S(2)}) collective-permute-start(bf16[2,2,128,128]{3,2,1,0:T(8,128)(2,1)S(1)} %get-tuple-element.21), channel_id=1, source_target_pairs={{0,16},{1,17},{2,18},{3,19},{4,20},{5,21},{6,22},{7,23},{8,24},{9,... | collective-permute-start | bytes 393224 | tf_op jit(solution)/shard_map/ppermute | solution.py:311
  10.8 7.6 %collective-permute-start.3 = (bf16[2,2,128,128]{3,2,1,0:T(8,128)(2,1)S(1)}, bf16[2,2,128,128]{3,2,1,0:T(8,128)(2,1)S(1)}, u32[]{:S(2)}, u32[]{:S(2)}) collective-permute-start(bf16[2,2,128,128]{3,2,1,0:T(8,128)(2,1)S(1)} %get-tuple-element.21), channel_id=1, source_target_pairs={{0,24},{1,25},{2,26},{3,27},{4,28},{5,29},{6,30},{7,31},{8,16},{9,... | collective-permute-start | bytes 393224 | tf_op jit(solution)/shard_map/ppermute | solution.py:311
  12.4 5.9 %collective-permute-start.1 = (bf16[2,2,128,128]{3,2,1,0:T(8,128)(2,1)S(1)}, bf16[2,2,128,128]{3,2,1,0:T(8,128)(2,1)S(1)}, u32[]{:S(2)}, u32[]{:S(2)}) collective-permute-start(bf16[2,2,128,128]{3,2,1,0:T(8,128)(2,1)S(1)} %get-tuple-element.20.rest_2_), channel_id=1, source_target_pairs={{0,8},{1,9},{2,10},{3,11},{4,12},{5,13},{6,14},{7,15},{8,0},{9,1},... | collective-permute-start | bytes 393224 | tf_op jit(solution)/shard_map/ppermute | solution.py:311
  13.1 9.8 %collective-permute-start.4 = (f32[2,128,128]{2,1,0:T(8,128)S(1)}, f32[2,128,128]{2,1,0:T(8,128)S(1)}, u32[]{:S(2)}, u32[]{:S(2)}) collective-permute-start(f32[2,128,128]{2,1,0:T(8,128)S(1)} %copy-done.4), channel_id=1, source_target_pairs={{0,4},{1,5},{2,6},{3,7},{4,0},{5,1},{6,2},{7,3},{8,12},{9,13},{10,... | collective-permute-start | bytes 393224 | tf_op jit(solution)/shard_map/ppermute | solution.py:311
  25.5 6.0 %collective-permute-start.5 = (bf16[2,272,128]{2,1,0:T(8,128)(2,1)S(1)}, bf16[2,272,128]{2,1,0:T(8,128)(2,1)S(1)}, u32[]{:S(2)}, u32[]{:S(2)}) collective-permute-start(bf16[2,272,128]{2,1,0:T(8,128)(2,1)S(1)} %get-tuple-element.26), channel_id=1, source_target_pairs={{0,16},{1,17},{2,18},{3,19},{4,20},{5,21},{6,22},{7,23},{8,24},{9,... | collective-permute-start | bytes 417800 | tf_op jit(solution)/shard_map/ppermute | solution.py:311
  27.1 5.4 %collective-permute-start.6 = (bf16[2,272,128]{2,1,0:T(8,128)(2,1)S(1)}, bf16[2,272,128]{2,1,0:T(8,128)(2,1)S(1)}, u32[]{:S(2)}, u32[]{:S(2)}) collective-permute-start(bf16[2,272,128]{2,1,0:T(8,128)(2,1)S(1)} %get-tuple-element.25.refs_0_), channel_id=1, source_target_pairs={{0,2},{1,3},{2,0},{3,1},{4,6},{5,7},{6,4},{7,5},{8,10},{9,11},{10,... | collective-permute-start | bytes 417800 | tf_op jit(solution)/shard_map/ppermute | solution.py:311
  28.7 6.0 %collective-permute-start.7 = (bf16[2,272,128]{2,1,0:T(8,128)(2,1)S(1)}, bf16[2,272,128]{2,1,0:T(8,128)(2,1)S(1)}, u32[]{:S(2)}, u32[]{:S(2)}) collective-permute-start(bf16[2,272,128]{2,1,0:T(8,128)(2,1)S(1)} %get-tuple-element.26), channel_id=1, source_target_pairs={{0,18},{1,19},{2,16},{3,17},{4,22},{5,23},{6,20},{7,21},{8,26},{9,... | collective-permute-start | bytes 417800 | tf_op jit(solution)/shard_map/ppermute | solution.py:311
  29.1 5.6 %collective-permute-start.8 = (bf16[2,272,128]{2,1,0:T(8,128)(2,1)S(1)}, bf16[2,272,128]{2,1,0:T(8,128)(2,1)S(1)}, u32[]{:S(2)}, u32[]{:S(2)}) collective-permute-start(bf16[2,272,128]{2,1,0:T(8,128)(2,1)S(1)} %get-tuple-element.25.refs_0_), channel_id=1, source_target_pairs={{0,1},{1,0},{2,3},{3,2},{4,5},{5,4},{6,7},{7,6},{8,9},{9,8},{10,11... | collective-permute-start | bytes 417800 | tf_op jit(solution)/shard_map/ppermute | solution.py:311
  31.5 3.1 %collective-permute-start.9 = (bf16[2,272,128]{2,1,0:T(8,128)(2,1)S(1)}, bf16[2,272,128]{2,1,0:T(8,128)(2,1)S(1)}, u32[]{:S(2)}, u32[]{:S(2)}) collective-permute-start(bf16[2,272,128]{2,1,0:T(8,128)(2,1)S(1)} %collective-permute-done.5.refs_1_), channel_id=1, source_target_pairs={{0,1},{1,0},{2,3},{3,2},{4,5},{5,4},{6,7},{7,6},{8,9},{9,8},{10,11... | collective-permute-start | bytes 417800 | tf_op jit(solution)/shard_map/ppermute | solution.py:311
  32.4 2.2 %collective-permute-start.10 = (bf16[2,272,128]{2,1,0:T(8,128)(2,1)S(1)}, bf16[2,272,128]{2,1,0:T(8,128)(2,1)S(1)}, u32[]{:S(2)}, u32[]{:S(2)}) collective-permute-start(bf16[2,272,128]{2,1,0:T(8,128)(2,1)S(1)} %collective-permute-done.6.refs_2_), channel_id=1, source_target_pairs={{0,1},{1,0},{2,3},{3,2},{4,5},{5,4},{6,7},{7,6},{8,9},{9,8},{10,11... | collective-permute-start | bytes 417800 | tf_op jit(solution)/shard_map/ppermute | solution.py:311
  34.6 1.4 %collective-permute-start.11 = (bf16[2,272,128]{2,1,0:T(8,128)(2,1)S(1)}, bf16[2,272,128]{2,1,0:T(8,128)(2,1)S(1)}, u32[]{:S(2)}, u32[]{:S(2)}) collective-permute-start(bf16[2,272,128]{2,1,0:T(8,128)(2,1)S(1)} %collective-permute-done.7.refs_3_), channel_id=1, source_target_pairs={{0,1},{1,0},{2,3},{3,2},{4,5},{5,4},{6,7},{7,6},{8,9},{9,8},{10,11... | collective-permute-start | bytes 417800 | tf_op jit(solution)/shard_map/ppermute | solution.py:311

commit v11 on v6

--- a/solution.py
+++ b/solution.py
@@ -36,74 +36,78 @@
 
 
 def window_kernel(members, obj_ref, *rest):
-    table, buf, table_sems, sems = rest[-4:]
-    clusters, count = buf.shape[:2]
-    pos_refs, out_refs, code_ref = rest[:clusters], rest[clusters:-5], rest[-5]
-    window = out_refs[0].shape[-1]
+    table, buf, cut, table_sems, sems = rest[-5:]
+    clusters, count, _, tall, wide = buf.shape
+    pos_refs, out_refs, code_ref = rest[:clusters], rest[clusters:-6], rest[-6]
+    window = cut.shape[-1]
     rows, cols = obj_ref.shape[-2:]
-    tall, wide = buf.shape[-2:]
     cluster = lax.div(lax.axis_index("dp"), members)
     home = lax.div(lax.axis_index("depth"), 2)
 
-    fetches = [
-        pltpu.make_async_copy(pos_refs[m], table.at[m], table_sems.at[m]) for m in range(clusters)
-    ]
-    for fetch in fetches:
-        fetch.start()
-    for fetch in fetches:
-        fetch.wait()
-
-    def corner(m, p):
-        at = home ^ cluster ^ m
-        row, col = table[at, p, 0], table[at, p, 1]
+    def corner(a, p):
+        row, col = table[a, p, 0], table[a, p, 1]
         row_base = pl.multiple_of(jnp.minimum(row >> 3, (rows - tall) // 8) * 8, 8)
         col_base = pl.multiple_of(jnp.minimum(col >> 7, (cols - wide) // 128) * 128, 128)
         return row_base, col_base, row - row_base, col - col_base
 
-    def copy(m, p):
-        row_base, col_base, _, _ = corner(m, p)
+    def copy(a, p):
+        row_base, col_base, _, _ = corner(a, p)
         return pltpu.make_async_copy(
-            obj_ref.at[:, pl.ds(row_base, tall), pl.ds(col_base, wide)], buf.at[m, p], sems.at[m, p]
+            obj_ref.at[:, pl.ds(row_base, tall), pl.ds(col_base, wide)], buf.at[a, p], sems.at[a, p]
         )
 
-    order = [(m, p) for m in reversed(range(clusters)) for p in range(count)]
-    for m, p in order:
-        copy(m, p).start()
+    arrivals = [
+        pltpu.make_async_copy(pos_refs[a], table.at[a], table_sems.at[a])
+        for a in range(1, clusters)
+    ]
+    for arrival in arrivals:
+        arrival.start()
+    for p in range(count):
+        for axis in range(2):
+            table[0, p, axis] = pos_refs[0][p, axis]
+        copy(0, p).start()
+    for a in range(1, clusters):
+        arrivals[a - 1].wait()
+        for p in range(count):
+            copy(a, p).start()
     line = lax.broadcasted_iota(jnp.int32, (code_rows, window), 0)
     for p in range(count):
         row, col = table[home ^ cluster, p, 0], table[home ^ cluster, p, 1]
         code = jnp.where(line == 0, row >> 3, jnp.where(line == 1, row & 7, 0))
         code = jnp.where(line == 2, col >> 3, jnp.where(line == 3, col & 7, code))
         code_ref[p] = code.astype(f32).astype(bf16)
-    for m, p in order:
-        copy(m, p).wait()
-        _, _, row_off, col_off = corner(m, p)
-        lift = jnp.where(row_off == 0, 0, tall - row_off)
-        shift = jnp.where(col_off == 0, 0, wide - col_off)
-        for part in range(2):
-            block = pltpu.roll(buf[m, p, part], shift, 1)[:, :window]
-            block = pltpu.roll(block, lift, 0)[:window]
-            out_refs[m][p, part] = block.astype(bf16)
+    for a in range(clusters):
+        for p in range(count):
+            copy(a, p).wait()
+            _, _, row_off, col_off = corner(a, p)
+            lift = jnp.where(row_off == 0, 0, tall - row_off)
+            shift = jnp.where(col_off == 0, 0, wide - col_off)
+            for part in range(2):
+                block = pltpu.roll(buf[a, p, part], shift, 1)[:, :window]
+                block = pltpu.roll(block, lift, 0)[:window]
+                cut[home ^ cluster ^ a, p, part] = block.astype(bf16)
+    for m, out_ref in enumerate(out_refs):
+        out_ref[...] = cut[m]
 
 
 def take_windows(obj, positions, window, members):
     clusters, count = len(positions), positions[0].shape[0]
-    tall, wide = window + 8, window + 128
     any_space = pl.BlockSpec(memory_space=pl.ANY)
+    smem = pl.BlockSpec(memory_space=pltpu.SMEM)
     vmem = pl.BlockSpec(memory_space=pltpu.VMEM)
     out = pl.pallas_call(
         functools.partial(window_kernel, members),
         out_shape=[jax.ShapeDtypeStruct((count, 2, window, window), bf16)] * clusters
         + [jax.ShapeDtypeStruct((count, code_rows, window), bf16)],
-        in_specs=[any_space] * (1 + clusters),
+        in_specs=[any_space, smem] + [any_space] * (clusters - 1),
         out_specs=[vmem] * (clusters + 1),
         scratch_shapes=[
             pltpu.SMEM((clusters, count, 2), jnp.int32),
-            pltpu.VMEM((clusters, count, 2, tall, wide), f32),
+            pltpu.VMEM((clusters, count, 2, window + 8, window + 128), f32),
+            pltpu.VMEM((clusters, count, 2, window, window), bf16),
             pltpu.SemaphoreType.DMA((clusters,)),
             pltpu.SemaphoreType.DMA((clusters, count)),
         ],
-        compiler_params=pltpu.CompilerParams(vmem_limit_bytes=24 * 1024 * 1024),
         name="take_windows",
     )(obj, *positions)
     return out[:clusters], out[clusters]
@@ -283,7 +287,7 @@
     homes = [m * members for m in range(1, clusters)]
     all_positions = [positions] + [swap(positions, 0, home) for home in homes]
     windows, code = take_windows(object_slices[0], all_positions, window, members)
-    measured, phase, code = lax.optimization_barrier((measured, propagator_phase, code))
+    phase, code = lax.optimization_barrier((propagator_phase, code))
     windows = [windows[0]] + [swap(windows[m // 2], m, 0) for m in range(1, depth)]
     targets = [measured] + [swap(measured, 0, home) for home in homes]
     kern = jnp.stack([jnp.cos(phase), jnp.sin(phase)])

time: 39.5 us -> 39.1 us (0.990); the launches traced: 39.2 us -> 38.3 us
  starting transfers between devices: 14.1 us -> 11.7 us
  Pallas kernels: 9.86 us -> 11.9 us
  local copies, waits for them, and re-layouts: 3.27 us -> 2.44 us
    ppermute x12, starting transfers between devices: 14.1 us -> 11.7 us  [swap(): return lax.ppermute(block, ('depth', 'dp'), route)]
    pallas_call x1, Pallas kernels: 1.31 us -> 3.43 us  [take_windows(): pl.pallas_call(functools.partial(window_kernel, members), out_shape=[jax....]
    unnamed x14 -> x16, local copies, waits for them, and re-layouts: 3.03 us -> 2.21 us
  transfers between devices with their start and end apart: 12 -> 12, of which waited for: 8 -> 7; matrix products, arithmetic and copies ran while one was open for 1% -> 1% of each run, Pallas kernels for 0% -> 9%
where the time goes in v11:
time: 39.1 us; the launch traced here: 38.3 us
  waiting for transfers between devices  12.2 us (31%)
  Pallas kernels  11.9 us (30%)
  starting transfers between devices  11.7 us (30%)
  local copies, waits for them, and re-layouts  2.44 us (6%)
    ppermute x12, waiting for transfers between devices, swap(): return lax.ppermute(block, ('depth', 'dp'), route)  12.2 us
    ppermute x12, starting transfers between devices, swap(): return lax.ppermute(block, ('depth', 'dp'), route)  11.7 us
    pallas_call x1, Pallas kernels, run_waves(): pl.pallas_call(functools.partial(wave_kernel, members, len(measured)), ou...  7.02 us
    pallas_call x1, Pallas kernels, take_windows(): pl.pallas_call(functools.partial(window_kernel, members), out_shape=[jax....  3.43 us
    unnamed x16, local copies, waits for them, and re-layouts  2.21 us
    pallas_call x1, Pallas kernels, place_windows(): pl.pallas_call(place_kernel, out_shape=jax.ShapeDtypeStruct((2, stripe, c...  1.48 us
  transfers between devices with their start and end apart: 12, of which 7 were waited for; matrix products, arithmetic and copies ran while one was open for 1% of the time, Pallas kernels for 9%

profile of v11, /device:TPU:0, one launch (start us, length us, event | category | flops | bytes accessed | tf_op | source)
XLA Modules:
  0.0 38.3 jit_solution(5877715266081831830)
XLA Ops:
  0.0 4.1 %collective-permute-start = (s32[2,2]{1,0:T(2,128)}, s32[2,2]{1,0:T(2,128)S(1)}, u32[]{:S(2)}, u32[]{:S(2)}) collective-permute-start(s32[2,2]{1,0:T(2,128)} %rest_0_.2), channel_id=1, source_target_pairs={{0,4},{1,5},{2,6},{3,7},{4,0},{5,1},{6,2},{7,3},{8,12},{9,13},{10,... | collective-permute-start | bytes 56 | tf_op jit(solution)/shard_map/ppermute | solution.py:277
  4.1 0.1 collective-permute-start.1
  4.2 1.7 %collective-permute-done.rest_1_ = s32[2,2]{1,0:T(2,128)S(1)} collective-permute-done((s32[2,2]{1,0:T(2,128)}, s32[2,2]{1,0:T(2,128)S(1)}, u32[]{:S(2)}, u32[]{:S(2)}) %collective-permute-start) | collective-permute-done | bytes 48 | tf_op jit(solution)/shard_map/ppermute | solution.py:277
  5.9 0.6 %copy-done.7 = s32[2,2]{1,0:T(2,128)} copy-done((s32[2,2]{1,0:T(2,128)}, s32[2,2]{1,0:T(2,128)S(1)}, u32[]{:S(2)}) %copy-start.7) | copy-done | bytes 40
  6.5 3.4 %take_windows.1 = (bf16[2,2,128,128]{3,2,1,0:T(8,128)(2,1)}, bf16[2,2,128,128]{3,2,1,0:T(8,128)(2,1)}, bf16[2,16,128]{2,1,0:T(8,128)(2,1)}) custom-call(f32[2,768,768]{2,1,0:T(8,128)} %bitcast.6, s32[2,2]{1,0:T(2,128)} %rest_0_.2, s32[2,2]{1,0:T(2,128)} %copy-done.7), custom_call_target="tpu_custom_call" | custom-call | tf_op jit(solution)/shard_map/take_windows/pallas_call | solution.py:98
  9.9 2.8 %collective-permute-start.4 = (bf16[2,2,128,128]{3,2,1,0:T(8,128)(2,1)}, bf16[2,2,128,128]{3,2,1,0:T(8,128)(2,1)S(1)}, u32[]{:S(2)}, u32[]{:S(2)}) collective-permute-start(bf16[2,2,128,128]{3,2,1,0:T(8,128)(2,1)} %get-tuple-element.16), channel_id=1, source_target_pairs={{0,24},{1,25},{2,26},{3,27},{4,28},{5,29},{6,30},{7,31},{8,16},{9,... | collective-permute-start | bytes 393224 | tf_op jit(solution)/shard_map/ppermute | solution.py:277
  12.8 0.5 %collective-permute-start.3 = (bf16[2,2,128,128]{3,2,1,0:T(8,128)(2,1)}, bf16[2,2,128,128]{3,2,1,0:T(8,128)(2,1)S(1)}, u32[]{:S(2)}, u32[]{:S(2)}) collective-permute-start(bf16[2,2,128,128]{3,2,1,0:T(8,128)(2,1)} %get-tuple-element.16), channel_id=1, source_target_pairs={{0,16},{1,17},{2,18},{3,19},{4,20},{5,21},{6,22},{7,23},{8,24},{9,... | collective-permute-start | bytes 393224 | tf_op jit(solution)/shard_map/ppermute | solution.py:277
  13.3 0.2 collective-permute-start.2
  13.5 0.2 cosine_bitcast_fusion
  13.8 4.7 %collective-permute-done.2.rest_3_ = bf16[2,2,128,128]{3,2,1,0:T(8,128)(2,1)S(1)} collective-permute-done((bf16[2,2,128,128]{3,2,1,0:T(8,128)(2,1)}, bf16[2,2,128,128]{3,2,1,0:T(8,128)(2,1)S(1)}, u32[]{:S(2)}, u32[]{:S(2)}) %collective-permute-start.2) | collective-permute-done | bytes 131104 | tf_op jit(solution)/shard_map/ppermute | solution.py:277
  18.5 0.0 copy-start.4
  18.5 0.9 %copy-done.4 = bf16[2,2,128,128]{3,2,1,0:T(8,128)(2,1)S(1)} copy-done((bf16[2,2,128,128]{3,2,1,0:T(8,128)(2,1)S(1)}, bf16[2,2,128,128]{3,2,1,0:T(8,128)(2,1)}, u32[]{:S(2)}) %copy-start.4) | copy-done | bytes 131096
  19.4 0.7 %copy-done.5 = bf16[2,16,128]{2,1,0:T(8,128)(2,1)S(1)} copy-done((bf16[2,16,128]{2,1,0:T(8,128)(2,1)S(1)}, bf16[2,16,128]{2,1,0:T(8,128)(2,1)}, u32[]{:S(2)}) %copy-start.5) | copy-done | bytes 8216
  20.1 7.0 %run_waves.1 = (bf16[2,272,128]{2,1,0:T(8,128)(2,1)S(1)}, bf16[2,272,128]{2,1,0:T(8,128)(2,1)S(1)}) custom-call(f32[2,128,128]{2,1,0:T(8,128)S(1)} %copy-done.2, f32[2,128,128]{2,1,0:T(8,128)S(1)} %pad_maximum_fusion.kern_ref, bf16[2,256,768]{2,1,0:T(8,128)(2,1)S(1)} %copy-done.1, bf16[2,768,256]{2,1,0:T(8,128)(2,1)S(1)} %copy-done, ...), custom_call_target="tpu_custom_call" | custom-call | tf_op jit(solution)/shard_map/run_waves/pallas_call | solution.py:206
  27.1 2.6 %collective-permute-start.7 = (bf16[2,272,128]{2,1,0:T(8,128)(2,1)S(1)}, bf16[2,272,128]{2,1,0:T(8,128)(2,1)S(1)}, u32[]{:S(2)}, u32[]{:S(2)}) collective-permute-start(bf16[2,272,128]{2,1,0:T(8,128)(2,1)S(1)} %get-tuple-element.18), channel_id=1, source_target_pairs={{0,18},{1,19},{2,16},{3,17},{4,22},{5,23},{6,20},{7,21},{8,26},{9,... | collective-permute-start | bytes 417800 | tf_op jit(solution)/shard_map/ppermute | solution.py:277
  29.7 0.5 %collective-permute-start.5 = (bf16[2,272,128]{2,1,0:T(8,128)(2,1)S(1)}, bf16[2,272,128]{2,1,0:T(8,128)(2,1)S(1)}, u32[]{:S(2)}, u32[]{:S(2)}) collective-permute-start(bf16[2,272,128]{2,1,0:T(8,128)(2,1)S(1)} %get-tuple-element.18), channel_id=1, source_target_pairs={{0,16},{1,17},{2,18},{3,19},{4,20},{5,21},{6,22},{7,23},{8,24},{9,... | collective-permute-start | bytes 417800 | tf_op jit(solution)/shard_map/ppermute | solution.py:277
  30.2 0.4 %collective-permute-start.6 = (bf16[2,272,128]{2,1,0:T(8,128)(2,1)S(1)}, bf16[2,272,128]{2,1,0:T(8,128)(2,1)S(1)}, u32[]{:S(2)}, u32[]{:S(2)}) collective-permute-start(bf16[2,272,128]{2,1,0:T(8,128)(2,1)S(1)} %get-tuple-element.17.refs_0_), channel_id=1, source_target_pairs={{0,2},{1,3},{2,0},{3,1},{4,6},{5,7},{6,4},{7,5},{8,10},{9,11},{10,... | collective-permute-start | bytes 417800 | tf_op jit(solution)/shard_map/ppermute | solution.py:277
  30.7 3.6 %collective-permute-done.7.refs_3_ = bf16[2,272,128]{2,1,0:T(8,128)(2,1)S(1)} collective-permute-done((bf16[2,272,128]{2,1,0:T(8,128)(2,1)S(1)}, bf16[2,272,128]{2,1,0:T(8,128)(2,1)S(1)}, u32[]{:S(2)}, u32[]{:S(2)}) %collective-permute-start.7) | collective-permute-done | bytes 139296 | tf_op jit(solution)/shard_map/ppermute | solution.py:277
  34.3 1.0 %collective-permute-done.5.refs_1_ = bf16[2,272,128]{2,1,0:T(8,128)(2,1)S(1)} collective-permute-done((bf16[2,272,128]{2,1,0:T(8,128)(2,1)S(1)}, bf16[2,272,128]{2,1,0:T(8,128)(2,1)S(1)}, u32[]{:S(2)}, u32[]{:S(2)}) %collective-permute-start.5) | collective-permute-done | bytes 139296 | tf_op jit(solution)/shard_map/ppermute | solution.py:277
  35.3 0.2 collective-permute-done.6.refs_2_
  35.5 0.4 collective-permute-start.10
  35.8 0.8 %collective-permute-done.9.refs_5_ = bf16[2,272,128]{2,1,0:T(8,128)(2,1)S(1)} collective-permute-done((bf16[2,272,128]{2,1,0:T(8,128)(2,1)S(1)}, bf16[2,272,128]{2,1,0:T(8,128)(2,1)S(1)}, u32[]{:S(2)}, u32[]{:S(2)}) %collective-permute-start.9) | collective-permute-done | bytes 139296 | tf_op jit(solution)/shard_map/ppermute | solution.py:277
  36.7 0.2 collective-permute-done.10.refs_6_
  36.9 1.5 %place_windows.1 = f32[2,96,768]{2,1,0:T(8,128)} custom-call(bf16[2,272,128]{2,1,0:T(8,128)(2,1)S(1)} %get-tuple-element.17.refs_0_, bf16[2,272,128]{2,1,0:T(8,128)(2,1)S(1)} %collective-permute-done.5.refs_1_, bf16[2,272,128]{2,1,0:T(8,128)(2,1)S(1)} %collective-permute-done.6.refs_2_, bf16[2,272,128]{2,1,0:T(8,128)(2,1)S(1)} %collective-permute-done.7.refs_3_, ...), custom_call_target="tpu_custom_call" | custom-call | tf_op jit(solution)/shard_map/place_windows/pallas_call | solution.py:259
  (21 shorter events, 0.1 us)
Async XLA Ops:
  0.0 18.5 %copy-start = (bf16[2,768,256]{2,1,0:T(8,128)(2,1)S(1)}, bf16[2,768,256]{2,1,0:T(8,128)(2,1)}, u32[]{:S(2)}) copy-start(bf16[2,768,256]{2,1,0:T(8,128)(2,1)} %constant.5.clone.right_ref) | copy-start | bytes 2359300
  0.0 18.5 %copy-start.1 = (bf16[2,256,768]{2,1,0:T(8,128)(2,1)S(1)}, bf16[2,256,768]{2,1,0:T(8,128)(2,1)}, u32[]{:S(2)}) copy-start(bf16[2,256,768]{2,1,0:T(8,128)(2,1)} %constant.4.clone.left_ref) | copy-start | bytes 2359300
  0.0 18.5 %copy-start.3 = (f32[2,128,128]{2,1,0:T(8,128)S(1)}, f32[2,128,128]{2,1,0:T(8,128)}, u32[]{:S(2)}) copy-start(f32[2,128,128]{2,1,0:T(8,128)} %rest_0_.3) | copy-start | bytes 393220
  0.0 13.5 %copy-start.6 = (f32[128,128]{1,0:T(8,128)S(1)}, f32[128,128]{1,0:T(8,128)}, u32[]{:S(2)}) copy-start(f32[128,128]{1,0:T(8,128)} %param.10) | copy-start | bytes 196612
  0.0 18.5 %copy-start.2 = (f32[2,128,128]{2,1,0:T(8,128)S(1)}, f32[2,128,128]{2,1,0:T(8,128)}, u32[]{:S(2)}) copy-start(f32[2,128,128]{2,1,0:T(8,128)} %probe_ref.1) | copy-start | bytes 393220
  0.0 5.9 %collective-permute-start = (s32[2,2]{1,0:T(2,128)}, s32[2,2]{1,0:T(2,128)S(1)}, u32[]{:S(2)}, u32[]{:S(2)}) collective-permute-start(s32[2,2]{1,0:T(2,128)} %rest_0_.2), channel_id=1, source_target_pairs={{0,4},{1,5},{2,6},{3,7},{4,0},{5,1},{6,2},{7,3},{8,12},{9,13},{10,... | collective-permute-start | bytes 56 | tf_op jit(solution)/shard_map/ppermute | solution.py:277
  4.1 9.6 %collective-permute-start.1 = (f32[2,128,128]{2,1,0:T(8,128)}, f32[2,128,128]{2,1,0:T(8,128)S(1)}, u32[]{:S(2)}, u32[]{:S(2)}) collective-permute-start(f32[2,128,128]{2,1,0:T(8,128)} %rest_0_.3), channel_id=1, source_target_pairs={{0,4},{1,5},{2,6},{3,7},{4,0},{5,1},{6,2},{7,3},{8,12},{9,13},{10,... | collective-permute-start | bytes 393224 | tf_op jit(solution)/shard_map/ppermute | solution.py:277
  5.9 0.6 %copy-start.7 = (s32[2,2]{1,0:T(2,128)}, s32[2,2]{1,0:T(2,128)S(1)}, u32[]{:S(2)}) copy-start(s32[2,2]{1,0:T(2,128)S(1)} %collective-permute-done.rest_1_) | copy-start | bytes 52
  9.9 8.5 %collective-permute-start.4 = (bf16[2,2,128,128]{3,2,1,0:T(8,128)(2,1)}, bf16[2,2,128,128]{3,2,1,0:T(8,128)(2,1)S(1)}, u32[]{:S(2)}, u32[]{:S(2)}) collective-permute-start(bf16[2,2,128,128]{3,2,1,0:T(8,128)(2,1)} %get-tuple-element.16), channel_id=1, source_target_pairs={{0,24},{1,25},{2,26},{3,27},{4,28},{5,29},{6,30},{7,31},{8,16},{9,... | collective-permute-start | bytes 393224 | tf_op jit(solution)/shard_map/ppermute | solution.py:277
  12.8 5.7 %collective-permute-start.3 = (bf16[2,2,128,128]{3,2,1,0:T(8,128)(2,1)}, bf16[2,2,128,128]{3,2,1,0:T(8,128)(2,1)S(1)}, u32[]{:S(2)}, u32[]{:S(2)}) collective-permute-start(bf16[2,2,128,128]{3,2,1,0:T(8,128)(2,1)} %get-tuple-element.16), channel_id=1, source_target_pairs={{0,16},{1,17},{2,18},{3,19},{4,20},{5,21},{6,22},{7,23},{8,24},{9,... | collective-permute-start | bytes 393224 | tf_op jit(solution)/shard_map/ppermute | solution.py:277
  13.3 5.2 %collective-permute-start.2 = (bf16[2,2,128,128]{3,2,1,0:T(8,128)(2,1)}, bf16[2,2,128,128]{3,2,1,0:T(8,128)(2,1)S(1)}, u32[]{:S(2)}, u32[]{:S(2)}) collective-permute-start(bf16[2,2,128,128]{3,2,1,0:T(8,128)(2,1)} %get-tuple-element.15.rest_2_), channel_id=1, source_target_pairs={{0,8},{1,9},{2,10},{3,11},{4,12},{5,13},{6,14},{7,15},{8,0},{9,1},... | collective-permute-start | bytes 393224 | tf_op jit(solution)/shard_map/ppermute | solution.py:277
  18.5 0.9 %copy-start.4 = (bf16[2,2,128,128]{3,2,1,0:T(8,128)(2,1)S(1)}, bf16[2,2,128,128]{3,2,1,0:T(8,128)(2,1)}, u32[]{:S(2)}) copy-start(bf16[2,2,128,128]{3,2,1,0:T(8,128)(2,1)} %get-tuple-element.15.rest_2_) | copy-start | bytes 393220
  19.4 0.7 %copy-start.5 = (bf16[2,16,128]{2,1,0:T(8,128)(2,1)S(1)}, bf16[2,16,128]{2,1,0:T(8,128)(2,1)}, u32[]{:S(2)}) copy-start(bf16[2,16,128]{2,1,0:T(8,128)(2,1)} %get-tuple-element.14.code_ref) | copy-start | bytes 24580
  27.1 7.2 %collective-permute-start.7 = (bf16[2,272,128]{2,1,0:T(8,128)(2,1)S(1)}, bf16[2,272,128]{2,1,0:T(8,128)(2,1)S(1)}, u32[]{:S(2)}, u32[]{:S(2)}) collective-permute-start(bf16[2,272,128]{2,1,0:T(8,128)(2,1)S(1)} %get-tuple-element.18), channel_id=1, source_target_pairs={{0,18},{1,19},{2,16},{3,17},{4,22},{5,23},{6,20},{7,21},{8,26},{9,... | collective-permute-start | bytes 417800 | tf_op jit(solution)/shard_map/ppermute | solution.py:277
  29.7 5.6 %collective-permute-start.5 = (bf16[2,272,128]{2,1,0:T(8,128)(2,1)S(1)}, bf16[2,272,128]{2,1,0:T(8,128)(2,1)S(1)}, u32[]{:S(2)}, u32[]{:S(2)}) collective-permute-start(bf16[2,272,128]{2,1,0:T(8,128)(2,1)S(1)} %get-tuple-element.18), channel_id=1, source_target_pairs={{0,16},{1,17},{2,18},{3,19},{4,20},{5,21},{6,22},{7,23},{8,24},{9,... | collective-permute-start | bytes 417800 | tf_op jit(solution)/shard_map/ppermute | solution.py:277
  30.2 5.2 %collective-permute-start.6 = (bf16[2,272,128]{2,1,0:T(8,128)(2,1)S(1)}, bf16[2,272,128]{2,1,0:T(8,128)(2,1)S(1)}, u32[]{:S(2)}, u32[]{:S(2)}) collective-permute-start(bf16[2,272,128]{2,1,0:T(8,128)(2,1)S(1)} %get-tuple-element.17.refs_0_), channel_id=1, source_target_pairs={{0,2},{1,3},{2,0},{3,1},{4,6},{5,7},{6,4},{7,5},{8,10},{9,11},{10,... | collective-permute-start | bytes 417800 | tf_op jit(solution)/shard_map/ppermute | solution.py:277
  30.7 5.1 %collective-permute-start.8 = (bf16[2,272,128]{2,1,0:T(8,128)(2,1)S(1)}, bf16[2,272,128]{2,1,0:T(8,128)(2,1)S(1)}, u32[]{:S(2)}, u32[]{:S(2)}) collective-permute-start(bf16[2,272,128]{2,1,0:T(8,128)(2,1)S(1)} %get-tuple-element.17.refs_0_), channel_id=1, source_target_pairs={{0,1},{1,0},{2,3},{3,2},{4,5},{5,4},{6,7},{7,6},{8,9},{9,8},{10,11... | collective-permute-start | bytes 417800 | tf_op jit(solution)/shard_map/ppermute | solution.py:277
  34.3 1.5 %collective-permute-start.11 = (bf16[2,272,128]{2,1,0:T(8,128)(2,1)S(1)}, bf16[2,272,128]{2,1,0:T(8,128)(2,1)S(1)}, u32[]{:S(2)}, u32[]{:S(2)}) collective-permute-start(bf16[2,272,128]{2,1,0:T(8,128)(2,1)S(1)} %collective-permute-done.7.refs_3_), channel_id=1, source_target_pairs={{0,1},{1,0},{2,3},{3,2},{4,5},{5,4},{6,7},{7,6},{8,9},{9,8},{10,11... | collective-permute-start | bytes 417800 | tf_op jit(solution)/shard_map/ppermute | solution.py:277
  35.3 1.4 %collective-permute-start.9 = (bf16[2,272,128]{2,1,0:T(8,128)(2,1)S(1)}, bf16[2,272,128]{2,1,0:T(8,128)(2,1)S(1)}, u32[]{:S(2)}, u32[]{:S(2)}) collective-permute-start(bf16[2,272,128]{2,1,0:T(8,128)(2,1)S(1)} %collective-permute-done.5.refs_1_), channel_id=1, source_target_pairs={{0,1},{1,0},{2,3},{3,2},{4,5},{5,4},{6,7},{7,6},{8,9},{9,8},{10,11... | collective-permute-start | bytes 417800 | tf_op jit(solution)/shard_map/ppermute | solution.py:277
  35.5 1.4 %collective-permute-start.10 = (bf16[2,272,128]{2,1,0:T(8,128)(2,1)S(1)}, bf16[2,272,128]{2,1,0:T(8,128)(2,1)S(1)}, u32[]{:S(2)}, u32[]{:S(2)}) collective-permute-start(bf16[2,272,128]{2,1,0:T(8,128)(2,1)S(1)} %collective-permute-done.6.refs_2_), channel_id=1, source_target_pairs={{0,1},{1,0},{2,3},{3,2},{4,5},{5,4},{6,7},{7,6},{8,9},{9,8},{10,11... | collective-permute-start | bytes 417800 | tf_op jit(solution)/shard_map/ppermute | solution.py:277

commit v12 on v7

--- a/solution.py
+++ b/solution.py
@@ -296,10 +296,11 @@
 
     homes = [m * members for m in range(1, clusters)]
     all_positions = [positions] + [swap(positions, 0, home) for home in homes]
-    windows, code = take_windows(fetch(object_slices[0]), all_positions, window, members)
+    obj, late = lax.optimization_barrier((fetch(object_slices[0]), measured))
+    windows, code = take_windows(obj, all_positions, window, members)
     phase, code = lax.optimization_barrier((propagator_phase, code))
     windows = [windows[0]] + [swap(windows[m // 2], m, 0) for m in range(1, depth)]
-    targets = [measured] + [swap(measured, 0, home) for home in homes]
+    targets = [measured] + [swap(late, 0, home) for home in homes]
     kern = jnp.stack([jnp.cos(phase), jnp.sin(phase)])
     terms = run_waves(probe_field, kern, code, targets, windows, members)
 

time: 37 us -> 37.3 us (level)
  waiting for transfers between devices: 12.3 us -> 11.5 us
  starting transfers between devices: 11.2 us -> 11.7 us
    ppermute x12, waiting for transfers between devices: 12.3 us -> 11.5 us  [swap(): return lax.ppermute(block, ('depth', 'dp'), route)]
    ppermute x12, starting transfers between devices: 11.2 us -> 11.7 us  [swap(): return lax.ppermute(block, ('depth', 'dp'), route)]
where the time goes in v12:
time: 37.3 us; the launch traced here: 36.9 us
  starting transfers between devices  11.7 us (31%)
  waiting for transfers between devices  11.5 us (31%)
  Pallas kernels  10.5 us (28%)
  local copies, waits for them, and re-layouts  3.16 us (8%)
    ppermute x12, starting transfers between devices, swap(): return lax.ppermute(block, ('depth', 'dp'), route)  11.7 us
    ppermute x12, waiting for transfers between devices, swap(): return lax.ppermute(block, ('depth', 'dp'), route)  11.5 us
    pallas_call x1, Pallas kernels, run_waves(): pl.pallas_call(functools.partial(wave_kernel, members, len(measured)), ou...  7.06 us
    unnamed x14, local copies, waits for them, and re-layouts  2.92 us
    pallas_call x1, Pallas kernels, place_windows(): pl.pallas_call(place_kernel, out_shape=jax.ShapeDtypeStruct((2, stripe, c...  1.61 us
    pallas_call x1, Pallas kernels, take_windows(): pl.pallas_call(functools.partial(window_kernel, members), out_shape=[jax....  1.46 us
  transfers between devices with their start and end apart: 12, of which 6 were waited for; matrix products, arithmetic and copies ran while one was open for 1% of the time, Pallas kernels for 5%

profile of v12, /device:TPU:0, one launch (start us, length us, event | category | flops | bytes accessed | tf_op | source)
XLA Modules:
  0.0 36.9 jit_solution(2631852317610644798)
XLA Ops:
  0.0 4.0 %collective-permute-start = (s32[2,2]{1,0:T(2,128)}, s32[2,2]{1,0:T(2,128)S(1)}, u32[]{:S(2)}, u32[]{:S(2)}) collective-permute-start(s32[2,2]{1,0:T(2,128)} %rest_0_.2), channel_id=1, source_target_pairs={{0,4},{1,5},{2,6},{3,7},{4,0},{5,1},{6,2},{7,3},{8,12},{9,13},{10,... | collective-permute-start | bytes 56 | tf_op jit(solution)/shard_map/ppermute | solution.py:287
  4.0 2.3 %copy-done = f32[1,2,768,768]{3,2,1,0:T(8,128)S(1)} copy-done((f32[1,2,768,768]{3,2,1,0:T(8,128)S(1)}, f32[1,2,768,768]{3,2,1,0:T(8,128)}, u32[]{:S(2)}) %copy-start) | copy-done | bytes 4718616
  6.4 0.3 fetch_slice.1.obj_ref
  6.7 0.6 %copy-done.4 = f32[2,128,128]{2,1,0:T(8,128)S(1)} copy-done((f32[2,128,128]{2,1,0:T(8,128)S(1)}, f32[2,128,128]{2,1,0:T(8,128)}, u32[]{:S(2)}) %copy-start.4) | copy-done | bytes 131096
  7.3 0.1 collective-permute-start.1
  7.4 1.5 %take_windows.1 = (bf16[2,2,128,128]{3,2,1,0:T(8,128)(2,1)S(1)}, bf16[2,2,128,128]{3,2,1,0:T(8,128)(2,1)S(1)}, bf16[2,16,128]{2,1,0:T(8,128)(2,1)S(1)}) custom-call(f32[2,768,768]{2,1,0:T(8,128)S(1)} %fetch_slice.1.obj_ref, s32[2,2]{1,0:T(2,128)S(1)} %copy-done.5, s32[2,2]{1,0:T(2,128)S(1)} %collective-permute-done.rest_1_), custom_call_target="tpu_custom_call" | custom-call | tf_op jit(solution)/shard_map/take_windows/pallas_call | solution.py:110
  8.9 2.8 %collective-permute-start.4 = (bf16[2,2,128,128]{3,2,1,0:T(8,128)(2,1)S(1)}, bf16[2,2,128,128]{3,2,1,0:T(8,128)(2,1)S(1)}, u32[]{:S(2)}, u32[]{:S(2)}) collective-permute-start(bf16[2,2,128,128]{3,2,1,0:T(8,128)(2,1)S(1)} %get-tuple-element.20), channel_id=1, source_target_pairs={{0,24},{1,25},{2,26},{3,27},{4,28},{5,29},{6,30},{7,31},{8,16},{9,... | collective-permute-start | bytes 393224 | tf_op jit(solution)/shard_map/ppermute | solution.py:287
  11.7 0.5 %collective-permute-start.3 = (bf16[2,2,128,128]{3,2,1,0:T(8,128)(2,1)S(1)}, bf16[2,2,128,128]{3,2,1,0:T(8,128)(2,1)S(1)}, u32[]{:S(2)}, u32[]{:S(2)}) collective-permute-start(bf16[2,2,128,128]{3,2,1,0:T(8,128)(2,1)S(1)} %get-tuple-element.20), channel_id=1, source_target_pairs={{0,16},{1,17},{2,18},{3,19},{4,20},{5,21},{6,22},{7,23},{8,24},{9,... | collective-permute-start | bytes 393224 | tf_op jit(solution)/shard_map/ppermute | solution.py:287
  12.2 0.2 collective-permute-start.2
  12.4 0.2 cosine_bitcast_fusion
  12.7 3.3 %collective-permute-done.1.rest_1_ = f32[2,128,128]{2,1,0:T(8,128)S(1)} collective-permute-done((f32[2,128,128]{2,1,0:T(8,128)S(1)}, f32[2,128,128]{2,1,0:T(8,128)S(1)}, u32[]{:S(2)}, u32[]{:S(2)}) %collective-permute-start.1) | collective-permute-done | bytes 131104 | tf_op jit(solution)/shard_map/ppermute | solution.py:287
  16.0 1.7 %collective-permute-done.2.rest_3_ = bf16[2,2,128,128]{3,2,1,0:T(8,128)(2,1)S(1)} collective-permute-done((bf16[2,2,128,128]{3,2,1,0:T(8,128)(2,1)S(1)}, bf16[2,2,128,128]{3,2,1,0:T(8,128)(2,1)S(1)}, u32[]{:S(2)}, u32[]{:S(2)}) %collective-permute-start.2) | collective-permute-done | bytes 131104 | tf_op jit(solution)/shard_map/ppermute | solution.py:287
  17.7 0.0 collective-permute-done.4.rest_5_
  17.7 7.1 %run_waves.1 = (bf16[2,272,128]{2,1,0:T(8,128)(2,1)S(1)}, bf16[2,272,128]{2,1,0:T(8,128)(2,1)S(1)}) custom-call(f32[2,128,128]{2,1,0:T(8,128)S(1)} %copy-done.3, f32[2,128,128]{2,1,0:T(8,128)S(1)} %pad_maximum_fusion.kern_ref, bf16[2,256,768]{2,1,0:T(8,128)(2,1)S(1)} %copy-done.2, bf16[2,768,256]{2,1,0:T(8,128)(2,1)S(1)} %copy-done.1, ...), custom_call_target="tpu_custom_call" | custom-call | tf_op jit(solution)/shard_map/run_waves/pallas_call | solution.py:216
  24.8 2.5 %collective-permute-start.7 = (bf16[2,272,128]{2,1,0:T(8,128)(2,1)S(1)}, bf16[2,272,128]{2,1,0:T(8,128)(2,1)S(1)}, u32[]{:S(2)}, u32[]{:S(2)}) collective-permute-start(bf16[2,272,128]{2,1,0:T(8,128)(2,1)S(1)} %get-tuple-element.22), channel_id=1, source_target_pairs={{0,18},{1,19},{2,16},{3,17},{4,22},{5,23},{6,20},{7,21},{8,26},{9,... | collective-permute-start | bytes 417800 | tf_op jit(solution)/shard_map/ppermute | solution.py:287
  27.3 0.6 %collective-permute-start.5 = (bf16[2,272,128]{2,1,0:T(8,128)(2,1)S(1)}, bf16[2,272,128]{2,1,0:T(8,128)(2,1)S(1)}, u32[]{:S(2)}, u32[]{:S(2)}) collective-permute-start(bf16[2,272,128]{2,1,0:T(8,128)(2,1)S(1)} %get-tuple-element.22), channel_id=1, source_target_pairs={{0,16},{1,17},{2,18},{3,19},{4,20},{5,21},{6,22},{7,23},{8,24},{9,... | collective-permute-start | bytes 417800 | tf_op jit(solution)/shard_map/ppermute | solution.py:287
  27.9 0.5 %collective-permute-start.6 = (bf16[2,272,128]{2,1,0:T(8,128)(2,1)S(1)}, bf16[2,272,128]{2,1,0:T(8,128)(2,1)S(1)}, u32[]{:S(2)}, u32[]{:S(2)}) collective-permute-start(bf16[2,272,128]{2,1,0:T(8,128)(2,1)S(1)} %get-tuple-element.21.refs_0_), channel_id=1, source_target_pairs={{0,2},{1,3},{2,0},{3,1},{4,6},{5,7},{6,4},{7,5},{8,10},{9,11},{10,... | collective-permute-start | bytes 417800 | tf_op jit(solution)/shard_map/ppermute | solution.py:287
  28.4 0.0 collective-permute-start.8
  28.4 3.1 %collective-permute-done.7.refs_3_ = bf16[2,272,128]{2,1,0:T(8,128)(2,1)S(1)} collective-permute-done((bf16[2,272,128]{2,1,0:T(8,128)(2,1)S(1)}, bf16[2,272,128]{2,1,0:T(8,128)(2,1)S(1)}, u32[]{:S(2)}, u32[]{:S(2)}) %collective-permute-start.7) | collective-permute-done | bytes 139296 | tf_op jit(solution)/shard_map/ppermute | solution.py:287
  31.4 2.4 %collective-permute-done.5.refs_1_ = bf16[2,272,128]{2,1,0:T(8,128)(2,1)S(1)} collective-permute-done((bf16[2,272,128]{2,1,0:T(8,128)(2,1)S(1)}, bf16[2,272,128]{2,1,0:T(8,128)(2,1)S(1)}, u32[]{:S(2)}, u32[]{:S(2)}) %collective-permute-start.5) | collective-permute-done | bytes 139296 | tf_op jit(solution)/shard_map/ppermute | solution.py:287
  33.8 0.5 %collective-permute-start.10 = (bf16[2,272,128]{2,1,0:T(8,128)(2,1)S(1)}, bf16[2,272,128]{2,1,0:T(8,128)(2,1)S(1)}, u32[]{:S(2)}, u32[]{:S(2)}) collective-permute-start(bf16[2,272,128]{2,1,0:T(8,128)(2,1)S(1)} %collective-permute-done.6.refs_2_), channel_id=1, source_target_pairs={{0,1},{1,0},{2,3},{3,2},{4,5},{5,4},{6,7},{7,6},{8,9},{9,8},{10,11... | collective-permute-start | bytes 417800 | tf_op jit(solution)/shard_map/ppermute | solution.py:287
  34.3 0.8 %collective-permute-done.9.refs_5_ = bf16[2,272,128]{2,1,0:T(8,128)(2,1)S(1)} collective-permute-done((bf16[2,272,128]{2,1,0:T(8,128)(2,1)S(1)}, bf16[2,272,128]{2,1,0:T(8,128)(2,1)S(1)}, u32[]{:S(2)}, u32[]{:S(2)}) %collective-permute-start.9) | collective-permute-done | bytes 139296 | tf_op jit(solution)/shard_map/ppermute | solution.py:287
  35.1 0.2 collective-permute-done.10.refs_6_
  35.3 1.6 %place_windows.1 = f32[2,96,768]{2,1,0:T(8,128)} custom-call(bf16[2,272,128]{2,1,0:T(8,128)(2,1)S(1)} %get-tuple-element.21.refs_0_, bf16[2,272,128]{2,1,0:T(8,128)(2,1)S(1)} %collective-permute-done.5.refs_1_, bf16[2,272,128]{2,1,0:T(8,128)(2,1)S(1)} %collective-permute-done.6.refs_2_, bf16[2,272,128]{2,1,0:T(8,128)(2,1)S(1)} %collective-permute-done.7.refs_3_, ...), custom_call_target="tpu_custom_call" | custom-call | tf_op jit(solution)/shard_map/place_windows/pallas_call | solution.py:269
  (20 shorter events, 0.1 us)
Async XLA Ops:
  0.0 7.4 %collective-permute-start = (s32[2,2]{1,0:T(2,128)}, s32[2,2]{1,0:T(2,128)S(1)}, u32[]{:S(2)}, u32[]{:S(2)}) collective-permute-start(s32[2,2]{1,0:T(2,128)} %rest_0_.2), channel_id=1, source_target_pairs={{0,4},{1,5},{2,6},{3,7},{4,0},{5,1},{6,2},{7,3},{8,12},{9,13},{10,... | collective-permute-start | bytes 56 | tf_op jit(solution)/shard_map/ppermute | solution.py:287
  4.0 2.3 %copy-start = (f32[1,2,768,768]{3,2,1,0:T(8,128)S(1)}, f32[1,2,768,768]{3,2,1,0:T(8,128)}, u32[]{:S(2)}) copy-start(f32[1,2,768,768]{3,2,1,0:T(8,128)} %param.7) | copy-start | bytes 14155780
  6.4 0.9 %copy-start.4 = (f32[2,128,128]{2,1,0:T(8,128)S(1)}, f32[2,128,128]{2,1,0:T(8,128)}, u32[]{:S(2)}) copy-start(f32[2,128,128]{2,1,0:T(8,128)} %rest_0_.3) | copy-start | bytes 393220
  6.4 1.0 %copy-start.5 = (s32[2,2]{1,0:T(2,128)S(1)}, s32[2,2]{1,0:T(2,128)}, u32[]{:S(2)}) copy-start(s32[2,2]{1,0:T(2,128)} %rest_0_.2) | copy-start | bytes 52
  7.3 5.1 %copy-start.6 = (f32[128,128]{1,0:T(8,128)S(1)}, f32[128,128]{1,0:T(8,128)}, u32[]{:S(2)}) copy-start(f32[128,128]{1,0:T(8,128)} %param.10) | copy-start | bytes 196612
  7.3 10.4 %copy-start.1 = (bf16[2,768,256]{2,1,0:T(8,128)(2,1)S(1)}, bf16[2,768,256]{2,1,0:T(8,128)(2,1)}, u32[]{:S(2)}) copy-start(bf16[2,768,256]{2,1,0:T(8,128)(2,1)} %constant.5.clone.right_ref) | copy-start | bytes 2359300
  7.3 10.4 %copy-start.2 = (bf16[2,256,768]{2,1,0:T(8,128)(2,1)S(1)}, bf16[2,256,768]{2,1,0:T(8,128)(2,1)}, u32[]{:S(2)}) copy-start(bf16[2,256,768]{2,1,0:T(8,128)(2,1)} %constant.4.clone.left_ref) | copy-start | bytes 2359300
  7.3 10.4 %copy-start.3 = (f32[2,128,128]{2,1,0:T(8,128)S(1)}, f32[2,128,128]{2,1,0:T(8,128)}, u32[]{:S(2)}) copy-start(f32[2,128,128]{2,1,0:T(8,128)} %probe_ref.1) | copy-start | bytes 393220
  7.3 8.7 %collective-permute-start.1 = (f32[2,128,128]{2,1,0:T(8,128)S(1)}, f32[2,128,128]{2,1,0:T(8,128)S(1)}, u32[]{:S(2)}, u32[]{:S(2)}) collective-permute-start(f32[2,128,128]{2,1,0:T(8,128)S(1)} %copy-done.4), channel_id=1, source_target_pairs={{0,4},{1,5},{2,6},{3,7},{4,0},{5,1},{6,2},{7,3},{8,12},{9,13},{10,... | collective-permute-start | bytes 393224 | tf_op jit(solution)/shard_map/ppermute | solution.py:287
  8.9 8.8 %collective-permute-start.4 = (bf16[2,2,128,128]{3,2,1,0:T(8,128)(2,1)S(1)}, bf16[2,2,128,128]{3,2,1,0:T(8,128)(2,1)S(1)}, u32[]{:S(2)}, u32[]{:S(2)}) collective-permute-start(bf16[2,2,128,128]{3,2,1,0:T(8,128)(2,1)S(1)} %get-tuple-element.20), channel_id=1, source_target_pairs={{0,24},{1,25},{2,26},{3,27},{4,28},{5,29},{6,30},{7,31},{8,16},{9,... | collective-permute-start | bytes 393224 | tf_op jit(solution)/shard_map/ppermute | solution.py:287
  11.7 6.0 %collective-permute-start.3 = (bf16[2,2,128,128]{3,2,1,0:T(8,128)(2,1)S(1)}, bf16[2,2,128,128]{3,2,1,0:T(8,128)(2,1)S(1)}, u32[]{:S(2)}, u32[]{:S(2)}) collective-permute-start(bf16[2,2,128,128]{3,2,1,0:T(8,128)(2,1)S(1)} %get-tuple-element.20), channel_id=1, source_target_pairs={{0,16},{1,17},{2,18},{3,19},{4,20},{5,21},{6,22},{7,23},{8,24},{9,... | collective-permute-start | bytes 393224 | tf_op jit(solution)/shard_map/ppermute | solution.py:287
  12.2 5.5 %collective-permute-start.2 = (bf16[2,2,128,128]{3,2,1,0:T(8,128)(2,1)S(1)}, bf16[2,2,128,128]{3,2,1,0:T(8,128)(2,1)S(1)}, u32[]{:S(2)}, u32[]{:S(2)}) collective-permute-start(bf16[2,2,128,128]{3,2,1,0:T(8,128)(2,1)S(1)} %get-tuple-element.19.rest_2_), channel_id=1, source_target_pairs={{0,8},{1,9},{2,10},{3,11},{4,12},{5,13},{6,14},{7,15},{8,0},{9,1},... | collective-permute-start | bytes 393224 | tf_op jit(solution)/shard_map/ppermute | solution.py:287
  24.8 6.6 %collective-permute-start.7 = (bf16[2,272,128]{2,1,0:T(8,128)(2,1)S(1)}, bf16[2,272,128]{2,1,0:T(8,128)(2,1)S(1)}, u32[]{:S(2)}, u32[]{:S(2)}) collective-permute-start(bf16[2,272,128]{2,1,0:T(8,128)(2,1)S(1)} %get-tuple-element.22), channel_id=1, source_target_pairs={{0,18},{1,19},{2,16},{3,17},{4,22},{5,23},{6,20},{7,21},{8,26},{9,... | collective-permute-start | bytes 417800 | tf_op jit(solution)/shard_map/ppermute | solution.py:287
  27.3 6.5 %collective-permute-start.5 = (bf16[2,272,128]{2,1,0:T(8,128)(2,1)S(1)}, bf16[2,272,128]{2,1,0:T(8,128)(2,1)S(1)}, u32[]{:S(2)}, u32[]{:S(2)}) collective-permute-start(bf16[2,272,128]{2,1,0:T(8,128)(2,1)S(1)} %get-tuple-element.22), channel_id=1, source_target_pairs={{0,16},{1,17},{2,18},{3,19},{4,20},{5,21},{6,22},{7,23},{8,24},{9,... | collective-permute-start | bytes 417800 | tf_op jit(solution)/shard_map/ppermute | solution.py:287
  27.9 5.9 %collective-permute-start.6 = (bf16[2,272,128]{2,1,0:T(8,128)(2,1)S(1)}, bf16[2,272,128]{2,1,0:T(8,128)(2,1)S(1)}, u32[]{:S(2)}, u32[]{:S(2)}) collective-permute-start(bf16[2,272,128]{2,1,0:T(8,128)(2,1)S(1)} %get-tuple-element.21.refs_0_), channel_id=1, source_target_pairs={{0,2},{1,3},{2,0},{3,1},{4,6},{5,7},{6,4},{7,5},{8,10},{9,11},{10,... | collective-permute-start | bytes 417800 | tf_op jit(solution)/shard_map/ppermute | solution.py:287
  28.4 5.9 %collective-permute-start.8 = (bf16[2,272,128]{2,1,0:T(8,128)(2,1)S(1)}, bf16[2,272,128]{2,1,0:T(8,128)(2,1)S(1)}, u32[]{:S(2)}, u32[]{:S(2)}) collective-permute-start(bf16[2,272,128]{2,1,0:T(8,128)(2,1)S(1)} %get-tuple-element.21.refs_0_), channel_id=1, source_target_pairs={{0,1},{1,0},{2,3},{3,2},{4,5},{5,4},{6,7},{7,6},{8,9},{9,8},{10,11... | collective-permute-start | bytes 417800 | tf_op jit(solution)/shard_map/ppermute | solution.py:287
  31.4 2.9 %collective-permute-start.11 = (bf16[2,272,128]{2,1,0:T(8,128)(2,1)S(1)}, bf16[2,272,128]{2,1,0:T(8,128)(2,1)S(1)}, u32[]{:S(2)}, u32[]{:S(2)}) collective-permute-start(bf16[2,272,128]{2,1,0:T(8,128)(2,1)S(1)} %collective-permute-done.7.refs_3_), channel_id=1, source_target_pairs={{0,1},{1,0},{2,3},{3,2},{4,5},{5,4},{6,7},{7,6},{8,9},{9,8},{10,11... | collective-permute-start | bytes 417800 | tf_op jit(solution)/shard_map/ppermute | solution.py:287
  33.8 1.4 %collective-permute-start.9 = (bf16[2,272,128]{2,1,0:T(8,128)(2,1)S(1)}, bf16[2,272,128]{2,1,0:T(8,128)(2,1)S(1)}, u32[]{:S(2)}, u32[]{:S(2)}) collective-permute-start(bf16[2,272,128]{2,1,0:T(8,128)(2,1)S(1)} %collective-permute-done.5.refs_1_), channel_id=1, source_target_pairs={{0,1},{1,0},{2,3},{3,2},{4,5},{5,4},{6,7},{7,6},{8,9},{9,8},{10,11... | collective-permute-start | bytes 417800 | tf_op jit(solution)/shard_map/ppermute | solution.py:287
  33.8 1.6 %collective-permute-start.10 = (bf16[2,272,128]{2,1,0:T(8,128)(2,1)S(1)}, bf16[2,272,128]{2,1,0:T(8,128)(2,1)S(1)}, u32[]{:S(2)}, u32[]{:S(2)}) collective-permute-start(bf16[2,272,128]{2,1,0:T(8,128)(2,1)S(1)} %collective-permute-done.6.refs_2_), channel_id=1, source_target_pairs={{0,1},{1,0},{2,3},{3,2},{4,5},{5,4},{6,7},{7,6},{8,9},{9,8},{10,11... | collective-permute-start | bytes 417800 | tf_op jit(solution)/shard_map/ppermute | solution.py:287

commit v13 on v7

--- a/solution.py
+++ b/solution.py
@@ -228,13 +228,11 @@
     )(probe, kern, jnp.asarray(left), jnp.asarray(right), code, *measured, *windows)
 
 
-def place_kernel(*refs):
-    block_refs, (out_ref, canvas) = refs[:-2], refs[-2:]
-    _, stripe, cols = out_ref.shape
+def add_blocks(block_refs, canvas, stripe):
     count, _, window = block_refs[0].shape
+    cols = canvas.shape[-1] - 128
     wide = window + 128
     first_row = lax.axis_index("dp") * stripe
-    canvas[:, window : window + stripe, :] = jnp.zeros((2, stripe, canvas.shape[2]), f32)
     corners = []
     for block_ref in block_refs:
         for p in range(count):
@@ -259,22 +257,46 @@
                 put = (part, pl.ds(row_base, window + 8), pl.ds(col_base, wide))
                 canvas[put] = canvas[put] + block
 
+
+def first_kernel(stripe, *refs):
+    block_refs, canvas = refs[:-1], refs[-1]
+    window = block_refs[0].shape[-1]
+    canvas[:, window : window + stripe, :] = jnp.zeros((2, stripe, canvas.shape[2]), f32)
+    add_blocks(block_refs, canvas, stripe)
+
+
+def second_kernel(start_ref, *refs):
+    block_refs, (out_ref, canvas) = refs[:-2], refs[-2:]
+    _, stripe, cols = out_ref.shape
+    window = block_refs[0].shape[-1]
+    canvas[:, window : window + stripe, :] = start_ref[:, window : window + stripe, :]
+    add_blocks(block_refs, canvas, stripe)
     out_ref[...] = canvas[:, window : window + stripe, :cols]
 
 
-def place_windows(blocks, stripe, cols):
-    window = blocks[0].shape[-1]
+def place_windows(near, far, stripe, cols):
+    window = near[0].shape[-1]
     vmem = pl.BlockSpec(memory_space=pltpu.VMEM)
     tall = window + (stripe + 7) // 8 * 8 + window + 8
+    canvas = (2, tall, cols + 128)
+    limit = pltpu.CompilerParams(vmem_limit_bytes=24 * 1024 * 1024)
+    start = pl.pallas_call(
+        functools.partial(first_kernel, stripe),
+        out_shape=jax.ShapeDtypeStruct(canvas, f32),
+        in_specs=[vmem] * len(near),
+        out_specs=vmem,
+        compiler_params=limit,
+        name="place_near",
+    )(*near)
     return pl.pallas_call(
-        place_kernel,
+        second_kernel,
         out_shape=jax.ShapeDtypeStruct((2, stripe, cols), f32),
-        in_specs=[vmem] * len(blocks),
+        in_specs=[vmem] * (1 + len(far)),
         out_specs=vmem,
-        scratch_shapes=[pltpu.VMEM((2, tall, cols + 128), f32)],
-        compiler_params=pltpu.CompilerParams(vmem_limit_bytes=48 * 1024 * 1024),
-        name="place_windows",
-    )(*blocks)
+        scratch_shapes=[pltpu.VMEM(canvas, f32)],
+        compiler_params=limit,
+        name="place_far",
+    )(start, *far)
 
 
 def swap(block, depth_distance, dp_distance):
@@ -308,8 +330,7 @@
         for plane in range(0, members, 2)
         for m in range(0, depth, 2)
     ]
-    blocks += [swap(block, 0, 1) for block in blocks]
-    return place_windows(blocks, rows // dp, cols)[None]
+    return place_windows(blocks, [swap(block, 0, 1) for block in blocks], rows // dp, cols)[None]
 
 
 def solution(mesh):

time: 37 us -> 36.6 us (0.989)
    pallas_call x1 -> x2, Pallas kernels: 1.61 us -> 1.41 us  [the longest x1 1.13 us: place_windows(): pl.pallas_call(second_kernel, out_shape=jax.ShapeDtypeStruct((2, stripe,...]
  transfers between devices with their start and end apart: 12 -> 12, of which waited for: 6 -> 6; matrix products, arithmetic and copies ran while one was open for 1% -> 1% of each run, Pallas kernels for 5% -> 6%
where the time goes in v13:
time: 36.6 us; the launch traced here: 36.5 us
  waiting for transfers between devices  12 us (33%)
  starting transfers between devices  11.2 us (31%)
  Pallas kernels  10.2 us (28%)
  local copies, waits for them, and re-layouts  2.88 us (8%)
    ppermute x12, waiting for transfers between devices, swap(): return lax.ppermute(block, ('depth', 'dp'), route)  12 us
    ppermute x12, starting transfers between devices, swap(): return lax.ppermute(block, ('depth', 'dp'), route)  11.2 us
    pallas_call x1, Pallas kernels, run_waves(): pl.pallas_call(functools.partial(wave_kernel, members, len(measured)), ou...  7.06 us
    unnamed x14, local copies, waits for them, and re-layouts  2.64 us
    pallas_call x1, Pallas kernels, take_windows(): pl.pallas_call(functools.partial(window_kernel, members), out_shape=[jax....  1.45 us
    pallas_call x1, Pallas kernels, place_windows(): pl.pallas_call(second_kernel, out_shape=jax.ShapeDtypeStruct((2, stripe,...  1.13 us
  transfers between devices with their start and end apart: 12, of which 6 were waited for; matrix products, arithmetic and copies ran while one was open for 1% of the time, Pallas kernels for 6%

profile of v13, /device:TPU:0, one launch (start us, length us, event | category | flops | bytes accessed | tf_op | source)
XLA Modules:
  0.0 36.5 jit_solution(4263992495039501738)
XLA Ops:
  0.0 4.0 %collective-permute-start = (s32[2,2]{1,0:T(2,128)}, s32[2,2]{1,0:T(2,128)S(1)}, u32[]{:S(2)}, u32[]{:S(2)}) collective-permute-start(s32[2,2]{1,0:T(2,128)} %rest_0_.2), channel_id=1, source_target_pairs={{0,4},{1,5},{2,6},{3,7},{4,0},{5,1},{6,2},{7,3},{8,12},{9,13},{10,... | collective-permute-start | bytes 56 | tf_op jit(solution)/shard_map/ppermute | solution.py:309
  4.0 0.0 collective-permute-start.1
  4.1 2.3 %copy-done = f32[1,2,768,768]{3,2,1,0:T(8,128)S(1)} copy-done((f32[1,2,768,768]{3,2,1,0:T(8,128)S(1)}, f32[1,2,768,768]{3,2,1,0:T(8,128)}, u32[]{:S(2)}) %copy-start) | copy-done | bytes 4718616
  6.4 0.3 fetch_slice.1.obj_ref
  6.8 0.0 copy-start.1
  6.8 0.0 copy-start.2
  6.8 0.3 copy-done.5
  7.1 1.5 %take_windows.1 = (bf16[2,2,128,128]{3,2,1,0:T(8,128)(2,1)S(1)}, bf16[2,2,128,128]{3,2,1,0:T(8,128)(2,1)S(1)}, bf16[2,16,128]{2,1,0:T(8,128)(2,1)S(1)}) custom-call(f32[2,768,768]{2,1,0:T(8,128)S(1)} %fetch_slice.1.obj_ref, s32[2,2]{1,0:T(2,128)S(1)} %copy-done.5, s32[2,2]{1,0:T(2,128)S(1)} %collective-permute-done.rest_1_), custom_call_target="tpu_custom_call" | custom-call | tf_op jit(solution)/shard_map/take_windows/pallas_call | solution.py:110
  8.5 1.9 %collective-permute-start.3 = (bf16[2,2,128,128]{3,2,1,0:T(8,128)(2,1)S(1)}, bf16[2,2,128,128]{3,2,1,0:T(8,128)(2,1)S(1)}, u32[]{:S(2)}, u32[]{:S(2)}) collective-permute-start(bf16[2,2,128,128]{3,2,1,0:T(8,128)(2,1)S(1)} %get-tuple-element.16), channel_id=1, source_target_pairs={{0,16},{1,17},{2,18},{3,19},{4,20},{5,21},{6,22},{7,23},{8,24},{9,... | collective-permute-start | bytes 393224 | tf_op jit(solution)/shard_map/ppermute | solution.py:309
  10.4 1.4 %collective-permute-start.4 = (bf16[2,2,128,128]{3,2,1,0:T(8,128)(2,1)S(1)}, bf16[2,2,128,128]{3,2,1,0:T(8,128)(2,1)S(1)}, u32[]{:S(2)}, u32[]{:S(2)}) collective-permute-start(bf16[2,2,128,128]{3,2,1,0:T(8,128)(2,1)S(1)} %get-tuple-element.16), channel_id=1, source_target_pairs={{0,24},{1,25},{2,26},{3,27},{4,28},{5,29},{6,30},{7,31},{8,16},{9,... | collective-permute-start | bytes 393224 | tf_op jit(solution)/shard_map/ppermute | solution.py:309
  11.9 0.2 collective-permute-start.2
  12.1 0.2 cosine_bitcast_fusion
  12.4 0.5 %collective-permute-done.1.rest_1_ = f32[2,128,128]{2,1,0:T(8,128)S(1)} collective-permute-done((f32[2,128,128]{2,1,0:T(8,128)}, f32[2,128,128]{2,1,0:T(8,128)S(1)}, u32[]{:S(2)}, u32[]{:S(2)}) %collective-permute-start.1) | collective-permute-done | bytes 131104 | tf_op jit(solution)/shard_map/ppermute | solution.py:309
  12.9 4.7 %collective-permute-done.2.rest_3_ = bf16[2,2,128,128]{3,2,1,0:T(8,128)(2,1)S(1)} collective-permute-done((bf16[2,2,128,128]{3,2,1,0:T(8,128)(2,1)S(1)}, bf16[2,2,128,128]{3,2,1,0:T(8,128)(2,1)S(1)}, u32[]{:S(2)}, u32[]{:S(2)}) %collective-permute-start.2) | collective-permute-done | bytes 131104 | tf_op jit(solution)/shard_map/ppermute | solution.py:309
  17.7 7.1 %run_waves.1 = (bf16[2,272,128]{2,1,0:T(8,128)(2,1)S(1)}, bf16[2,272,128]{2,1,0:T(8,128)(2,1)S(1)}) custom-call(f32[2,128,128]{2,1,0:T(8,128)S(1)} %copy-done.3, f32[2,128,128]{2,1,0:T(8,128)S(1)} %pad_maximum_fusion.kern_ref, bf16[2,256,768]{2,1,0:T(8,128)(2,1)S(1)} %copy-done.1, bf16[2,768,256]{2,1,0:T(8,128)(2,1)S(1)} %copy-done.2, ...), custom_call_target="tpu_custom_call" | custom-call | tf_op jit(solution)/shard_map/run_waves/pallas_call | solution.py:216
  24.7 1.7 %collective-permute-start.6 = (bf16[2,272,128]{2,1,0:T(8,128)(2,1)S(1)}, bf16[2,272,128]{2,1,0:T(8,128)(2,1)S(1)}, u32[]{:S(2)}, u32[]{:S(2)}) collective-permute-start(bf16[2,272,128]{2,1,0:T(8,128)(2,1)S(1)} %get-tuple-element.17.refs_0_), channel_id=1, source_target_pairs={{0,2},{1,3},{2,0},{3,1},{4,6},{5,7},{6,4},{7,5},{8,10},{9,11},{10,... | collective-permute-start | bytes 417800 | tf_op jit(solution)/shard_map/ppermute | solution.py:309
  26.4 1.4 %collective-permute-start.7 = (bf16[2,272,128]{2,1,0:T(8,128)(2,1)S(1)}, bf16[2,272,128]{2,1,0:T(8,128)(2,1)S(1)}, u32[]{:S(2)}, u32[]{:S(2)}) collective-permute-start(bf16[2,272,128]{2,1,0:T(8,128)(2,1)S(1)} %get-tuple-element.18), channel_id=1, source_target_pairs={{0,18},{1,19},{2,16},{3,17},{4,22},{5,23},{6,20},{7,21},{8,26},{9,... | collective-permute-start | bytes 417800 | tf_op jit(solution)/shard_map/ppermute | solution.py:309
  27.8 0.5 %collective-permute-start.5 = (bf16[2,272,128]{2,1,0:T(8,128)(2,1)S(1)}, bf16[2,272,128]{2,1,0:T(8,128)(2,1)S(1)}, u32[]{:S(2)}, u32[]{:S(2)}) collective-permute-start(bf16[2,272,128]{2,1,0:T(8,128)(2,1)S(1)} %get-tuple-element.18), channel_id=1, source_target_pairs={{0,16},{1,17},{2,18},{3,19},{4,20},{5,21},{6,22},{7,23},{8,24},{9,... | collective-permute-start | bytes 417800 | tf_op jit(solution)/shard_map/ppermute | solution.py:309
  28.3 2.5 %collective-permute-done.6.refs_2_ = bf16[2,272,128]{2,1,0:T(8,128)(2,1)S(1)} collective-permute-done((bf16[2,272,128]{2,1,0:T(8,128)(2,1)S(1)}, bf16[2,272,128]{2,1,0:T(8,128)(2,1)S(1)}, u32[]{:S(2)}, u32[]{:S(2)}) %collective-permute-start.6) | collective-permute-done | bytes 139296 | tf_op jit(solution)/shard_map/ppermute | solution.py:309
  30.7 1.8 %collective-permute-done.7.refs_3_ = bf16[2,272,128]{2,1,0:T(8,128)(2,1)S(1)} collective-permute-done((bf16[2,272,128]{2,1,0:T(8,128)(2,1)S(1)}, bf16[2,272,128]{2,1,0:T(8,128)(2,1)S(1)}, u32[]{:S(2)}, u32[]{:S(2)}) %collective-permute-start.7) | collective-permute-done | bytes 139296 | tf_op jit(solution)/shard_map/ppermute | solution.py:309
  32.6 1.4 %collective-permute-done.5.refs_1_ = bf16[2,272,128]{2,1,0:T(8,128)(2,1)S(1)} collective-permute-done((bf16[2,272,128]{2,1,0:T(8,128)(2,1)S(1)}, bf16[2,272,128]{2,1,0:T(8,128)(2,1)S(1)}, u32[]{:S(2)}, u32[]{:S(2)}) %collective-permute-start.5) | collective-permute-done | bytes 139296 | tf_op jit(solution)/shard_map/ppermute | solution.py:309
  34.0 0.3 place_near.1.start_ref
  34.3 1.0 %collective-permute-done.9.refs_1_ = bf16[2,272,128]{2,1,0:T(8,128)(2,1)S(1)} collective-permute-done((bf16[2,272,128]{2,1,0:T(8,128)(2,1)S(1)}, bf16[2,272,128]{2,1,0:T(8,128)(2,1)S(1)}, u32[]{:S(2)}, u32[]{:S(2)}) %collective-permute-start.9) | collective-permute-done | bytes 139296 | tf_op jit(solution)/shard_map/ppermute | solution.py:309
  35.3 1.1 %place_far.1 = f32[2,96,768]{2,1,0:T(8,128)} custom-call(f32[2,360,896]{2,1,0:T(8,128)S(1)} %place_near.1.start_ref, bf16[2,272,128]{2,1,0:T(8,128)(2,1)S(1)} %collective-permute-done.8.refs_0_, bf16[2,272,128]{2,1,0:T(8,128)(2,1)S(1)} %collective-permute-done.9.refs_1_, bf16[2,272,128]{2,1,0:T(8,128)(2,1)S(1)} %collective-permute-done.10.refs_2_, ...), custom_call_target="tpu_custom_call" | custom-call | tf_op jit(solution)/shard_map/place_far/pallas_call | solution.py:291
  (21 shorter events, 0.1 us)
Async XLA Ops:
  0.0 6.8 %collective-permute-start = (s32[2,2]{1,0:T(2,128)}, s32[2,2]{1,0:T(2,128)S(1)}, u32[]{:S(2)}, u32[]{:S(2)}) collective-permute-start(s32[2,2]{1,0:T(2,128)} %rest_0_.2), channel_id=1, source_target_pairs={{0,4},{1,5},{2,6},{3,7},{4,0},{5,1},{6,2},{7,3},{8,12},{9,13},{10,... | collective-permute-start | bytes 56 | tf_op jit(solution)/shard_map/ppermute | solution.py:309
  4.0 8.9 %collective-permute-start.1 = (f32[2,128,128]{2,1,0:T(8,128)}, f32[2,128,128]{2,1,0:T(8,128)S(1)}, u32[]{:S(2)}, u32[]{:S(2)}) collective-permute-start(f32[2,128,128]{2,1,0:T(8,128)} %rest_0_.3), channel_id=1, source_target_pairs={{0,4},{1,5},{2,6},{3,7},{4,0},{5,1},{6,2},{7,3},{8,12},{9,13},{10,... | collective-permute-start | bytes 393224 | tf_op jit(solution)/shard_map/ppermute | solution.py:309
  4.1 2.3 %copy-start = (f32[1,2,768,768]{3,2,1,0:T(8,128)S(1)}, f32[1,2,768,768]{3,2,1,0:T(8,128)}, u32[]{:S(2)}) copy-start(f32[1,2,768,768]{3,2,1,0:T(8,128)} %param.7) | copy-start | bytes 14155780
  6.4 0.7 %copy-start.5 = (s32[2,2]{1,0:T(2,128)S(1)}, s32[2,2]{1,0:T(2,128)}, u32[]{:S(2)}) copy-start(s32[2,2]{1,0:T(2,128)} %rest_0_.2) | copy-start | bytes 52
  6.7 5.4 %copy-start.6 = (f32[128,128]{1,0:T(8,128)S(1)}, f32[128,128]{1,0:T(8,128)}, u32[]{:S(2)}) copy-start(f32[128,128]{1,0:T(8,128)} %param.10) | copy-start | bytes 196612
  6.8 10.9 %copy-start.1 = (bf16[2,256,768]{2,1,0:T(8,128)(2,1)S(1)}, bf16[2,256,768]{2,1,0:T(8,128)(2,1)}, u32[]{:S(2)}) copy-start(bf16[2,256,768]{2,1,0:T(8,128)(2,1)} %constant.4.clone.left_ref) | copy-start | bytes 2359300
  6.8 10.9 %copy-start.2 = (bf16[2,768,256]{2,1,0:T(8,128)(2,1)S(1)}, bf16[2,768,256]{2,1,0:T(8,128)(2,1)}, u32[]{:S(2)}) copy-start(bf16[2,768,256]{2,1,0:T(8,128)(2,1)} %constant.5.clone.right_ref) | copy-start | bytes 2359300
  6.8 10.9 %copy-start.3 = (f32[2,128,128]{2,1,0:T(8,128)S(1)}, f32[2,128,128]{2,1,0:T(8,128)}, u32[]{:S(2)}) copy-start(f32[2,128,128]{2,1,0:T(8,128)} %probe_ref.1) | copy-start | bytes 393220
  6.8 10.9 %copy-start.4 = (f32[2,128,128]{2,1,0:T(8,128)S(1)}, f32[2,128,128]{2,1,0:T(8,128)}, u32[]{:S(2)}) copy-start(f32[2,128,128]{2,1,0:T(8,128)} %rest_0_.3) | copy-start | bytes 393220
  8.5 9.1 %collective-permute-start.3 = (bf16[2,2,128,128]{3,2,1,0:T(8,128)(2,1)S(1)}, bf16[2,2,128,128]{3,2,1,0:T(8,128)(2,1)S(1)}, u32[]{:S(2)}, u32[]{:S(2)}) collective-permute-start(bf16[2,2,128,128]{3,2,1,0:T(8,128)(2,1)S(1)} %get-tuple-element.16), channel_id=1, source_target_pairs={{0,16},{1,17},{2,18},{3,19},{4,20},{5,21},{6,22},{7,23},{8,24},{9,... | collective-permute-start | bytes 393224 | tf_op jit(solution)/shard_map/ppermute | solution.py:309
  10.4 7.2 %collective-permute-start.4 = (bf16[2,2,128,128]{3,2,1,0:T(8,128)(2,1)S(1)}, bf16[2,2,128,128]{3,2,1,0:T(8,128)(2,1)S(1)}, u32[]{:S(2)}, u32[]{:S(2)}) collective-permute-start(bf16[2,2,128,128]{3,2,1,0:T(8,128)(2,1)S(1)} %get-tuple-element.16), channel_id=1, source_target_pairs={{0,24},{1,25},{2,26},{3,27},{4,28},{5,29},{6,30},{7,31},{8,16},{9,... | collective-permute-start | bytes 393224 | tf_op jit(solution)/shard_map/ppermute | solution.py:309
  11.9 5.7 %collective-permute-start.2 = (bf16[2,2,128,128]{3,2,1,0:T(8,128)(2,1)S(1)}, bf16[2,2,128,128]{3,2,1,0:T(8,128)(2,1)S(1)}, u32[]{:S(2)}, u32[]{:S(2)}) collective-permute-start(bf16[2,2,128,128]{3,2,1,0:T(8,128)(2,1)S(1)} %get-tuple-element.15.rest_2_), channel_id=1, source_target_pairs={{0,8},{1,9},{2,10},{3,11},{4,12},{5,13},{6,14},{7,15},{8,0},{9,1},... | collective-permute-start | bytes 393224 | tf_op jit(solution)/shard_map/ppermute | solution.py:309
  24.7 6.0 %collective-permute-start.6 = (bf16[2,272,128]{2,1,0:T(8,128)(2,1)S(1)}, bf16[2,272,128]{2,1,0:T(8,128)(2,1)S(1)}, u32[]{:S(2)}, u32[]{:S(2)}) collective-permute-start(bf16[2,272,128]{2,1,0:T(8,128)(2,1)S(1)} %get-tuple-element.17.refs_0_), channel_id=1, source_target_pairs={{0,2},{1,3},{2,0},{3,1},{4,6},{5,7},{6,4},{7,5},{8,10},{9,11},{10,... | collective-permute-start | bytes 417800 | tf_op jit(solution)/shard_map/ppermute | solution.py:309
  26.4 6.2 %collective-permute-start.7 = (bf16[2,272,128]{2,1,0:T(8,128)(2,1)S(1)}, bf16[2,272,128]{2,1,0:T(8,128)(2,1)S(1)}, u32[]{:S(2)}, u32[]{:S(2)}) collective-permute-start(bf16[2,272,128]{2,1,0:T(8,128)(2,1)S(1)} %get-tuple-element.18), channel_id=1, source_target_pairs={{0,18},{1,19},{2,16},{3,17},{4,22},{5,23},{6,20},{7,21},{8,26},{9,... | collective-permute-start | bytes 417800 | tf_op jit(solution)/shard_map/ppermute | solution.py:309
  27.8 6.2 %collective-permute-start.5 = (bf16[2,272,128]{2,1,0:T(8,128)(2,1)S(1)}, bf16[2,272,128]{2,1,0:T(8,128)(2,1)S(1)}, u32[]{:S(2)}, u32[]{:S(2)}) collective-permute-start(bf16[2,272,128]{2,1,0:T(8,128)(2,1)S(1)} %get-tuple-element.18), channel_id=1, source_target_pairs={{0,16},{1,17},{2,18},{3,19},{4,20},{5,21},{6,22},{7,23},{8,24},{9,... | collective-permute-start | bytes 417800 | tf_op jit(solution)/shard_map/ppermute | solution.py:309
  28.3 6.0 %collective-permute-start.8 = (bf16[2,272,128]{2,1,0:T(8,128)(2,1)S(1)}, bf16[2,272,128]{2,1,0:T(8,128)(2,1)S(1)}, u32[]{:S(2)}, u32[]{:S(2)}) collective-permute-start(bf16[2,272,128]{2,1,0:T(8,128)(2,1)S(1)} %get-tuple-element.17.refs_0_), channel_id=1, source_target_pairs={{0,1},{1,0},{2,3},{3,2},{4,5},{5,4},{6,7},{7,6},{8,9},{9,8},{10,11... | collective-permute-start | bytes 417800 | tf_op jit(solution)/shard_map/ppermute | solution.py:309
  30.7 3.5 %collective-permute-start.10 = (bf16[2,272,128]{2,1,0:T(8,128)(2,1)S(1)}, bf16[2,272,128]{2,1,0:T(8,128)(2,1)S(1)}, u32[]{:S(2)}, u32[]{:S(2)}) collective-permute-start(bf16[2,272,128]{2,1,0:T(8,128)(2,1)S(1)} %collective-permute-done.6.refs_2_), channel_id=1, source_target_pairs={{0,1},{1,0},{2,3},{3,2},{4,5},{5,4},{6,7},{7,6},{8,9},{9,8},{10,11... | collective-permute-start | bytes 417800 | tf_op jit(solution)/shard_map/ppermute | solution.py:309
  32.6 1.7 %collective-permute-start.11 = (bf16[2,272,128]{2,1,0:T(8,128)(2,1)S(1)}, bf16[2,272,128]{2,1,0:T(8,128)(2,1)S(1)}, u32[]{:S(2)}, u32[]{:S(2)}) collective-permute-start(bf16[2,272,128]{2,1,0:T(8,128)(2,1)S(1)} %collective-permute-done.7.refs_3_), channel_id=1, source_target_pairs={{0,1},{1,0},{2,3},{3,2},{4,5},{5,4},{6,7},{7,6},{8,9},{9,8},{10,11... | collective-permute-start | bytes 417800 | tf_op jit(solution)/shard_map/ppermute | solution.py:309
  34.0 1.4 %collective-permute-start.9 = (bf16[2,272,128]{2,1,0:T(8,128)(2,1)S(1)}, bf16[2,272,128]{2,1,0:T(8,128)(2,1)S(1)}, u32[]{:S(2)}, u32[]{:S(2)}) collective-permute-start(bf16[2,272,128]{2,1,0:T(8,128)(2,1)S(1)} %collective-permute-done.5.refs_1_), channel_id=1, source_target_pairs={{0,1},{1,0},{2,3},{3,2},{4,5},{5,4},{6,7},{7,6},{8,9},{9,8},{10,11... | collective-permute-start | bytes 417800 | tf_op jit(solution)/shard_map/ppermute | solution.py:309

commit v14 on v9

--- a/solution.py
+++ b/solution.py
@@ -28,12 +28,14 @@
         parts.append((high, low))
     (ph, plo), (mh, mlo) = parts
     right = np.stack([np.concatenate([ph, ph, plo], 0), np.concatenate([mh, mh, mlo], 0)])
-    left = np.stack([mh, ph])
-    thin = np.concatenate([minus[:, :size] for minus in (mh, mh, mlo)], 1)
-    return jnp.asarray(thin), jnp.asarray(left), jnp.asarray(right)
+    left = np.stack([np.concatenate([mh, mh, mlo], 1), np.concatenate([ph, ph, plo], 1)])
+    return jnp.asarray(left), jnp.asarray(right)
 
 
 code_rows = 16
+
+limit = pltpu.CompilerParams(vmem_limit_bytes=32 * 1024 * 1024)
+vmem = pl.BlockSpec(memory_space=pltpu.VMEM)
 
 
 def fetch_kernel(obj_ref, out_ref, sem):
@@ -137,29 +139,28 @@
     return a[0] * b[0] + a[1] * b[1], a[0] * b[1] - a[1] * b[0]
 
 
-def transform(field, sign, tables, exact):
-    thin_ref, left_ref, right_ref = tables
-    re, im = field
-    size = re.shape[0]
-    if exact:
-        high, low = split(jnp.concatenate([re, im], axis=1))
-        x = jnp.concatenate([high, low, high], axis=0)
-        y = jnp.dot(thin_ref[...], x, preferred_element_type=f32)
-        cr, ci, sr, si = y[:size, :size], y[:size, size:], y[size:, :size], y[size:, size:]
-        re, im = (cr - si, ci + sr) if sign == 0 else (cr + si, ci - sr)
-        high, low = split(jnp.concatenate([re, im], axis=1))
-        x = jnp.concatenate([high, low, high], axis=1)
-        y = jnp.dot(x, right_ref[sign], preferred_element_type=f32)
-    else:
-        x = jnp.concatenate([re, im], axis=0).astype(bf16)
-        y = jnp.dot(left_ref[sign], x, preferred_element_type=f32)
-        x = jnp.concatenate([y[:size], y[size:]], axis=1).astype(bf16)
-        y = jnp.dot(x, right_ref[sign, : 2 * size], preferred_element_type=f32)
-    return y[:, :size], y[:, size:]
+def transform(fields, sign, tables, exact):
+    left_ref, right_ref = tables
+    size = fields[0][0].shape[0]
+
+    def passes(x, axis):
+        if not exact:
+            return x.astype(bf16)
+        high, low = split(x)
+        return jnp.concatenate([high, low, high], axis=axis)
+
+    x = passes(jnp.concatenate([jnp.concatenate(f, axis=0) for f in fields], axis=1), 0)
+    y = jnp.dot(left_ref[sign, :, : x.shape[0]], x, preferred_element_type=f32)
+    fields = [y[:, n * size : (n + 1) * size] for n in range(len(fields))]
+    fields = [jnp.concatenate([f[:size], f[size:]], axis=1) for f in fields]
+    x = passes(jnp.concatenate(fields, axis=0), 1)
+    y = jnp.dot(x, right_ref[sign, : x.shape[1]], preferred_element_type=f32)
+    fields = [y[n * size : (n + 1) * size] for n in range(len(fields))]
+    return [(f[:, :size], f[:, size:]) for f in fields]
 
 
 def forward_kernel(probe_ref, kern_ref, *rest):
-    tables, t_refs, (trans, waves) = rest[:3], rest[3:-2], rest[-2:]
+    tables, t_refs, (trans, waves) = rest[:2], rest[2:-2], rest[-2:]
     slices, count = trans.shape[:2]
     own = lax.axis_index("depth")
     everyone = range(count)
@@ -169,16 +170,17 @@
     psi = [(probe_ref[0], probe_ref[1])] * count
     for k in range(slices):
         field = [cmul((trans[k, p, 0].astype(f32), trans[k, p, 1].astype(f32)), psi[p]) for p in everyone]
-        psi = [transform(f, 1, tables, True) for f in field]
+        psi = transform(field, 1, tables, True)
         if k < slices - 1:
-            psi = [transform(cmul(kern, s), 0, tables, True) for s in psi]
+            psi = transform([cmul(kern, s) for s in psi], 0, tables, True)
         for p in everyone:
             waves[k, p, 0] = psi[p][0]
             waves[k, p, 1] = psi[p][1]
 
 
 def backward_kernel(members, clusters, probe_ref, kern_ref, code_ref, trans, waves, *rest):
-    tables, meas_refs, out_refs, (terms, meas) = rest[:3], rest[3 : 3 + clusters], rest[3 + clusters : -2], rest[-2:]
+    tables, meas_refs = rest[:2], rest[2 : 2 + clusters]
+    out_refs, (terms, meas) = rest[2 + clusters : -2], rest[-2:]
     slices, count, _, window, _ = trans.shape
     own, cluster = lax.axis_index("depth"), lax.div(lax.axis_index("dp"), members)
     everyone = range(count)
@@ -195,7 +197,7 @@
         scale = 2.0 * (re * re + im * im - meas[p])
         return scale * re, scale * im
 
-    returned = [transform(source(p), 0, tables, False) for p in everyone]
+    returned = transform([source(p) for p in everyone], 0, tables, False)
     for k in reversed(range(slices)):
         for p in everyone:
             wave = (waves[k - 1, p, 0], waves[k - 1, p, 1]) if k else (probe_ref[0], probe_ref[1])
@@ -207,15 +209,11 @@
                 cmul_conj((trans[k, p, 0].astype(f32), trans[k, p, 1].astype(f32)), returned[p])
                 for p in everyone
             ]
-            chi = [transform(c, 1, tables, False) for c in chi]
-            returned = [transform(cmul_conj(kern, c), 0, tables, False) for c in chi]
+            chi = transform(chi, 1, tables, False)
+            returned = transform([cmul_conj(kern, c) for c in chi], 0, tables, False)
     for n, out_ref in enumerate(out_refs):
         out_ref[:, : 2 * window] = terms[2 * n]
         out_ref[:, 2 * window :] = code_ref[...]
-
-
-limit = pltpu.CompilerParams(vmem_limit_bytes=32 * 1024 * 1024)
-vmem = pl.BlockSpec(memory_space=pltpu.VMEM)
 
 
 def run_forward(probe, kern, tables, windows):
@@ -226,7 +224,7 @@
             jax.ShapeDtypeStruct((slices,) + shape, bf16),
             jax.ShapeDtypeStruct((slices,) + shape, f32),
         ],
-        in_specs=[vmem] * (5 + slices),
+        in_specs=[vmem] * (4 + slices),
         out_specs=[vmem, vmem],
         compiler_params=limit,
         name="run_forward",
@@ -239,7 +237,7 @@
     return pl.pallas_call(
         functools.partial(backward_kernel, members, len(measured)),
         out_shape=[block] * (slices // 2),
-        in_specs=[vmem] * (8 + len(measured)),
+        in_specs=[vmem] * (7 + len(measured)),
         out_specs=[vmem] * (slices // 2),
         scratch_shapes=[
             pltpu.VMEM((slices, count, 2 * window, window), bf16),
@@ -250,13 +248,11 @@
     )(probe, kern, code, trans, waves, *tables, *measured)
 
 
-def place_kernel(*refs):
-    block_refs, (out_ref, canvas) = refs[:-2], refs[-2:]
-    _, stripe, cols = out_ref.shape
+def add_blocks(block_refs, canvas, stripe):
     count, _, window = block_refs[0].shape
+    cols = canvas.shape[-1] - 128
     wide = window + 128
     first_row = lax.axis_index("dp") * stripe
-    canvas[:, window : window + stripe, :] = jnp.zeros((2, stripe, canvas.shape[2]), f32)
     corners = []
     for block_ref in block_refs:
         for p in range(count):
@@ -281,22 +277,46 @@
                 put = (part, pl.ds(row_base, window + 8), pl.ds(col_base, wide))
                 canvas[put] = canvas[put] + block
 
+
+def first_kernel(stripe, *refs):
+    block_refs, canvas = refs[:-1], refs[-1]
+    window = block_refs[0].shape[-1]
+    canvas[:, window : window + stripe, :] = jnp.zeros((2, stripe, canvas.shape[2]), f32)
+    add_blocks(block_refs, canvas, stripe)
+
+
+def second_kernel(start_ref, *refs):
+    block_refs, (out_ref, canvas) = refs[:-2], refs[-2:]
+    _, stripe, cols = out_ref.shape
+    window = block_refs[0].shape[-1]
+    canvas[:, window : window + stripe, :] = start_ref[:, window : window + stripe, :]
+    add_blocks(block_refs, canvas, stripe)
     out_ref[...] = canvas[:, window : window + stripe, :cols]
 
 
-def place_windows(blocks, stripe, cols):
-    window = blocks[0].shape[-1]
+def place_windows(near, far, stripe, cols):
+    window = near[0].shape[-1]
     vmem = pl.BlockSpec(memory_space=pltpu.VMEM)
     tall = window + (stripe + 7) // 8 * 8 + window + 8
+    canvas = (2, tall, cols + 128)
+    limit = pltpu.CompilerParams(vmem_limit_bytes=24 * 1024 * 1024)
+    start = pl.pallas_call(
+        functools.partial(first_kernel, stripe),
+        out_shape=jax.ShapeDtypeStruct(canvas, f32),
+        in_specs=[vmem] * len(near),
+        out_specs=vmem,
+        compiler_params=limit,
+        name="place_near",
+    )(*near)
     return pl.pallas_call(
-        place_kernel,
+        second_kernel,
         out_shape=jax.ShapeDtypeStruct((2, stripe, cols), f32),
-        in_specs=[vmem] * len(blocks),
+        in_specs=[vmem] * (1 + len(far)),
         out_specs=vmem,
-        scratch_shapes=[pltpu.VMEM((2, tall, cols + 128), f32)],
-        compiler_params=pltpu.CompilerParams(vmem_limit_bytes=48 * 1024 * 1024),
-        name="place_windows",
-    )(*blocks)
+        scratch_shapes=[pltpu.VMEM(canvas, f32)],
+        compiler_params=limit,
+        name="place_far",
+    )(start, *far)
 
 
 def swap(block, depth_distance, dp_distance):
@@ -333,8 +353,7 @@
         for plane in range(0, members, 2)
         for m in range(0, depth, 2)
     ]
-    blocks += [swap(block, 0, 1) for block in blocks]
-    return place_windows(blocks, rows // dp, cols)[None]
+    return place_windows(blocks, [swap(block, 0, 1) for block in blocks], rows // dp, cols)[None]
 
 
 def solution(mesh):

time: 37.6 us -> 36.9 us (0.981)
  waiting for transfers between devices: 10.2 us -> 9.75 us
    pallas_call x1 -> x2, Pallas kernels: 1.35 us -> 1.8 us  [the longest x1 1.39 us: place_windows(): pl.pallas_call(second_kernel, out_shape=jax.ShapeDtypeStruct((2, stripe,...]
    ppermute x12, waiting for transfers between devices: 10.2 us -> 9.75 us  [swap(): return lax.ppermute(block, ('depth', 'dp'), route)]
    unnamed x16 -> x14, local copies, waits for them, and re-layouts: 2.64 us -> 2.64 us
where the time goes in v14:
time: 36.9 us; the launch traced here: 36.8 us
  starting transfers between devices  13.3 us (36%)
  Pallas kernels  10.7 us (29%)
  waiting for transfers between devices  9.75 us (26%)
  local copies, waits for them, and re-layouts  2.88 us (8%)
    ppermute x12, starting transfers between devices, swap(): return lax.ppermute(block, ('depth', 'dp'), route)  13.3 us
    ppermute x12, waiting for transfers between devices, swap(): return lax.ppermute(block, ('depth', 'dp'), route)  9.75 us
    pallas_call x1, Pallas kernels, run_forward(): pl.pallas_call(forward_kernel, out_shape=[jax.ShapeDtypeStruct((slices,)...  4.48 us
    pallas_call x1, Pallas kernels, run_backward(): pl.pallas_call(functools.partial(backward_kernel, members, len(measured))...  2.66 us
    unnamed x14, local copies, waits for them, and re-layouts  2.64 us
    pallas_call x1, Pallas kernels, take_windows(): pl.pallas_call(functools.partial(window_kernel, members), out_shape=[jax....  1.45 us
    pallas_call x1, Pallas kernels, place_windows(): pl.pallas_call(second_kernel, out_shape=jax.ShapeDtypeStruct((2, stripe,...  1.39 us
  transfers between devices with their start and end apart: 12, of which 6 were waited for; matrix products, arithmetic and copies ran while one was open for 1% of the time, Pallas kernels for 14%

profile of v14, /device:TPU:0, one launch (start us, length us, event | category | flops | bytes accessed | tf_op | source)
XLA Modules:
  0.0 36.8 jit_solution(16696859485957886918)
XLA Ops:
  0.0 4.0 %collective-permute-start = (s32[2,2]{1,0:T(2,128)}, s32[2,2]{1,0:T(2,128)S(1)}, u32[]{:S(2)}, u32[]{:S(2)}) collective-permute-start(s32[2,2]{1,0:T(2,128)} %rest_0_.3), channel_id=1, source_target_pairs={{0,4},{1,5},{2,6},{3,7},{4,0},{5,1},{6,2},{7,3},{8,12},{9,13},{10,... | collective-permute-start | bytes 56 | tf_op jit(solution)/shard_map/ppermute | solution.py:329
  4.0 2.3 %copy-done = f32[1,2,768,768]{3,2,1,0:T(8,128)S(1)} copy-done((f32[1,2,768,768]{3,2,1,0:T(8,128)S(1)}, f32[1,2,768,768]{3,2,1,0:T(8,128)}, u32[]{:S(2)}) %copy-start) | copy-done | bytes 4718616
  6.4 0.3 fetch_slice.1.obj_ref
  6.8 0.3 copy-done.5
  7.1 1.5 %take_windows.1 = (bf16[2,2,128,128]{3,2,1,0:T(8,128)(2,1)S(1)}, bf16[2,2,128,128]{3,2,1,0:T(8,128)(2,1)S(1)}, bf16[2,16,128]{2,1,0:T(8,128)(2,1)S(1)}) custom-call(f32[2,768,768]{2,1,0:T(8,128)S(1)} %fetch_slice.1.obj_ref, s32[2,2]{1,0:T(2,128)S(1)} %copy-done.5, s32[2,2]{1,0:T(2,128)S(1)} %collective-permute-done.rest_1_), custom_call_target="tpu_custom_call" | custom-call | tf_op jit(solution)/shard_map/take_windows/pallas_call | solution.py:113
  8.5 2.5 %collective-permute-start.3 = (bf16[2,2,128,128]{3,2,1,0:T(8,128)(2,1)S(1)}, bf16[2,2,128,128]{3,2,1,0:T(8,128)(2,1)S(1)}, u32[]{:S(2)}, u32[]{:S(2)}) collective-permute-start(bf16[2,2,128,128]{3,2,1,0:T(8,128)(2,1)S(1)} %get-tuple-element.21), channel_id=1, source_target_pairs={{0,24},{1,25},{2,26},{3,27},{4,28},{5,29},{6,30},{7,31},{8,16},{9,... | collective-permute-start | bytes 393224 | tf_op jit(solution)/shard_map/ppermute | solution.py:329
  11.0 0.5 %collective-permute-start.2 = (bf16[2,2,128,128]{3,2,1,0:T(8,128)(2,1)S(1)}, bf16[2,2,128,128]{3,2,1,0:T(8,128)(2,1)S(1)}, u32[]{:S(2)}, u32[]{:S(2)}) collective-permute-start(bf16[2,2,128,128]{3,2,1,0:T(8,128)(2,1)S(1)} %get-tuple-element.21), channel_id=1, source_target_pairs={{0,16},{1,17},{2,18},{3,19},{4,20},{5,21},{6,22},{7,23},{8,24},{9,... | collective-permute-start | bytes 393224 | tf_op jit(solution)/shard_map/ppermute | solution.py:329
  11.5 0.2 cosine_bitcast_fusion
  11.8 0.6 %collective-permute-start.1 = (bf16[2,2,128,128]{3,2,1,0:T(8,128)(2,1)S(1)}, bf16[2,2,128,128]{3,2,1,0:T(8,128)(2,1)S(1)}, u32[]{:S(2)}, u32[]{:S(2)}) collective-permute-start(bf16[2,2,128,128]{3,2,1,0:T(8,128)(2,1)S(1)} %get-tuple-element.20.rest_2_), channel_id=1, source_target_pairs={{0,8},{1,9},{2,10},{3,11},{4,12},{5,13},{6,14},{7,15},{8,0},{9,1},... | collective-permute-start | bytes 393224 | tf_op jit(solution)/shard_map/ppermute | solution.py:329
  12.4 1.7 %collective-permute-start.4 = (f32[2,128,128]{2,1,0:T(8,128)S(1)}, f32[2,128,128]{2,1,0:T(8,128)S(1)}, u32[]{:S(2)}, u32[]{:S(2)}) collective-permute-start(f32[2,128,128]{2,1,0:T(8,128)S(1)} %copy-done.4), channel_id=1, source_target_pairs={{0,4},{1,5},{2,6},{3,7},{4,0},{5,1},{6,2},{7,3},{8,12},{9,13},{10,... | collective-permute-start | bytes 393224 | tf_op jit(solution)/shard_map/ppermute | solution.py:329
  14.1 3.2 %collective-permute-done.1.rest_3_ = bf16[2,2,128,128]{3,2,1,0:T(8,128)(2,1)S(1)} collective-permute-done((bf16[2,2,128,128]{3,2,1,0:T(8,128)(2,1)S(1)}, bf16[2,2,128,128]{3,2,1,0:T(8,128)(2,1)S(1)}, u32[]{:S(2)}, u32[]{:S(2)}) %collective-permute-start.1) | collective-permute-done | bytes 131104 | tf_op jit(solution)/shard_map/ppermute | solution.py:329
  17.3 4.5 %run_forward.1 = (bf16[4,2,2,128,128]{4,3,2,1,0:T(8,128)(2,1)S(1)}, f32[4,2,2,128,128]{4,3,2,1,0:T(8,128)S(1)}) custom-call(f32[2,128,128]{2,1,0:T(8,128)S(1)} %copy-done.3, f32[2,128,128]{2,1,0:T(8,128)S(1)} %pad_maximum_fusion.kern_ref, bf16[2,256,768]{2,1,0:T(8,128)(2,1)S(1)} %copy-done.2, bf16[2,768,256]{2,1,0:T(8,128)(2,1)S(1)} %copy-done.1, ...), custom_call_target="tpu_custom_call" | custom-call | tf_op jit(solution)/shard_map/run_forward/pallas_call | solution.py:221
  21.8 2.7 %run_backward.1 = (bf16[2,272,128]{2,1,0:T(8,128)(2,1)S(1)}, bf16[2,272,128]{2,1,0:T(8,128)(2,1)S(1)}) custom-call(f32[2,128,128]{2,1,0:T(8,128)S(1)} %copy-done.3, f32[2,128,128]{2,1,0:T(8,128)S(1)} %pad_maximum_fusion.kern_ref, bf16[2,16,128]{2,1,0:T(8,128)(2,1)S(1)} %get-tuple-element.19.code_ref, ...), custom_call_target="tpu_custom_call" | custom-call | tf_op jit(solution)/shard_map/run_backward/pallas_call | solution.py:237
  24.5 2.5 %collective-permute-start.7 = (bf16[2,272,128]{2,1,0:T(8,128)(2,1)S(1)}, bf16[2,272,128]{2,1,0:T(8,128)(2,1)S(1)}, u32[]{:S(2)}, u32[]{:S(2)}) collective-permute-start(bf16[2,272,128]{2,1,0:T(8,128)(2,1)S(1)} %get-tuple-element.26), channel_id=1, source_target_pairs={{0,18},{1,19},{2,16},{3,17},{4,22},{5,23},{6,20},{7,21},{8,26},{9,... | collective-permute-start | bytes 417800 | tf_op jit(solution)/shard_map/ppermute | solution.py:329
  27.0 0.6 %collective-permute-start.5 = (bf16[2,272,128]{2,1,0:T(8,128)(2,1)S(1)}, bf16[2,272,128]{2,1,0:T(8,128)(2,1)S(1)}, u32[]{:S(2)}, u32[]{:S(2)}) collective-permute-start(bf16[2,272,128]{2,1,0:T(8,128)(2,1)S(1)} %get-tuple-element.26), channel_id=1, source_target_pairs={{0,16},{1,17},{2,18},{3,19},{4,20},{5,21},{6,22},{7,23},{8,24},{9,... | collective-permute-start | bytes 417800 | tf_op jit(solution)/shard_map/ppermute | solution.py:329
  27.6 0.4 %collective-permute-start.6 = (bf16[2,272,128]{2,1,0:T(8,128)(2,1)S(1)}, bf16[2,272,128]{2,1,0:T(8,128)(2,1)S(1)}, u32[]{:S(2)}, u32[]{:S(2)}) collective-permute-start(bf16[2,272,128]{2,1,0:T(8,128)(2,1)S(1)} %get-tuple-element.25.refs_0_), channel_id=1, source_target_pairs={{0,2},{1,3},{2,0},{3,1},{4,6},{5,7},{6,4},{7,5},{8,10},{9,11},{10,... | collective-permute-start | bytes 417800 | tf_op jit(solution)/shard_map/ppermute | solution.py:329
  28.1 3.2 %collective-permute-done.7.refs_3_ = bf16[2,272,128]{2,1,0:T(8,128)(2,1)S(1)} collective-permute-done((bf16[2,272,128]{2,1,0:T(8,128)(2,1)S(1)}, bf16[2,272,128]{2,1,0:T(8,128)(2,1)S(1)}, u32[]{:S(2)}, u32[]{:S(2)}) %collective-permute-start.7) | collective-permute-done | bytes 139296 | tf_op jit(solution)/shard_map/ppermute | solution.py:329
  31.3 2.6 %collective-permute-done.5.refs_1_ = bf16[2,272,128]{2,1,0:T(8,128)(2,1)S(1)} collective-permute-done((bf16[2,272,128]{2,1,0:T(8,128)(2,1)S(1)}, bf16[2,272,128]{2,1,0:T(8,128)(2,1)S(1)}, u32[]{:S(2)}, u32[]{:S(2)}) %collective-permute-start.5) | collective-permute-done | bytes 139296 | tf_op jit(solution)/shard_map/ppermute | solution.py:329
  33.9 0.1 collective-permute-done.6.refs_2_
  34.0 0.4 %collective-permute-start.10 = (bf16[2,272,128]{2,1,0:T(8,128)(2,1)S(1)}, bf16[2,272,128]{2,1,0:T(8,128)(2,1)S(1)}, u32[]{:S(2)}, u32[]{:S(2)}) collective-permute-start(bf16[2,272,128]{2,1,0:T(8,128)(2,1)S(1)} %collective-permute-done.6.refs_2_), channel_id=1, source_target_pairs={{0,1},{1,0},{2,3},{3,2},{4,5},{5,4},{6,7},{7,6},{8,9},{9,8},{10,11... | collective-permute-start | bytes 417800 | tf_op jit(solution)/shard_map/ppermute | solution.py:329
  34.4 0.4 %place_near.1.start_ref = f32[2,360,896]{2,1,0:T(8,128)S(1)} custom-call(bf16[2,272,128]{2,1,0:T(8,128)(2,1)S(1)} %get-tuple-element.25.refs_0_, bf16[2,272,128]{2,1,0:T(8,128)(2,1)S(1)} %collective-permute-done.5.refs_1_, bf16[2,272,128]{2,1,0:T(8,128)(2,1)S(1)} %collective-permute-done.6.refs_2_, bf16[2,272,128]{2,1,0:T(8,128)(2,1)S(1)} %collective-permute-done.7.refs_3_), custom_call_target="tpu_custom_call" | custom-call | tf_op jit(solution)/shard_map/place_near/pallas_call | solution.py:303
  34.8 0.4 %collective-permute-done.9.refs_1_ = bf16[2,272,128]{2,1,0:T(8,128)(2,1)S(1)} collective-permute-done((bf16[2,272,128]{2,1,0:T(8,128)(2,1)S(1)}, bf16[2,272,128]{2,1,0:T(8,128)(2,1)S(1)}, u32[]{:S(2)}, u32[]{:S(2)}) %collective-permute-start.9) | collective-permute-done | bytes 139296 | tf_op jit(solution)/shard_map/ppermute | solution.py:329
  35.3 0.2 collective-permute-done.10.refs_2_
  35.5 1.4 %place_far.1 = f32[2,96,768]{2,1,0:T(8,128)} custom-call(f32[2,360,896]{2,1,0:T(8,128)S(1)} %place_near.1.start_ref, bf16[2,272,128]{2,1,0:T(8,128)(2,1)S(1)} %collective-permute-done.8.refs_0_, bf16[2,272,128]{2,1,0:T(8,128)(2,1)S(1)} %collective-permute-done.9.refs_1_, bf16[2,272,128]{2,1,0:T(8,128)(2,1)S(1)} %collective-permute-done.10.refs_2_, ...), custom_call_target="tpu_custom_call" | custom-call | tf_op jit(solution)/shard_map/place_far/pallas_call | solution.py:311
  (22 shorter events, 0.1 us)
Async XLA Ops:
  0.0 6.8 %collective-permute-start = (s32[2,2]{1,0:T(2,128)}, s32[2,2]{1,0:T(2,128)S(1)}, u32[]{:S(2)}, u32[]{:S(2)}) collective-permute-start(s32[2,2]{1,0:T(2,128)} %rest_0_.3), channel_id=1, source_target_pairs={{0,4},{1,5},{2,6},{3,7},{4,0},{5,1},{6,2},{7,3},{8,12},{9,13},{10,... | collective-permute-start | bytes 56 | tf_op jit(solution)/shard_map/ppermute | solution.py:329
  4.0 2.3 %copy-start = (f32[1,2,768,768]{3,2,1,0:T(8,128)S(1)}, f32[1,2,768,768]{3,2,1,0:T(8,128)}, u32[]{:S(2)}) copy-start(f32[1,2,768,768]{3,2,1,0:T(8,128)} %param.7) | copy-start | bytes 14155780
  6.4 0.7 %copy-start.5 = (s32[2,2]{1,0:T(2,128)S(1)}, s32[2,2]{1,0:T(2,128)}, u32[]{:S(2)}) copy-start(s32[2,2]{1,0:T(2,128)} %rest_0_.3) | copy-start | bytes 52
  6.7 4.8 %copy-start.6 = (f32[128,128]{1,0:T(8,128)S(1)}, f32[128,128]{1,0:T(8,128)}, u32[]{:S(2)}) copy-start(f32[128,128]{1,0:T(8,128)} %param.10) | copy-start | bytes 196612
  6.7 5.7 %copy-start.4 = (f32[2,128,128]{2,1,0:T(8,128)S(1)}, f32[2,128,128]{2,1,0:T(8,128)}, u32[]{:S(2)}) copy-start(f32[2,128,128]{2,1,0:T(8,128)} %rest_2_.1) | copy-start | bytes 393220
  6.7 10.6 %copy-start.1 = (bf16[2,768,256]{2,1,0:T(8,128)(2,1)S(1)}, bf16[2,768,256]{2,1,0:T(8,128)(2,1)}, u32[]{:S(2)}) copy-start(bf16[2,768,256]{2,1,0:T(8,128)(2,1)} %constant.5.clone.rest_1_) | copy-start | bytes 2359300
  6.7 10.6 %copy-start.2 = (bf16[2,256,768]{2,1,0:T(8,128)(2,1)S(1)}, bf16[2,256,768]{2,1,0:T(8,128)(2,1)}, u32[]{:S(2)}) copy-start(bf16[2,256,768]{2,1,0:T(8,128)(2,1)} %constant.4.clone.rest_0_) | copy-start | bytes 2359300
  6.8 10.6 %copy-start.3 = (f32[2,128,128]{2,1,0:T(8,128)S(1)}, f32[2,128,128]{2,1,0:T(8,128)}, u32[]{:S(2)}) copy-start(f32[2,128,128]{2,1,0:T(8,128)} %probe_ref.3) | copy-start | bytes 393220
  8.5 8.8 %collective-permute-start.3 = (bf16[2,2,128,128]{3,2,1,0:T(8,128)(2,1)S(1)}, bf16[2,2,128,128]{3,2,1,0:T(8,128)(2,1)S(1)}, u32[]{:S(2)}, u32[]{:S(2)}) collective-permute-start(bf16[2,2,128,128]{3,2,1,0:T(8,128)(2,1)S(1)} %get-tuple-element.21), channel_id=1, source_target_pairs={{0,24},{1,25},{2,26},{3,27},{4,28},{5,29},{6,30},{7,31},{8,16},{9,... | collective-permute-start | bytes 393224 | tf_op jit(solution)/shard_map/ppermute | solution.py:329
  11.0 6.3 %collective-permute-start.2 = (bf16[2,2,128,128]{3,2,1,0:T(8,128)(2,1)S(1)}, bf16[2,2,128,128]{3,2,1,0:T(8,128)(2,1)S(1)}, u32[]{:S(2)}, u32[]{:S(2)}) collective-permute-start(bf16[2,2,128,128]{3,2,1,0:T(8,128)(2,1)S(1)} %get-tuple-element.21), channel_id=1, source_target_pairs={{0,16},{1,17},{2,18},{3,19},{4,20},{5,21},{6,22},{7,23},{8,24},{9,... | collective-permute-start | bytes 393224 | tf_op jit(solution)/shard_map/ppermute | solution.py:329
  11.8 5.5 %collective-permute-start.1 = (bf16[2,2,128,128]{3,2,1,0:T(8,128)(2,1)S(1)}, bf16[2,2,128,128]{3,2,1,0:T(8,128)(2,1)S(1)}, u32[]{:S(2)}, u32[]{:S(2)}) collective-permute-start(bf16[2,2,128,128]{3,2,1,0:T(8,128)(2,1)S(1)} %get-tuple-element.20.rest_2_), channel_id=1, source_target_pairs={{0,8},{1,9},{2,10},{3,11},{4,12},{5,13},{6,14},{7,15},{8,0},{9,1},... | collective-permute-start | bytes 393224 | tf_op jit(solution)/shard_map/ppermute | solution.py:329
  12.4 9.4 %collective-permute-start.4 = (f32[2,128,128]{2,1,0:T(8,128)S(1)}, f32[2,128,128]{2,1,0:T(8,128)S(1)}, u32[]{:S(2)}, u32[]{:S(2)}) collective-permute-start(f32[2,128,128]{2,1,0:T(8,128)S(1)} %copy-done.4), channel_id=1, source_target_pairs={{0,4},{1,5},{2,6},{3,7},{4,0},{5,1},{6,2},{7,3},{8,12},{9,13},{10,... | collective-permute-start | bytes 393224 | tf_op jit(solution)/shard_map/ppermute | solution.py:329
  24.5 6.8 %collective-permute-start.7 = (bf16[2,272,128]{2,1,0:T(8,128)(2,1)S(1)}, bf16[2,272,128]{2,1,0:T(8,128)(2,1)S(1)}, u32[]{:S(2)}, u32[]{:S(2)}) collective-permute-start(bf16[2,272,128]{2,1,0:T(8,128)(2,1)S(1)} %get-tuple-element.26), channel_id=1, source_target_pairs={{0,18},{1,19},{2,16},{3,17},{4,22},{5,23},{6,20},{7,21},{8,26},{9,... | collective-permute-start | bytes 417800 | tf_op jit(solution)/shard_map/ppermute | solution.py:329
  27.0 6.9 %collective-permute-start.5 = (bf16[2,272,128]{2,1,0:T(8,128)(2,1)S(1)}, bf16[2,272,128]{2,1,0:T(8,128)(2,1)S(1)}, u32[]{:S(2)}, u32[]{:S(2)}) collective-permute-start(bf16[2,272,128]{2,1,0:T(8,128)(2,1)S(1)} %get-tuple-element.26), channel_id=1, source_target_pairs={{0,16},{1,17},{2,18},{3,19},{4,20},{5,21},{6,22},{7,23},{8,24},{9,... | collective-permute-start | bytes 417800 | tf_op jit(solution)/shard_map/ppermute | solution.py:329
  27.6 6.4 %collective-permute-start.6 = (bf16[2,272,128]{2,1,0:T(8,128)(2,1)S(1)}, bf16[2,272,128]{2,1,0:T(8,128)(2,1)S(1)}, u32[]{:S(2)}, u32[]{:S(2)}) collective-permute-start(bf16[2,272,128]{2,1,0:T(8,128)(2,1)S(1)} %get-tuple-element.25.refs_0_), channel_id=1, source_target_pairs={{0,2},{1,3},{2,0},{3,1},{4,6},{5,7},{6,4},{7,5},{8,10},{9,11},{10,... | collective-permute-start | bytes 417800 | tf_op jit(solution)/shard_map/ppermute | solution.py:329
  28.1 6.8 %collective-permute-start.8 = (bf16[2,272,128]{2,1,0:T(8,128)(2,1)S(1)}, bf16[2,272,128]{2,1,0:T(8,128)(2,1)S(1)}, u32[]{:S(2)}, u32[]{:S(2)}) collective-permute-start(bf16[2,272,128]{2,1,0:T(8,128)(2,1)S(1)} %get-tuple-element.25.refs_0_), channel_id=1, source_target_pairs={{0,1},{1,0},{2,3},{3,2},{4,5},{5,4},{6,7},{7,6},{8,9},{9,8},{10,11... | collective-permute-start | bytes 417800 | tf_op jit(solution)/shard_map/ppermute | solution.py:329
  31.3 3.6 %collective-permute-start.11 = (bf16[2,272,128]{2,1,0:T(8,128)(2,1)S(1)}, bf16[2,272,128]{2,1,0:T(8,128)(2,1)S(1)}, u32[]{:S(2)}, u32[]{:S(2)}) collective-permute-start(bf16[2,272,128]{2,1,0:T(8,128)(2,1)S(1)} %collective-permute-done.7.refs_3_), channel_id=1, source_target_pairs={{0,1},{1,0},{2,3},{3,2},{4,5},{5,4},{6,7},{7,6},{8,9},{9,8},{10,11... | collective-permute-start | bytes 417800 | tf_op jit(solution)/shard_map/ppermute | solution.py:329
  33.9 1.4 %collective-permute-start.9 = (bf16[2,272,128]{2,1,0:T(8,128)(2,1)S(1)}, bf16[2,272,128]{2,1,0:T(8,128)(2,1)S(1)}, u32[]{:S(2)}, u32[]{:S(2)}) collective-permute-start(bf16[2,272,128]{2,1,0:T(8,128)(2,1)S(1)} %collective-permute-done.5.refs_1_), channel_id=1, source_target_pairs={{0,1},{1,0},{2,3},{3,2},{4,5},{5,4},{6,7},{7,6},{8,9},{9,8},{10,11... | collective-permute-start | bytes 417800 | tf_op jit(solution)/shard_map/ppermute | solution.py:329
  34.0 1.4 %collective-permute-start.10 = (bf16[2,272,128]{2,1,0:T(8,128)(2,1)S(1)}, bf16[2,272,128]{2,1,0:T(8,128)(2,1)S(1)}, u32[]{:S(2)}, u32[]{:S(2)}) collective-permute-start(bf16[2,272,128]{2,1,0:T(8,128)(2,1)S(1)} %collective-permute-done.6.refs_2_), channel_id=1, source_target_pairs={{0,1},{1,0},{2,3},{3,2},{4,5},{5,4},{6,7},{7,6},{8,9},{9,8},{10,11... | collective-permute-start | bytes 417800 | tf_op jit(solution)/shard_map/ppermute | solution.py:329

commit v15 on v14

--- a/solution.py
+++ b/solution.py
@@ -340,7 +340,8 @@
     all_positions = [positions] + [swap(positions, 0, home) for home in homes]
     windows, code = take_windows(fetch(object_slices[0]), all_positions, window, members)
     phase, code = lax.optimization_barrier((propagator_phase, code))
-    windows = [windows[0]] + [swap(windows[m // 2], m, 0) for m in range(1, depth)]
+    arrivals = [swap(windows[m // 2], m, 0) for m in reversed(range(1, depth))]
+    windows = [windows[0]] + arrivals[::-1]
     kern = jnp.stack([jnp.cos(phase), jnp.sin(phase)])
     kern, late = lax.optimization_barrier((kern, measured))
     targets = [measured] + [swap(late, 0, home) for home in homes]
@@ -350,8 +351,8 @@
 
     blocks = [
         swap(terms[m // 2], m, plane) if m or plane else terms[0]
-        for plane in range(0, members, 2)
-        for m in range(0, depth, 2)
+        for plane in reversed(range(0, members, 2))
+        for m in reversed(range(0, depth, 2))
     ]
     return place_windows(blocks, [swap(block, 0, 1) for block in blocks], rows // dp, cols)[None]
 

time: 36.9 us -> 36.9 us (level)
  waiting for transfers between devices: 9.75 us -> 10.3 us
  starting transfers between devices: 13.3 us -> 12.9 us
    ppermute x12, waiting for transfers between devices: 9.75 us -> 10.3 us  [swap(): return lax.ppermute(block, ('depth', 'dp'), route)]
    ppermute x12, starting transfers between devices: 13.3 us -> 12.9 us  [swap(): return lax.ppermute(block, ('depth', 'dp'), route)]
where the time goes in v15:
time: 36.9 us; the launch traced here: 36.7 us
  starting transfers between devices  12.9 us (35%)
  Pallas kernels  10.5 us (28%)
  waiting for transfers between devices  10.3 us (28%)
  local copies, waits for them, and re-layouts  2.88 us (8%)
    ppermute x12, starting transfers between devices, swap(): return lax.ppermute(block, ('depth', 'dp'), route)  12.9 us
    ppermute x12, waiting for transfers between devices, swap(): return lax.ppermute(block, ('depth', 'dp'), route)  10.3 us
    pallas_call x1, Pallas kernels, run_forward(): pl.pallas_call(forward_kernel, out_shape=[jax.ShapeDtypeStruct((slices,)...  4.47 us
    pallas_call x1, Pallas kernels, run_backward(): pl.pallas_call(functools.partial(backward_kernel, members, len(measured))...  2.66 us
    unnamed x14, local copies, waits for them, and re-layouts  2.64 us
    pallas_call x1, Pallas kernels, take_windows(): pl.pallas_call(functools.partial(window_kernel, members), out_shape=[jax....  1.46 us
    pallas_call x1, Pallas kernels, place_windows(): pl.pallas_call(second_kernel, out_shape=jax.ShapeDtypeStruct((2, stripe,...  1.13 us
  transfers between devices with their start and end apart: 12, of which 6 were waited for; matrix products, arithmetic and copies ran while one was open for 1% of the time, Pallas kernels for 14%

profile of v15, /device:TPU:0, one launch (start us, length us, event | category | flops | bytes accessed | tf_op | source)
XLA Modules:
  0.0 36.7 jit_solution(18177694120683314958)
XLA Ops:
  0.0 4.0 %collective-permute-start = (s32[2,2]{1,0:T(2,128)}, s32[2,2]{1,0:T(2,128)S(1)}, u32[]{:S(2)}, u32[]{:S(2)}) collective-permute-start(s32[2,2]{1,0:T(2,128)} %rest_0_.3), channel_id=1, source_target_pairs={{0,4},{1,5},{2,6},{3,7},{4,0},{5,1},{6,2},{7,3},{8,12},{9,13},{10,... | collective-permute-start | bytes 56 | tf_op jit(solution)/shard_map/ppermute | solution.py:329
  4.0 2.3 %copy-done = f32[1,2,768,768]{3,2,1,0:T(8,128)S(1)} copy-done((f32[1,2,768,768]{3,2,1,0:T(8,128)S(1)}, f32[1,2,768,768]{3,2,1,0:T(8,128)}, u32[]{:S(2)}) %copy-start) | copy-done | bytes 4718616
  6.4 0.3 fetch_slice.1.obj_ref
  6.7 0.0 copy-start.1
  6.8 0.3 copy-done.5
  7.1 1.5 %take_windows.1 = (bf16[2,2,128,128]{3,2,1,0:T(8,128)(2,1)S(1)}, bf16[2,2,128,128]{3,2,1,0:T(8,128)(2,1)S(1)}, bf16[2,16,128]{2,1,0:T(8,128)(2,1)S(1)}) custom-call(f32[2,768,768]{2,1,0:T(8,128)S(1)} %fetch_slice.1.obj_ref, s32[2,2]{1,0:T(2,128)S(1)} %copy-done.5, s32[2,2]{1,0:T(2,128)S(1)} %collective-permute-done.rest_1_), custom_call_target="tpu_custom_call" | custom-call | tf_op jit(solution)/shard_map/take_windows/pallas_call | solution.py:113
  8.5 2.5 %collective-permute-start.3 = (bf16[2,2,128,128]{3,2,1,0:T(8,128)(2,1)S(1)}, bf16[2,2,128,128]{3,2,1,0:T(8,128)(2,1)S(1)}, u32[]{:S(2)}, u32[]{:S(2)}) collective-permute-start(bf16[2,2,128,128]{3,2,1,0:T(8,128)(2,1)S(1)} %get-tuple-element.21), channel_id=1, source_target_pairs={{0,24},{1,25},{2,26},{3,27},{4,28},{5,29},{6,30},{7,31},{8,16},{9,... | collective-permute-start | bytes 393224 | tf_op jit(solution)/shard_map/ppermute | solution.py:329
  11.0 0.5 %collective-permute-start.2 = (bf16[2,2,128,128]{3,2,1,0:T(8,128)(2,1)S(1)}, bf16[2,2,128,128]{3,2,1,0:T(8,128)(2,1)S(1)}, u32[]{:S(2)}, u32[]{:S(2)}) collective-permute-start(bf16[2,2,128,128]{3,2,1,0:T(8,128)(2,1)S(1)} %get-tuple-element.21), channel_id=1, source_target_pairs={{0,16},{1,17},{2,18},{3,19},{4,20},{5,21},{6,22},{7,23},{8,24},{9,... | collective-permute-start | bytes 393224 | tf_op jit(solution)/shard_map/ppermute | solution.py:329
  11.5 0.2 cosine_bitcast_fusion
  11.8 0.6 %collective-permute-start.1 = (bf16[2,2,128,128]{3,2,1,0:T(8,128)(2,1)S(1)}, bf16[2,2,128,128]{3,2,1,0:T(8,128)(2,1)S(1)}, u32[]{:S(2)}, u32[]{:S(2)}) collective-permute-start(bf16[2,2,128,128]{3,2,1,0:T(8,128)(2,1)S(1)} %get-tuple-element.20.rest_2_), channel_id=1, source_target_pairs={{0,8},{1,9},{2,10},{3,11},{4,12},{5,13},{6,14},{7,15},{8,0},{9,1},... | collective-permute-start | bytes 393224 | tf_op jit(solution)/shard_map/ppermute | solution.py:329
  12.4 1.7 %collective-permute-start.4 = (f32[2,128,128]{2,1,0:T(8,128)S(1)}, f32[2,128,128]{2,1,0:T(8,128)S(1)}, u32[]{:S(2)}, u32[]{:S(2)}) collective-permute-start(f32[2,128,128]{2,1,0:T(8,128)S(1)} %copy-done.4), channel_id=1, source_target_pairs={{0,4},{1,5},{2,6},{3,7},{4,0},{5,1},{6,2},{7,3},{8,12},{9,13},{10,... | collective-permute-start | bytes 393224 | tf_op jit(solution)/shard_map/ppermute | solution.py:329
  14.1 3.2 %collective-permute-done.1.rest_3_ = bf16[2,2,128,128]{3,2,1,0:T(8,128)(2,1)S(1)} collective-permute-done((bf16[2,2,128,128]{3,2,1,0:T(8,128)(2,1)S(1)}, bf16[2,2,128,128]{3,2,1,0:T(8,128)(2,1)S(1)}, u32[]{:S(2)}, u32[]{:S(2)}) %collective-permute-start.1) | collective-permute-done | bytes 131104 | tf_op jit(solution)/shard_map/ppermute | solution.py:329
  17.3 4.5 %run_forward.1 = (bf16[4,2,2,128,128]{4,3,2,1,0:T(8,128)(2,1)S(1)}, f32[4,2,2,128,128]{4,3,2,1,0:T(8,128)S(1)}) custom-call(f32[2,128,128]{2,1,0:T(8,128)S(1)} %copy-done.3, f32[2,128,128]{2,1,0:T(8,128)S(1)} %pad_maximum_fusion.kern_ref, bf16[2,256,768]{2,1,0:T(8,128)(2,1)S(1)} %copy-done.2, bf16[2,768,256]{2,1,0:T(8,128)(2,1)S(1)} %copy-done.1, ...), custom_call_target="tpu_custom_call" | custom-call | tf_op jit(solution)/shard_map/run_forward/pallas_call | solution.py:221
  21.8 2.7 %run_backward.1 = (bf16[2,272,128]{2,1,0:T(8,128)(2,1)S(1)}, bf16[2,272,128]{2,1,0:T(8,128)(2,1)S(1)}) custom-call(f32[2,128,128]{2,1,0:T(8,128)S(1)} %copy-done.3, f32[2,128,128]{2,1,0:T(8,128)S(1)} %pad_maximum_fusion.kern_ref, bf16[2,16,128]{2,1,0:T(8,128)(2,1)S(1)} %get-tuple-element.19.code_ref, ...), custom_call_target="tpu_custom_call" | custom-call | tf_op jit(solution)/shard_map/run_backward/pallas_call | solution.py:237
  24.5 1.5 %collective-permute-start.7 = (bf16[2,272,128]{2,1,0:T(8,128)(2,1)S(1)}, bf16[2,272,128]{2,1,0:T(8,128)(2,1)S(1)}, u32[]{:S(2)}, u32[]{:S(2)}) collective-permute-start(bf16[2,272,128]{2,1,0:T(8,128)(2,1)S(1)} %get-tuple-element.25), channel_id=1, source_target_pairs={{0,16},{1,17},{2,18},{3,19},{4,20},{5,21},{6,22},{7,23},{8,24},{9,... | collective-permute-start | bytes 417800 | tf_op jit(solution)/shard_map/ppermute | solution.py:329
  26.0 1.6 %collective-permute-start.5 = (bf16[2,272,128]{2,1,0:T(8,128)(2,1)S(1)}, bf16[2,272,128]{2,1,0:T(8,128)(2,1)S(1)}, u32[]{:S(2)}, u32[]{:S(2)}) collective-permute-start(bf16[2,272,128]{2,1,0:T(8,128)(2,1)S(1)} %get-tuple-element.25), channel_id=1, source_target_pairs={{0,18},{1,19},{2,16},{3,17},{4,22},{5,23},{6,20},{7,21},{8,26},{9,... | collective-permute-start | bytes 417800 | tf_op jit(solution)/shard_map/ppermute | solution.py:329
  27.6 0.5 %collective-permute-start.6 = (bf16[2,272,128]{2,1,0:T(8,128)(2,1)S(1)}, bf16[2,272,128]{2,1,0:T(8,128)(2,1)S(1)}, u32[]{:S(2)}, u32[]{:S(2)}) collective-permute-start(bf16[2,272,128]{2,1,0:T(8,128)(2,1)S(1)} %get-tuple-element.26.refs_3_), channel_id=1, source_target_pairs={{0,2},{1,3},{2,0},{3,1},{4,6},{5,7},{6,4},{7,5},{8,10},{9,11},{10,... | collective-permute-start | bytes 417800 | tf_op jit(solution)/shard_map/ppermute | solution.py:329
  28.1 4.5 %collective-permute-done.7.refs_2_ = bf16[2,272,128]{2,1,0:T(8,128)(2,1)S(1)} collective-permute-done((bf16[2,272,128]{2,1,0:T(8,128)(2,1)S(1)}, bf16[2,272,128]{2,1,0:T(8,128)(2,1)S(1)}, u32[]{:S(2)}, u32[]{:S(2)}) %collective-permute-start.7) | collective-permute-done | bytes 139296 | tf_op jit(solution)/shard_map/ppermute | solution.py:329
  32.5 0.9 %collective-permute-done.5.refs_0_ = bf16[2,272,128]{2,1,0:T(8,128)(2,1)S(1)} collective-permute-done((bf16[2,272,128]{2,1,0:T(8,128)(2,1)S(1)}, bf16[2,272,128]{2,1,0:T(8,128)(2,1)S(1)}, u32[]{:S(2)}, u32[]{:S(2)}) %collective-permute-start.5) | collective-permute-done | bytes 139296 | tf_op jit(solution)/shard_map/ppermute | solution.py:329
  33.5 0.8 %collective-permute-done.6.refs_1_ = bf16[2,272,128]{2,1,0:T(8,128)(2,1)S(1)} collective-permute-done((bf16[2,272,128]{2,1,0:T(8,128)(2,1)S(1)}, bf16[2,272,128]{2,1,0:T(8,128)(2,1)S(1)}, u32[]{:S(2)}, u32[]{:S(2)}) %collective-permute-start.6) | collective-permute-done | bytes 139296 | tf_op jit(solution)/shard_map/ppermute | solution.py:329
  34.2 0.4 %place_near.1.start_ref = f32[2,360,896]{2,1,0:T(8,128)S(1)} custom-call(bf16[2,272,128]{2,1,0:T(8,128)(2,1)S(1)} %collective-permute-done.5.refs_0_, bf16[2,272,128]{2,1,0:T(8,128)(2,1)S(1)} %collective-permute-done.6.refs_1_, bf16[2,272,128]{2,1,0:T(8,128)(2,1)S(1)} %collective-permute-done.7.refs_2_, bf16[2,272,128]{2,1,0:T(8,128)(2,1)S(1)} %get-tuple-element.26.refs_3_), custom_call_target="tpu_custom_call" | custom-call | tf_op jit(solution)/shard_map/place_near/pallas_call | solution.py:303
  34.7 0.2 collective-permute-done.8.refs_0_
  34.8 0.8 %collective-permute-done.9.refs_1_ = bf16[2,272,128]{2,1,0:T(8,128)(2,1)S(1)} collective-permute-done((bf16[2,272,128]{2,1,0:T(8,128)(2,1)S(1)}, bf16[2,272,128]{2,1,0:T(8,128)(2,1)S(1)}, u32[]{:S(2)}, u32[]{:S(2)}) %collective-permute-start.9) | collective-permute-done | bytes 139296 | tf_op jit(solution)/shard_map/ppermute | solution.py:329
  35.6 1.1 %place_far.1 = f32[2,96,768]{2,1,0:T(8,128)} custom-call(f32[2,360,896]{2,1,0:T(8,128)S(1)} %place_near.1.start_ref, bf16[2,272,128]{2,1,0:T(8,128)(2,1)S(1)} %collective-permute-done.8.refs_0_, bf16[2,272,128]{2,1,0:T(8,128)(2,1)S(1)} %collective-permute-done.9.refs_1_, bf16[2,272,128]{2,1,0:T(8,128)(2,1)S(1)} %collective-permute-done.10.refs_2_, ...), custom_call_target="tpu_custom_call" | custom-call | tf_op jit(solution)/shard_map/place_far/pallas_call | solution.py:311
  (22 shorter events, 0.1 us)
Async XLA Ops:
  0.0 6.8 %collective-permute-start = (s32[2,2]{1,0:T(2,128)}, s32[2,2]{1,0:T(2,128)S(1)}, u32[]{:S(2)}, u32[]{:S(2)}) collective-permute-start(s32[2,2]{1,0:T(2,128)} %rest_0_.3), channel_id=1, source_target_pairs={{0,4},{1,5},{2,6},{3,7},{4,0},{5,1},{6,2},{7,3},{8,12},{9,13},{10,... | collective-permute-start | bytes 56 | tf_op jit(solution)/shard_map/ppermute | solution.py:329
  4.0 2.3 %copy-start = (f32[1,2,768,768]{3,2,1,0:T(8,128)S(1)}, f32[1,2,768,768]{3,2,1,0:T(8,128)}, u32[]{:S(2)}) copy-start(f32[1,2,768,768]{3,2,1,0:T(8,128)} %param.7) | copy-start | bytes 14155780
  6.4 0.7 %copy-start.5 = (s32[2,2]{1,0:T(2,128)S(1)}, s32[2,2]{1,0:T(2,128)}, u32[]{:S(2)}) copy-start(s32[2,2]{1,0:T(2,128)} %rest_0_.3) | copy-start | bytes 52
  6.7 4.8 %copy-start.6 = (f32[128,128]{1,0:T(8,128)S(1)}, f32[128,128]{1,0:T(8,128)}, u32[]{:S(2)}) copy-start(f32[128,128]{1,0:T(8,128)} %param.10) | copy-start | bytes 196612
  6.7 5.7 %copy-start.4 = (f32[2,128,128]{2,1,0:T(8,128)S(1)}, f32[2,128,128]{2,1,0:T(8,128)}, u32[]{:S(2)}) copy-start(f32[2,128,128]{2,1,0:T(8,128)} %rest_2_.1) | copy-start | bytes 393220
  6.7 10.6 %copy-start.1 = (bf16[2,768,256]{2,1,0:T(8,128)(2,1)S(1)}, bf16[2,768,256]{2,1,0:T(8,128)(2,1)}, u32[]{:S(2)}) copy-start(bf16[2,768,256]{2,1,0:T(8,128)(2,1)} %constant.5.clone.rest_1_) | copy-start | bytes 2359300
  6.7 10.6 %copy-start.2 = (bf16[2,256,768]{2,1,0:T(8,128)(2,1)S(1)}, bf16[2,256,768]{2,1,0:T(8,128)(2,1)}, u32[]{:S(2)}) copy-start(bf16[2,256,768]{2,1,0:T(8,128)(2,1)} %constant.4.clone.rest_0_) | copy-start | bytes 2359300
  6.8 10.6 %copy-start.3 = (f32[2,128,128]{2,1,0:T(8,128)S(1)}, f32[2,128,128]{2,1,0:T(8,128)}, u32[]{:S(2)}) copy-start(f32[2,128,128]{2,1,0:T(8,128)} %probe_ref.3) | copy-start | bytes 393220
  8.5 8.8 %collective-permute-start.3 = (bf16[2,2,128,128]{3,2,1,0:T(8,128)(2,1)S(1)}, bf16[2,2,128,128]{3,2,1,0:T(8,128)(2,1)S(1)}, u32[]{:S(2)}, u32[]{:S(2)}) collective-permute-start(bf16[2,2,128,128]{3,2,1,0:T(8,128)(2,1)S(1)} %get-tuple-element.21), channel_id=1, source_target_pairs={{0,24},{1,25},{2,26},{3,27},{4,28},{5,29},{6,30},{7,31},{8,16},{9,... | collective-permute-start | bytes 393224 | tf_op jit(solution)/shard_map/ppermute | solution.py:329
  11.0 6.3 %collective-permute-start.2 = (bf16[2,2,128,128]{3,2,1,0:T(8,128)(2,1)S(1)}, bf16[2,2,128,128]{3,2,1,0:T(8,128)(2,1)S(1)}, u32[]{:S(2)}, u32[]{:S(2)}) collective-permute-start(bf16[2,2,128,128]{3,2,1,0:T(8,128)(2,1)S(1)} %get-tuple-element.21), channel_id=1, source_target_pairs={{0,16},{1,17},{2,18},{3,19},{4,20},{5,21},{6,22},{7,23},{8,24},{9,... | collective-permute-start | bytes 393224 | tf_op jit(solution)/shard_map/ppermute | solution.py:329
  11.8 5.5 %collective-permute-start.1 = (bf16[2,2,128,128]{3,2,1,0:T(8,128)(2,1)S(1)}, bf16[2,2,128,128]{3,2,1,0:T(8,128)(2,1)S(1)}, u32[]{:S(2)}, u32[]{:S(2)}) collective-permute-start(bf16[2,2,128,128]{3,2,1,0:T(8,128)(2,1)S(1)} %get-tuple-element.20.rest_2_), channel_id=1, source_target_pairs={{0,8},{1,9},{2,10},{3,11},{4,12},{5,13},{6,14},{7,15},{8,0},{9,1},... | collective-permute-start | bytes 393224 | tf_op jit(solution)/shard_map/ppermute | solution.py:329
  12.4 9.4 %collective-permute-start.4 = (f32[2,128,128]{2,1,0:T(8,128)S(1)}, f32[2,128,128]{2,1,0:T(8,128)S(1)}, u32[]{:S(2)}, u32[]{:S(2)}) collective-permute-start(f32[2,128,128]{2,1,0:T(8,128)S(1)} %copy-done.4), channel_id=1, source_target_pairs={{0,4},{1,5},{2,6},{3,7},{4,0},{5,1},{6,2},{7,3},{8,12},{9,13},{10,... | collective-permute-start | bytes 393224 | tf_op jit(solution)/shard_map/ppermute | solution.py:329
  24.5 8.0 %collective-permute-start.7 = (bf16[2,272,128]{2,1,0:T(8,128)(2,1)S(1)}, bf16[2,272,128]{2,1,0:T(8,128)(2,1)S(1)}, u32[]{:S(2)}, u32[]{:S(2)}) collective-permute-start(bf16[2,272,128]{2,1,0:T(8,128)(2,1)S(1)} %get-tuple-element.25), channel_id=1, source_target_pairs={{0,16},{1,17},{2,18},{3,19},{4,20},{5,21},{6,22},{7,23},{8,24},{9,... | collective-permute-start | bytes 417800 | tf_op jit(solution)/shard_map/ppermute | solution.py:329
  26.0 7.5 %collective-permute-start.5 = (bf16[2,272,128]{2,1,0:T(8,128)(2,1)S(1)}, bf16[2,272,128]{2,1,0:T(8,128)(2,1)S(1)}, u32[]{:S(2)}, u32[]{:S(2)}) collective-permute-start(bf16[2,272,128]{2,1,0:T(8,128)(2,1)S(1)} %get-tuple-element.25), channel_id=1, source_target_pairs={{0,18},{1,19},{2,16},{3,17},{4,22},{5,23},{6,20},{7,21},{8,26},{9,... | collective-permute-start | bytes 417800 | tf_op jit(solution)/shard_map/ppermute | solution.py:329
  27.6 6.6 %collective-permute-start.6 = (bf16[2,272,128]{2,1,0:T(8,128)(2,1)S(1)}, bf16[2,272,128]{2,1,0:T(8,128)(2,1)S(1)}, u32[]{:S(2)}, u32[]{:S(2)}) collective-permute-start(bf16[2,272,128]{2,1,0:T(8,128)(2,1)S(1)} %get-tuple-element.26.refs_3_), channel_id=1, source_target_pairs={{0,2},{1,3},{2,0},{3,1},{4,6},{5,7},{6,4},{7,5},{8,10},{9,11},{10,... | collective-permute-start | bytes 417800 | tf_op jit(solution)/shard_map/ppermute | solution.py:329
  28.1 6.6 %collective-permute-start.11 = (bf16[2,272,128]{2,1,0:T(8,128)(2,1)S(1)}, bf16[2,272,128]{2,1,0:T(8,128)(2,1)S(1)}, u32[]{:S(2)}, u32[]{:S(2)}) collective-permute-start(bf16[2,272,128]{2,1,0:T(8,128)(2,1)S(1)} %get-tuple-element.26.refs_3_), channel_id=1, source_target_pairs={{0,1},{1,0},{2,3},{3,2},{4,5},{5,4},{6,7},{7,6},{8,9},{9,8},{10,11... | collective-permute-start | bytes 417800 | tf_op jit(solution)/shard_map/ppermute | solution.py:329
  32.5 2.1 %collective-permute-start.10 = (bf16[2,272,128]{2,1,0:T(8,128)(2,1)S(1)}, bf16[2,272,128]{2,1,0:T(8,128)(2,1)S(1)}, u32[]{:S(2)}, u32[]{:S(2)}) collective-permute-start(bf16[2,272,128]{2,1,0:T(8,128)(2,1)S(1)} %collective-permute-done.7.refs_2_), channel_id=1, source_target_pairs={{0,1},{1,0},{2,3},{3,2},{4,5},{5,4},{6,7},{7,6},{8,9},{9,8},{10,11... | collective-permute-start | bytes 417800 | tf_op jit(solution)/shard_map/ppermute | solution.py:329
  33.5 1.4 %collective-permute-start.8 = (bf16[2,272,128]{2,1,0:T(8,128)(2,1)S(1)}, bf16[2,272,128]{2,1,0:T(8,128)(2,1)S(1)}, u32[]{:S(2)}, u32[]{:S(2)}) collective-permute-start(bf16[2,272,128]{2,1,0:T(8,128)(2,1)S(1)} %collective-permute-done.5.refs_0_), channel_id=1, source_target_pairs={{0,1},{1,0},{2,3},{3,2},{4,5},{5,4},{6,7},{7,6},{8,9},{9,8},{10,11... | collective-permute-start | bytes 417800 | tf_op jit(solution)/shard_map/ppermute | solution.py:329
  34.2 1.4 %collective-permute-start.9 = (bf16[2,272,128]{2,1,0:T(8,128)(2,1)S(1)}, bf16[2,272,128]{2,1,0:T(8,128)(2,1)S(1)}, u32[]{:S(2)}, u32[]{:S(2)}) collective-permute-start(bf16[2,272,128]{2,1,0:T(8,128)(2,1)S(1)} %collective-permute-done.6.refs_1_), channel_id=1, source_target_pairs={{0,1},{1,0},{2,3},{3,2},{4,5},{5,4},{6,7},{7,6},{8,9},{9,8},{10,11... | collective-permute-start | bytes 417800 | tf_op jit(solution)/shard_map/ppermute | solution.py:329

commit v16 on v13

--- a/solution.py
+++ b/solution.py
@@ -27,9 +27,7 @@
         low = (full - high.astype(np.float32)).astype(bf16)
         parts.append((high, low))
     (ph, plo), (mh, mlo) = parts
-    right = np.stack([np.concatenate([ph, ph, plo], 0), np.concatenate([mh, mh, mlo], 0)])
-    left = np.stack([np.concatenate([mh, mh, mlo], 1), np.concatenate([ph, ph, plo], 1)])
-    return left, right
+    return jnp.asarray(np.stack([np.concatenate([ph, plo]), np.concatenate([mh, mlo])]))
 
 
 code_rows = 16
@@ -136,7 +134,7 @@
     return a[0] * b[0] + a[1] * b[1], a[0] * b[1] - a[1] * b[0]
 
 
-def wave_kernel(members, clusters, probe_ref, kern_ref, left_ref, right_ref, code_ref, *rest):
+def wave_kernel(members, clusters, probe_ref, kern_ref, tables_ref, code_ref, *rest):
     trans, terms, meas = rest[-3:]
     slices, count, _, _, window = trans.shape
     meas_refs, t_refs, out_refs = rest[:clusters], rest[clusters : clusters + slices], rest[clusters + slices : -3]
@@ -154,23 +152,30 @@
     def t_of(k, p):
         return trans[k, p, 0].astype(f32), trans[k, p, 1].astype(f32)
 
-    def passes(x, axis, exact):
-        if not exact:
-            return x.astype(bf16)
-        high, low = split(x)
-        return jnp.concatenate([high, low, high], axis=axis)
+    def dot(a, b):
+        return jnp.dot(a, b, preferred_element_type=f32)
 
     def rows(fields, sign, exact):
         x = jnp.concatenate([jnp.concatenate(f, axis=0) for f in fields], axis=1)
-        x = passes(x, 0, exact)
-        y = jnp.dot(left_ref[sign, :, : x.shape[0]], x, preferred_element_type=f32)
+        table_ref = tables_ref.at[1 - sign]
+        if exact:
+            high, low = split(x)
+            y = dot(table_ref[...], high)
+            y = y[: 2 * window] + y[2 * window :] + dot(table_ref[: 2 * window], low)
+        else:
+            y = dot(table_ref[: 2 * window], x.astype(bf16))
         cut = [y[:, p * window : (p + 1) * window] for p in everyone]
         return [(c[:window], c[window:]) for c in cut]
 
     def cols(fields, sign, exact):
         x = jnp.concatenate([jnp.concatenate(f, axis=1) for f in fields], axis=0)
-        x = passes(x, 1, exact)
-        y = jnp.dot(x, right_ref[sign, : x.shape[1]], preferred_element_type=f32)
+        table_ref = tables_ref.at[sign]
+        if exact:
+            high, low = split(x)
+            y = dot(jnp.concatenate([high, low], axis=0), table_ref[: 2 * window])
+            y = y[: count * window] + y[count * window :] + dot(high, table_ref[2 * window :])
+        else:
+            y = dot(x.astype(bf16), table_ref[: 2 * window])
         cut = [y[p * window : (p + 1) * window] for p in everyone]
         return [(c[:, :window], c[:, window:]) for c in cut]
 
@@ -210,13 +215,12 @@
 
 def run_waves(probe, kern, code, measured, windows, members):
     slices, count, window = len(windows), code.shape[0], code.shape[-1]
-    left, right = dft_matrices(window)
     vmem = pl.BlockSpec(memory_space=pltpu.VMEM)
     block = jax.ShapeDtypeStruct((count, 2 * window + code_rows, window), bf16)
     return pl.pallas_call(
         functools.partial(wave_kernel, members, len(measured)),
         out_shape=[block] * (slices // 2),
-        in_specs=[vmem] * (5 + len(measured) + slices),
+        in_specs=[vmem] * (4 + len(measured) + slices),
         out_specs=[vmem] * (slices // 2),
         scratch_shapes=[
             pltpu.VMEM((slices, count, 2, window, window), bf16),
@@ -225,7 +229,7 @@
         ],
         compiler_params=pltpu.CompilerParams(vmem_limit_bytes=40 * 1024 * 1024),
         name="run_waves",
-    )(probe, kern, jnp.asarray(left), jnp.asarray(right), code, *measured, *windows)
+    )(probe, kern, dft_matrices(window), code, *measured, *windows)
 
 
 def add_blocks(block_refs, canvas, stripe):

time: 36.6 us -> 36.6 us (level)
    unnamed x14 -> x12, local copies, waits for them, and re-layouts: 2.64 us -> 2.65 us
where the time goes in v16:
time: 36.6 us
  waiting for transfers between devices  12 us (33%)
  starting transfers between devices  11.2 us (31%)
  Pallas kernels  10.4 us (28%)
  local copies, waits for them, and re-layouts  2.89 us (8%)
    ppermute x12, waiting for transfers between devices, swap(): return lax.ppermute(block, ('depth', 'dp'), route)  12 us
    ppermute x12, starting transfers between devices, swap(): return lax.ppermute(block, ('depth', 'dp'), route)  11.2 us
    pallas_call x1, Pallas kernels, run_waves(): pl.pallas_call(functools.partial(wave_kernel, members, len(measured)), ou...  7.06 us
    unnamed x12, local copies, waits for them, and re-layouts  2.65 us
    pallas_call x1, Pallas kernels, take_windows(): pl.pallas_call(functools.partial(window_kernel, members), out_shape=[jax....  1.45 us
    pallas_call x1, Pallas kernels, place_windows(): pl.pallas_call(second_kernel, out_shape=jax.ShapeDtypeStruct((2, stripe,...  1.26 us
  transfers between devices with their start and end apart: 12, of which 6 were waited for; matrix products, arithmetic and copies ran while one was open for 1% of the time, Pallas kernels for 6%

profile of v16, /device:TPU:0, one launch (start us, length us, event | category | flops | bytes accessed | tf_op | source)
XLA Modules:
  0.0 36.6 jit_solution(4801889227764775468)
XLA Ops:
  0.0 4.0 %collective-permute-start = (s32[2,2]{1,0:T(2,128)}, s32[2,2]{1,0:T(2,128)S(1)}, u32[]{:S(2)}, u32[]{:S(2)}) collective-permute-start(s32[2,2]{1,0:T(2,128)} %rest_0_.2), channel_id=1, source_target_pairs={{0,4},{1,5},{2,6},{3,7},{4,0},{5,1},{6,2},{7,3},{8,12},{9,13},{10,... | collective-permute-start | bytes 56 | tf_op jit(solution)/shard_map/ppermute | solution.py:313
  4.0 0.0 collective-permute-start.1
  4.1 2.3 %copy-done = f32[1,2,768,768]{3,2,1,0:T(8,128)S(1)} copy-done((f32[1,2,768,768]{3,2,1,0:T(8,128)S(1)}, f32[1,2,768,768]{3,2,1,0:T(8,128)}, u32[]{:S(2)}) %copy-start) | copy-done | bytes 4718616
  6.4 0.3 fetch_slice.1.obj_ref
  6.7 0.0 copy-start.5
  6.8 0.0 copy-start.1
  6.8 0.3 copy-done.4
  7.1 1.5 %take_windows.1 = (bf16[2,2,128,128]{3,2,1,0:T(8,128)(2,1)S(1)}, bf16[2,2,128,128]{3,2,1,0:T(8,128)(2,1)S(1)}, bf16[2,16,128]{2,1,0:T(8,128)(2,1)S(1)}) custom-call(f32[2,768,768]{2,1,0:T(8,128)S(1)} %fetch_slice.1.obj_ref, s32[2,2]{1,0:T(2,128)S(1)} %copy-done.4, s32[2,2]{1,0:T(2,128)S(1)} %collective-permute-done.rest_1_), custom_call_target="tpu_custom_call" | custom-call | tf_op jit(solution)/shard_map/take_windows/pallas_call | solution.py:108
  8.5 1.9 %collective-permute-start.3 = (bf16[2,2,128,128]{3,2,1,0:T(8,128)(2,1)S(1)}, bf16[2,2,128,128]{3,2,1,0:T(8,128)(2,1)S(1)}, u32[]{:S(2)}, u32[]{:S(2)}) collective-permute-start(bf16[2,2,128,128]{3,2,1,0:T(8,128)(2,1)S(1)} %get-tuple-element.16), channel_id=1, source_target_pairs={{0,16},{1,17},{2,18},{3,19},{4,20},{5,21},{6,22},{7,23},{8,24},{9,... | collective-permute-start | bytes 393224 | tf_op jit(solution)/shard_map/ppermute | solution.py:313
  10.4 1.4 %collective-permute-start.4 = (bf16[2,2,128,128]{3,2,1,0:T(8,128)(2,1)S(1)}, bf16[2,2,128,128]{3,2,1,0:T(8,128)(2,1)S(1)}, u32[]{:S(2)}, u32[]{:S(2)}) collective-permute-start(bf16[2,2,128,128]{3,2,1,0:T(8,128)(2,1)S(1)} %get-tuple-element.16), channel_id=1, source_target_pairs={{0,24},{1,25},{2,26},{3,27},{4,28},{5,29},{6,30},{7,31},{8,16},{9,... | collective-permute-start | bytes 393224 | tf_op jit(solution)/shard_map/ppermute | solution.py:313
  11.9 0.2 collective-permute-start.2
  12.1 0.2 cosine_bitcast_fusion
  12.4 0.5 %collective-permute-done.1.rest_1_ = f32[2,128,128]{2,1,0:T(8,128)S(1)} collective-permute-done((f32[2,128,128]{2,1,0:T(8,128)}, f32[2,128,128]{2,1,0:T(8,128)S(1)}, u32[]{:S(2)}, u32[]{:S(2)}) %collective-permute-start.1) | collective-permute-done | bytes 131104 | tf_op jit(solution)/shard_map/ppermute | solution.py:313
  12.9 4.7 %collective-permute-done.2.rest_3_ = bf16[2,2,128,128]{3,2,1,0:T(8,128)(2,1)S(1)} collective-permute-done((bf16[2,2,128,128]{3,2,1,0:T(8,128)(2,1)S(1)}, bf16[2,2,128,128]{3,2,1,0:T(8,128)(2,1)S(1)}, u32[]{:S(2)}, u32[]{:S(2)}) %collective-permute-start.2) | collective-permute-done | bytes 131104 | tf_op jit(solution)/shard_map/ppermute | solution.py:313
  17.6 7.1 %run_waves.1 = (bf16[2,272,128]{2,1,0:T(8,128)(2,1)S(1)}, bf16[2,272,128]{2,1,0:T(8,128)(2,1)S(1)}) custom-call(f32[2,128,128]{2,1,0:T(8,128)S(1)} %copy-done.2, f32[2,128,128]{2,1,0:T(8,128)S(1)} %pad_maximum_fusion.kern_ref, bf16[2,512,256]{2,1,0:T(8,128)(2,1)S(1)} %copy-done.1, bf16[2,16,128]{2,1,0:T(8,128)(2,1)S(1)} %get-tuple-element.14.code_ref, ...), custom_call_target="tpu_custom_call" | custom-call | tf_op jit(solution)/shard_map/run_waves/pallas_call | solution.py:220
  24.7 1.7 %collective-permute-start.6 = (bf16[2,272,128]{2,1,0:T(8,128)(2,1)S(1)}, bf16[2,272,128]{2,1,0:T(8,128)(2,1)S(1)}, u32[]{:S(2)}, u32[]{:S(2)}) collective-permute-start(bf16[2,272,128]{2,1,0:T(8,128)(2,1)S(1)} %get-tuple-element.17.refs_0_), channel_id=1, source_target_pairs={{0,2},{1,3},{2,0},{3,1},{4,6},{5,7},{6,4},{7,5},{8,10},{9,11},{10,... | collective-permute-start | bytes 417800 | tf_op jit(solution)/shard_map/ppermute | solution.py:313
  26.4 1.4 %collective-permute-start.7 = (bf16[2,272,128]{2,1,0:T(8,128)(2,1)S(1)}, bf16[2,272,128]{2,1,0:T(8,128)(2,1)S(1)}, u32[]{:S(2)}, u32[]{:S(2)}) collective-permute-start(bf16[2,272,128]{2,1,0:T(8,128)(2,1)S(1)} %get-tuple-element.18), channel_id=1, source_target_pairs={{0,18},{1,19},{2,16},{3,17},{4,22},{5,23},{6,20},{7,21},{8,26},{9,... | collective-permute-start | bytes 417800 | tf_op jit(solution)/shard_map/ppermute | solution.py:313
  27.8 0.5 %collective-permute-start.5 = (bf16[2,272,128]{2,1,0:T(8,128)(2,1)S(1)}, bf16[2,272,128]{2,1,0:T(8,128)(2,1)S(1)}, u32[]{:S(2)}, u32[]{:S(2)}) collective-permute-start(bf16[2,272,128]{2,1,0:T(8,128)(2,1)S(1)} %get-tuple-element.18), channel_id=1, source_target_pairs={{0,16},{1,17},{2,18},{3,19},{4,20},{5,21},{6,22},{7,23},{8,24},{9,... | collective-permute-start | bytes 417800 | tf_op jit(solution)/shard_map/ppermute | solution.py:313
  28.3 2.5 %collective-permute-done.6.refs_2_ = bf16[2,272,128]{2,1,0:T(8,128)(2,1)S(1)} collective-permute-done((bf16[2,272,128]{2,1,0:T(8,128)(2,1)S(1)}, bf16[2,272,128]{2,1,0:T(8,128)(2,1)S(1)}, u32[]{:S(2)}, u32[]{:S(2)}) %collective-permute-start.6) | collective-permute-done | bytes 139296 | tf_op jit(solution)/shard_map/ppermute | solution.py:313
  30.7 1.8 %collective-permute-done.7.refs_3_ = bf16[2,272,128]{2,1,0:T(8,128)(2,1)S(1)} collective-permute-done((bf16[2,272,128]{2,1,0:T(8,128)(2,1)S(1)}, bf16[2,272,128]{2,1,0:T(8,128)(2,1)S(1)}, u32[]{:S(2)}, u32[]{:S(2)}) %collective-permute-start.7) | collective-permute-done | bytes 139296 | tf_op jit(solution)/shard_map/ppermute | solution.py:313
  32.6 1.4 %collective-permute-done.5.refs_1_ = bf16[2,272,128]{2,1,0:T(8,128)(2,1)S(1)} collective-permute-done((bf16[2,272,128]{2,1,0:T(8,128)(2,1)S(1)}, bf16[2,272,128]{2,1,0:T(8,128)(2,1)S(1)}, u32[]{:S(2)}, u32[]{:S(2)}) %collective-permute-start.5) | collective-permute-done | bytes 139296 | tf_op jit(solution)/shard_map/ppermute | solution.py:313
  34.0 0.3 place_near.1.start_ref
  34.3 1.0 %collective-permute-done.9.refs_1_ = bf16[2,272,128]{2,1,0:T(8,128)(2,1)S(1)} collective-permute-done((bf16[2,272,128]{2,1,0:T(8,128)(2,1)S(1)}, bf16[2,272,128]{2,1,0:T(8,128)(2,1)S(1)}, u32[]{:S(2)}, u32[]{:S(2)}) %collective-permute-start.9) | collective-permute-done | bytes 139296 | tf_op jit(solution)/shard_map/ppermute | solution.py:313
  35.3 1.3 %place_far.1 = f32[2,96,768]{2,1,0:T(8,128)} custom-call(f32[2,360,896]{2,1,0:T(8,128)S(1)} %place_near.1.start_ref, bf16[2,272,128]{2,1,0:T(8,128)(2,1)S(1)} %collective-permute-done.8.refs_0_, bf16[2,272,128]{2,1,0:T(8,128)(2,1)S(1)} %collective-permute-done.9.refs_1_, bf16[2,272,128]{2,1,0:T(8,128)(2,1)S(1)} %collective-permute-done.10.refs_2_, ...), custom_call_target="tpu_custom_call" | custom-call | tf_op jit(solution)/shard_map/place_far/pallas_call | solution.py:295
  (19 shorter events, 0.1 us)
Async XLA Ops:
  0.0 6.8 %collective-permute-start = (s32[2,2]{1,0:T(2,128)}, s32[2,2]{1,0:T(2,128)S(1)}, u32[]{:S(2)}, u32[]{:S(2)}) collective-permute-start(s32[2,2]{1,0:T(2,128)} %rest_0_.2), channel_id=1, source_target_pairs={{0,4},{1,5},{2,6},{3,7},{4,0},{5,1},{6,2},{7,3},{8,12},{9,13},{10,... | collective-permute-start | bytes 56 | tf_op jit(solution)/shard_map/ppermute | solution.py:313
  4.0 8.9 %collective-permute-start.1 = (f32[2,128,128]{2,1,0:T(8,128)}, f32[2,128,128]{2,1,0:T(8,128)S(1)}, u32[]{:S(2)}, u32[]{:S(2)}) collective-permute-start(f32[2,128,128]{2,1,0:T(8,128)} %rest_0_.3), channel_id=1, source_target_pairs={{0,4},{1,5},{2,6},{3,7},{4,0},{5,1},{6,2},{7,3},{8,12},{9,13},{10,... | collective-permute-start | bytes 393224 | tf_op jit(solution)/shard_map/ppermute | solution.py:313
  4.1 2.3 %copy-start = (f32[1,2,768,768]{3,2,1,0:T(8,128)S(1)}, f32[1,2,768,768]{3,2,1,0:T(8,128)}, u32[]{:S(2)}) copy-start(f32[1,2,768,768]{3,2,1,0:T(8,128)} %param.6) | copy-start | bytes 14155780
  6.4 0.7 %copy-start.4 = (s32[2,2]{1,0:T(2,128)S(1)}, s32[2,2]{1,0:T(2,128)}, u32[]{:S(2)}) copy-start(s32[2,2]{1,0:T(2,128)} %rest_0_.2) | copy-start | bytes 52
  6.7 5.4 %copy-start.5 = (f32[128,128]{1,0:T(8,128)S(1)}, f32[128,128]{1,0:T(8,128)}, u32[]{:S(2)}) copy-start(f32[128,128]{1,0:T(8,128)} %param.9) | copy-start | bytes 196612
  6.8 10.9 %copy-start.1 = (bf16[2,512,256]{2,1,0:T(8,128)(2,1)S(1)}, bf16[2,512,256]{2,1,0:T(8,128)(2,1)}, u32[]{:S(2)}) copy-start(bf16[2,512,256]{2,1,0:T(8,128)(2,1)} %constant.2.clone.tables_ref) | copy-start | bytes 1572868
  6.8 10.9 %copy-start.2 = (f32[2,128,128]{2,1,0:T(8,128)S(1)}, f32[2,128,128]{2,1,0:T(8,128)}, u32[]{:S(2)}) copy-start(f32[2,128,128]{2,1,0:T(8,128)} %probe_ref.1) | copy-start | bytes 393220
  6.8 10.9 %copy-start.3 = (f32[2,128,128]{2,1,0:T(8,128)S(1)}, f32[2,128,128]{2,1,0:T(8,128)}, u32[]{:S(2)}) copy-start(f32[2,128,128]{2,1,0:T(8,128)} %rest_0_.3) | copy-start | bytes 393220
  8.5 9.1 %collective-permute-start.3 = (bf16[2,2,128,128]{3,2,1,0:T(8,128)(2,1)S(1)}, bf16[2,2,128,128]{3,2,1,0:T(8,128)(2,1)S(1)}, u32[]{:S(2)}, u32[]{:S(2)}) collective-permute-start(bf16[2,2,128,128]{3,2,1,0:T(8,128)(2,1)S(1)} %get-tuple-element.16), channel_id=1, source_target_pairs={{0,16},{1,17},{2,18},{3,19},{4,20},{5,21},{6,22},{7,23},{8,24},{9,... | collective-permute-start | bytes 393224 | tf_op jit(solution)/shard_map/ppermute | solution.py:313
  10.4 7.2 %collective-permute-start.4 = (bf16[2,2,128,128]{3,2,1,0:T(8,128)(2,1)S(1)}, bf16[2,2,128,128]{3,2,1,0:T(8,128)(2,1)S(1)}, u32[]{:S(2)}, u32[]{:S(2)}) collective-permute-start(bf16[2,2,128,128]{3,2,1,0:T(8,128)(2,1)S(1)} %get-tuple-element.16), channel_id=1, source_target_pairs={{0,24},{1,25},{2,26},{3,27},{4,28},{5,29},{6,30},{7,31},{8,16},{9,... | collective-permute-start | bytes 393224 | tf_op jit(solution)/shard_map/ppermute | solution.py:313
  11.9 5.7 %collective-permute-start.2 = (bf16[2,2,128,128]{3,2,1,0:T(8,128)(2,1)S(1)}, bf16[2,2,128,128]{3,2,1,0:T(8,128)(2,1)S(1)}, u32[]{:S(2)}, u32[]{:S(2)}) collective-permute-start(bf16[2,2,128,128]{3,2,1,0:T(8,128)(2,1)S(1)} %get-tuple-element.15.rest_2_), channel_id=1, source_target_pairs={{0,8},{1,9},{2,10},{3,11},{4,12},{5,13},{6,14},{7,15},{8,0},{9,1},... | collective-permute-start | bytes 393224 | tf_op jit(solution)/shard_map/ppermute | solution.py:313
  24.7 6.0 %collective-permute-start.6 = (bf16[2,272,128]{2,1,0:T(8,128)(2,1)S(1)}, bf16[2,272,128]{2,1,0:T(8,128)(2,1)S(1)}, u32[]{:S(2)}, u32[]{:S(2)}) collective-permute-start(bf16[2,272,128]{2,1,0:T(8,128)(2,1)S(1)} %get-tuple-element.17.refs_0_), channel_id=1, source_target_pairs={{0,2},{1,3},{2,0},{3,1},{4,6},{5,7},{6,4},{7,5},{8,10},{9,11},{10,... | collective-permute-start | bytes 417800 | tf_op jit(solution)/shard_map/ppermute | solution.py:313
  26.4 6.2 %collective-permute-start.7 = (bf16[2,272,128]{2,1,0:T(8,128)(2,1)S(1)}, bf16[2,272,128]{2,1,0:T(8,128)(2,1)S(1)}, u32[]{:S(2)}, u32[]{:S(2)}) collective-permute-start(bf16[2,272,128]{2,1,0:T(8,128)(2,1)S(1)} %get-tuple-element.18), channel_id=1, source_target_pairs={{0,18},{1,19},{2,16},{3,17},{4,22},{5,23},{6,20},{7,21},{8,26},{9,... | collective-permute-start | bytes 417800 | tf_op jit(solution)/shard_map/ppermute | solution.py:313
  27.8 6.2 %collective-permute-start.5 = (bf16[2,272,128]{2,1,0:T(8,128)(2,1)S(1)}, bf16[2,272,128]{2,1,0:T(8,128)(2,1)S(1)}, u32[]{:S(2)}, u32[]{:S(2)}) collective-permute-start(bf16[2,272,128]{2,1,0:T(8,128)(2,1)S(1)} %get-tuple-element.18), channel_id=1, source_target_pairs={{0,16},{1,17},{2,18},{3,19},{4,20},{5,21},{6,22},{7,23},{8,24},{9,... | collective-permute-start | bytes 417800 | tf_op jit(solution)/shard_map/ppermute | solution.py:313
  28.3 6.0 %collective-permute-start.8 = (bf16[2,272,128]{2,1,0:T(8,128)(2,1)S(1)}, bf16[2,272,128]{2,1,0:T(8,128)(2,1)S(1)}, u32[]{:S(2)}, u32[]{:S(2)}) collective-permute-start(bf16[2,272,128]{2,1,0:T(8,128)(2,1)S(1)} %get-tuple-element.17.refs_0_), channel_id=1, source_target_pairs={{0,1},{1,0},{2,3},{3,2},{4,5},{5,4},{6,7},{7,6},{8,9},{9,8},{10,11... | collective-permute-start | bytes 417800 | tf_op jit(solution)/shard_map/ppermute | solution.py:313
  30.7 3.5 %collective-permute-start.10 = (bf16[2,272,128]{2,1,0:T(8,128)(2,1)S(1)}, bf16[2,272,128]{2,1,0:T(8,128)(2,1)S(1)}, u32[]{:S(2)}, u32[]{:S(2)}) collective-permute-start(bf16[2,272,128]{2,1,0:T(8,128)(2,1)S(1)} %collective-permute-done.6.refs_2_), channel_id=1, source_target_pairs={{0,1},{1,0},{2,3},{3,2},{4,5},{5,4},{6,7},{7,6},{8,9},{9,8},{10,11... | collective-permute-start | bytes 417800 | tf_op jit(solution)/shard_map/ppermute | solution.py:313
  32.6 1.7 %collective-permute-start.11 = (bf16[2,272,128]{2,1,0:T(8,128)(2,1)S(1)}, bf16[2,272,128]{2,1,0:T(8,128)(2,1)S(1)}, u32[]{:S(2)}, u32[]{:S(2)}) collective-permute-start(bf16[2,272,128]{2,1,0:T(8,128)(2,1)S(1)} %collective-permute-done.7.refs_3_), channel_id=1, source_target_pairs={{0,1},{1,0},{2,3},{3,2},{4,5},{5,4},{6,7},{7,6},{8,9},{9,8},{10,11... | collective-permute-start | bytes 417800 | tf_op jit(solution)/shard_map/ppermute | solution.py:313
  34.0 1.4 %collective-permute-start.9 = (bf16[2,272,128]{2,1,0:T(8,128)(2,1)S(1)}, bf16[2,272,128]{2,1,0:T(8,128)(2,1)S(1)}, u32[]{:S(2)}, u32[]{:S(2)}) collective-permute-start(bf16[2,272,128]{2,1,0:T(8,128)(2,1)S(1)} %collective-permute-done.5.refs_1_), channel_id=1, source_target_pairs={{0,1},{1,0},{2,3},{3,2},{4,5},{5,4},{6,7},{7,6},{8,9},{9,8},{10,11... | collective-permute-start | bytes 417800 | tf_op jit(solution)/shard_map/ppermute | solution.py:313

commit v17 on v13

--- a/solution.py
+++ b/solution.py
@@ -35,27 +35,27 @@
 code_rows = 16
 
 
-def fetch_kernel(obj_ref, out_ref, sem):
-    copy = pltpu.make_async_copy(obj_ref, out_ref, sem)
-    copy.start()
-    copy.wait()
-
-
-def fetch(obj):
-    size = 4 * math.prod(obj.shape)
+def touch_kernel(obj_ref, out_ref):
+    out_ref[...] = obj_ref[0, :8, :128]
+
+
+def touch(obj):
+    vmem = pl.BlockSpec(memory_space=pltpu.VMEM)
     return pl.pallas_call(
-        fetch_kernel,
-        out_shape=jax.ShapeDtypeStruct(obj.shape, obj.dtype),
-        in_specs=[pl.BlockSpec(memory_space=pltpu.HBM)],
-        out_specs=pl.BlockSpec(memory_space=pltpu.VMEM),
-        scratch_shapes=[pltpu.SemaphoreType.DMA],
+        touch_kernel,
+        out_shape=jax.ShapeDtypeStruct((8, 128), obj.dtype),
+        in_specs=[vmem],
+        out_specs=vmem,
         compiler_params=pltpu.CompilerParams(vmem_limit_bytes=16 * 1024 * 1024),
-        cost_estimate=pl.CostEstimate(flops=0, bytes_accessed=2 * size, transcendentals=0),
-        name="fetch_slice",
+        cost_estimate=pl.CostEstimate(
+            flops=0, bytes_accessed=4 * math.prod(obj.shape), transcendentals=0
+        ),
+        name="touch_slice",
     )(obj)
 
 
-def window_kernel(members, obj_ref, *rest):
+def window_kernel(members, obj_ref, touched_ref, *rest):
+    del touched_ref
     table, table_sems = rest[-2:]
     clusters, count = table.shape[:2]
     pos_refs, out_refs, code_ref = rest[:clusters], rest[clusters:-3], rest[-3]
@@ -85,11 +85,12 @@
         return row_base, col_base, row - row_base, col - col_base
 
     line = lax.broadcasted_iota(jnp.int32, (code_rows, window), 0)
+    code = jnp.zeros((code_rows, window), jnp.int32)
     for p in range(count):
         row, col = table[home ^ cluster, p, 0], table[home ^ cluster, p, 1]
-        code = jnp.where(line == 0, row >> 3, jnp.where(line == 1, row & 7, 0))
-        code = jnp.where(line == 2, col >> 3, jnp.where(line == 3, col & 7, code))
-        code_ref[p] = code.astype(f32).astype(bf16)
+        for n, value in enumerate((row >> 3, row & 7, col >> 3, col & 7)):
+            code = jnp.where(line == 4 * p + n, value, code)
+    code_ref[...] = code.astype(f32).astype(bf16)
     for m in reversed(range(clusters)):
         for p in range(count):
             row_base, col_base, row_off, col_off = corner(m, p)
@@ -102,7 +103,7 @@
                 out_refs[m][p, part] = block.astype(bf16)
 
 
-def take_windows(obj, positions, window, members):
+def take_windows(obj, touched, positions, window, members):
     clusters, count = len(positions), positions[0].shape[0]
     any_space = pl.BlockSpec(memory_space=pl.ANY)
     smem = pl.BlockSpec(memory_space=pltpu.SMEM)
@@ -110,8 +111,8 @@
     out = pl.pallas_call(
         functools.partial(window_kernel, members),
         out_shape=[jax.ShapeDtypeStruct((count, 2, window, window), bf16)] * clusters
-        + [jax.ShapeDtypeStruct((count, code_rows, window), bf16)],
-        in_specs=[vmem, smem] + [any_space] * (clusters - 1),
+        + [jax.ShapeDtypeStruct((code_rows, window), bf16)],
+        in_specs=[vmem, vmem, smem] + [any_space] * (clusters - 1),
         out_specs=[vmem] * (clusters + 1),
         scratch_shapes=[
             pltpu.SMEM((clusters, count, 2), jnp.int32),
@@ -119,7 +120,7 @@
         ],
         compiler_params=pltpu.CompilerParams(vmem_limit_bytes=16 * 1024 * 1024),
         name="take_windows",
-    )(obj, *positions)
+    )(obj, touched, *positions)
     return out[:clusters], out[clusters]
 
 
@@ -204,15 +205,16 @@
             spectrum = transform(chi, minus, False)
             returned = transform([cmul_conj(kern, s) for s in spectrum], plus, False)
     for n, out_ref in enumerate(out_refs):
-        out_ref[:, : 2 * window] = terms[2 * n]
-        out_ref[:, 2 * window :] = code_ref[...]
+        for p in everyone:
+            out_ref[2 * p * window : 2 * (p + 1) * window] = terms[2 * n, p]
+        out_ref[2 * count * window :] = code_ref[...]
 
 
 def run_waves(probe, kern, code, measured, windows, members):
-    slices, count, window = len(windows), code.shape[0], code.shape[-1]
+    slices, (count, _, _, window) = len(windows), windows[0].shape
     left, right = dft_matrices(window)
     vmem = pl.BlockSpec(memory_space=pltpu.VMEM)
-    block = jax.ShapeDtypeStruct((count, 2 * window + code_rows, window), bf16)
+    block = jax.ShapeDtypeStruct((2 * count * window + code_rows, window), bf16)
     return pl.pallas_call(
         functools.partial(wave_kernel, members, len(measured)),
         out_shape=[block] * (slices // 2),
@@ -229,16 +231,17 @@
 
 
 def add_blocks(block_refs, canvas, stripe):
-    count, _, window = block_refs[0].shape
+    height, window = block_refs[0].shape
+    count = (height - code_rows) // (2 * window)
     cols = canvas.shape[-1] - 128
     wide = window + 128
     first_row = lax.axis_index("dp") * stripe
     corners = []
     for block_ref in block_refs:
+        code = block_ref[2 * count * window :].astype(f32)
         for p in range(count):
-            code = block_ref[p, 2 * window :].astype(f32)
-            row = (8.0 * code[0:1] + code[1:2]).astype(jnp.int32)
-            col = (8.0 * code[2:3] + code[3:4]).astype(jnp.int32)
+            row = (8.0 * code[4 * p : 4 * p + 1] + code[4 * p + 1 : 4 * p + 2]).astype(jnp.int32)
+            col = (8.0 * code[4 * p + 2 : 4 * p + 3] + code[4 * p + 3 : 4 * p + 4]).astype(jnp.int32)
             corners.append((row[0, 0], col[0, 0]))
     for n, (row, col) in enumerate(corners):
         block_ref, p = block_refs[n // count], n % count
@@ -249,7 +252,7 @@
         @pl.when((row > 0) & (row < window + stripe))
         def _():
             for part in range(2):
-                block = block_ref[p, part * window : (part + 1) * window].astype(f32)
+                block = block_ref[(2 * p + part) * window : (2 * p + part + 1) * window].astype(f32)
                 block = jnp.concatenate([block, jnp.zeros((8, window), f32)], axis=0)
                 block = pltpu.roll(block, row - row_base, 0)
                 block = jnp.concatenate([block, jnp.zeros((window + 8, 128), f32)], axis=1)
@@ -318,7 +321,8 @@
 
     homes = [m * members for m in range(1, clusters)]
     all_positions = [positions] + [swap(positions, 0, home) for home in homes]
-    windows, code = take_windows(fetch(object_slices[0]), all_positions, window, members)
+    obj = object_slices[0]
+    windows, code = take_windows(obj, touch(obj), all_positions, window, members)
     phase, code = lax.optimization_barrier((propagator_phase, code))
     windows = [windows[0]] + [swap(windows[m // 2], m, 0) for m in range(1, depth)]
     targets = [measured] + [swap(measured, 0, home) for home in homes]

time: 36.6 us -> 35.5 us (0.970)
  waiting for transfers between devices: 12 us -> 11 us
  starting transfers between devices: 11.2 us -> 11.7 us
    ppermute x12, waiting for transfers between devices: 12 us -> 11 us  [swap(): return lax.ppermute(block, ('depth', 'dp'), route)]
    ppermute x12, starting transfers between devices: 11.2 us -> 11.7 us  [swap(): return lax.ppermute(block, ('depth', 'dp'), route)]
  transfers between devices with their start and end apart: 12 -> 12, of which waited for: 6 -> 6; matrix products, arithmetic and copies ran while one was open for 1% -> 1% of each run, Pallas kernels for 6% -> 5%
where the time goes in v17:
time: 35.5 us; the launch traced here: 35.4 us
  starting transfers between devices  11.7 us (33%)
  waiting for transfers between devices  11 us (31%)
  Pallas kernels  9.92 us (28%)
  local copies, waits for them, and re-layouts  2.6 us (7%)
    ppermute x12, starting transfers between devices, swap(): return lax.ppermute(block, ('depth', 'dp'), route)  11.7 us
    ppermute x12, waiting for transfers between devices, swap(): return lax.ppermute(block, ('depth', 'dp'), route)  11 us
    pallas_call x1, Pallas kernels, run_waves(): pl.pallas_call(functools.partial(wave_kernel, members, len(measured)), ou...  7.05 us
    unnamed x14, local copies, waits for them, and re-layouts  2.36 us
    pallas_call x1, Pallas kernels, take_windows(): pl.pallas_call(functools.partial(window_kernel, members), out_shape=[jax....  1.46 us
    pallas_call x1, Pallas kernels, place_windows(): pl.pallas_call(second_kernel, out_shape=jax.ShapeDtypeStruct((2, stripe,...  1.13 us
  transfers between devices with their start and end apart: 12, of which 6 were waited for; matrix products, arithmetic and copies ran while one was open for 1% of the time, Pallas kernels for 5%

profile of v17, /device:TPU:0, one launch (start us, length us, event | category | flops | bytes accessed | tf_op | source)
XLA Modules:
  0.0 35.4 jit_solution(15517200976515115623)
XLA Ops:
  0.0 4.0 %collective-permute-start = (s32[2,2]{1,0:T(2,128)}, s32[2,2]{1,0:T(2,128)S(1)}, u32[]{:S(2)}, u32[]{:S(2)}) collective-permute-start(s32[2,2]{1,0:T(2,128)} %rest_0_.2), channel_id=1, source_target_pairs={{0,4},{1,5},{2,6},{3,7},{4,0},{5,1},{6,2},{7,3},{8,12},{9,13},{10,... | collective-permute-start | bytes 56 | tf_op jit(solution)/shard_map/ppermute | solution.py:312
  4.0 0.1 collective-permute-start.1
  4.1 2.3 %copy-done = f32[1,2,768,768]{3,2,1,0:T(8,128)S(1)} copy-done((f32[1,2,768,768]{3,2,1,0:T(8,128)S(1)}, f32[1,2,768,768]{3,2,1,0:T(8,128)}, u32[]{:S(2)}) %copy-start) | copy-done | bytes 4718616
  6.5 1.5 %take_windows.1 = (bf16[2,2,128,128]{3,2,1,0:T(8,128)(2,1)S(1)}, bf16[2,2,128,128]{3,2,1,0:T(8,128)(2,1)S(1)}, bf16[16,128]{1,0:T(8,128)(2,1)S(1)}) custom-call(f32[2,768,768]{2,1,0:T(8,128)S(1)} %bitcast.7, f32[8,128]{1,0:T(8,128)S(1)} %touch_slice.1.touched_ref, s32[2,2]{1,0:T(2,128)S(1)} %copy-done.5, s32[2,2]{1,0:T(2,128)S(1)} %collective-permute-done.rest_1_), custom_call_target="tpu_custom_call" | custom-call | tf_op jit(solution)/shard_map/take_windows/pallas_call | solution.py:111
  8.0 2.8 %collective-permute-start.4 = (bf16[2,2,128,128]{3,2,1,0:T(8,128)(2,1)S(1)}, bf16[2,2,128,128]{3,2,1,0:T(8,128)(2,1)S(1)}, u32[]{:S(2)}, u32[]{:S(2)}) collective-permute-start(bf16[2,2,128,128]{3,2,1,0:T(8,128)(2,1)S(1)} %get-tuple-element.16), channel_id=1, source_target_pairs={{0,24},{1,25},{2,26},{3,27},{4,28},{5,29},{6,30},{7,31},{8,16},{9,... | collective-permute-start | bytes 393224 | tf_op jit(solution)/shard_map/ppermute | solution.py:312
  10.7 0.5 %collective-permute-start.3 = (bf16[2,2,128,128]{3,2,1,0:T(8,128)(2,1)S(1)}, bf16[2,2,128,128]{3,2,1,0:T(8,128)(2,1)S(1)}, u32[]{:S(2)}, u32[]{:S(2)}) collective-permute-start(bf16[2,2,128,128]{3,2,1,0:T(8,128)(2,1)S(1)} %get-tuple-element.16), channel_id=1, source_target_pairs={{0,16},{1,17},{2,18},{3,19},{4,20},{5,21},{6,22},{7,23},{8,24},{9,... | collective-permute-start | bytes 393224 | tf_op jit(solution)/shard_map/ppermute | solution.py:312
  11.2 0.3 collective-permute-start.2
  11.5 0.2 cosine_bitcast_fusion
  11.8 1.1 %collective-permute-done.1.rest_1_ = f32[2,128,128]{2,1,0:T(8,128)S(1)} collective-permute-done((f32[2,128,128]{2,1,0:T(8,128)}, f32[2,128,128]{2,1,0:T(8,128)S(1)}, u32[]{:S(2)}, u32[]{:S(2)}) %collective-permute-start.1) | collective-permute-done | bytes 131104 | tf_op jit(solution)/shard_map/ppermute | solution.py:312
  12.9 3.9 %collective-permute-done.2.rest_3_ = bf16[2,2,128,128]{3,2,1,0:T(8,128)(2,1)S(1)} collective-permute-done((bf16[2,2,128,128]{3,2,1,0:T(8,128)(2,1)S(1)}, bf16[2,2,128,128]{3,2,1,0:T(8,128)(2,1)S(1)}, u32[]{:S(2)}, u32[]{:S(2)}) %collective-permute-start.2) | collective-permute-done | bytes 131104 | tf_op jit(solution)/shard_map/ppermute | solution.py:312
  16.8 7.1 %run_waves.1 = (bf16[528,128]{1,0:T(8,128)(2,1)S(1)}, bf16[528,128]{1,0:T(8,128)(2,1)S(1)}) custom-call(f32[2,128,128]{2,1,0:T(8,128)S(1)} %copy-done.3, f32[2,128,128]{2,1,0:T(8,128)S(1)} %pad_maximum_fusion.kern_ref, bf16[2,256,768]{2,1,0:T(8,128)(2,1)S(1)} %copy-done.2, bf16[2,768,256]{2,1,0:T(8,128)(2,1)S(1)} %copy-done.1, ...), custom_call_target="tpu_custom_call" | custom-call | tf_op jit(solution)/shard_map/run_waves/pallas_call | solution.py:218
  23.9 2.5 %collective-permute-start.7 = (bf16[528,128]{1,0:T(8,128)(2,1)S(1)}, bf16[528,128]{1,0:T(8,128)(2,1)S(1)}, u32[]{:S(2)}, u32[]{:S(2)}) collective-permute-start(bf16[528,128]{1,0:T(8,128)(2,1)S(1)} %get-tuple-element.18), channel_id=1, source_target_pairs={{0,18},{1,19},{2,16},{3,17},{4,22},{5,23},{6,20},{7,21},{8,26},{9,... | collective-permute-start | bytes 405512 | tf_op jit(solution)/shard_map/ppermute | solution.py:312
  26.4 0.6 %collective-permute-start.5 = (bf16[528,128]{1,0:T(8,128)(2,1)S(1)}, bf16[528,128]{1,0:T(8,128)(2,1)S(1)}, u32[]{:S(2)}, u32[]{:S(2)}) collective-permute-start(bf16[528,128]{1,0:T(8,128)(2,1)S(1)} %get-tuple-element.18), channel_id=1, source_target_pairs={{0,16},{1,17},{2,18},{3,19},{4,20},{5,21},{6,22},{7,23},{8,24},{9,... | collective-permute-start | bytes 405512 | tf_op jit(solution)/shard_map/ppermute | solution.py:312
  27.0 0.5 %collective-permute-start.6 = (bf16[528,128]{1,0:T(8,128)(2,1)S(1)}, bf16[528,128]{1,0:T(8,128)(2,1)S(1)}, u32[]{:S(2)}, u32[]{:S(2)}) collective-permute-start(bf16[528,128]{1,0:T(8,128)(2,1)S(1)} %get-tuple-element.17.refs_0_), channel_id=1, source_target_pairs={{0,2},{1,3},{2,0},{3,1},{4,6},{5,7},{6,4},{7,5},{8,10},{9,11},{10,... | collective-permute-start | bytes 405512 | tf_op jit(solution)/shard_map/ppermute | solution.py:312
  27.4 0.0 collective-permute-start.8
  27.4 2.9 %collective-permute-done.7.refs_3_ = bf16[528,128]{1,0:T(8,128)(2,1)S(1)} collective-permute-done((bf16[528,128]{1,0:T(8,128)(2,1)S(1)}, bf16[528,128]{1,0:T(8,128)(2,1)S(1)}, u32[]{:S(2)}, u32[]{:S(2)}) %collective-permute-start.7) | collective-permute-done | bytes 135200 | tf_op jit(solution)/shard_map/ppermute | solution.py:312
  30.4 0.0 collective-permute-start.11
  30.4 2.3 %collective-permute-done.5.refs_1_ = bf16[528,128]{1,0:T(8,128)(2,1)S(1)} collective-permute-done((bf16[528,128]{1,0:T(8,128)(2,1)S(1)}, bf16[528,128]{1,0:T(8,128)(2,1)S(1)}, u32[]{:S(2)}, u32[]{:S(2)}) %collective-permute-start.5) | collective-permute-done | bytes 135200 | tf_op jit(solution)/shard_map/ppermute | solution.py:312
  32.7 0.0 collective-permute-start.9
  32.7 0.5 %collective-permute-start.10 = (bf16[528,128]{1,0:T(8,128)(2,1)S(1)}, bf16[528,128]{1,0:T(8,128)(2,1)S(1)}, u32[]{:S(2)}, u32[]{:S(2)}) collective-permute-start(bf16[528,128]{1,0:T(8,128)(2,1)S(1)} %collective-permute-done.6.refs_2_), channel_id=1, source_target_pairs={{0,1},{1,0},{2,3},{3,2},{4,5},{5,4},{6,7},{7,6},{8,9},{9,8},{10,11... | collective-permute-start | bytes 405512 | tf_op jit(solution)/shard_map/ppermute | solution.py:312
  33.2 0.3 place_near.1.start_ref
  33.5 0.5 %collective-permute-done.9.refs_1_ = bf16[528,128]{1,0:T(8,128)(2,1)S(1)} collective-permute-done((bf16[528,128]{1,0:T(8,128)(2,1)S(1)}, bf16[528,128]{1,0:T(8,128)(2,1)S(1)}, u32[]{:S(2)}, u32[]{:S(2)}) %collective-permute-start.9) | collective-permute-done | bytes 135200 | tf_op jit(solution)/shard_map/ppermute | solution.py:312
  34.1 0.2 collective-permute-done.10.refs_2_
  34.3 1.1 %place_far.1 = f32[2,96,768]{2,1,0:T(8,128)} custom-call(f32[2,360,896]{2,1,0:T(8,128)S(1)} %place_near.1.start_ref, bf16[528,128]{1,0:T(8,128)(2,1)S(1)} %collective-permute-done.8.refs_0_, bf16[528,128]{1,0:T(8,128)(2,1)S(1)} %collective-permute-done.9.refs_1_, bf16[528,128]{1,0:T(8,128)(2,1)S(1)} %collective-permute-done.10.refs_2_, ...), custom_call_target="tpu_custom_call" | custom-call | tf_op jit(solution)/shard_map/place_far/pallas_call | solution.py:294
  (21 shorter events, 0.1 us)
Async XLA Ops:
  0.0 6.5 %copy-start.5 = (s32[2,2]{1,0:T(2,128)S(1)}, s32[2,2]{1,0:T(2,128)}, u32[]{:S(2)}) copy-start(s32[2,2]{1,0:T(2,128)} %rest_0_.2) | copy-start | bytes 52
  0.0 6.5 %collective-permute-start = (s32[2,2]{1,0:T(2,128)}, s32[2,2]{1,0:T(2,128)S(1)}, u32[]{:S(2)}, u32[]{:S(2)}) collective-permute-start(s32[2,2]{1,0:T(2,128)} %rest_0_.2), channel_id=1, source_target_pairs={{0,4},{1,5},{2,6},{3,7},{4,0},{5,1},{6,2},{7,3},{8,12},{9,13},{10,... | collective-permute-start | bytes 56 | tf_op jit(solution)/shard_map/ppermute | solution.py:312
  4.0 8.9 %collective-permute-start.1 = (f32[2,128,128]{2,1,0:T(8,128)}, f32[2,128,128]{2,1,0:T(8,128)S(1)}, u32[]{:S(2)}, u32[]{:S(2)}) collective-permute-start(f32[2,128,128]{2,1,0:T(8,128)} %rest_0_.3), channel_id=1, source_target_pairs={{0,4},{1,5},{2,6},{3,7},{4,0},{5,1},{6,2},{7,3},{8,12},{9,13},{10,... | collective-permute-start | bytes 393224 | tf_op jit(solution)/shard_map/ppermute | solution.py:312
  4.1 2.3 %copy-start = (f32[1,2,768,768]{3,2,1,0:T(8,128)S(1)}, f32[1,2,768,768]{3,2,1,0:T(8,128)}, u32[]{:S(2)}) copy-start(f32[1,2,768,768]{3,2,1,0:T(8,128)} %param.7) | copy-start | bytes 14155780
  6.4 5.1 %copy-start.6 = (f32[128,128]{1,0:T(8,128)S(1)}, f32[128,128]{1,0:T(8,128)}, u32[]{:S(2)}) copy-start(f32[128,128]{1,0:T(8,128)} %param.10) | copy-start | bytes 196612
  6.4 10.3 %copy-start.1 = (bf16[2,768,256]{2,1,0:T(8,128)(2,1)S(1)}, bf16[2,768,256]{2,1,0:T(8,128)(2,1)}, u32[]{:S(2)}) copy-start(bf16[2,768,256]{2,1,0:T(8,128)(2,1)} %constant.5.clone.right_ref) | copy-start | bytes 2359300
  6.4 10.3 %copy-start.2 = (bf16[2,256,768]{2,1,0:T(8,128)(2,1)S(1)}, bf16[2,256,768]{2,1,0:T(8,128)(2,1)}, u32[]{:S(2)}) copy-start(bf16[2,256,768]{2,1,0:T(8,128)(2,1)} %constant.4.clone.left_ref) | copy-start | bytes 2359300
  6.4 10.4 %copy-start.3 = (f32[2,128,128]{2,1,0:T(8,128)S(1)}, f32[2,128,128]{2,1,0:T(8,128)}, u32[]{:S(2)}) copy-start(f32[2,128,128]{2,1,0:T(8,128)} %probe_ref.1) | copy-start | bytes 393220
  6.5 10.4 %copy-start.4 = (f32[2,128,128]{2,1,0:T(8,128)S(1)}, f32[2,128,128]{2,1,0:T(8,128)}, u32[]{:S(2)}) copy-start(f32[2,128,128]{2,1,0:T(8,128)} %rest_0_.3) | copy-start | bytes 393220
  8.0 8.8 %collective-permute-start.4 = (bf16[2,2,128,128]{3,2,1,0:T(8,128)(2,1)S(1)}, bf16[2,2,128,128]{3,2,1,0:T(8,128)(2,1)S(1)}, u32[]{:S(2)}, u32[]{:S(2)}) collective-permute-start(bf16[2,2,128,128]{3,2,1,0:T(8,128)(2,1)S(1)} %get-tuple-element.16), channel_id=1, source_target_pairs={{0,24},{1,25},{2,26},{3,27},{4,28},{5,29},{6,30},{7,31},{8,16},{9,... | collective-permute-start | bytes 393224 | tf_op jit(solution)/shard_map/ppermute | solution.py:312
  10.7 6.0 %collective-permute-start.3 = (bf16[2,2,128,128]{3,2,1,0:T(8,128)(2,1)S(1)}, bf16[2,2,128,128]{3,2,1,0:T(8,128)(2,1)S(1)}, u32[]{:S(2)}, u32[]{:S(2)}) collective-permute-start(bf16[2,2,128,128]{3,2,1,0:T(8,128)(2,1)S(1)} %get-tuple-element.16), channel_id=1, source_target_pairs={{0,16},{1,17},{2,18},{3,19},{4,20},{5,21},{6,22},{7,23},{8,24},{9,... | collective-permute-start | bytes 393224 | tf_op jit(solution)/shard_map/ppermute | solution.py:312
  11.2 5.5 %collective-permute-start.2 = (bf16[2,2,128,128]{3,2,1,0:T(8,128)(2,1)S(1)}, bf16[2,2,128,128]{3,2,1,0:T(8,128)(2,1)S(1)}, u32[]{:S(2)}, u32[]{:S(2)}) collective-permute-start(bf16[2,2,128,128]{3,2,1,0:T(8,128)(2,1)S(1)} %get-tuple-element.15.rest_2_), channel_id=1, source_target_pairs={{0,8},{1,9},{2,10},{3,11},{4,12},{5,13},{6,14},{7,15},{8,0},{9,1},... | collective-permute-start | bytes 393224 | tf_op jit(solution)/shard_map/ppermute | solution.py:312
  23.9 6.5 %collective-permute-start.7 = (bf16[528,128]{1,0:T(8,128)(2,1)S(1)}, bf16[528,128]{1,0:T(8,128)(2,1)S(1)}, u32[]{:S(2)}, u32[]{:S(2)}) collective-permute-start(bf16[528,128]{1,0:T(8,128)(2,1)S(1)} %get-tuple-element.18), channel_id=1, source_target_pairs={{0,18},{1,19},{2,16},{3,17},{4,22},{5,23},{6,20},{7,21},{8,26},{9,... | collective-permute-start | bytes 405512 | tf_op jit(solution)/shard_map/ppermute | solution.py:312
  26.4 6.4 %collective-permute-start.5 = (bf16[528,128]{1,0:T(8,128)(2,1)S(1)}, bf16[528,128]{1,0:T(8,128)(2,1)S(1)}, u32[]{:S(2)}, u32[]{:S(2)}) collective-permute-start(bf16[528,128]{1,0:T(8,128)(2,1)S(1)} %get-tuple-element.18), channel_id=1, source_target_pairs={{0,16},{1,17},{2,18},{3,19},{4,20},{5,21},{6,22},{7,23},{8,24},{9,... | collective-permute-start | bytes 405512 | tf_op jit(solution)/shard_map/ppermute | solution.py:312
  27.0 5.8 %collective-permute-start.6 = (bf16[528,128]{1,0:T(8,128)(2,1)S(1)}, bf16[528,128]{1,0:T(8,128)(2,1)S(1)}, u32[]{:S(2)}, u32[]{:S(2)}) collective-permute-start(bf16[528,128]{1,0:T(8,128)(2,1)S(1)} %get-tuple-element.17.refs_0_), channel_id=1, source_target_pairs={{0,2},{1,3},{2,0},{3,1},{4,6},{5,7},{6,4},{7,5},{8,10},{9,11},{10,... | collective-permute-start | bytes 405512 | tf_op jit(solution)/shard_map/ppermute | solution.py:312
  27.4 6.1 %collective-permute-start.8 = (bf16[528,128]{1,0:T(8,128)(2,1)S(1)}, bf16[528,128]{1,0:T(8,128)(2,1)S(1)}, u32[]{:S(2)}, u32[]{:S(2)}) collective-permute-start(bf16[528,128]{1,0:T(8,128)(2,1)S(1)} %get-tuple-element.17.refs_0_), channel_id=1, source_target_pairs={{0,1},{1,0},{2,3},{3,2},{4,5},{5,4},{6,7},{7,6},{8,9},{9,8},{10,11... | collective-permute-start | bytes 405512 | tf_op jit(solution)/shard_map/ppermute | solution.py:312
  30.4 3.2 %collective-permute-start.11 = (bf16[528,128]{1,0:T(8,128)(2,1)S(1)}, bf16[528,128]{1,0:T(8,128)(2,1)S(1)}, u32[]{:S(2)}, u32[]{:S(2)}) collective-permute-start(bf16[528,128]{1,0:T(8,128)(2,1)S(1)} %collective-permute-done.7.refs_3_), channel_id=1, source_target_pairs={{0,1},{1,0},{2,3},{3,2},{4,5},{5,4},{6,7},{7,6},{8,9},{9,8},{10,11... | collective-permute-start | bytes 405512 | tf_op jit(solution)/shard_map/ppermute | solution.py:312
  32.7 1.4 %collective-permute-start.9 = (bf16[528,128]{1,0:T(8,128)(2,1)S(1)}, bf16[528,128]{1,0:T(8,128)(2,1)S(1)}, u32[]{:S(2)}, u32[]{:S(2)}) collective-permute-start(bf16[528,128]{1,0:T(8,128)(2,1)S(1)} %collective-permute-done.5.refs_1_), channel_id=1, source_target_pairs={{0,1},{1,0},{2,3},{3,2},{4,5},{5,4},{6,7},{7,6},{8,9},{9,8},{10,11... | collective-permute-start | bytes 405512 | tf_op jit(solution)/shard_map/ppermute | solution.py:312
  32.7 1.5 %collective-permute-start.10 = (bf16[528,128]{1,0:T(8,128)(2,1)S(1)}, bf16[528,128]{1,0:T(8,128)(2,1)S(1)}, u32[]{:S(2)}, u32[]{:S(2)}) collective-permute-start(bf16[528,128]{1,0:T(8,128)(2,1)S(1)} %collective-permute-done.6.refs_2_), channel_id=1, source_target_pairs={{0,1},{1,0},{2,3},{3,2},{4,5},{5,4},{6,7},{7,6},{8,9},{9,8},{10,11... | collective-permute-start | bytes 405512 | tf_op jit(solution)/shard_map/ppermute | solution.py:312

commit v18 on v17

--- a/solution.py
+++ b/solution.py
@@ -56,9 +56,9 @@
 
 def window_kernel(members, obj_ref, touched_ref, *rest):
     del touched_ref
-    table, table_sems = rest[-2:]
+    table, cut, table_sems = rest[-3:]
     clusters, count = table.shape[:2]
-    pos_refs, out_refs, code_ref = rest[:clusters], rest[clusters:-3], rest[-3]
+    pos_refs, out_refs, code_ref = rest[:clusters], rest[clusters:-4], rest[-4]
     window = out_refs[0].shape[-1]
     rows, cols = obj_ref.shape[-2:]
     tall, wide = window + 8, window + 128
@@ -74,16 +74,24 @@
     for p in range(count):
         for axis in range(2):
             table[0, p, axis] = pos_refs[0][p, axis]
-    for fetch in fetches:
-        fetch.wait()
-
-    def corner(m, p):
-        at = home ^ cluster ^ m
-        row, col = table[at, p, 0], table[at, p, 1]
-        row_base = pl.multiple_of(jnp.minimum(row >> 3, (rows - tall) // 8) * 8, 8)
-        col_base = pl.multiple_of(jnp.minimum(col >> 7, (cols - wide) // 128) * 128, 128)
-        return row_base, col_base, row - row_base, col - col_base
-
+
+    def take(a):
+        for p in range(count):
+            row, col = table[a, p, 0], table[a, p, 1]
+            row_base = pl.multiple_of(jnp.minimum(row >> 3, (rows - tall) // 8) * 8, 8)
+            col_base = pl.multiple_of(jnp.minimum(col >> 7, (cols - wide) // 128) * 128, 128)
+            lift = jnp.where(row == row_base, 0, tall - (row - row_base))
+            shift = jnp.where(col == col_base, 0, wide - (col - col_base))
+            for part in range(2):
+                block = obj_ref[part, pl.ds(row_base, tall), pl.ds(col_base, wide)]
+                block = pltpu.roll(block, shift, 1)[:, :window]
+                block = pltpu.roll(block, lift, 0)[:window]
+                cut[home ^ cluster ^ a, p, part] = block.astype(bf16)
+
+    take(0)
+    for a in range(1, clusters):
+        fetches[a - 1].wait()
+        take(a)
     line = lax.broadcasted_iota(jnp.int32, (code_rows, window), 0)
     code = jnp.zeros((code_rows, window), jnp.int32)
     for p in range(count):
@@ -91,16 +99,8 @@
         for n, value in enumerate((row >> 3, row & 7, col >> 3, col & 7)):
             code = jnp.where(line == 4 * p + n, value, code)
     code_ref[...] = code.astype(f32).astype(bf16)
-    for m in reversed(range(clusters)):
-        for p in range(count):
-            row_base, col_base, row_off, col_off = corner(m, p)
-            lift = jnp.where(row_off == 0, 0, tall - row_off)
-            shift = jnp.where(col_off == 0, 0, wide - col_off)
-            for part in range(2):
-                block = obj_ref[part, pl.ds(row_base, tall), pl.ds(col_base, wide)]
-                block = pltpu.roll(block, shift, 1)[:, :window]
-                block = pltpu.roll(block, lift, 0)[:window]
-                out_refs[m][p, part] = block.astype(bf16)
+    for m, out_ref in enumerate(out_refs):
+        out_ref[...] = cut[m]
 
 
 def take_windows(obj, touched, positions, window, members):
@@ -116,6 +116,7 @@
         out_specs=[vmem] * (clusters + 1),
         scratch_shapes=[
             pltpu.SMEM((clusters, count, 2), jnp.int32),
+            pltpu.VMEM((clusters, count, 2, window, window), bf16),
             pltpu.SemaphoreType.DMA((clusters,)),
         ],
         compiler_params=pltpu.CompilerParams(vmem_limit_bytes=16 * 1024 * 1024),

time: 35.5 us -> 35.7 us (level)
  no operation moved by 1% of the time
where the time goes in v18:
time: 35.7 us; the launch traced here: 35.4 us
  starting transfers between devices  11.7 us (33%)
  waiting for transfers between devices  11 us (31%)
  Pallas kernels  9.93 us (28%)
  local copies, waits for them, and re-layouts  2.6 us (7%)
    ppermute x12, starting transfers between devices, swap(): return lax.ppermute(block, ('depth', 'dp'), route)  11.7 us
    ppermute x12, waiting for transfers between devices, swap(): return lax.ppermute(block, ('depth', 'dp'), route)  11 us
    pallas_call x1, Pallas kernels, run_waves(): pl.pallas_call(functools.partial(wave_kernel, members, len(measured)), ou...  7.05 us
    unnamed x14, local copies, waits for them, and re-layouts  2.36 us
    pallas_call x1, Pallas kernels, take_windows(): pl.pallas_call(functools.partial(window_kernel, members), out_shape=[jax....  1.34 us
    pallas_call x1, Pallas kernels, place_windows(): pl.pallas_call(second_kernel, out_shape=jax.ShapeDtypeStruct((2, stripe,...  1.26 us
  transfers between devices with their start and end apart: 12, of which 6 were waited for; matrix products, arithmetic and copies ran while one was open for 1% of the time, Pallas kernels for 5%

profile of v18, /device:TPU:0, one launch (start us, length us, event | category | flops | bytes accessed | tf_op | source)
XLA Modules:
  0.0 35.4 jit_solution(762146890158942544)
XLA Ops:
  0.0 4.0 %collective-permute-start = (s32[2,2]{1,0:T(2,128)}, s32[2,2]{1,0:T(2,128)S(1)}, u32[]{:S(2)}, u32[]{:S(2)}) collective-permute-start(s32[2,2]{1,0:T(2,128)} %rest_0_.2), channel_id=1, source_target_pairs={{0,4},{1,5},{2,6},{3,7},{4,0},{5,1},{6,2},{7,3},{8,12},{9,13},{10,... | collective-permute-start | bytes 56 | tf_op jit(solution)/shard_map/ppermute | solution.py:313
  4.0 0.1 collective-permute-start.1
  4.1 2.3 %copy-done = f32[1,2,768,768]{3,2,1,0:T(8,128)S(1)} copy-done((f32[1,2,768,768]{3,2,1,0:T(8,128)S(1)}, f32[1,2,768,768]{3,2,1,0:T(8,128)}, u32[]{:S(2)}) %copy-start) | copy-done | bytes 4718616
  6.5 0.0 collective-permute-done.rest_1_
  6.5 1.3 %take_windows.1 = (bf16[2,2,128,128]{3,2,1,0:T(8,128)(2,1)S(1)}, bf16[2,2,128,128]{3,2,1,0:T(8,128)(2,1)S(1)}, bf16[16,128]{1,0:T(8,128)(2,1)S(1)}) custom-call(f32[2,768,768]{2,1,0:T(8,128)S(1)} %bitcast.7, f32[8,128]{1,0:T(8,128)S(1)} %touch_slice.1.touched_ref, s32[2,2]{1,0:T(2,128)S(1)} %copy-done.5, s32[2,2]{1,0:T(2,128)S(1)} %collective-permute-done.rest_1_), custom_call_target="tpu_custom_call" | custom-call | tf_op jit(solution)/shard_map/take_windows/pallas_call | solution.py:111
  7.8 2.8 %collective-permute-start.4 = (bf16[2,2,128,128]{3,2,1,0:T(8,128)(2,1)S(1)}, bf16[2,2,128,128]{3,2,1,0:T(8,128)(2,1)S(1)}, u32[]{:S(2)}, u32[]{:S(2)}) collective-permute-start(bf16[2,2,128,128]{3,2,1,0:T(8,128)(2,1)S(1)} %get-tuple-element.16), channel_id=1, source_target_pairs={{0,24},{1,25},{2,26},{3,27},{4,28},{5,29},{6,30},{7,31},{8,16},{9,... | collective-permute-start | bytes 393224 | tf_op jit(solution)/shard_map/ppermute | solution.py:313
  10.6 0.5 %collective-permute-start.3 = (bf16[2,2,128,128]{3,2,1,0:T(8,128)(2,1)S(1)}, bf16[2,2,128,128]{3,2,1,0:T(8,128)(2,1)S(1)}, u32[]{:S(2)}, u32[]{:S(2)}) collective-permute-start(bf16[2,2,128,128]{3,2,1,0:T(8,128)(2,1)S(1)} %get-tuple-element.16), channel_id=1, source_target_pairs={{0,16},{1,17},{2,18},{3,19},{4,20},{5,21},{6,22},{7,23},{8,24},{9,... | collective-permute-start | bytes 393224 | tf_op jit(solution)/shard_map/ppermute | solution.py:313
  11.1 0.3 collective-permute-start.2
  11.4 0.2 cosine_bitcast_fusion
  11.7 1.3 %collective-permute-done.1.rest_1_ = f32[2,128,128]{2,1,0:T(8,128)S(1)} collective-permute-done((f32[2,128,128]{2,1,0:T(8,128)}, f32[2,128,128]{2,1,0:T(8,128)S(1)}, u32[]{:S(2)}, u32[]{:S(2)}) %collective-permute-start.1) | collective-permute-done | bytes 131104 | tf_op jit(solution)/shard_map/ppermute | solution.py:313
  12.9 3.7 %collective-permute-done.2.rest_3_ = bf16[2,2,128,128]{3,2,1,0:T(8,128)(2,1)S(1)} collective-permute-done((bf16[2,2,128,128]{3,2,1,0:T(8,128)(2,1)S(1)}, bf16[2,2,128,128]{3,2,1,0:T(8,128)(2,1)S(1)}, u32[]{:S(2)}, u32[]{:S(2)}) %collective-permute-start.2) | collective-permute-done | bytes 131104 | tf_op jit(solution)/shard_map/ppermute | solution.py:313
  16.7 0.0 collective-permute-done.3.rest_4_
  16.7 7.1 %run_waves.1 = (bf16[528,128]{1,0:T(8,128)(2,1)S(1)}, bf16[528,128]{1,0:T(8,128)(2,1)S(1)}) custom-call(f32[2,128,128]{2,1,0:T(8,128)S(1)} %copy-done.3, f32[2,128,128]{2,1,0:T(8,128)S(1)} %pad_maximum_fusion.kern_ref, bf16[2,256,768]{2,1,0:T(8,128)(2,1)S(1)} %copy-done.2, bf16[2,768,256]{2,1,0:T(8,128)(2,1)S(1)} %copy-done.1, ...), custom_call_target="tpu_custom_call" | custom-call | tf_op jit(solution)/shard_map/run_waves/pallas_call | solution.py:219
  23.8 2.5 %collective-permute-start.7 = (bf16[528,128]{1,0:T(8,128)(2,1)S(1)}, bf16[528,128]{1,0:T(8,128)(2,1)S(1)}, u32[]{:S(2)}, u32[]{:S(2)}) collective-permute-start(bf16[528,128]{1,0:T(8,128)(2,1)S(1)} %get-tuple-element.18), channel_id=1, source_target_pairs={{0,18},{1,19},{2,16},{3,17},{4,22},{5,23},{6,20},{7,21},{8,26},{9,... | collective-permute-start | bytes 405512 | tf_op jit(solution)/shard_map/ppermute | solution.py:313
  26.2 0.6 %collective-permute-start.5 = (bf16[528,128]{1,0:T(8,128)(2,1)S(1)}, bf16[528,128]{1,0:T(8,128)(2,1)S(1)}, u32[]{:S(2)}, u32[]{:S(2)}) collective-permute-start(bf16[528,128]{1,0:T(8,128)(2,1)S(1)} %get-tuple-element.18), channel_id=1, source_target_pairs={{0,16},{1,17},{2,18},{3,19},{4,20},{5,21},{6,22},{7,23},{8,24},{9,... | collective-permute-start | bytes 405512 | tf_op jit(solution)/shard_map/ppermute | solution.py:313
  26.9 0.4 %collective-permute-start.6 = (bf16[528,128]{1,0:T(8,128)(2,1)S(1)}, bf16[528,128]{1,0:T(8,128)(2,1)S(1)}, u32[]{:S(2)}, u32[]{:S(2)}) collective-permute-start(bf16[528,128]{1,0:T(8,128)(2,1)S(1)} %get-tuple-element.17.refs_0_), channel_id=1, source_target_pairs={{0,2},{1,3},{2,0},{3,1},{4,6},{5,7},{6,4},{7,5},{8,10},{9,11},{10,... | collective-permute-start | bytes 405512 | tf_op jit(solution)/shard_map/ppermute | solution.py:313
  27.3 0.0 collective-permute-start.8
  27.3 2.9 %collective-permute-done.7.refs_3_ = bf16[528,128]{1,0:T(8,128)(2,1)S(1)} collective-permute-done((bf16[528,128]{1,0:T(8,128)(2,1)S(1)}, bf16[528,128]{1,0:T(8,128)(2,1)S(1)}, u32[]{:S(2)}, u32[]{:S(2)}) %collective-permute-start.7) | collective-permute-done | bytes 135200 | tf_op jit(solution)/shard_map/ppermute | solution.py:313
  30.3 2.4 %collective-permute-done.5.refs_1_ = bf16[528,128]{1,0:T(8,128)(2,1)S(1)} collective-permute-done((bf16[528,128]{1,0:T(8,128)(2,1)S(1)}, bf16[528,128]{1,0:T(8,128)(2,1)S(1)}, u32[]{:S(2)}, u32[]{:S(2)}) %collective-permute-start.5) | collective-permute-done | bytes 135200 | tf_op jit(solution)/shard_map/ppermute | solution.py:313
  32.6 0.5 %collective-permute-start.10 = (bf16[528,128]{1,0:T(8,128)(2,1)S(1)}, bf16[528,128]{1,0:T(8,128)(2,1)S(1)}, u32[]{:S(2)}, u32[]{:S(2)}) collective-permute-start(bf16[528,128]{1,0:T(8,128)(2,1)S(1)} %collective-permute-done.6.refs_2_), channel_id=1, source_target_pairs={{0,1},{1,0},{2,3},{3,2},{4,5},{5,4},{6,7},{7,6},{8,9},{9,8},{10,11... | collective-permute-start | bytes 405512 | tf_op jit(solution)/shard_map/ppermute | solution.py:313
  33.1 0.3 place_near.1.start_ref
  33.4 0.5 %collective-permute-done.9.refs_1_ = bf16[528,128]{1,0:T(8,128)(2,1)S(1)} collective-permute-done((bf16[528,128]{1,0:T(8,128)(2,1)S(1)}, bf16[528,128]{1,0:T(8,128)(2,1)S(1)}, u32[]{:S(2)}, u32[]{:S(2)}) %collective-permute-start.9) | collective-permute-done | bytes 135200 | tf_op jit(solution)/shard_map/ppermute | solution.py:313
  34.0 0.2 collective-permute-done.10.refs_2_
  34.2 1.3 %place_far.1 = f32[2,96,768]{2,1,0:T(8,128)} custom-call(f32[2,360,896]{2,1,0:T(8,128)S(1)} %place_near.1.start_ref, bf16[528,128]{1,0:T(8,128)(2,1)S(1)} %collective-permute-done.8.refs_0_, bf16[528,128]{1,0:T(8,128)(2,1)S(1)} %collective-permute-done.9.refs_1_, bf16[528,128]{1,0:T(8,128)(2,1)S(1)} %collective-permute-done.10.refs_2_, ...), custom_call_target="tpu_custom_call" | custom-call | tf_op jit(solution)/shard_map/place_far/pallas_call | solution.py:295
  (21 shorter events, 0.1 us)
Async XLA Ops:
  0.0 6.5 %copy-start.5 = (s32[2,2]{1,0:T(2,128)S(1)}, s32[2,2]{1,0:T(2,128)}, u32[]{:S(2)}) copy-start(s32[2,2]{1,0:T(2,128)} %rest_0_.2) | copy-start | bytes 52
  0.0 6.5 %collective-permute-start = (s32[2,2]{1,0:T(2,128)}, s32[2,2]{1,0:T(2,128)S(1)}, u32[]{:S(2)}, u32[]{:S(2)}) collective-permute-start(s32[2,2]{1,0:T(2,128)} %rest_0_.2), channel_id=1, source_target_pairs={{0,4},{1,5},{2,6},{3,7},{4,0},{5,1},{6,2},{7,3},{8,12},{9,13},{10,... | collective-permute-start | bytes 56 | tf_op jit(solution)/shard_map/ppermute | solution.py:313
  4.0 8.9 %collective-permute-start.1 = (f32[2,128,128]{2,1,0:T(8,128)}, f32[2,128,128]{2,1,0:T(8,128)S(1)}, u32[]{:S(2)}, u32[]{:S(2)}) collective-permute-start(f32[2,128,128]{2,1,0:T(8,128)} %rest_0_.3), channel_id=1, source_target_pairs={{0,4},{1,5},{2,6},{3,7},{4,0},{5,1},{6,2},{7,3},{8,12},{9,13},{10,... | collective-permute-start | bytes 393224 | tf_op jit(solution)/shard_map/ppermute | solution.py:313
  4.1 2.3 %copy-start = (f32[1,2,768,768]{3,2,1,0:T(8,128)S(1)}, f32[1,2,768,768]{3,2,1,0:T(8,128)}, u32[]{:S(2)}) copy-start(f32[1,2,768,768]{3,2,1,0:T(8,128)} %param.7) | copy-start | bytes 14155780
  6.4 5.0 %copy-start.6 = (f32[128,128]{1,0:T(8,128)S(1)}, f32[128,128]{1,0:T(8,128)}, u32[]{:S(2)}) copy-start(f32[128,128]{1,0:T(8,128)} %param.10) | copy-start | bytes 196612
  6.4 10.2 %copy-start.1 = (bf16[2,768,256]{2,1,0:T(8,128)(2,1)S(1)}, bf16[2,768,256]{2,1,0:T(8,128)(2,1)}, u32[]{:S(2)}) copy-start(bf16[2,768,256]{2,1,0:T(8,128)(2,1)} %constant.5.clone.right_ref) | copy-start | bytes 2359300
  6.4 10.2 %copy-start.2 = (bf16[2,256,768]{2,1,0:T(8,128)(2,1)S(1)}, bf16[2,256,768]{2,1,0:T(8,128)(2,1)}, u32[]{:S(2)}) copy-start(bf16[2,256,768]{2,1,0:T(8,128)(2,1)} %constant.4.clone.left_ref) | copy-start | bytes 2359300
  6.4 10.2 %copy-start.3 = (f32[2,128,128]{2,1,0:T(8,128)S(1)}, f32[2,128,128]{2,1,0:T(8,128)}, u32[]{:S(2)}) copy-start(f32[2,128,128]{2,1,0:T(8,128)} %probe_ref.1) | copy-start | bytes 393220
  6.5 10.2 %copy-start.4 = (f32[2,128,128]{2,1,0:T(8,128)S(1)}, f32[2,128,128]{2,1,0:T(8,128)}, u32[]{:S(2)}) copy-start(f32[2,128,128]{2,1,0:T(8,128)} %rest_0_.3) | copy-start | bytes 393220
  7.8 8.8 %collective-permute-start.4 = (bf16[2,2,128,128]{3,2,1,0:T(8,128)(2,1)S(1)}, bf16[2,2,128,128]{3,2,1,0:T(8,128)(2,1)S(1)}, u32[]{:S(2)}, u32[]{:S(2)}) collective-permute-start(bf16[2,2,128,128]{3,2,1,0:T(8,128)(2,1)S(1)} %get-tuple-element.16), channel_id=1, source_target_pairs={{0,24},{1,25},{2,26},{3,27},{4,28},{5,29},{6,30},{7,31},{8,16},{9,... | collective-permute-start | bytes 393224 | tf_op jit(solution)/shard_map/ppermute | solution.py:313
  10.6 6.0 %collective-permute-start.3 = (bf16[2,2,128,128]{3,2,1,0:T(8,128)(2,1)S(1)}, bf16[2,2,128,128]{3,2,1,0:T(8,128)(2,1)S(1)}, u32[]{:S(2)}, u32[]{:S(2)}) collective-permute-start(bf16[2,2,128,128]{3,2,1,0:T(8,128)(2,1)S(1)} %get-tuple-element.16), channel_id=1, source_target_pairs={{0,16},{1,17},{2,18},{3,19},{4,20},{5,21},{6,22},{7,23},{8,24},{9,... | collective-permute-start | bytes 393224 | tf_op jit(solution)/shard_map/ppermute | solution.py:313
  11.1 5.5 %collective-permute-start.2 = (bf16[2,2,128,128]{3,2,1,0:T(8,128)(2,1)S(1)}, bf16[2,2,128,128]{3,2,1,0:T(8,128)(2,1)S(1)}, u32[]{:S(2)}, u32[]{:S(2)}) collective-permute-start(bf16[2,2,128,128]{3,2,1,0:T(8,128)(2,1)S(1)} %get-tuple-element.15.rest_2_), channel_id=1, source_target_pairs={{0,8},{1,9},{2,10},{3,11},{4,12},{5,13},{6,14},{7,15},{8,0},{9,1},... | collective-permute-start | bytes 393224 | tf_op jit(solution)/shard_map/ppermute | solution.py:313
  23.8 6.5 %collective-permute-start.7 = (bf16[528,128]{1,0:T(8,128)(2,1)S(1)}, bf16[528,128]{1,0:T(8,128)(2,1)S(1)}, u32[]{:S(2)}, u32[]{:S(2)}) collective-permute-start(bf16[528,128]{1,0:T(8,128)(2,1)S(1)} %get-tuple-element.18), channel_id=1, source_target_pairs={{0,18},{1,19},{2,16},{3,17},{4,22},{5,23},{6,20},{7,21},{8,26},{9,... | collective-permute-start | bytes 405512 | tf_op jit(solution)/shard_map/ppermute | solution.py:313
  26.2 6.4 %collective-permute-start.5 = (bf16[528,128]{1,0:T(8,128)(2,1)S(1)}, bf16[528,128]{1,0:T(8,128)(2,1)S(1)}, u32[]{:S(2)}, u32[]{:S(2)}) collective-permute-start(bf16[528,128]{1,0:T(8,128)(2,1)S(1)} %get-tuple-element.18), channel_id=1, source_target_pairs={{0,16},{1,17},{2,18},{3,19},{4,20},{5,21},{6,22},{7,23},{8,24},{9,... | collective-permute-start | bytes 405512 | tf_op jit(solution)/shard_map/ppermute | solution.py:313
  26.9 5.8 %collective-permute-start.6 = (bf16[528,128]{1,0:T(8,128)(2,1)S(1)}, bf16[528,128]{1,0:T(8,128)(2,1)S(1)}, u32[]{:S(2)}, u32[]{:S(2)}) collective-permute-start(bf16[528,128]{1,0:T(8,128)(2,1)S(1)} %get-tuple-element.17.refs_0_), channel_id=1, source_target_pairs={{0,2},{1,3},{2,0},{3,1},{4,6},{5,7},{6,4},{7,5},{8,10},{9,11},{10,... | collective-permute-start | bytes 405512 | tf_op jit(solution)/shard_map/ppermute | solution.py:313
  27.3 6.1 %collective-permute-start.8 = (bf16[528,128]{1,0:T(8,128)(2,1)S(1)}, bf16[528,128]{1,0:T(8,128)(2,1)S(1)}, u32[]{:S(2)}, u32[]{:S(2)}) collective-permute-start(bf16[528,128]{1,0:T(8,128)(2,1)S(1)} %get-tuple-element.17.refs_0_), channel_id=1, source_target_pairs={{0,1},{1,0},{2,3},{3,2},{4,5},{5,4},{6,7},{7,6},{8,9},{9,8},{10,11... | collective-permute-start | bytes 405512 | tf_op jit(solution)/shard_map/ppermute | solution.py:313
  30.3 3.2 %collective-permute-start.11 = (bf16[528,128]{1,0:T(8,128)(2,1)S(1)}, bf16[528,128]{1,0:T(8,128)(2,1)S(1)}, u32[]{:S(2)}, u32[]{:S(2)}) collective-permute-start(bf16[528,128]{1,0:T(8,128)(2,1)S(1)} %collective-permute-done.7.refs_3_), channel_id=1, source_target_pairs={{0,1},{1,0},{2,3},{3,2},{4,5},{5,4},{6,7},{7,6},{8,9},{9,8},{10,11... | collective-permute-start | bytes 405512 | tf_op jit(solution)/shard_map/ppermute | solution.py:313
  32.6 1.4 %collective-permute-start.9 = (bf16[528,128]{1,0:T(8,128)(2,1)S(1)}, bf16[528,128]{1,0:T(8,128)(2,1)S(1)}, u32[]{:S(2)}, u32[]{:S(2)}) collective-permute-start(bf16[528,128]{1,0:T(8,128)(2,1)S(1)} %collective-permute-done.5.refs_1_), channel_id=1, source_target_pairs={{0,1},{1,0},{2,3},{3,2},{4,5},{5,4},{6,7},{7,6},{8,9},{9,8},{10,11... | collective-permute-start | bytes 405512 | tf_op jit(solution)/shard_map/ppermute | solution.py:313
  32.6 1.5 %collective-permute-start.10 = (bf16[528,128]{1,0:T(8,128)(2,1)S(1)}, bf16[528,128]{1,0:T(8,128)(2,1)S(1)}, u32[]{:S(2)}, u32[]{:S(2)}) collective-permute-start(bf16[528,128]{1,0:T(8,128)(2,1)S(1)} %collective-permute-done.6.refs_2_), channel_id=1, source_target_pairs={{0,1},{1,0},{2,3},{3,2},{4,5},{5,4},{6,7},{7,6},{8,9},{9,8},{10,11... | collective-permute-start | bytes 405512 | tf_op jit(solution)/shard_map/ppermute | solution.py:313

commit v19 on v18

--- a/solution.py
+++ b/solution.py
@@ -335,7 +335,9 @@
         for plane in range(0, members, 2)
         for m in range(0, depth, 2)
     ]
-    return place_windows(blocks, [swap(block, 0, 1) for block in blocks], rows // dp, cols)[None]
+    passed = [swap(block, 0, 1) for block in blocks]
+    early, late = blocks + [passed[0], passed[-1]], passed[1:-1]
+    return place_windows(early, late, rows // dp, cols)[None]
 
 
 def solution(mesh):

time: 35.7 us -> 34.6 us (0.969)
  waiting for transfers between devices: 11 us -> 10.4 us
  starting transfers between devices: 11.7 us -> 11.3 us
    ppermute x12, waiting for transfers between devices: 11 us -> 10.4 us  [swap(): return lax.ppermute(block, ('depth', 'dp'), route)]
    ppermute x12, starting transfers between devices: 11.7 us -> 11.3 us  [swap(): return lax.ppermute(block, ('depth', 'dp'), route)]
  transfers between devices with their start and end apart: 12 -> 12, of which waited for: 6 -> 7; matrix products, arithmetic and copies ran while one was open for 1% -> 1% of each run, Pallas kernels for 5% -> 6%
where the time goes in v19:
time: 34.6 us; the launch traced here: 34.4 us
  starting transfers between devices  11.3 us (33%)
  waiting for transfers between devices  10.4 us (30%)
  Pallas kernels  9.95 us (29%)
  local copies, waits for them, and re-layouts  2.6 us (8%)
    ppermute x12, starting transfers between devices, swap(): return lax.ppermute(block, ('depth', 'dp'), route)  11.3 us
    ppermute x12, waiting for transfers between devices, swap(): return lax.ppermute(block, ('depth', 'dp'), route)  10.4 us
    pallas_call x1, Pallas kernels, run_waves(): pl.pallas_call(functools.partial(wave_kernel, members, len(measured)), ou...  7.06 us
    unnamed x14, local copies, waits for them, and re-layouts  2.36 us
    pallas_call x1, Pallas kernels, take_windows(): pl.pallas_call(functools.partial(window_kernel, members), out_shape=[jax....  1.34 us
    pallas_call x1, Pallas kernels, place_windows(): pl.pallas_call(second_kernel, out_shape=jax.ShapeDtypeStruct((2, stripe,...  0.97 us
  transfers between devices with their start and end apart: 12, of which 7 were waited for; matrix products, arithmetic and copies ran while one was open for 1% of the time, Pallas kernels for 6%

profile of v19, /device:TPU:0, one launch (start us, length us, event | category | flops | bytes accessed | tf_op | source)
XLA Modules:
  0.0 34.4 jit_solution(6310464109571241022)
XLA Ops:
  0.0 4.0 %collective-permute-start = (s32[2,2]{1,0:T(2,128)}, s32[2,2]{1,0:T(2,128)S(1)}, u32[]{:S(2)}, u32[]{:S(2)}) collective-permute-start(s32[2,2]{1,0:T(2,128)} %rest_0_.2), channel_id=1, source_target_pairs={{0,4},{1,5},{2,6},{3,7},{4,0},{5,1},{6,2},{7,3},{8,12},{9,13},{10,... | collective-permute-start | bytes 56 | tf_op jit(solution)/shard_map/ppermute | solution.py:313
  4.0 0.1 collective-permute-start.1
  4.1 2.3 %copy-done = f32[1,2,768,768]{3,2,1,0:T(8,128)S(1)} copy-done((f32[1,2,768,768]{3,2,1,0:T(8,128)S(1)}, f32[1,2,768,768]{3,2,1,0:T(8,128)}, u32[]{:S(2)}) %copy-start) | copy-done | bytes 4718616
  6.5 0.0 collective-permute-done.rest_1_
  6.5 1.3 %take_windows.1 = (bf16[2,2,128,128]{3,2,1,0:T(8,128)(2,1)S(1)}, bf16[2,2,128,128]{3,2,1,0:T(8,128)(2,1)S(1)}, bf16[16,128]{1,0:T(8,128)(2,1)S(1)}) custom-call(f32[2,768,768]{2,1,0:T(8,128)S(1)} %bitcast.7, f32[8,128]{1,0:T(8,128)S(1)} %touch_slice.1.touched_ref, s32[2,2]{1,0:T(2,128)S(1)} %copy-done.5, s32[2,2]{1,0:T(2,128)S(1)} %collective-permute-done.rest_1_), custom_call_target="tpu_custom_call" | custom-call | tf_op jit(solution)/shard_map/take_windows/pallas_call | solution.py:111
  7.8 1.9 %collective-permute-start.3 = (bf16[2,2,128,128]{3,2,1,0:T(8,128)(2,1)S(1)}, bf16[2,2,128,128]{3,2,1,0:T(8,128)(2,1)S(1)}, u32[]{:S(2)}, u32[]{:S(2)}) collective-permute-start(bf16[2,2,128,128]{3,2,1,0:T(8,128)(2,1)S(1)} %get-tuple-element.16), channel_id=1, source_target_pairs={{0,16},{1,17},{2,18},{3,19},{4,20},{5,21},{6,22},{7,23},{8,24},{9,... | collective-permute-start | bytes 393224 | tf_op jit(solution)/shard_map/ppermute | solution.py:313
  9.7 1.4 %collective-permute-start.4 = (bf16[2,2,128,128]{3,2,1,0:T(8,128)(2,1)S(1)}, bf16[2,2,128,128]{3,2,1,0:T(8,128)(2,1)S(1)}, u32[]{:S(2)}, u32[]{:S(2)}) collective-permute-start(bf16[2,2,128,128]{3,2,1,0:T(8,128)(2,1)S(1)} %get-tuple-element.16), channel_id=1, source_target_pairs={{0,24},{1,25},{2,26},{3,27},{4,28},{5,29},{6,30},{7,31},{8,16},{9,... | collective-permute-start | bytes 393224 | tf_op jit(solution)/shard_map/ppermute | solution.py:313
  11.1 0.3 collective-permute-start.2
  11.4 0.2 cosine_bitcast_fusion
  11.7 1.3 %collective-permute-done.1.rest_1_ = f32[2,128,128]{2,1,0:T(8,128)S(1)} collective-permute-done((f32[2,128,128]{2,1,0:T(8,128)}, f32[2,128,128]{2,1,0:T(8,128)S(1)}, u32[]{:S(2)}, u32[]{:S(2)}) %collective-permute-start.1) | collective-permute-done | bytes 131104 | tf_op jit(solution)/shard_map/ppermute | solution.py:313
  12.9 4.0 %collective-permute-done.2.rest_3_ = bf16[2,2,128,128]{3,2,1,0:T(8,128)(2,1)S(1)} collective-permute-done((bf16[2,2,128,128]{3,2,1,0:T(8,128)(2,1)S(1)}, bf16[2,2,128,128]{3,2,1,0:T(8,128)(2,1)S(1)}, u32[]{:S(2)}, u32[]{:S(2)}) %collective-permute-start.2) | collective-permute-done | bytes 131104 | tf_op jit(solution)/shard_map/ppermute | solution.py:313
  16.9 0.0 collective-permute-done.3.rest_4_
  16.9 7.1 %run_waves.1 = (bf16[528,128]{1,0:T(8,128)(2,1)S(1)}, bf16[528,128]{1,0:T(8,128)(2,1)S(1)}) custom-call(f32[2,128,128]{2,1,0:T(8,128)S(1)} %copy-done.3, f32[2,128,128]{2,1,0:T(8,128)S(1)} %pad_maximum_fusion.kern_ref, bf16[2,256,768]{2,1,0:T(8,128)(2,1)S(1)} %copy-done.1, bf16[2,768,256]{2,1,0:T(8,128)(2,1)S(1)} %copy-done.2, ...), custom_call_target="tpu_custom_call" | custom-call | tf_op jit(solution)/shard_map/run_waves/pallas_call | solution.py:219
  24.0 2.6 %collective-permute-start.7 = (bf16[528,128]{1,0:T(8,128)(2,1)S(1)}, bf16[528,128]{1,0:T(8,128)(2,1)S(1)}, u32[]{:S(2)}, u32[]{:S(2)}) collective-permute-start(bf16[528,128]{1,0:T(8,128)(2,1)S(1)} %get-tuple-element.18), channel_id=1, source_target_pairs={{0,18},{1,19},{2,16},{3,17},{4,22},{5,23},{6,20},{7,21},{8,26},{9,... | collective-permute-start | bytes 405512 | tf_op jit(solution)/shard_map/ppermute | solution.py:313
  26.6 0.4 %collective-permute-start.6 = (bf16[528,128]{1,0:T(8,128)(2,1)S(1)}, bf16[528,128]{1,0:T(8,128)(2,1)S(1)}, u32[]{:S(2)}, u32[]{:S(2)}) collective-permute-start(bf16[528,128]{1,0:T(8,128)(2,1)S(1)} %get-tuple-element.17.refs_0_), channel_id=1, source_target_pairs={{0,2},{1,3},{2,0},{3,1},{4,6},{5,7},{6,4},{7,5},{8,10},{9,11},{10,... | collective-permute-start | bytes 405512 | tf_op jit(solution)/shard_map/ppermute | solution.py:313
  27.0 0.5 %collective-permute-start.5 = (bf16[528,128]{1,0:T(8,128)(2,1)S(1)}, bf16[528,128]{1,0:T(8,128)(2,1)S(1)}, u32[]{:S(2)}, u32[]{:S(2)}) collective-permute-start(bf16[528,128]{1,0:T(8,128)(2,1)S(1)} %get-tuple-element.18), channel_id=1, source_target_pairs={{0,16},{1,17},{2,18},{3,19},{4,20},{5,21},{6,22},{7,23},{8,24},{9,... | collective-permute-start | bytes 405512 | tf_op jit(solution)/shard_map/ppermute | solution.py:313
  27.6 2.7 %collective-permute-done.7.refs_3_ = bf16[528,128]{1,0:T(8,128)(2,1)S(1)} collective-permute-done((bf16[528,128]{1,0:T(8,128)(2,1)S(1)}, bf16[528,128]{1,0:T(8,128)(2,1)S(1)}, u32[]{:S(2)}, u32[]{:S(2)}) %collective-permute-start.7) | collective-permute-done | bytes 135200 | tf_op jit(solution)/shard_map/ppermute | solution.py:313
  30.3 1.3 %collective-permute-done.6.refs_2_ = bf16[528,128]{1,0:T(8,128)(2,1)S(1)} collective-permute-done((bf16[528,128]{1,0:T(8,128)(2,1)S(1)}, bf16[528,128]{1,0:T(8,128)(2,1)S(1)}, u32[]{:S(2)}, u32[]{:S(2)}) %collective-permute-start.6) | collective-permute-done | bytes 135200 | tf_op jit(solution)/shard_map/ppermute | solution.py:313
  31.6 0.4 %collective-permute-done.5.refs_1_ = bf16[528,128]{1,0:T(8,128)(2,1)S(1)} collective-permute-done((bf16[528,128]{1,0:T(8,128)(2,1)S(1)}, bf16[528,128]{1,0:T(8,128)(2,1)S(1)}, u32[]{:S(2)}, u32[]{:S(2)}) %collective-permute-start.5) | collective-permute-done | bytes 135200 | tf_op jit(solution)/shard_map/ppermute | solution.py:313
  32.0 0.1 collective-permute-start.10
  32.1 0.6 %place_near.1.start_ref = f32[2,360,896]{2,1,0:T(8,128)S(1)} custom-call(bf16[528,128]{1,0:T(8,128)(2,1)S(1)} %get-tuple-element.17.refs_0_, bf16[528,128]{1,0:T(8,128)(2,1)S(1)} %collective-permute-done.5.refs_1_, bf16[528,128]{1,0:T(8,128)(2,1)S(1)} %collective-permute-done.6.refs_2_, bf16[528,128]{1,0:T(8,128)(2,1)S(1)} %collective-permute-done.7.refs_3_, ...), custom_call_target="tpu_custom_call" | custom-call | tf_op jit(solution)/shard_map/place_near/pallas_call | solution.py:287
  32.7 0.2 collective-permute-done.11.refs_1_
  33.0 0.4 %collective-permute-done.10.refs_0_ = bf16[528,128]{1,0:T(8,128)(2,1)S(1)} collective-permute-done((bf16[528,128]{1,0:T(8,128)(2,1)S(1)}, bf16[528,128]{1,0:T(8,128)(2,1)S(1)}, u32[]{:S(2)}, u32[]{:S(2)}) %collective-permute-start.10) | collective-permute-done | bytes 135200 | tf_op jit(solution)/shard_map/ppermute | solution.py:313
  33.4 1.0 %place_far.1 = f32[2,96,768]{2,1,0:T(8,128)} custom-call(f32[2,360,896]{2,1,0:T(8,128)S(1)} %place_near.1.start_ref, bf16[528,128]{1,0:T(8,128)(2,1)S(1)} %collective-permute-done.10.refs_0_, bf16[528,128]{1,0:T(8,128)(2,1)S(1)} %collective-permute-done.11.refs_1_), custom_call_target="tpu_custom_call" | custom-call | tf_op jit(solution)/shard_map/place_far/pallas_call | solution.py:295
  (21 shorter events, 0.1 us)
Async XLA Ops:
  0.0 6.5 %copy-start.5 = (s32[2,2]{1,0:T(2,128)S(1)}, s32[2,2]{1,0:T(2,128)}, u32[]{:S(2)}) copy-start(s32[2,2]{1,0:T(2,128)} %rest_0_.2) | copy-start | bytes 52
  0.0 6.5 %collective-permute-start = (s32[2,2]{1,0:T(2,128)}, s32[2,2]{1,0:T(2,128)S(1)}, u32[]{:S(2)}, u32[]{:S(2)}) collective-permute-start(s32[2,2]{1,0:T(2,128)} %rest_0_.2), channel_id=1, source_target_pairs={{0,4},{1,5},{2,6},{3,7},{4,0},{5,1},{6,2},{7,3},{8,12},{9,13},{10,... | collective-permute-start | bytes 56 | tf_op jit(solution)/shard_map/ppermute | solution.py:313
  4.0 8.9 %collective-permute-start.1 = (f32[2,128,128]{2,1,0:T(8,128)}, f32[2,128,128]{2,1,0:T(8,128)S(1)}, u32[]{:S(2)}, u32[]{:S(2)}) collective-permute-start(f32[2,128,128]{2,1,0:T(8,128)} %rest_0_.3), channel_id=1, source_target_pairs={{0,4},{1,5},{2,6},{3,7},{4,0},{5,1},{6,2},{7,3},{8,12},{9,13},{10,... | collective-permute-start | bytes 393224 | tf_op jit(solution)/shard_map/ppermute | solution.py:313
  4.1 2.3 %copy-start = (f32[1,2,768,768]{3,2,1,0:T(8,128)S(1)}, f32[1,2,768,768]{3,2,1,0:T(8,128)}, u32[]{:S(2)}) copy-start(f32[1,2,768,768]{3,2,1,0:T(8,128)} %param.7) | copy-start | bytes 14155780
  6.4 5.0 %copy-start.6 = (f32[128,128]{1,0:T(8,128)S(1)}, f32[128,128]{1,0:T(8,128)}, u32[]{:S(2)}) copy-start(f32[128,128]{1,0:T(8,128)} %param.10) | copy-start | bytes 196612
  6.4 10.5 %copy-start.1 = (bf16[2,256,768]{2,1,0:T(8,128)(2,1)S(1)}, bf16[2,256,768]{2,1,0:T(8,128)(2,1)}, u32[]{:S(2)}) copy-start(bf16[2,256,768]{2,1,0:T(8,128)(2,1)} %constant.4.clone.left_ref) | copy-start | bytes 2359300
  6.4 10.5 %copy-start.2 = (bf16[2,768,256]{2,1,0:T(8,128)(2,1)S(1)}, bf16[2,768,256]{2,1,0:T(8,128)(2,1)}, u32[]{:S(2)}) copy-start(bf16[2,768,256]{2,1,0:T(8,128)(2,1)} %constant.5.clone.right_ref) | copy-start | bytes 2359300
  6.4 10.5 %copy-start.3 = (f32[2,128,128]{2,1,0:T(8,128)S(1)}, f32[2,128,128]{2,1,0:T(8,128)}, u32[]{:S(2)}) copy-start(f32[2,128,128]{2,1,0:T(8,128)} %probe_ref.1) | copy-start | bytes 393220
  6.5 10.5 %copy-start.4 = (f32[2,128,128]{2,1,0:T(8,128)S(1)}, f32[2,128,128]{2,1,0:T(8,128)}, u32[]{:S(2)}) copy-start(f32[2,128,128]{2,1,0:T(8,128)} %rest_0_.3) | copy-start | bytes 393220
  7.8 9.1 %collective-permute-start.3 = (bf16[2,2,128,128]{3,2,1,0:T(8,128)(2,1)S(1)}, bf16[2,2,128,128]{3,2,1,0:T(8,128)(2,1)S(1)}, u32[]{:S(2)}, u32[]{:S(2)}) collective-permute-start(bf16[2,2,128,128]{3,2,1,0:T(8,128)(2,1)S(1)} %get-tuple-element.16), channel_id=1, source_target_pairs={{0,16},{1,17},{2,18},{3,19},{4,20},{5,21},{6,22},{7,23},{8,24},{9,... | collective-permute-start | bytes 393224 | tf_op jit(solution)/shard_map/ppermute | solution.py:313
  9.7 7.2 %collective-permute-start.4 = (bf16[2,2,128,128]{3,2,1,0:T(8,128)(2,1)S(1)}, bf16[2,2,128,128]{3,2,1,0:T(8,128)(2,1)S(1)}, u32[]{:S(2)}, u32[]{:S(2)}) collective-permute-start(bf16[2,2,128,128]{3,2,1,0:T(8,128)(2,1)S(1)} %get-tuple-element.16), channel_id=1, source_target_pairs={{0,24},{1,25},{2,26},{3,27},{4,28},{5,29},{6,30},{7,31},{8,16},{9,... | collective-permute-start | bytes 393224 | tf_op jit(solution)/shard_map/ppermute | solution.py:313
  11.1 5.8 %collective-permute-start.2 = (bf16[2,2,128,128]{3,2,1,0:T(8,128)(2,1)S(1)}, bf16[2,2,128,128]{3,2,1,0:T(8,128)(2,1)S(1)}, u32[]{:S(2)}, u32[]{:S(2)}) collective-permute-start(bf16[2,2,128,128]{3,2,1,0:T(8,128)(2,1)S(1)} %get-tuple-element.15.rest_2_), channel_id=1, source_target_pairs={{0,8},{1,9},{2,10},{3,11},{4,12},{5,13},{6,14},{7,15},{8,0},{9,1},... | collective-permute-start | bytes 393224 | tf_op jit(solution)/shard_map/ppermute | solution.py:313
  24.0 6.3 %collective-permute-start.7 = (bf16[528,128]{1,0:T(8,128)(2,1)S(1)}, bf16[528,128]{1,0:T(8,128)(2,1)S(1)}, u32[]{:S(2)}, u32[]{:S(2)}) collective-permute-start(bf16[528,128]{1,0:T(8,128)(2,1)S(1)} %get-tuple-element.18), channel_id=1, source_target_pairs={{0,18},{1,19},{2,16},{3,17},{4,22},{5,23},{6,20},{7,21},{8,26},{9,... | collective-permute-start | bytes 405512 | tf_op jit(solution)/shard_map/ppermute | solution.py:313
  26.6 5.0 %collective-permute-start.6 = (bf16[528,128]{1,0:T(8,128)(2,1)S(1)}, bf16[528,128]{1,0:T(8,128)(2,1)S(1)}, u32[]{:S(2)}, u32[]{:S(2)}) collective-permute-start(bf16[528,128]{1,0:T(8,128)(2,1)S(1)} %get-tuple-element.17.refs_0_), channel_id=1, source_target_pairs={{0,2},{1,3},{2,0},{3,1},{4,6},{5,7},{6,4},{7,5},{8,10},{9,11},{10,... | collective-permute-start | bytes 405512 | tf_op jit(solution)/shard_map/ppermute | solution.py:313
  27.0 5.0 %collective-permute-start.5 = (bf16[528,128]{1,0:T(8,128)(2,1)S(1)}, bf16[528,128]{1,0:T(8,128)(2,1)S(1)}, u32[]{:S(2)}, u32[]{:S(2)}) collective-permute-start(bf16[528,128]{1,0:T(8,128)(2,1)S(1)} %get-tuple-element.18), channel_id=1, source_target_pairs={{0,16},{1,17},{2,18},{3,19},{4,20},{5,21},{6,22},{7,23},{8,24},{9,... | collective-permute-start | bytes 405512 | tf_op jit(solution)/shard_map/ppermute | solution.py:313
  27.6 4.6 %collective-permute-start.8 = (bf16[528,128]{1,0:T(8,128)(2,1)S(1)}, bf16[528,128]{1,0:T(8,128)(2,1)S(1)}, u32[]{:S(2)}, u32[]{:S(2)}) collective-permute-start(bf16[528,128]{1,0:T(8,128)(2,1)S(1)} %get-tuple-element.17.refs_0_), channel_id=1, source_target_pairs={{0,1},{1,0},{2,3},{3,2},{4,5},{5,4},{6,7},{7,6},{8,9},{9,8},{10,11... | collective-permute-start | bytes 405512 | tf_op jit(solution)/shard_map/ppermute | solution.py:313
  30.3 1.8 %collective-permute-start.9 = (bf16[528,128]{1,0:T(8,128)(2,1)S(1)}, bf16[528,128]{1,0:T(8,128)(2,1)S(1)}, u32[]{:S(2)}, u32[]{:S(2)}) collective-permute-start(bf16[528,128]{1,0:T(8,128)(2,1)S(1)} %collective-permute-done.7.refs_3_), channel_id=1, source_target_pairs={{0,1},{1,0},{2,3},{3,2},{4,5},{5,4},{6,7},{7,6},{8,9},{9,8},{10,11... | collective-permute-start | bytes 405512 | tf_op jit(solution)/shard_map/ppermute | solution.py:313
  31.6 1.4 %collective-permute-start.11 = (bf16[528,128]{1,0:T(8,128)(2,1)S(1)}, bf16[528,128]{1,0:T(8,128)(2,1)S(1)}, u32[]{:S(2)}, u32[]{:S(2)}) collective-permute-start(bf16[528,128]{1,0:T(8,128)(2,1)S(1)} %collective-permute-done.6.refs_2_), channel_id=1, source_target_pairs={{0,1},{1,0},{2,3},{3,2},{4,5},{5,4},{6,7},{7,6},{8,9},{9,8},{10,11... | collective-permute-start | bytes 405512 | tf_op jit(solution)/shard_map/ppermute | solution.py:313
  32.0 1.4 %collective-permute-start.10 = (bf16[528,128]{1,0:T(8,128)(2,1)S(1)}, bf16[528,128]{1,0:T(8,128)(2,1)S(1)}, u32[]{:S(2)}, u32[]{:S(2)}) collective-permute-start(bf16[528,128]{1,0:T(8,128)(2,1)S(1)} %collective-permute-done.5.refs_1_), channel_id=1, source_target_pairs={{0,1},{1,0},{2,3},{3,2},{4,5},{5,4},{6,7},{7,6},{8,9},{9,8},{10,11... | collective-permute-start | bytes 405512 | tf_op jit(solution)/shard_map/ppermute | solution.py:313

commit v20 on v19

--- a/solution.py
+++ b/solution.py
@@ -325,7 +325,8 @@
     obj = object_slices[0]
     windows, code = take_windows(obj, touch(obj), all_positions, window, members)
     phase, code = lax.optimization_barrier((propagator_phase, code))
-    windows = [windows[0]] + [swap(windows[m // 2], m, 0) for m in range(1, depth)]
+    arrivals = [swap(windows[m // 2], m, 0) for m in reversed(range(1, depth))]
+    windows = [windows[0]] + arrivals[::-1]
     targets = [measured] + [swap(measured, 0, home) for home in homes]
     kern = jnp.stack([jnp.cos(phase), jnp.sin(phase)])
     terms = run_waves(probe_field, kern, code, targets, windows, members)

time: 34.6 us -> 34.6 us (level)
  transfers between devices with their start and end apart: 12 -> 12, of which waited for: 7 -> 7; matrix products, arithmetic and copies ran while one was open for 1% -> 1% of each run, Pallas kernels for 6% -> 5%
where the time goes in v20:
time: 34.6 us; the launch traced here: 34.5 us
  starting transfers between devices  11.3 us (33%)
  waiting for transfers between devices  10.7 us (31%)
  Pallas kernels  9.82 us (28%)
  local copies, waits for them, and re-layouts  2.6 us (8%)
    ppermute x12, starting transfers between devices, swap(): return lax.ppermute(block, ('depth', 'dp'), route)  11.3 us
    ppermute x12, waiting for transfers between devices, swap(): return lax.ppermute(block, ('depth', 'dp'), route)  10.7 us
    pallas_call x1, Pallas kernels, run_waves(): pl.pallas_call(functools.partial(wave_kernel, members, len(measured)), ou...  7.06 us
    unnamed x14, local copies, waits for them, and re-layouts  2.36 us
    pallas_call x1, Pallas kernels, take_windows(): pl.pallas_call(functools.partial(window_kernel, members), out_shape=[jax....  1.34 us
    pallas_call x1, Pallas kernels, place_windows(): pl.pallas_call(second_kernel, out_shape=jax.ShapeDtypeStruct((2, stripe,...  1.1 us
  transfers between devices with their start and end apart: 12, of which 7 were waited for; matrix products, arithmetic and copies ran while one was open for 1% of the time, Pallas kernels for 5%

profile of v20, /device:TPU:0, one launch (start us, length us, event | category | flops | bytes accessed | tf_op | source)
XLA Modules:
  0.0 34.5 jit_solution(6310464109571241022)
XLA Ops:
  0.0 4.0 %collective-permute-start = (s32[2,2]{1,0:T(2,128)}, s32[2,2]{1,0:T(2,128)S(1)}, u32[]{:S(2)}, u32[]{:S(2)}) collective-permute-start(s32[2,2]{1,0:T(2,128)} %rest_0_.2), channel_id=1, source_target_pairs={{0,4},{1,5},{2,6},{3,7},{4,0},{5,1},{6,2},{7,3},{8,12},{9,13},{10,... | collective-permute-start | bytes 56 | tf_op jit(solution)/shard_map/ppermute | solution.py:313
  4.0 0.1 collective-permute-start.1
  4.1 2.3 %copy-done = f32[1,2,768,768]{3,2,1,0:T(8,128)S(1)} copy-done((f32[1,2,768,768]{3,2,1,0:T(8,128)S(1)}, f32[1,2,768,768]{3,2,1,0:T(8,128)}, u32[]{:S(2)}) %copy-start) | copy-done | bytes 4718616
  6.5 0.0 collective-permute-done.rest_1_
  6.5 1.3 %take_windows.1 = (bf16[2,2,128,128]{3,2,1,0:T(8,128)(2,1)S(1)}, bf16[2,2,128,128]{3,2,1,0:T(8,128)(2,1)S(1)}, bf16[16,128]{1,0:T(8,128)(2,1)S(1)}) custom-call(f32[2,768,768]{2,1,0:T(8,128)S(1)} %bitcast.7, f32[8,128]{1,0:T(8,128)S(1)} %touch_slice.1.touched_ref, s32[2,2]{1,0:T(2,128)S(1)} %copy-done.5, s32[2,2]{1,0:T(2,128)S(1)} %collective-permute-done.rest_1_), custom_call_target="tpu_custom_call" | custom-call | tf_op jit(solution)/shard_map/take_windows/pallas_call | solution.py:111
  7.8 1.9 %collective-permute-start.3 = (bf16[2,2,128,128]{3,2,1,0:T(8,128)(2,1)S(1)}, bf16[2,2,128,128]{3,2,1,0:T(8,128)(2,1)S(1)}, u32[]{:S(2)}, u32[]{:S(2)}) collective-permute-start(bf16[2,2,128,128]{3,2,1,0:T(8,128)(2,1)S(1)} %get-tuple-element.16), channel_id=1, source_target_pairs={{0,16},{1,17},{2,18},{3,19},{4,20},{5,21},{6,22},{7,23},{8,24},{9,... | collective-permute-start | bytes 393224 | tf_op jit(solution)/shard_map/ppermute | solution.py:313
  9.7 1.4 %collective-permute-start.4 = (bf16[2,2,128,128]{3,2,1,0:T(8,128)(2,1)S(1)}, bf16[2,2,128,128]{3,2,1,0:T(8,128)(2,1)S(1)}, u32[]{:S(2)}, u32[]{:S(2)}) collective-permute-start(bf16[2,2,128,128]{3,2,1,0:T(8,128)(2,1)S(1)} %get-tuple-element.16), channel_id=1, source_target_pairs={{0,24},{1,25},{2,26},{3,27},{4,28},{5,29},{6,30},{7,31},{8,16},{9,... | collective-permute-start | bytes 393224 | tf_op jit(solution)/shard_map/ppermute | solution.py:313
  11.1 0.3 collective-permute-start.2
  11.4 0.2 cosine_bitcast_fusion
  11.7 1.3 %collective-permute-done.1.rest_1_ = f32[2,128,128]{2,1,0:T(8,128)S(1)} collective-permute-done((f32[2,128,128]{2,1,0:T(8,128)}, f32[2,128,128]{2,1,0:T(8,128)S(1)}, u32[]{:S(2)}, u32[]{:S(2)}) %collective-permute-start.1) | collective-permute-done | bytes 131104 | tf_op jit(solution)/shard_map/ppermute | solution.py:313
  12.9 4.0 %collective-permute-done.2.rest_3_ = bf16[2,2,128,128]{3,2,1,0:T(8,128)(2,1)S(1)} collective-permute-done((bf16[2,2,128,128]{3,2,1,0:T(8,128)(2,1)S(1)}, bf16[2,2,128,128]{3,2,1,0:T(8,128)(2,1)S(1)}, u32[]{:S(2)}, u32[]{:S(2)}) %collective-permute-start.2) | collective-permute-done | bytes 131104 | tf_op jit(solution)/shard_map/ppermute | solution.py:313
  16.9 0.0 collective-permute-done.4.rest_5_
  16.9 7.1 %run_waves.1 = (bf16[528,128]{1,0:T(8,128)(2,1)S(1)}, bf16[528,128]{1,0:T(8,128)(2,1)S(1)}) custom-call(f32[2,128,128]{2,1,0:T(8,128)S(1)} %copy-done.3, f32[2,128,128]{2,1,0:T(8,128)S(1)} %pad_maximum_fusion.kern_ref, bf16[2,256,768]{2,1,0:T(8,128)(2,1)S(1)} %copy-done.1, bf16[2,768,256]{2,1,0:T(8,128)(2,1)S(1)} %copy-done.2, ...), custom_call_target="tpu_custom_call" | custom-call | tf_op jit(solution)/shard_map/run_waves/pallas_call | solution.py:219
  24.0 2.6 %collective-permute-start.7 = (bf16[528,128]{1,0:T(8,128)(2,1)S(1)}, bf16[528,128]{1,0:T(8,128)(2,1)S(1)}, u32[]{:S(2)}, u32[]{:S(2)}) collective-permute-start(bf16[528,128]{1,0:T(8,128)(2,1)S(1)} %get-tuple-element.18), channel_id=1, source_target_pairs={{0,18},{1,19},{2,16},{3,17},{4,22},{5,23},{6,20},{7,21},{8,26},{9,... | collective-permute-start | bytes 405512 | tf_op jit(solution)/shard_map/ppermute | solution.py:313
  26.6 0.4 %collective-permute-start.6 = (bf16[528,128]{1,0:T(8,128)(2,1)S(1)}, bf16[528,128]{1,0:T(8,128)(2,1)S(1)}, u32[]{:S(2)}, u32[]{:S(2)}) collective-permute-start(bf16[528,128]{1,0:T(8,128)(2,1)S(1)} %get-tuple-element.17.refs_0_), channel_id=1, source_target_pairs={{0,2},{1,3},{2,0},{3,1},{4,6},{5,7},{6,4},{7,5},{8,10},{9,11},{10,... | collective-permute-start | bytes 405512 | tf_op jit(solution)/shard_map/ppermute | solution.py:313
  27.0 0.5 %collective-permute-start.5 = (bf16[528,128]{1,0:T(8,128)(2,1)S(1)}, bf16[528,128]{1,0:T(8,128)(2,1)S(1)}, u32[]{:S(2)}, u32[]{:S(2)}) collective-permute-start(bf16[528,128]{1,0:T(8,128)(2,1)S(1)} %get-tuple-element.18), channel_id=1, source_target_pairs={{0,16},{1,17},{2,18},{3,19},{4,20},{5,21},{6,22},{7,23},{8,24},{9,... | collective-permute-start | bytes 405512 | tf_op jit(solution)/shard_map/ppermute | solution.py:313
  27.6 2.7 %collective-permute-done.7.refs_3_ = bf16[528,128]{1,0:T(8,128)(2,1)S(1)} collective-permute-done((bf16[528,128]{1,0:T(8,128)(2,1)S(1)}, bf16[528,128]{1,0:T(8,128)(2,1)S(1)}, u32[]{:S(2)}, u32[]{:S(2)}) %collective-permute-start.7) | collective-permute-done | bytes 135200 | tf_op jit(solution)/shard_map/ppermute | solution.py:313
  30.3 1.3 %collective-permute-done.6.refs_2_ = bf16[528,128]{1,0:T(8,128)(2,1)S(1)} collective-permute-done((bf16[528,128]{1,0:T(8,128)(2,1)S(1)}, bf16[528,128]{1,0:T(8,128)(2,1)S(1)}, u32[]{:S(2)}, u32[]{:S(2)}) %collective-permute-start.6) | collective-permute-done | bytes 135200 | tf_op jit(solution)/shard_map/ppermute | solution.py:313
  31.6 0.4 %collective-permute-done.5.refs_1_ = bf16[528,128]{1,0:T(8,128)(2,1)S(1)} collective-permute-done((bf16[528,128]{1,0:T(8,128)(2,1)S(1)}, bf16[528,128]{1,0:T(8,128)(2,1)S(1)}, u32[]{:S(2)}, u32[]{:S(2)}) %collective-permute-start.5) | collective-permute-done | bytes 135200 | tf_op jit(solution)/shard_map/ppermute | solution.py:313
  32.0 0.1 collective-permute-start.10
  32.1 0.3 place_near.1.start_ref
  32.5 0.5 %collective-permute-done.11.refs_1_ = bf16[528,128]{1,0:T(8,128)(2,1)S(1)} collective-permute-done((bf16[528,128]{1,0:T(8,128)(2,1)S(1)}, bf16[528,128]{1,0:T(8,128)(2,1)S(1)}, u32[]{:S(2)}, u32[]{:S(2)}) %collective-permute-start.11) | collective-permute-done | bytes 135200 | tf_op jit(solution)/shard_map/ppermute | solution.py:313
  33.0 0.4 %collective-permute-done.10.refs_0_ = bf16[528,128]{1,0:T(8,128)(2,1)S(1)} collective-permute-done((bf16[528,128]{1,0:T(8,128)(2,1)S(1)}, bf16[528,128]{1,0:T(8,128)(2,1)S(1)}, u32[]{:S(2)}, u32[]{:S(2)}) %collective-permute-start.10) | collective-permute-done | bytes 135200 | tf_op jit(solution)/shard_map/ppermute | solution.py:313
  33.4 1.1 %place_far.1 = f32[2,96,768]{2,1,0:T(8,128)} custom-call(f32[2,360,896]{2,1,0:T(8,128)S(1)} %place_near.1.start_ref, bf16[528,128]{1,0:T(8,128)(2,1)S(1)} %collective-permute-done.10.refs_0_, bf16[528,128]{1,0:T(8,128)(2,1)S(1)} %collective-permute-done.11.refs_1_), custom_call_target="tpu_custom_call" | custom-call | tf_op jit(solution)/shard_map/place_far/pallas_call | solution.py:295
  (21 shorter events, 0.1 us)
Async XLA Ops:
  0.0 6.5 %copy-start.5 = (s32[2,2]{1,0:T(2,128)S(1)}, s32[2,2]{1,0:T(2,128)}, u32[]{:S(2)}) copy-start(s32[2,2]{1,0:T(2,128)} %rest_0_.2) | copy-start | bytes 52
  0.0 6.5 %collective-permute-start = (s32[2,2]{1,0:T(2,128)}, s32[2,2]{1,0:T(2,128)S(1)}, u32[]{:S(2)}, u32[]{:S(2)}) collective-permute-start(s32[2,2]{1,0:T(2,128)} %rest_0_.2), channel_id=1, source_target_pairs={{0,4},{1,5},{2,6},{3,7},{4,0},{5,1},{6,2},{7,3},{8,12},{9,13},{10,... | collective-permute-start | bytes 56 | tf_op jit(solution)/shard_map/ppermute | solution.py:313
  4.0 8.9 %collective-permute-start.1 = (f32[2,128,128]{2,1,0:T(8,128)}, f32[2,128,128]{2,1,0:T(8,128)S(1)}, u32[]{:S(2)}, u32[]{:S(2)}) collective-permute-start(f32[2,128,128]{2,1,0:T(8,128)} %rest_0_.3), channel_id=1, source_target_pairs={{0,4},{1,5},{2,6},{3,7},{4,0},{5,1},{6,2},{7,3},{8,12},{9,13},{10,... | collective-permute-start | bytes 393224 | tf_op jit(solution)/shard_map/ppermute | solution.py:313
  4.1 2.3 %copy-start = (f32[1,2,768,768]{3,2,1,0:T(8,128)S(1)}, f32[1,2,768,768]{3,2,1,0:T(8,128)}, u32[]{:S(2)}) copy-start(f32[1,2,768,768]{3,2,1,0:T(8,128)} %param.7) | copy-start | bytes 14155780
  6.4 5.0 %copy-start.6 = (f32[128,128]{1,0:T(8,128)S(1)}, f32[128,128]{1,0:T(8,128)}, u32[]{:S(2)}) copy-start(f32[128,128]{1,0:T(8,128)} %param.10) | copy-start | bytes 196612
  6.4 10.5 %copy-start.1 = (bf16[2,256,768]{2,1,0:T(8,128)(2,1)S(1)}, bf16[2,256,768]{2,1,0:T(8,128)(2,1)}, u32[]{:S(2)}) copy-start(bf16[2,256,768]{2,1,0:T(8,128)(2,1)} %constant.4.clone.left_ref) | copy-start | bytes 2359300
  6.4 10.5 %copy-start.2 = (bf16[2,768,256]{2,1,0:T(8,128)(2,1)S(1)}, bf16[2,768,256]{2,1,0:T(8,128)(2,1)}, u32[]{:S(2)}) copy-start(bf16[2,768,256]{2,1,0:T(8,128)(2,1)} %constant.5.clone.right_ref) | copy-start | bytes 2359300
  6.4 10.5 %copy-start.3 = (f32[2,128,128]{2,1,0:T(8,128)S(1)}, f32[2,128,128]{2,1,0:T(8,128)}, u32[]{:S(2)}) copy-start(f32[2,128,128]{2,1,0:T(8,128)} %probe_ref.1) | copy-start | bytes 393220
  6.5 10.5 %copy-start.4 = (f32[2,128,128]{2,1,0:T(8,128)S(1)}, f32[2,128,128]{2,1,0:T(8,128)}, u32[]{:S(2)}) copy-start(f32[2,128,128]{2,1,0:T(8,128)} %rest_0_.3) | copy-start | bytes 393220
  7.8 9.1 %collective-permute-start.3 = (bf16[2,2,128,128]{3,2,1,0:T(8,128)(2,1)S(1)}, bf16[2,2,128,128]{3,2,1,0:T(8,128)(2,1)S(1)}, u32[]{:S(2)}, u32[]{:S(2)}) collective-permute-start(bf16[2,2,128,128]{3,2,1,0:T(8,128)(2,1)S(1)} %get-tuple-element.16), channel_id=1, source_target_pairs={{0,16},{1,17},{2,18},{3,19},{4,20},{5,21},{6,22},{7,23},{8,24},{9,... | collective-permute-start | bytes 393224 | tf_op jit(solution)/shard_map/ppermute | solution.py:313
  9.7 7.2 %collective-permute-start.4 = (bf16[2,2,128,128]{3,2,1,0:T(8,128)(2,1)S(1)}, bf16[2,2,128,128]{3,2,1,0:T(8,128)(2,1)S(1)}, u32[]{:S(2)}, u32[]{:S(2)}) collective-permute-start(bf16[2,2,128,128]{3,2,1,0:T(8,128)(2,1)S(1)} %get-tuple-element.16), channel_id=1, source_target_pairs={{0,24},{1,25},{2,26},{3,27},{4,28},{5,29},{6,30},{7,31},{8,16},{9,... | collective-permute-start | bytes 393224 | tf_op jit(solution)/shard_map/ppermute | solution.py:313
  11.1 5.8 %collective-permute-start.2 = (bf16[2,2,128,128]{3,2,1,0:T(8,128)(2,1)S(1)}, bf16[2,2,128,128]{3,2,1,0:T(8,128)(2,1)S(1)}, u32[]{:S(2)}, u32[]{:S(2)}) collective-permute-start(bf16[2,2,128,128]{3,2,1,0:T(8,128)(2,1)S(1)} %get-tuple-element.15.rest_2_), channel_id=1, source_target_pairs={{0,8},{1,9},{2,10},{3,11},{4,12},{5,13},{6,14},{7,15},{8,0},{9,1},... | collective-permute-start | bytes 393224 | tf_op jit(solution)/shard_map/ppermute | solution.py:313
  24.0 6.3 %collective-permute-start.7 = (bf16[528,128]{1,0:T(8,128)(2,1)S(1)}, bf16[528,128]{1,0:T(8,128)(2,1)S(1)}, u32[]{:S(2)}, u32[]{:S(2)}) collective-permute-start(bf16[528,128]{1,0:T(8,128)(2,1)S(1)} %get-tuple-element.18), channel_id=1, source_target_pairs={{0,18},{1,19},{2,16},{3,17},{4,22},{5,23},{6,20},{7,21},{8,26},{9,... | collective-permute-start | bytes 405512 | tf_op jit(solution)/shard_map/ppermute | solution.py:313
  26.6 5.0 %collective-permute-start.6 = (bf16[528,128]{1,0:T(8,128)(2,1)S(1)}, bf16[528,128]{1,0:T(8,128)(2,1)S(1)}, u32[]{:S(2)}, u32[]{:S(2)}) collective-permute-start(bf16[528,128]{1,0:T(8,128)(2,1)S(1)} %get-tuple-element.17.refs_0_), channel_id=1, source_target_pairs={{0,2},{1,3},{2,0},{3,1},{4,6},{5,7},{6,4},{7,5},{8,10},{9,11},{10,... | collective-permute-start | bytes 405512 | tf_op jit(solution)/shard_map/ppermute | solution.py:313
  27.0 5.0 %collective-permute-start.5 = (bf16[528,128]{1,0:T(8,128)(2,1)S(1)}, bf16[528,128]{1,0:T(8,128)(2,1)S(1)}, u32[]{:S(2)}, u32[]{:S(2)}) collective-permute-start(bf16[528,128]{1,0:T(8,128)(2,1)S(1)} %get-tuple-element.18), channel_id=1, source_target_pairs={{0,16},{1,17},{2,18},{3,19},{4,20},{5,21},{6,22},{7,23},{8,24},{9,... | collective-permute-start | bytes 405512 | tf_op jit(solution)/shard_map/ppermute | solution.py:313
  27.6 4.6 %collective-permute-start.8 = (bf16[528,128]{1,0:T(8,128)(2,1)S(1)}, bf16[528,128]{1,0:T(8,128)(2,1)S(1)}, u32[]{:S(2)}, u32[]{:S(2)}) collective-permute-start(bf16[528,128]{1,0:T(8,128)(2,1)S(1)} %get-tuple-element.17.refs_0_), channel_id=1, source_target_pairs={{0,1},{1,0},{2,3},{3,2},{4,5},{5,4},{6,7},{7,6},{8,9},{9,8},{10,11... | collective-permute-start | bytes 405512 | tf_op jit(solution)/shard_map/ppermute | solution.py:313
  30.3 1.8 %collective-permute-start.9 = (bf16[528,128]{1,0:T(8,128)(2,1)S(1)}, bf16[528,128]{1,0:T(8,128)(2,1)S(1)}, u32[]{:S(2)}, u32[]{:S(2)}) collective-permute-start(bf16[528,128]{1,0:T(8,128)(2,1)S(1)} %collective-permute-done.7.refs_3_), channel_id=1, source_target_pairs={{0,1},{1,0},{2,3},{3,2},{4,5},{5,4},{6,7},{7,6},{8,9},{9,8},{10,11... | collective-permute-start | bytes 405512 | tf_op jit(solution)/shard_map/ppermute | solution.py:313
  31.6 1.4 %collective-permute-start.11 = (bf16[528,128]{1,0:T(8,128)(2,1)S(1)}, bf16[528,128]{1,0:T(8,128)(2,1)S(1)}, u32[]{:S(2)}, u32[]{:S(2)}) collective-permute-start(bf16[528,128]{1,0:T(8,128)(2,1)S(1)} %collective-permute-done.6.refs_2_), channel_id=1, source_target_pairs={{0,1},{1,0},{2,3},{3,2},{4,5},{5,4},{6,7},{7,6},{8,9},{9,8},{10,11... | collective-permute-start | bytes 405512 | tf_op jit(solution)/shard_map/ppermute | solution.py:313
  32.0 1.4 %collective-permute-start.10 = (bf16[528,128]{1,0:T(8,128)(2,1)S(1)}, bf16[528,128]{1,0:T(8,128)(2,1)S(1)}, u32[]{:S(2)}, u32[]{:S(2)}) collective-permute-start(bf16[528,128]{1,0:T(8,128)(2,1)S(1)} %collective-permute-done.5.refs_1_), channel_id=1, source_target_pairs={{0,1},{1,0},{2,3},{3,2},{4,5},{5,4},{6,7},{7,6},{8,9},{9,8},{10,11... | collective-permute-start | bytes 405512 | tf_op jit(solution)/shard_map/ppermute | solution.py:313
